TPU v7x, 32 devices: a whole 2x2x4 slice. The times are simulated.
32 devices in a mesh: clips: 2 (over y), patch: 16 (over z, x, core).
Axes of the slice: x: 2, y: 2, z: 4, core: 2. Of those that a mesh axis runs over, the one named last changes fastest.
Arguments:
- queries: bfloat16 [1024, 2560], P(('clips', 'patch')), parts along dimension 0, may hold values from -130 to 130
- keys_new: bfloat16 [1024, 2560], P(('clips', 'patch')), parts along dimension 0, may hold values from -6 to 6
- values_new: bfloat16 [1024, 2560], P(('clips', 'patch')), parts along dimension 0, may hold values from -6 to 6
- keys_copy: bfloat16 [32, 512, 640], P(('clips', 'patch')), parts along dimension 0, may hold values from -6 to 6, as said below
- values_copy: bfloat16 [32, 512, 640], P(('clips', 'patch')), parts along dimension 0, may hold values from -6 to 6, as said below
- key_bounds: float32 [1024, 20], P('clips'), parts along dimension 0, may hold values from 0.5 to 3
- value_bounds: float32 [1024, 20], P('clips'), parts along dimension 0, may hold values from 0.5 to 3
Outputs:
- attended: bfloat16 [1024, 2560], P(('clips', 'patch')), parts along dimension 0
There are 2 independent parts, one for each index of `clips`. A program takes and returns all parts, laid end to end along the dimension named above; each array names one. Nothing has to cross between parts.
Inputs may be any that keep to these rules, and one draw needn't show every extreme that they name: `keys_copy`: copies p and q are equal when p % 4 == q % 4; copy p holds features (p % 4) * 640 onward of one previous-step key array. `values_copy`: copies p and q are equal when p % 4 == q % 4; copy p holds features (p % 4) * 640 onward of one previous-step value array.
All inputs are finite; a program needn't handle non-finite values.
Results may differ from a plain program's by a relative error of at most 0.0083.
Values may be sent and summed in bfloat16 or wider, within the bound.
No kernel may reach another device: no remote copies, remote signals or barrier semaphores. Data moves between devices by JAX's collectives and lax.ppermute only.
A program may use at most 128 MiB of HBM per device.

v0:
```python
import jax
import jax.numpy as jnp
from jax import lax
from jax.sharding import PartitionSpec as P


def swapped(array, axis, distance):
    return lax.ppermute(array, axis, [(i, i ^ 1 << distance) for i in range(lax.axis_size(axis))])


def clamped(current, previous, bounds, head_size):
    limits = jnp.repeat(bounds, head_size, axis=1)
    return jnp.clip(
        current.astype(jnp.float32) - previous.astype(jnp.float32), -limits, limits
    ).astype(jnp.bfloat16)


def restore(previous, change):
    return (previous.astype(jnp.float32) + change.astype(jnp.float32)).astype(jnp.bfloat16)


def shards(queries, keys_new, values_new, keys_copy, values_copy, key_bounds, value_bounds):
    tok_rows = queries.shape[0]
    feature_count = queries.shape[1]
    head_count = key_bounds.shape[1]
    head_size = feature_count // head_count
    quarter_heads = head_count // 4
    quarter_width = feature_count // 4
    group_rows = 4 * tok_rows
    all_tokens = keys_copy.shape[1]
    factor = head_size ** (-0.5)
    place = lax.axis_index("patch")
    member = place % 4
    levels = lax.axis_size("patch").bit_length() - 1
    blocks = (
        jnp.stack([queries, keys_new, values_new])
        .reshape(3, tok_rows, 4, quarter_width)
        .transpose(2, 0, 1, 3)
    )
    for bit in (0, 1):
        mine = place >> bit & 1
        paired = blocks.reshape(blocks.shape[0] // 2, 2, 3, blocks.shape[2], quarter_width)
        keep = jnp.where(mine == 0, paired[:, 0], paired[:, 1])
        sending = jnp.where(mine == 0, paired[:, 1], paired[:, 0])
        arrived = swapped(sending, "patch", bit)
        lower = jnp.where(mine == 0, keep, arrived)
        upper = jnp.where(mine == 0, arrived, keep)
        blocks = jnp.concatenate([lower, upper], axis=2)
    query_group = blocks[0, 0]
    key_group = blocks[0, 1]
    value_group = blocks[0, 2]
    row_start = place // 4 * group_rows
    head_start = member * quarter_heads
    key_limits = lax.dynamic_slice(key_bounds, (row_start, head_start), (group_rows, quarter_heads))
    value_limits = lax.dynamic_slice(
        value_bounds, (row_start, head_start), (group_rows, quarter_heads)
    )
    own_keys = lax.dynamic_slice_in_dim(keys_copy[0], row_start, group_rows, 0)
    own_values = lax.dynamic_slice_in_dim(values_copy[0], row_start, group_rows, 0)
    changes = jnp.stack(
        [
            clamped(key_group, own_keys, key_limits, head_size),
            clamped(value_group, own_values, value_limits, head_size),
        ]
    )
    bit_list = list(range(2, levels))
    gathered = changes
    for bit in bit_list:
        mine = place >> bit & 1
        arrived = swapped(gathered, "patch", bit)
        lower = jnp.where(mine == 0, gathered, arrived)
        upper = jnp.where(mine == 0, arrived, gathered)
        gathered = jnp.stack([lower, upper], axis=1)
    gathered = gathered.reshape(2, all_tokens, quarter_width)
    keys_used = restore(keys_copy[0], gathered[0]).reshape(all_tokens, quarter_heads, head_size)
    values_used = restore(values_copy[0], gathered[1]).reshape(all_tokens, quarter_heads, head_size)
    query_heads = query_group.reshape(group_rows, quarter_heads, head_size)
    scores = (
        jnp.einsum("qhd,khd->hqk", query_heads, keys_used, preferred_element_type=jnp.float32)
        * factor
    )
    peaks = jnp.max(scores, axis=2, keepdims=True)
    probs = jnp.exp(scores - peaks)
    totals = jnp.sum(probs, axis=2)
    weighted = jnp.einsum(
        "hqk,khd->qhd", probs.astype(jnp.bfloat16), values_used, preferred_element_type=jnp.float32
    )
    result = (
        (weighted / totals.T[:, :, None]).reshape(group_rows, quarter_width).astype(jnp.bfloat16)
    )
    pieces = result[None]
    for bit in (1, 0):
        mine = place >> bit & 1
        half = pieces.shape[1] // 2
        first = pieces[:, :half]
        second = pieces[:, half:]
        keep = jnp.where(mine == 0, first, second)
        sending = jnp.where(mine == 0, second, first)
        arrived = swapped(sending, "patch", bit)
        lower = jnp.where(mine == 0, keep, arrived)
        upper = jnp.where(mine == 0, arrived, keep)
        pieces = jnp.stack([lower, upper], axis=1).reshape(-1, half, quarter_width)
    return pieces.transpose(1, 0, 2).reshape(tok_rows, feature_count)


def solution(mesh):
    placed = (
        P(("clips", "patch"), None),
        P(("clips", "patch"), None),
        P(("clips", "patch"), None),
        P(("clips", "patch"), None, None),
        P(("clips", "patch"), None, None),
        P("clips", None),
        P("clips", None),
    )
    return jax.shard_map(
        shards, mesh=mesh, in_specs=placed, out_specs=P(("clips", "patch"), None), check_vma=False
    )
```

profile of v0, /device:TPU:0, one launch (start us, length us, event | category | flops | bytes accessed | tf_op | source)
XLA Modules:
  0.0 84.5 jit_solution(10636897927281005034)
XLA Ops:
  0.0 1.0 %stack.53 = bf16[1,32,4,640]{3,2,1,0:T(4,128)(2,1)S(1)} reshape(bf16[32,2560]{1,0:T(8,128)(2,1)} %param.7) | data formatting | bytes 327680 | tf_op jit(solution)/shard_map/stack | solution.py:36
  1.0 1.0 %stack.54 = bf16[1,32,4,640]{3,2,1,0:T(4,128)(2,1)S(1)} reshape(bf16[32,2560]{1,0:T(8,128)(2,1)} %param.8) | data formatting | bytes 327680 | tf_op jit(solution)/shard_map/stack | solution.py:36
  1.9 1.0 %stack.55 = bf16[1,32,4,640]{3,2,1,0:T(4,128)(2,1)S(1)} reshape(bf16[32,2560]{1,0:T(8,128)(2,1)} %param.9) | data formatting | bytes 327680 | tf_op jit(solution)/shard_map/stack | solution.py:36
  5.4 1.1 %collective-permute-done = bf16[2,3,32,640]{3,2,1,0:T(8,128)(2,1)S(1)} collective-permute-done((bf16[2,3,32,640]{3,2,1,0:T(8,128)(2,1)S(1)}, bf16[2,3,32,640]{3,2,1,0:T(8,128)(2,1)S(1)}, u32[]{:S(2)}, u32[]{:S(2)}) %collective-permute-start) | collective-permute-done | bytes 245792 | tf_op jit(solution)/shard_map/ppermute | solution.py:8
  7.7 0.8 select_bitcast_fusion.3
  8.6 2.9 %collective-permute-start.1 = (bf16[1,3,64,640]{2,3,1,0:T(8,128)(2,1)}, bf16[1,3,64,640]{2,3,1,0:T(8,128)(2,1)}, u32[]{:S(2)}, u32[]{:S(2)}) collective-permute-start(bf16[1,3,64,640]{2,3,1,0:T(8,128)(2,1)} %select_bitcast_fusion.3), channel_id=1, source_target_pairs={{0,2},{1,3},{2,0},{3,1},{4,6},{5,7},{6,4},{7,5},{8,10},{9,11},{10,... | collective-permute-start | bytes 737288 | tf_op jit(solution)/shard_map/ppermute | solution.py:8
  11.4 0.8 dynamic_slice.12
  12.2 0.8 dynamic_slice.14
  13.5 9.8 %collective-permute-done.1 = bf16[1,3,64,640]{2,3,1,0:T(8,128)(2,1)} collective-permute-done((bf16[1,3,64,640]{2,3,1,0:T(8,128)(2,1)}, bf16[1,3,64,640]{2,3,1,0:T(8,128)(2,1)}, u32[]{:S(2)}, u32[]{:S(2)}) %collective-permute-start.1) | collective-permute-done | bytes 245792 | tf_op jit(solution)/shard_map/ppermute | solution.py:8
  23.3 1.1 %bitcast_select_fusion.3 = (bf16[1,3,64,640]{2,3,1,0:T(8,128)(2,1)S(1)}, bf16[1,3,64,640]{2,3,1,0:T(8,128)(2,1)S(1)}) fusion(bf16[1,3,64,640]{2,3,1,0:T(8,128)(2,1)} %collective-permute-done.1, pred[]{:T(512)S(6)} %eq.11, bf16[1,2,3,64,640]{3,4,2,1,0:T(8,128)(2,1)S(1)} %maximum_bitcast_fusion), kind=kLoop, calls=%fused_computation.30 | loop fusion | flops 368640 | bytes 1229824 | tf_op jit(solution)/shard_map/jit(_where)/select_n | solution.py:46
  24.7 1.9 %collective-permute-start.2 = (bf16[2,128,640]{1,2,0:T(8,128)(2,1)S(1)}, bf16[2,128,640]{1,2,0:T(8,128)(2,1)S(1)}, u32[]{:S(2)}, u32[]{:S(2)}) collective-permute-start(bf16[2,128,640]{1,2,0:T(8,128)(2,1)S(1)} %pad_maximum_fusion.2), channel_id=1, source_target_pairs={{0,4},{1,5},{2,6},{3,7},{4,0},{5,1},{6,2},{7,3},{8,12},{9,13},{10,... | collective-permute-start | bytes 983048 | tf_op jit(solution)/shard_map/ppermute | solution.py:8
  26.6 7.4 %collective-permute-done.2 = bf16[2,128,640]{1,2,0:T(8,128)(2,1)S(1)} collective-permute-done((bf16[2,128,640]{1,2,0:T(8,128)(2,1)S(1)}, bf16[2,128,640]{1,2,0:T(8,128)(2,1)S(1)}, u32[]{:S(2)}, u32[]{:S(2)}) %collective-permute-start.2) | collective-permute-done | bytes 327712 | tf_op jit(solution)/shard_map/ppermute | solution.py:8
  34.2 2.6 %collective-permute-start.3 = (bf16[2,2,128,640]{2,3,0,1:T(8,128)(2,1)S(1)}, bf16[2,2,128,640]{2,3,0,1:T(8,128)(2,1)}, u32[]{:S(2)}, u32[]{:S(2)}) collective-permute-start(bf16[2,2,128,640]{2,3,0,1:T(8,128)(2,1)S(1)} %pad_maximum_fusion.1), channel_id=1, source_target_pairs={{0,8},{1,9},{2,10},{3,11},{4,12},{5,13},{6,14},{7,15},{8,0},{9,1},... | collective-permute-start | bytes 1966088 | tf_op jit(solution)/shard_map/ppermute | solution.py:8
  36.9 27.8 %collective-permute-done.3 = bf16[2,2,128,640]{2,3,0,1:T(8,128)(2,1)} collective-permute-done((bf16[2,2,128,640]{2,3,0,1:T(8,128)(2,1)S(1)}, bf16[2,2,128,640]{2,3,0,1:T(8,128)(2,1)}, u32[]{:S(2)}, u32[]{:S(2)}) %collective-permute-start.3) | collective-permute-done | bytes 655392 | tf_op jit(solution)/shard_map/ppermute | solution.py:8
  64.6 1.2 %select_bitcast_fusion.2 = (bf16[2,1,2,128,640]{3,4,0,2,1:T(8,128)(2,1)S(1)}, bf16[2,1,2,128,640]{3,4,0,2,1:T(8,128)(2,1)S(1)}) fusion(bf16[2,2,128,640]{2,3,0,1:T(8,128)(2,1)} %collective-permute-done.3, pred[]{:T(512)S(6)} %eq.12, bf16[2,1,128,640]{2,3,0,1:T(8,128)(2,1)S(1)} %get-tuple-element.16, bf16[2,1,128,640]{2,3,0,1:T(8,128)(2,1)S(1)} %get-tuple-element.15), kind=kLoop, calls=%fused_computation.25 | loop fusion | flops 983040 | bytes 2621441 | tf_op jit(solution)/shard_map/stack | solution.py:73
  65.8 1.2 %fusion.10 = (f32[1,2,2,128,640]{3,4,0,2,1:T(8,128)S(1)}, f32[1,2,2,128,640]{3,4,0,2,1:T(8,128)}) fusion(bf16[2,1,2,128,640]{3,4,0,2,1:T(8,128)(2,1)S(1)} %get-tuple-element.11, bf16[2,1,2,128,640]{3,4,0,2,1:T(8,128)(2,1)S(1)} %get-tuple-element.12), kind=kLoop, calls=%fused_computation.19 | loop fusion | flops 1310720 | bytes 3932160 | tf_op jit(solution)/shard_map/convert_element_type | solution.py:19
  67.1 1.0 %copy.51 = f32[1,2,2,128,640]{3,2,1,4,0:T(2,128)S(1)} copy(f32[1,2,2,128,640]{3,4,0,2,1:T(8,128)S(1)} %get-tuple-element.9) | data formatting | bytes 2621440 | tf_op jit(solution)/shard_map/convert_element_type | solution.py:19
  68.1 1.1 %reshape.165 = f32[512,5,128]{0,2,1:T(8,128)S(1)} reshape(f32[1,2,2,128,640]{3,2,1,4,0:T(2,128)S(1)} %copy.51) | data formatting | bytes 2621440 | tf_op jit(solution)/shard_map/convert_element_type | solution.py:19
  69.1 3.4 %copy.53 = f32[1,2,2,128,640]{3,2,1,4,0:T(2,128)} copy(f32[1,2,2,128,640]{3,4,0,2,1:T(8,128)} %get-tuple-element.10) | data formatting | bytes 2621440 | tf_op jit(solution)/shard_map/convert_element_type | solution.py:19
  72.5 2.3 %reshape.167 = f32[512,5,128]{0,2,1:T(8,128)S(1)} reshape(f32[1,2,2,128,640]{3,2,1,4,0:T(2,128)} %copy.53) | data formatting | bytes 2621440 | tf_op jit(solution)/shard_map/convert_element_type | solution.py:19
  74.9 1.5 %fusion.23 = (f32[5,128]{1,0:T(8,128)S(1)}, f32[5,128,512]{2,1,0:T(8,128)S(1)}) fusion(bf16[128,5,128]{0,2,1:T(8,128)(2,1)S(1)} %bitcast.91, f32[512,5,128]{0,2,1:T(8,128)S(1)} %reshape.167, bf16[512,5,128]{0,2,1:T(8,128)(2,1)} %bitcast.87), kind=kOutput, calls=%fused_computation.65 | convolution fusion | flops 85523840 | bytes 3443200 | tf_op jit(solution)/shard_map/qhd,khd->hqk/dot_general | solution.py:79
  77.8 1.1 %collective-permute-start.4 = (bf16[1,64,640]{2,1,0:T(8,128)(2,1)S(1)}, bf16[1,64,640]{2,1,0:T(8,128)(2,1)S(1)}, u32[]{:S(2)}, u32[]{:S(2)}) collective-permute-start(bf16[1,64,640]{2,1,0:T(8,128)(2,1)S(1)} %broadcast_select_fusion.2), channel_id=1, source_target_pairs={{0,2},{1,3},{2,0},{3,1},{4,6},{5,7},{6,4},{7,5},{8,10},{9,11},{10,... | collective-permute-start | bytes 245768 | tf_op jit(solution)/shard_map/ppermute | solution.py:8
  78.9 3.4 %collective-permute-done.4 = bf16[1,64,640]{2,1,0:T(8,128)(2,1)S(1)} collective-permute-done((bf16[1,64,640]{2,1,0:T(8,128)(2,1)S(1)}, bf16[1,64,640]{2,1,0:T(8,128)(2,1)S(1)}, u32[]{:S(2)}, u32[]{:S(2)}) %collective-permute-start.4) | collective-permute-done | bytes 81952 | tf_op jit(solution)/shard_map/ppermute | solution.py:8
  82.4 1.3 %collective-permute-done.5 = bf16[2,32,640]{2,1,0:T(8,128)(2,1)S(1)} collective-permute-done((bf16[2,32,640]{2,1,0:T(8,128)(2,1)S(1)}, bf16[2,32,640]{2,1,0:T(8,128)(2,1)S(1)}, u32[]{:S(2)}, u32[]{:S(2)}) %collective-permute-start.5) | collective-permute-done | bytes 81952 | tf_op jit(solution)/shard_map/ppermute | solution.py:8
  (37 shorter events, 6.9 us)
Async XLA Ops:
  4.8 1.7 %collective-permute-start = (bf16[2,3,32,640]{3,2,1,0:T(8,128)(2,1)S(1)}, bf16[2,3,32,640]{3,2,1,0:T(8,128)(2,1)S(1)}, u32[]{:S(2)}, u32[]{:S(2)}) collective-permute-start(bf16[2,3,32,640]{3,2,1,0:T(8,128)(2,1)S(1)} %copy.46), channel_id=1, source_target_pairs={{0,1},{1,0},{2,3},{3,2},{4,5},{5,4},{6,7},{7,6},{8,9},{9,8},{10,11... | collective-permute-start | bytes 737288 | tf_op jit(solution)/shard_map/ppermute | solution.py:8
  7.7 5.3 %copy-start.1 = (bf16[1,512,640]{2,1,0:T(8,128)(2,1)S(1)}, bf16[1,512,640]{2,1,0:T(8,128)(2,1)}, u32[]{:S(2)}) copy-start(bf16[1,512,640]{2,1,0:T(8,128)(2,1)} %param.10) | copy-start | bytes 1966084
  7.7 5.5 %copy-start.2 = (bf16[1,512,640]{2,1,0:T(8,128)(2,1)S(1)}, bf16[1,512,640]{2,1,0:T(8,128)(2,1)}, u32[]{:S(2)}) copy-start(bf16[1,512,640]{2,1,0:T(8,128)(2,1)} %param.11) | copy-start | bytes 1966084
  8.6 14.7 %collective-permute-start.1 = (bf16[1,3,64,640]{2,3,1,0:T(8,128)(2,1)}, bf16[1,3,64,640]{2,3,1,0:T(8,128)(2,1)}, u32[]{:S(2)}, u32[]{:S(2)}) collective-permute-start(bf16[1,3,64,640]{2,3,1,0:T(8,128)(2,1)} %select_bitcast_fusion.3), channel_id=1, source_target_pairs={{0,2},{1,3},{2,0},{3,1},{4,6},{5,7},{6,4},{7,5},{8,10},{9,11},{10,... | collective-permute-start | bytes 737288 | tf_op jit(solution)/shard_map/ppermute | solution.py:8
  13.3 11.1 %copy-start = (bf16[1,512,640]{1,2,0:T(8,128)(2,1)}, bf16[1,512,640]{1,2,0:T(8,128)(2,1)S(1)}, u32[]{:S(2)}) copy-start(bf16[1,512,640]{1,2,0:T(8,128)(2,1)S(1)} %copy.49) | copy-start | bytes 1966084
  24.7 9.3 %collective-permute-start.2 = (bf16[2,128,640]{1,2,0:T(8,128)(2,1)S(1)}, bf16[2,128,640]{1,2,0:T(8,128)(2,1)S(1)}, u32[]{:S(2)}, u32[]{:S(2)}) collective-permute-start(bf16[2,128,640]{1,2,0:T(8,128)(2,1)S(1)} %pad_maximum_fusion.2), channel_id=1, source_target_pairs={{0,4},{1,5},{2,6},{3,7},{4,0},{5,1},{6,2},{7,3},{8,12},{9,13},{10,... | collective-permute-start | bytes 983048 | tf_op jit(solution)/shard_map/ppermute | solution.py:8
  34.2 30.5 %collective-permute-start.3 = (bf16[2,2,128,640]{2,3,0,1:T(8,128)(2,1)S(1)}, bf16[2,2,128,640]{2,3,0,1:T(8,128)(2,1)}, u32[]{:S(2)}, u32[]{:S(2)}) collective-permute-start(bf16[2,2,128,640]{2,3,0,1:T(8,128)(2,1)S(1)} %pad_maximum_fusion.1), channel_id=1, source_target_pairs={{0,8},{1,9},{2,10},{3,11},{4,12},{5,13},{6,14},{7,15},{8,0},{9,1},... | collective-permute-start | bytes 1966088 | tf_op jit(solution)/shard_map/ppermute | solution.py:8
  77.8 4.5 %collective-permute-start.4 = (bf16[1,64,640]{2,1,0:T(8,128)(2,1)S(1)}, bf16[1,64,640]{2,1,0:T(8,128)(2,1)S(1)}, u32[]{:S(2)}, u32[]{:S(2)}) collective-permute-start(bf16[1,64,640]{2,1,0:T(8,128)(2,1)S(1)} %broadcast_select_fusion.2), channel_id=1, source_target_pairs={{0,2},{1,3},{2,0},{3,1},{4,6},{5,7},{6,4},{7,5},{8,10},{9,11},{10,... | collective-permute-start | bytes 245768 | tf_op jit(solution)/shard_map/ppermute | solution.py:8
  82.4 1.3 %collective-permute-start.5 = (bf16[2,32,640]{2,1,0:T(8,128)(2,1)S(1)}, bf16[2,32,640]{2,1,0:T(8,128)(2,1)S(1)}, u32[]{:S(2)}, u32[]{:S(2)}) collective-permute-start(bf16[2,32,640]{2,1,0:T(8,128)(2,1)S(1)} %broadcast_select_fusion.4), channel_id=1, source_target_pairs={{0,1},{1,0},{2,3},{3,2},{4,5},{5,4},{6,7},{7,6},{8,9},{9,8},{10,11... | collective-permute-start | bytes 245768 | tf_op jit(solution)/shard_map/ppermute | solution.py:8
where the time goes:
time: 84.9 us; the launch traced here: 84.5 us
  waiting for transfers between devices  50.7 us (60%)
  local copies, waits for them, and re-layouts  15.7 us (18%)
  starting transfers between devices  9.08 us (11%)
  other arithmetic  6.71 us (8%)
  matrix products  2.05 us (2%)
    ppermute x6, waiting for transfers between devices, swapped(): lax.ppermute(array, axis, [(i, i ^ 1 << distance) for i in range(lax.axis...  50.7 us
    ppermute x6, starting transfers between devices, swapped(): lax.ppermute(array, axis, [(i, i ^ 1 << distance) for i in range(lax.axis...  9.08 us
    convert_element_type x4, local copies, waits for them, and re-layouts, restore(): change.astype(jnp.float32)  7.77 us
    another operation x3, local copies, waits for them, and re-layouts, shards(): jnp.stack([queries, keys_new, values_new])  2.88 us
    unnamed x12, local copies, waits for them, and re-layouts  1.76 us
  transfers between devices with their start and end apart: 6, of which 6 were waited for; matrix products, arithmetic and copies ran while one was open for 3% of the time, Pallas kernels for 0%

commit v1 on v0

v1 whole, which is shorter than its diff:
```python
import functools

import jax
import jax.numpy as jnp
from jax import lax
from jax.experimental import pallas as pl
from jax.experimental.pallas import tpu as pltpu
from jax.sharding import PartitionSpec as P

GROUP = 4
STAT_ROWS = 16
LOG2E = 1.4426950408889634
HBM = pl.BlockSpec(memory_space=pl.ANY)
VMEM = pl.BlockSpec(memory_space=pltpu.VMEM)


def swapped(array, mask):
    size = lax.axis_size("patch")
    return lax.ppermute(array, "patch", [(i, i ^ mask) for i in range(size)])


def position():
    place = lax.axis_index("patch")
    return place // GROUP, place % GROUP


def columns(member, width):
    return pl.ds(pl.multiple_of(member * width, width), width)


def run_copies(pairs, sems):
    copies = [pltpu.make_async_copy(a, b, sems.at[i]) for i, (a, b) in enumerate(pairs)]
    for copy in copies:
        copy.start()
    for copy in copies:
        copy.wait()


def cut_kernel(count, *refs):
    slabs, outs, sems = refs[:count], refs[count:-1], refs[-1]
    width = slabs[0].shape[1] // GROUP
    _, member = position()
    pairs = []
    for k in range(1, GROUP):
        for i, slab in enumerate(slabs):
            pairs.append((slab.at[:, columns(member ^ k, width)], outs[k - 1].at[i]))
    run_copies(pairs, sems)


def cut(*slabs):
    rows, features = slabs[0].shape
    shape = jax.ShapeDtypeStruct((len(slabs), rows, features // GROUP), slabs[0].dtype)
    return pl.pallas_call(
        functools.partial(cut_kernel, len(slabs)),
        out_shape=[shape] * (GROUP - 1),
        in_specs=[HBM] * len(slabs),
        out_specs=[HBM] * (GROUP - 1),
        scratch_shapes=[pltpu.SemaphoreType.DMA((len(slabs) * (GROUP - 1),))],
        cost_estimate=pl.CostEstimate(flops=0, bytes_accessed=1_500_000, transcendentals=0),
        name="cut",
    )(*slabs)


def rebuild_kernel(
    heads, keys_ref, values_ref, a1, a2, a3, keys_copy, values_copy, kb, vb, out, own, old, sems
):
    rows, features = keys_ref.shape
    width = features // GROUP
    head = width // heads
    group, member = position()
    pairs = []
    for i, (slab, copy) in enumerate(((keys_ref, keys_copy), (values_ref, values_copy))):
        pairs.append((slab.at[:, columns(member, width)], own.at[i]))
        start = pl.multiple_of(group * GROUP * rows, GROUP * rows)
        pairs.append((copy.at[0, pl.ds(start, GROUP * rows), :], old.at[i]))
    run_copies(pairs, sems)
    for k, piece in enumerate((own, a1, a2, a3)):
        place = pl.ds(pl.multiple_of((member ^ k) * rows, rows), rows)
        for i, bounds in enumerate((kb, vb)):
            limits = bounds[place, :]
            for h in range(heads):
                lanes = slice(h * head, (h + 1) * head)
                limit = limits[:, h : h + 1]
                previous = old[i, place, lanes].astype(jnp.float32)
                change = jnp.clip(piece[i, :, lanes].astype(jnp.float32) - previous, -limit, limit)
                change = change.astype(jnp.bfloat16).astype(jnp.float32)
                out[i, k * rows : (k + 1) * rows, lanes] = (previous + change).astype(out.dtype)


def rebuild(heads, keys_new, values_new, arrived, keys_copy, values_copy, kb, vb):
    rows, features = keys_new.shape
    width = features // GROUP
    return pl.pallas_call(
        functools.partial(rebuild_kernel, heads),
        out_shape=jax.ShapeDtypeStruct((2, GROUP * rows, width), keys_new.dtype),
        in_specs=[HBM] * 2 + [VMEM] * 3 + [HBM] * 2 + [VMEM] * 2,
        out_specs=VMEM,
        scratch_shapes=[
            pltpu.VMEM((2, rows, width), keys_new.dtype),
            pltpu.VMEM((2, GROUP * rows, width), keys_new.dtype),
            pltpu.SemaphoreType.DMA((4,)),
        ],
        cost_estimate=pl.CostEstimate(flops=0, bytes_accessed=3_000_000, transcendentals=0),
        name="rebuild",
    )(keys_new, values_new, *arrived, keys_copy, values_copy, kb, vb)


def attend_kernel(heads, slab, q1, q2, q3, near, far, o0, o1, o2, o3, own, sem):
    rows, features = slab.shape
    width = features // GROUP
    head = width // heads
    _, member = position()
    run_copies([(slab.at[:, columns(member, width)], own)], sem)
    scale = head ** (-0.5) * LOG2E
    lane = lax.broadcasted_iota(jnp.int32, (GROUP * rows, head), 1)
    stats = jnp.zeros((GROUP * rows, head), jnp.float32)
    contract = (((1,), (1,)), ((), ()))
    outs = (o0, o1, o2, o3)
    for h in range(heads):
        lanes = slice(h * head, (h + 1) * head)
        query = jnp.concatenate([own[:, lanes], q1[0, :, lanes], q2[0, :, lanes], q3[0, :, lanes]], axis=0)
        scores = [
            lax.dot_general(query, block[0, :, lanes], contract, preferred_element_type=jnp.float32)
            for block in (near, far)
        ]
        peak = jnp.maximum(
            jnp.max(scores[0], axis=1, keepdims=True), jnp.max(scores[1], axis=1, keepdims=True)
        )
        level = (peak * scale).astype(jnp.bfloat16).astype(jnp.float32)
        total = None
        for block, score in zip((near, far), scores):
            probs = jnp.exp2(score * scale - level).astype(jnp.bfloat16)
            value = block[1, :, lanes]
            joined = jnp.concatenate([value, jnp.ones_like(value)], axis=1)
            part = jnp.dot(probs, joined, preferred_element_type=jnp.float32)
            total = part if total is None else total + part
        weighted = total[:, :head].astype(jnp.bfloat16)
        weight = total[:, head:]
        high = weight.astype(jnp.bfloat16).astype(jnp.float32)
        stats = jnp.where(lane == h, level, stats)
        stats = jnp.where(lane == heads + h, high, stats)
        stats = jnp.where(lane == 2 * heads + h, weight - high, stats)
        for k, out in enumerate(outs):
            out[h * rows : (h + 1) * rows, :] = weighted[k * rows : (k + 1) * rows]
    half = rows // 2
    for k, out in enumerate(outs):
        first = stats[k * rows : k * rows + half]
        second = stats[k * rows + half : (k + 1) * rows]
        packed = first + pltpu.roll(second, 16, 1)
        out[heads * rows :, :] = packed.astype(out.dtype)


def attend(heads, slab, pieces, near, far):
    rows, features = slab.shape
    width = features // GROUP
    head = width // heads
    out = jax.ShapeDtypeStruct((heads * rows + rows // 2, head), slab.dtype)
    return pl.pallas_call(
        functools.partial(attend_kernel, heads),
        out_shape=[out] * GROUP,
        in_specs=[HBM] + [VMEM] * 5,
        out_specs=[VMEM] * GROUP,
        scratch_shapes=[
            pltpu.VMEM((rows, width), slab.dtype),
            pltpu.SemaphoreType.DMA((1,)),
        ],
        compiler_params=pltpu.CompilerParams(vmem_limit_bytes=48 * 1024 * 1024),
        cost_estimate=pl.CostEstimate(flops=0, bytes_accessed=5_000_000, transcendentals=0),
        name="attend",
    )(slab, *pieces, near, far)


def merge_kernel(heads, n0, n1, n2, n3, f0, f1, f2, f3, out):
    rows = out.shape[0]
    head = n0.shape[1]
    width = heads * head
    half = rows // 2
    _, member = position()

    def unpack(ref):
        packed = ref[heads * rows :, :].astype(jnp.float32)
        stats = jnp.concatenate([packed, pltpu.roll(packed, head - 16, 1)], axis=0)
        weight = pltpu.roll(stats, head - heads, 1) + pltpu.roll(stats, head - 2 * heads, 1)
        return stats, weight

    for k, (near, far) in enumerate(((n0, f0), (n1, f1), (n2, f2), (n3, f3))):
        near_level, near_weight = unpack(near)
        far_level, far_weight = unpack(far)
        top = jnp.maximum(near_level, far_level)
        near_scale = jnp.exp2(near_level - top)
        far_scale = jnp.exp2(far_level - top)
        total = near_scale * near_weight + far_scale * far_weight
        near_scale = near_scale / total
        far_scale = far_scale / total
        for h in range(heads):
            part = slice(h * rows, (h + 1) * rows)
            mixed = near[part, :].astype(jnp.float32) * near_scale[:, h : h + 1]
            mixed = mixed + far[part, :].astype(jnp.float32) * far_scale[:, h : h + 1]
            start = pl.multiple_of((member ^ k) * width + h * head, head)
            out[:, pl.ds(start, head)] = mixed.astype(out.dtype)


def merge(heads, near, far, rows):
    head = near[0].shape[1]
    return pl.pallas_call(
        functools.partial(merge_kernel, heads),
        out_shape=jax.ShapeDtypeStruct((rows, GROUP * heads * head), near[0].dtype),
        in_specs=[VMEM] * 8,
        out_specs=VMEM,
        cost_estimate=pl.CostEstimate(flops=0, bytes_accessed=2_000_000, transcendentals=0),
        name="merge",
    )(*near, *far)


def shards(queries, keys_new, values_new, keys_copy, values_copy, key_bounds, value_bounds):
    rows = queries.shape[0]
    heads = key_bounds.shape[1] // GROUP
    levels = lax.axis_size("patch").bit_length() - 1
    across = 1 << levels - 1
    group, member = position()

    far_slab = swapped(queries, across)
    kv_sent = cut(keys_new, values_new)
    arrived = [swapped(kv_sent[k - 1], k) for k in range(1, GROUP)]
    corner = (group * GROUP * rows, member * heads)
    limits = [lax.dynamic_slice(b, corner, (GROUP * rows, heads)) for b in (key_bounds, value_bounds)]
    near = rebuild(heads, keys_new, values_new, arrived, keys_copy, values_copy, *limits)
    for bit in range(2, levels - 2):
        near = jnp.concatenate([near, swapped(near, 1 << bit)], axis=1)
    far = swapped(near, 1 << levels - 2)
    own_sent = cut(queries)
    own_pieces = [swapped(own_sent[k - 1], k) for k in range(1, GROUP)]
    far_sent = cut(far_slab)
    far_pieces = [swapped(far_sent[k - 1], k) for k in range(1, GROUP)]
    far_out = attend(heads, far_slab, far_pieces, near, far)
    far_back = [swapped(far_out[k], across + k) for k in range(GROUP)]
    own_out = attend(heads, queries, own_pieces, near, far)
    own_back = [own_out[0]] + [swapped(own_out[k], k) for k in range(1, GROUP)]
    return merge(heads, own_back, far_back, rows)


def solution(mesh):
    rows = P(("clips", "patch"), None)
    copies = P(("clips", "patch"), None, None)
    bounds = P("clips", None)
    return jax.shard_map(
        shards,
        mesh=mesh,
        in_specs=(rows, rows, rows, copies, copies, bounds, bounds),
        out_specs=rows,
        check_vma=False,
    )
```

time: 84.9 us -> 72.8 us (0.86)
  waiting for transfers between devices: 50.7 us -> 17.4 us
  Pallas kernels: 0 us -> 25.3 us
  starting transfers between devices: 9.08 us -> 22.1 us
  local copies, waits for them, and re-layouts: 15.7 us -> 7.41 us
  other arithmetic: 6.71 us -> 0 us
  matrix products: 2.05 us -> 0 us
    ppermute x6 -> x18, waiting for transfers between devices: 50.7 us -> 17.4 us  [swapped(): return lax.ppermute(array, 'patch', [(i, i ^ mask) for i in range(size)])]
    pallas_call x0 -> x7, Pallas kernels: none -> 25.3 us  [the longest x3 18.3 us: cut(): pl.pallas_call(functools.partial(cut_kernel, len(slabs)), out_shape=[shap...]
    ppermute x6 -> x18, starting transfers between devices: 9.08 us -> 22.1 us  [swapped(): return lax.ppermute(array, 'patch', [(i, i ^ mask) for i in range(size)])]
    convert_element_type x4 -> x0, local copies, waits for them, and re-layouts: 7.77 us -> none  [restore(): change.astype(jnp.float32)]
    unnamed x12 -> x36, local copies, waits for them, and re-layouts: 1.76 us -> 5.87 us
    another operation x3 -> x0, local copies, waits for them, and re-layouts: 2.88 us -> none  [shards(): jnp.stack([queries, keys_new, values_new])]
    select_n x6 -> x0, other arithmetic: 2.26 us -> none  [the longest x2 1.29 us: shards(): lower = jnp.where(mine == 0, keep, arrived)]
    dot_general x2 -> x0, matrix products: 2.05 us -> none  [the longest x1 1.55 us: shards(): jnp.einsum('qhd,khd->hqk', query_heads, keys_used, preferred_element_type...]
  transfers between devices with their start and end apart: 6 -> 18, of which waited for: 6 -> 8; matrix products, arithmetic and copies ran while one was open for 3% -> 4% of each run, Pallas kernels for 0% -> 15%
where the time goes in v1:
time: 72.8 us; the launch traced here: 72.4 us
  Pallas kernels  25.3 us (35%)
  starting transfers between devices  22.1 us (30%)
  waiting for transfers between devices  17.4 us (24%)
  local copies, waits for them, and re-layouts  7.41 us (10%)
    ppermute x18, starting transfers between devices, swapped(): return lax.ppermute(array, 'patch', [(i, i ^ mask) for i in range(size)])  22.1 us
    pallas_call x3, Pallas kernels, cut(): pl.pallas_call(functools.partial(cut_kernel, len(slabs)), out_shape=[shap...  18.3 us
    ppermute x18, waiting for transfers between devices, swapped(): return lax.ppermute(array, 'patch', [(i, i ^ mask) for i in range(size)])  17.4 us
    unnamed x36, local copies, waits for them, and re-layouts  5.87 us
    pallas_call x1, Pallas kernels, rebuild(): pl.pallas_call(functools.partial(rebuild_kernel, heads), out_shape=jax.Sh...  3.11 us
    pallas_call x1, Pallas kernels, merge(): pl.pallas_call(functools.partial(merge_kernel, heads), out_shape=jax.Shap...  2.17 us
    pallas_call x2, Pallas kernels, attend(): pl.pallas_call(functools.partial(attend_kernel, heads), out_shape=[out] *...  1.73 us
    dynamic_slice x2, local copies, waits for them, and re-layouts, shards(): lax.dynamic_slice(b, corner, (GROUP * rows, heads))  1.54 us
  transfers between devices with their start and end apart: 18, of which 8 were waited for; matrix products, arithmetic and copies ran while one was open for 4% of the time, Pallas kernels for 15%

profile of v1, /device:TPU:0, one launch (start us, length us, event | category | flops | bytes accessed | tf_op | source)
XLA Modules:
  0.0 72.4 jit_solution(14517095385686796235)
XLA Ops:
  0.0 8.6 %cut.4 = (bf16[2,32,640]{2,1,0:T(8,128)(2,1)}, bf16[2,32,640]{2,1,0:T(8,128)(2,1)}, bf16[2,32,640]{2,1,0:T(8,128)(2,1)}) custom-call(bf16[32,2560]{1,0:T(8,128)(2,1)} %keys_ref.1, bf16[32,2560]{1,0:T(8,128)(2,1)} %values_ref.1), custom_call_target="tpu_custom_call" | custom-call | bytes 1500000 | tf_op jit(solution)/shard_map/cut/pallas_call | solution.py:53
  9.1 2.6 %collective-permute-start.4 = (bf16[2,32,640]{2,1,0:T(8,128)(2,1)}, bf16[2,32,640]{2,1,0:T(8,128)(2,1)S(1)}, u32[]{:S(2)}, u32[]{:S(2)}) collective-permute-start(bf16[2,32,640]{2,1,0:T(8,128)(2,1)} %get-tuple-element.26), channel_id=1, source_target_pairs={{0,2},{1,3},{2,0},{3,1},{4,6},{5,7},{6,4},{7,5},{8,10},{9,11},{10,... | collective-permute-start | bytes 245768 | tf_op jit(solution)/shard_map/ppermute | solution.py:19
  14.9 1.5 %collective-permute-done.5.a3 = bf16[2,32,640]{2,1,0:T(8,128)(2,1)S(1)} collective-permute-done((bf16[2,32,640]{2,1,0:T(8,128)(2,1)}, bf16[2,32,640]{2,1,0:T(8,128)(2,1)S(1)}, u32[]{:S(2)}, u32[]{:S(2)}) %collective-permute-start.5) | collective-permute-done | bytes 81952 | tf_op jit(solution)/shard_map/ppermute | solution.py:19
  17.0 3.1 %rebuild.1.near = bf16[2,128,640]{2,1,0:T(8,128)(2,1)} custom-call(bf16[32,2560]{1,0:T(8,128)(2,1)} %keys_ref.1, bf16[32,2560]{1,0:T(8,128)(2,1)} %values_ref.1, bf16[2,32,640]{2,1,0:T(8,128)(2,1)} %copy-done.7, bf16[2,32,640]{2,1,0:T(8,128)(2,1)} %copy-done.8, bf16[2,32,640]{2,1,0:T(8,128)(2,1)} %copy-done.9, bf16[1,512,640]{2,1,0:T(8,128)(2,1)} %keys_copy.1, ...), custom_call_target="tpu_custom_call" | custom-call | bytes 3000000 | tf_op jit(solution)/shard_map/rebuild/pallas_call | solution.py:93
  20.2 1.9 %collective-permute-start.6 = (bf16[2,128,640]{2,1,0:T(8,128)(2,1)}, bf16[2,128,640]{2,1,0:T(8,128)(2,1)S(1)}, u32[]{:S(2)}, u32[]{:S(2)}) collective-permute-start(bf16[2,128,640]{2,1,0:T(8,128)(2,1)} %rebuild.1.near), channel_id=1, source_target_pairs={{0,4},{1,5},{2,6},{3,7},{4,0},{5,1},{6,2},{7,3},{8,12},{9,13},{10,... | collective-permute-start | bytes 983048 | tf_op jit(solution)/shard_map/ppermute | solution.py:19
  22.0 2.6 %collective-permute-start.10 = (bf16[32,2560]{1,0:T(8,128)(2,1)S(1)}, bf16[32,2560]{1,0:T(8,128)(2,1)S(1)}, u32[]{:S(2)}, u32[]{:S(2)}) collective-permute-start(bf16[32,2560]{1,0:T(8,128)(2,1)S(1)} %copy-done.2), channel_id=1, source_target_pairs={{0,8},{1,9},{2,10},{3,11},{4,12},{5,13},{6,14},{7,15},{8,0},{9,1},... | collective-permute-start | bytes 491528 | tf_op jit(solution)/shard_map/ppermute | solution.py:19
  24.6 8.4 %collective-permute-done.10.refs_0_.slab = bf16[32,2560]{1,0:T(8,128)(2,1)S(1)} collective-permute-done((bf16[32,2560]{1,0:T(8,128)(2,1)S(1)}, bf16[32,2560]{1,0:T(8,128)(2,1)S(1)}, u32[]{:S(2)}, u32[]{:S(2)}) %collective-permute-start.10) | collective-permute-done | bytes 163872 | tf_op jit(solution)/shard_map/ppermute | solution.py:19
  33.7 4.8 %cut.5 = (bf16[1,32,640]{2,1,0:T(8,128)(2,1)}, bf16[1,32,640]{2,1,0:T(8,128)(2,1)}, bf16[1,32,640]{2,1,0:T(8,128)(2,1)}) custom-call(bf16[32,2560]{1,0:T(8,128)(2,1)} %copy-done.4), custom_call_target="tpu_custom_call" | custom-call | bytes 1500000 | tf_op jit(solution)/shard_map/cut/pallas_call | solution.py:53
  38.6 1.6 %collective-permute-start.12 = (bf16[1,32,640]{2,1,0:T(8,128)(2,1)}, bf16[1,32,640]{2,1,0:T(8,128)(2,1)S(1)}, u32[]{:S(2)}, u32[]{:S(2)}) collective-permute-start(bf16[1,32,640]{2,1,0:T(8,128)(2,1)} %get-tuple-element.33), channel_id=1, source_target_pairs={{0,2},{1,3},{2,0},{3,1},{4,6},{5,7},{6,4},{7,5},{8,10},{9,11},{10,... | collective-permute-start | bytes 122888 | tf_op jit(solution)/shard_map/ppermute | solution.py:19
  40.5 2.4 %collective-permute-done.12.q2 = bf16[1,32,640]{2,1,0:T(8,128)(2,1)S(1)} collective-permute-done((bf16[1,32,640]{2,1,0:T(8,128)(2,1)}, bf16[1,32,640]{2,1,0:T(8,128)(2,1)S(1)}, u32[]{:S(2)}, u32[]{:S(2)}) %collective-permute-start.12) | collective-permute-done | bytes 40992 | tf_op jit(solution)/shard_map/ppermute | solution.py:19
  42.9 1.1 %collective-permute-done.13.q3 = bf16[1,32,640]{2,1,0:T(8,128)(2,1)S(1)} collective-permute-done((bf16[1,32,640]{2,1,0:T(8,128)(2,1)}, bf16[1,32,640]{2,1,0:T(8,128)(2,1)S(1)}, u32[]{:S(2)}, u32[]{:S(2)}) %collective-permute-start.13) | collective-permute-done | bytes 40992 | tf_op jit(solution)/shard_map/ppermute | solution.py:19
  44.0 1.0 %copy-done = bf16[2,128,640]{2,1,0:T(8,128)(2,1)S(1)} copy-done((bf16[2,128,640]{2,1,0:T(8,128)(2,1)S(1)}, bf16[2,128,640]{2,1,0:T(8,128)(2,1)}, u32[]{:S(2)}) %copy-start) | copy-done | bytes 327704
  45.0 0.9 %copy-done.5 = bf16[32,2560]{1,0:T(8,128)(2,1)S(1)} copy-done((bf16[32,2560]{1,0:T(8,128)(2,1)S(1)}, bf16[32,2560]{1,0:T(8,128)(2,1)}, u32[]{:S(2)}) %copy-start.5) | copy-done | bytes 163864
  46.8 3.4 %collective-permute-start.14 = (bf16[176,128]{1,0:T(8,128)(2,1)S(1)}, bf16[176,128]{1,0:T(8,128)(2,1)S(1)}, u32[]{:S(2)}, u32[]{:S(2)}) collective-permute-start(bf16[176,128]{1,0:T(8,128)(2,1)S(1)} %get-tuple-element.35), channel_id=1, source_target_pairs={{0,8},{1,9},{2,10},{3,11},{4,12},{5,13},{6,14},{7,15},{8,0},{9,1},... | collective-permute-start | bytes 135176 | tf_op jit(solution)/shard_map/ppermute | solution.py:19
  50.2 4.8 %cut.3 = (bf16[1,32,640]{2,1,0:T(8,128)(2,1)}, bf16[1,32,640]{2,1,0:T(8,128)(2,1)}, bf16[1,32,640]{2,1,0:T(8,128)(2,1)}) custom-call(bf16[32,2560]{1,0:T(8,128)(2,1)} %slab.1), custom_call_target="tpu_custom_call" | custom-call | bytes 1500000 | tf_op jit(solution)/shard_map/cut/pallas_call | solution.py:53
  57.0 2.8 %collective-permute-start.16 = (bf16[176,128]{1,0:T(8,128)(2,1)S(1)}, bf16[176,128]{1,0:T(8,128)(2,1)S(1)}, u32[]{:S(2)}, u32[]{:S(2)}) collective-permute-start(bf16[176,128]{1,0:T(8,128)(2,1)S(1)} %get-tuple-element.37), channel_id=1, source_target_pairs={{0,10},{1,11},{2,8},{3,9},{4,14},{5,15},{6,12},{7,13},{8,2},{9,3},... | collective-permute-start | bytes 135176 | tf_op jit(solution)/shard_map/ppermute | solution.py:19
  59.9 1.3 %collective-permute-start.17 = (bf16[176,128]{1,0:T(8,128)(2,1)S(1)}, bf16[176,128]{1,0:T(8,128)(2,1)S(1)}, u32[]{:S(2)}, u32[]{:S(2)}) collective-permute-start(bf16[176,128]{1,0:T(8,128)(2,1)S(1)} %get-tuple-element.38), channel_id=1, source_target_pairs={{0,11},{1,10},{2,9},{3,8},{4,15},{5,14},{6,13},{7,12},{8,3},{9,2},... | collective-permute-start | bytes 135176 | tf_op jit(solution)/shard_map/ppermute | solution.py:19
  61.2 0.9 %attend.2 = (bf16[176,128]{1,0:T(8,128)(2,1)S(1)}, bf16[176,128]{1,0:T(8,128)(2,1)S(1)}, bf16[176,128]{1,0:T(8,128)(2,1)S(1)}, bf16[176,128]{1,0:T(8,128)(2,1)S(1)}) custom-call(bf16[32,2560]{1,0:T(8,128)(2,1)S(1)} %copy-done.3, bf16[1,32,640]{2,1,0:T(8,128)(2,1)S(1)} %collective-permute-done.q1, bf16[1,32,640]{2,1,0:T(8,128)(2,1)S(1)} %collective-permute-done.1.q2, ...), custom_call_target="tpu_custom_call" | custom-call | bytes 5000000 | tf_op jit(solution)/shard_map/attend/pallas_call | solution.py:158
  62.7 1.6 %collective-permute-start.7 = (bf16[176,128]{1,0:T(8,128)(2,1)S(1)}, bf16[176,128]{1,0:T(8,128)(2,1)S(1)}, u32[]{:S(2)}, u32[]{:S(2)}) collective-permute-start(bf16[176,128]{1,0:T(8,128)(2,1)S(1)} %get-tuple-element.29), channel_id=1, source_target_pairs={{0,1},{1,0},{2,3},{3,2},{4,5},{5,4},{6,7},{7,6},{8,9},{9,8},{10,11... | collective-permute-start | bytes 135176 | tf_op jit(solution)/shard_map/ppermute | solution.py:19
  64.3 1.5 %collective-permute-start.8 = (bf16[176,128]{1,0:T(8,128)(2,1)S(1)}, bf16[176,128]{1,0:T(8,128)(2,1)S(1)}, u32[]{:S(2)}, u32[]{:S(2)}) collective-permute-start(bf16[176,128]{1,0:T(8,128)(2,1)S(1)} %get-tuple-element.30), channel_id=1, source_target_pairs={{0,2},{1,3},{2,0},{3,1},{4,6},{5,7},{6,4},{7,5},{8,10},{9,11},{10,... | collective-permute-start | bytes 135176 | tf_op jit(solution)/shard_map/ppermute | solution.py:19
  65.8 0.9 %collective-permute-done.17.f3 = bf16[176,128]{1,0:T(8,128)(2,1)S(1)} collective-permute-done((bf16[176,128]{1,0:T(8,128)(2,1)S(1)}, bf16[176,128]{1,0:T(8,128)(2,1)S(1)}, u32[]{:S(2)}, u32[]{:S(2)}) %collective-permute-start.17) | collective-permute-done | bytes 45088 | tf_op jit(solution)/shard_map/ppermute | solution.py:19
  66.6 1.7 %collective-permute-done.8.n2 = bf16[176,128]{1,0:T(8,128)(2,1)S(1)} collective-permute-done((bf16[176,128]{1,0:T(8,128)(2,1)S(1)}, bf16[176,128]{1,0:T(8,128)(2,1)S(1)}, u32[]{:S(2)}, u32[]{:S(2)}) %collective-permute-start.8) | collective-permute-done | bytes 45088 | tf_op jit(solution)/shard_map/ppermute | solution.py:19
  68.3 1.3 %collective-permute-done.9.n3 = bf16[176,128]{1,0:T(8,128)(2,1)S(1)} collective-permute-done((bf16[176,128]{1,0:T(8,128)(2,1)S(1)}, bf16[176,128]{1,0:T(8,128)(2,1)S(1)}, u32[]{:S(2)}, u32[]{:S(2)}) %collective-permute-start.9) | collective-permute-done | bytes 45088 | tf_op jit(solution)/shard_map/ppermute | solution.py:19
  70.3 2.2 %merge.1 = bf16[32,2560]{1,0:T(8,128)(2,1)} custom-call(bf16[176,128]{1,0:T(8,128)(2,1)} %copy-done.6, bf16[176,128]{1,0:T(8,128)(2,1)} %copy-done.14, bf16[176,128]{1,0:T(8,128)(2,1)} %copy-done.15, bf16[176,128]{1,0:T(8,128)(2,1)} %copy-done.16, bf16[176,128]{1,0:T(8,128)(2,1)} %copy-done.10, bf16[176,128]{1,0:T(8,128)(2,1)} %copy-done.11, ...), custom_call_target="tpu_custom_call" | custom-call | bytes 2000000 | tf_op jit(solution)/shard_map/merge/pallas_call | solution.py:205
  (57 shorter events, 9.5 us)
Async XLA Ops:
  8.6 6.2 %collective-permute-start.3 = (bf16[2,32,640]{2,1,0:T(8,128)(2,1)}, bf16[2,32,640]{2,1,0:T(8,128)(2,1)S(1)}, u32[]{:S(2)}, u32[]{:S(2)}) collective-permute-start(bf16[2,32,640]{2,1,0:T(8,128)(2,1)} %get-tuple-element.25), channel_id=1, source_target_pairs={{0,1},{1,0},{2,3},{3,2},{4,5},{5,4},{6,7},{7,6},{8,9},{9,8},{10,11... | collective-permute-start | bytes 245768 | tf_op jit(solution)/shard_map/ppermute | solution.py:19
  9.1 5.8 %collective-permute-start.4 = (bf16[2,32,640]{2,1,0:T(8,128)(2,1)}, bf16[2,32,640]{2,1,0:T(8,128)(2,1)S(1)}, u32[]{:S(2)}, u32[]{:S(2)}) collective-permute-start(bf16[2,32,640]{2,1,0:T(8,128)(2,1)} %get-tuple-element.26), channel_id=1, source_target_pairs={{0,2},{1,3},{2,0},{3,1},{4,6},{5,7},{6,4},{7,5},{8,10},{9,11},{10,... | collective-permute-start | bytes 245768 | tf_op jit(solution)/shard_map/ppermute | solution.py:19
  11.7 4.7 %collective-permute-start.5 = (bf16[2,32,640]{2,1,0:T(8,128)(2,1)}, bf16[2,32,640]{2,1,0:T(8,128)(2,1)S(1)}, u32[]{:S(2)}, u32[]{:S(2)}) collective-permute-start(bf16[2,32,640]{2,1,0:T(8,128)(2,1)} %get-tuple-element.27), channel_id=1, source_target_pairs={{0,3},{1,2},{2,1},{3,0},{4,7},{5,6},{6,5},{7,4},{8,11},{9,10},{10,... | collective-permute-start | bytes 245768 | tf_op jit(solution)/shard_map/ppermute | solution.py:19
  14.8 7.3 %copy-start.2 = (bf16[32,2560]{1,0:T(8,128)(2,1)S(1)}, bf16[32,2560]{1,0:T(8,128)(2,1)}, u32[]{:S(2)}) copy-start(bf16[32,2560]{1,0:T(8,128)(2,1)} %slab.1) | copy-start | bytes 491524
  20.2 23.9 %collective-permute-start.6 = (bf16[2,128,640]{2,1,0:T(8,128)(2,1)}, bf16[2,128,640]{2,1,0:T(8,128)(2,1)S(1)}, u32[]{:S(2)}, u32[]{:S(2)}) collective-permute-start(bf16[2,128,640]{2,1,0:T(8,128)(2,1)} %rebuild.1.near), channel_id=1, source_target_pairs={{0,4},{1,5},{2,6},{3,7},{4,0},{5,1},{6,2},{7,3},{8,12},{9,13},{10,... | collective-permute-start | bytes 983048 | tf_op jit(solution)/shard_map/ppermute | solution.py:19
  22.0 11.0 %collective-permute-start.10 = (bf16[32,2560]{1,0:T(8,128)(2,1)S(1)}, bf16[32,2560]{1,0:T(8,128)(2,1)S(1)}, u32[]{:S(2)}, u32[]{:S(2)}) collective-permute-start(bf16[32,2560]{1,0:T(8,128)(2,1)S(1)} %copy-done.2), channel_id=1, source_target_pairs={{0,8},{1,9},{2,10},{3,11},{4,12},{5,13},{6,14},{7,15},{8,0},{9,1},... | collective-permute-start | bytes 491528 | tf_op jit(solution)/shard_map/ppermute | solution.py:19
  38.6 1.9 %collective-permute-start.11 = (bf16[1,32,640]{2,1,0:T(8,128)(2,1)}, bf16[1,32,640]{2,1,0:T(8,128)(2,1)S(1)}, u32[]{:S(2)}, u32[]{:S(2)}) collective-permute-start(bf16[1,32,640]{2,1,0:T(8,128)(2,1)} %get-tuple-element.32), channel_id=1, source_target_pairs={{0,1},{1,0},{2,3},{3,2},{4,5},{5,4},{6,7},{7,6},{8,9},{9,8},{10,11... | collective-permute-start | bytes 122888 | tf_op jit(solution)/shard_map/ppermute | solution.py:19
  38.6 4.3 %collective-permute-start.12 = (bf16[1,32,640]{2,1,0:T(8,128)(2,1)}, bf16[1,32,640]{2,1,0:T(8,128)(2,1)S(1)}, u32[]{:S(2)}, u32[]{:S(2)}) collective-permute-start(bf16[1,32,640]{2,1,0:T(8,128)(2,1)} %get-tuple-element.33), channel_id=1, source_target_pairs={{0,2},{1,3},{2,0},{3,1},{4,6},{5,7},{6,4},{7,5},{8,10},{9,11},{10,... | collective-permute-start | bytes 122888 | tf_op jit(solution)/shard_map/ppermute | solution.py:19
  40.2 3.8 %collective-permute-start.13 = (bf16[1,32,640]{2,1,0:T(8,128)(2,1)}, bf16[1,32,640]{2,1,0:T(8,128)(2,1)S(1)}, u32[]{:S(2)}, u32[]{:S(2)}) collective-permute-start(bf16[1,32,640]{2,1,0:T(8,128)(2,1)} %get-tuple-element.34), channel_id=1, source_target_pairs={{0,3},{1,2},{2,1},{3,0},{4,7},{5,6},{6,5},{7,4},{8,11},{9,10},{10,... | collective-permute-start | bytes 122888 | tf_op jit(solution)/shard_map/ppermute | solution.py:19
  45.9 15.3 %copy-start.1 = (bf16[2,128,640]{2,1,0:T(8,128)(2,1)S(1)}, bf16[2,128,640]{2,1,0:T(8,128)(2,1)}, u32[]{:S(2)}) copy-start(bf16[2,128,640]{2,1,0:T(8,128)(2,1)} %rebuild.1.near) | copy-start | bytes 983044
  46.8 14.4 %copy-start.3 = (bf16[32,2560]{1,0:T(8,128)(2,1)S(1)}, bf16[32,2560]{1,0:T(8,128)(2,1)}, u32[]{:S(2)}) copy-start(bf16[32,2560]{1,0:T(8,128)(2,1)} %slab.1) | copy-start | bytes 491524
  46.8 17.5 %collective-permute-start.14 = (bf16[176,128]{1,0:T(8,128)(2,1)S(1)}, bf16[176,128]{1,0:T(8,128)(2,1)S(1)}, u32[]{:S(2)}, u32[]{:S(2)}) collective-permute-start(bf16[176,128]{1,0:T(8,128)(2,1)S(1)} %get-tuple-element.35), channel_id=1, source_target_pairs={{0,8},{1,9},{2,10},{3,11},{4,12},{5,13},{6,14},{7,15},{8,0},{9,1},... | collective-permute-start | bytes 135176 | tf_op jit(solution)/shard_map/ppermute | solution.py:19
  50.2 15.5 %collective-permute-start.15 = (bf16[176,128]{1,0:T(8,128)(2,1)S(1)}, bf16[176,128]{1,0:T(8,128)(2,1)S(1)}, u32[]{:S(2)}, u32[]{:S(2)}) collective-permute-start(bf16[176,128]{1,0:T(8,128)(2,1)S(1)} %get-tuple-element.36), channel_id=1, source_target_pairs={{0,9},{1,8},{2,11},{3,10},{4,13},{5,12},{6,15},{7,14},{8,1},{9,0},... | collective-permute-start | bytes 135176 | tf_op jit(solution)/shard_map/ppermute | solution.py:19
  55.1 1.9 %collective-permute-start = (bf16[1,32,640]{2,1,0:T(8,128)(2,1)}, bf16[1,32,640]{2,1,0:T(8,128)(2,1)S(1)}, u32[]{:S(2)}, u32[]{:S(2)}) collective-permute-start(bf16[1,32,640]{2,1,0:T(8,128)(2,1)} %get-tuple-element.22), channel_id=1, source_target_pairs={{0,1},{1,0},{2,3},{3,2},{4,5},{5,4},{6,7},{7,6},{8,9},{9,8},{10,11... | collective-permute-start | bytes 122888 | tf_op jit(solution)/shard_map/ppermute | solution.py:19
  55.3 4.5 %collective-permute-start.1 = (bf16[1,32,640]{2,1,0:T(8,128)(2,1)}, bf16[1,32,640]{2,1,0:T(8,128)(2,1)S(1)}, u32[]{:S(2)}, u32[]{:S(2)}) collective-permute-start(bf16[1,32,640]{2,1,0:T(8,128)(2,1)} %get-tuple-element.23), channel_id=1, source_target_pairs={{0,2},{1,3},{2,0},{3,1},{4,6},{5,7},{6,4},{7,5},{8,10},{9,11},{10,... | collective-permute-start | bytes 122888 | tf_op jit(solution)/shard_map/ppermute | solution.py:19
  56.1 5.0 %collective-permute-start.2 = (bf16[1,32,640]{2,1,0:T(8,128)(2,1)}, bf16[1,32,640]{2,1,0:T(8,128)(2,1)S(1)}, u32[]{:S(2)}, u32[]{:S(2)}) collective-permute-start(bf16[1,32,640]{2,1,0:T(8,128)(2,1)} %get-tuple-element.24), channel_id=1, source_target_pairs={{0,3},{1,2},{2,1},{3,0},{4,7},{5,6},{6,5},{7,4},{8,11},{9,10},{10,... | collective-permute-start | bytes 122888 | tf_op jit(solution)/shard_map/ppermute | solution.py:19
  57.0 8.7 %collective-permute-start.16 = (bf16[176,128]{1,0:T(8,128)(2,1)S(1)}, bf16[176,128]{1,0:T(8,128)(2,1)S(1)}, u32[]{:S(2)}, u32[]{:S(2)}) collective-permute-start(bf16[176,128]{1,0:T(8,128)(2,1)S(1)} %get-tuple-element.37), channel_id=1, source_target_pairs={{0,10},{1,11},{2,8},{3,9},{4,14},{5,15},{6,12},{7,13},{8,2},{9,3},... | collective-permute-start | bytes 135176 | tf_op jit(solution)/shard_map/ppermute | solution.py:19
  59.9 6.8 %collective-permute-start.17 = (bf16[176,128]{1,0:T(8,128)(2,1)S(1)}, bf16[176,128]{1,0:T(8,128)(2,1)S(1)}, u32[]{:S(2)}, u32[]{:S(2)}) collective-permute-start(bf16[176,128]{1,0:T(8,128)(2,1)S(1)} %get-tuple-element.38), channel_id=1, source_target_pairs={{0,11},{1,10},{2,9},{3,8},{4,15},{5,14},{6,13},{7,12},{8,3},{9,2},... | collective-permute-start | bytes 135176 | tf_op jit(solution)/shard_map/ppermute | solution.py:19
  62.7 4.0 %collective-permute-start.7 = (bf16[176,128]{1,0:T(8,128)(2,1)S(1)}, bf16[176,128]{1,0:T(8,128)(2,1)S(1)}, u32[]{:S(2)}, u32[]{:S(2)}) collective-permute-start(bf16[176,128]{1,0:T(8,128)(2,1)S(1)} %get-tuple-element.29), channel_id=1, source_target_pairs={{0,1},{1,0},{2,3},{3,2},{4,5},{5,4},{6,7},{7,6},{8,9},{9,8},{10,11... | collective-permute-start | bytes 135176 | tf_op jit(solution)/shard_map/ppermute | solution.py:19
  64.3 5.4 %copy-start.10 = (bf16[176,128]{1,0:T(8,128)(2,1)}, bf16[176,128]{1,0:T(8,128)(2,1)S(1)}, u32[]{:S(2)}) copy-start(bf16[176,128]{1,0:T(8,128)(2,1)S(1)} %collective-permute-done.14.f0) | copy-start | bytes 135172
  64.3 4.0 %collective-permute-start.8 = (bf16[176,128]{1,0:T(8,128)(2,1)S(1)}, bf16[176,128]{1,0:T(8,128)(2,1)S(1)}, u32[]{:S(2)}, u32[]{:S(2)}) collective-permute-start(bf16[176,128]{1,0:T(8,128)(2,1)S(1)} %get-tuple-element.30), channel_id=1, source_target_pairs={{0,2},{1,3},{2,0},{3,1},{4,6},{5,7},{6,4},{7,5},{8,10},{9,11},{10,... | collective-permute-start | bytes 135176 | tf_op jit(solution)/shard_map/ppermute | solution.py:19
  65.7 3.9 %copy-start.11 = (bf16[176,128]{1,0:T(8,128)(2,1)}, bf16[176,128]{1,0:T(8,128)(2,1)S(1)}, u32[]{:S(2)}) copy-start(bf16[176,128]{1,0:T(8,128)(2,1)S(1)} %collective-permute-done.15.f1) | copy-start | bytes 135172
  65.7 3.9 %collective-permute-start.9 = (bf16[176,128]{1,0:T(8,128)(2,1)S(1)}, bf16[176,128]{1,0:T(8,128)(2,1)S(1)}, u32[]{:S(2)}, u32[]{:S(2)}) collective-permute-start(bf16[176,128]{1,0:T(8,128)(2,1)S(1)} %get-tuple-element.31), channel_id=1, source_target_pairs={{0,3},{1,2},{2,1},{3,0},{4,7},{5,6},{6,5},{7,4},{8,11},{9,10},{10,... | collective-permute-start | bytes 135176 | tf_op jit(solution)/shard_map/ppermute | solution.py:19
  65.8 3.9 %copy-start.12 = (bf16[176,128]{1,0:T(8,128)(2,1)}, bf16[176,128]{1,0:T(8,128)(2,1)S(1)}, u32[]{:S(2)}) copy-start(bf16[176,128]{1,0:T(8,128)(2,1)S(1)} %collective-permute-done.16.f2) | copy-start | bytes 135172
  (11 other events, 14.9 us)

commit v2 on v1

--- a/solution.py
+++ b/solution.py
@@ -14,6 +14,17 @@
 VMEM = pl.BlockSpec(memory_space=pltpu.VMEM)
 
 
+MB = 1 << 20
+
+
+def limit(size):
+    return pltpu.CompilerParams(vmem_limit_bytes=size)
+
+
+def cost(size):
+    return pl.CostEstimate(flops=0, bytes_accessed=size, transcendentals=0)
+
+
 def swapped(array, mask):
     size = lax.axis_size("patch")
     return lax.ppermute(array, "patch", [(i, i ^ mask) for i in range(size)])
@@ -37,14 +48,12 @@
 
 
 def cut_kernel(count, *refs):
-    slabs, outs, sems = refs[:count], refs[count:-1], refs[-1]
+    slabs, outs = refs[:count], refs[count:]
     width = slabs[0].shape[1] // GROUP
     _, member = position()
-    pairs = []
     for k in range(1, GROUP):
         for i, slab in enumerate(slabs):
-            pairs.append((slab.at[:, columns(member ^ k, width)], outs[k - 1].at[i]))
-    run_copies(pairs, sems)
+            outs[k - 1][i] = slab[:, columns(member ^ k, width)]
 
 
 def cut(*slabs):
@@ -53,34 +62,38 @@
     return pl.pallas_call(
         functools.partial(cut_kernel, len(slabs)),
         out_shape=[shape] * (GROUP - 1),
-        in_specs=[HBM] * len(slabs),
-        out_specs=[HBM] * (GROUP - 1),
-        scratch_shapes=[pltpu.SemaphoreType.DMA((len(slabs) * (GROUP - 1),))],
-        cost_estimate=pl.CostEstimate(flops=0, bytes_accessed=1_500_000, transcendentals=0),
+        in_specs=[VMEM] * len(slabs),
+        out_specs=[VMEM] * (GROUP - 1),
+        compiler_params=limit(4 * MB),
+        cost_estimate=cost(1000),
         name="cut",
     )(*slabs)
 
 
 def rebuild_kernel(
-    heads, keys_ref, values_ref, a1, a2, a3, keys_copy, values_copy, kb, vb, out, own, old, sems
+    heads, keys_ref, values_ref, a1, a2, a3, keys_copy, values_copy, kb, vb, out, own, old, bounds, sems
 ):
     rows, features = keys_ref.shape
     width = features // GROUP
     head = width // heads
     group, member = position()
     pairs = []
-    for i, (slab, copy) in enumerate(((keys_ref, keys_copy), (values_ref, values_copy))):
+    start = pl.multiple_of(group * GROUP * rows, GROUP * rows)
+    block = pl.ds(start, GROUP * rows)
+    for i, (slab, copy, bound) in enumerate(((keys_ref, keys_copy, kb), (values_ref, values_copy, vb))):
         pairs.append((slab.at[:, columns(member, width)], own.at[i]))
-        start = pl.multiple_of(group * GROUP * rows, GROUP * rows)
-        pairs.append((copy.at[0, pl.ds(start, GROUP * rows), :], old.at[i]))
+        pairs.append((copy.at[0, block, :], old.at[i]))
+        pairs.append((bound.at[block, :], bounds.at[i]))
     run_copies(pairs, sems)
+    lane = lax.broadcasted_iota(jnp.int32, (rows, bounds.shape[2]), 1)
     for k, piece in enumerate((own, a1, a2, a3)):
         place = pl.ds(pl.multiple_of((member ^ k) * rows, rows), rows)
-        for i, bounds in enumerate((kb, vb)):
-            limits = bounds[place, :]
+        for i in range(2):
+            limits = bounds[i, place, :]
             for h in range(heads):
                 lanes = slice(h * head, (h + 1) * head)
-                limit = limits[:, h : h + 1]
+                chosen = jnp.where(lane == member * heads + h, limits, 0.0)
+                limit = jnp.sum(chosen, axis=1, keepdims=True)
                 previous = old[i, place, lanes].astype(jnp.float32)
                 change = jnp.clip(piece[i, :, lanes].astype(jnp.float32) - previous, -limit, limit)
                 change = change.astype(jnp.bfloat16).astype(jnp.float32)
@@ -93,14 +106,16 @@
     return pl.pallas_call(
         functools.partial(rebuild_kernel, heads),
         out_shape=jax.ShapeDtypeStruct((2, GROUP * rows, width), keys_new.dtype),
-        in_specs=[HBM] * 2 + [VMEM] * 3 + [HBM] * 2 + [VMEM] * 2,
+        in_specs=[HBM] * 2 + [VMEM] * 3 + [HBM] * 4,
         out_specs=VMEM,
         scratch_shapes=[
             pltpu.VMEM((2, rows, width), keys_new.dtype),
             pltpu.VMEM((2, GROUP * rows, width), keys_new.dtype),
-            pltpu.SemaphoreType.DMA((4,)),
+            pltpu.VMEM((2, GROUP * rows, kb.shape[1]), kb.dtype),
+            pltpu.SemaphoreType.DMA((6,)),
         ],
-        cost_estimate=pl.CostEstimate(flops=0, bytes_accessed=3_000_000, transcendentals=0),
+        compiler_params=limit(8 * MB),
+        cost_estimate=cost(1000),
         name="rebuild",
     )(keys_new, values_new, *arrived, keys_copy, values_copy, kb, vb)
 
@@ -164,8 +179,8 @@
             pltpu.VMEM((rows, width), slab.dtype),
             pltpu.SemaphoreType.DMA((1,)),
         ],
-        compiler_params=pltpu.CompilerParams(vmem_limit_bytes=48 * 1024 * 1024),
-        cost_estimate=pl.CostEstimate(flops=0, bytes_accessed=5_000_000, transcendentals=0),
+        compiler_params=limit(4 * MB + 4 * near.size * near.dtype.itemsize + 32 * GROUP * rows * near.shape[1]),
+        cost_estimate=cost(1000),
         name="attend",
     )(slab, *pieces, near, far)
 
@@ -207,7 +222,8 @@
         out_shape=jax.ShapeDtypeStruct((rows, GROUP * heads * head), near[0].dtype),
         in_specs=[VMEM] * 8,
         out_specs=VMEM,
-        cost_estimate=pl.CostEstimate(flops=0, bytes_accessed=2_000_000, transcendentals=0),
+        compiler_params=limit(4 * MB),
+        cost_estimate=cost(1000),
         name="merge",
     )(*near, *far)
 
@@ -217,14 +233,11 @@
     heads = key_bounds.shape[1] // GROUP
     levels = lax.axis_size("patch").bit_length() - 1
     across = 1 << levels - 1
-    group, member = position()
 
     far_slab = swapped(queries, across)
     kv_sent = cut(keys_new, values_new)
     arrived = [swapped(kv_sent[k - 1], k) for k in range(1, GROUP)]
-    corner = (group * GROUP * rows, member * heads)
-    limits = [lax.dynamic_slice(b, corner, (GROUP * rows, heads)) for b in (key_bounds, value_bounds)]
-    near = rebuild(heads, keys_new, values_new, arrived, keys_copy, values_copy, *limits)
+    near = rebuild(heads, keys_new, values_new, arrived, keys_copy, values_copy, key_bounds, value_bounds)
     for bit in range(2, levels - 2):
         near = jnp.concatenate([near, swapped(near, 1 << bit)], axis=1)
     far = swapped(near, 1 << levels - 2)

time: 72.8 us -> 49.8 us (0.68)
  Pallas kernels: 25.3 us -> 3.92 us
  local copies, waits for them, and re-layouts: 7.41 us -> 5.81 us
    pallas_call x3, Pallas kernels: 18.3 us -> 0.04 us  [cut(): pl.pallas_call(functools.partial(cut_kernel, len(slabs)), out_shape=[shap...]
    pallas_call x1, Pallas kernels: 3.11 us -> 0.94 us  [rebuild(): pl.pallas_call(functools.partial(rebuild_kernel, heads), out_shape=jax.Sh...]
    dynamic_slice x2 -> x0, local copies, waits for them, and re-layouts: 1.54 us -> none  [shards(): lax.dynamic_slice(b, corner, (GROUP * rows, heads))]
    pallas_call x1, Pallas kernels: 2.17 us -> 1.21 us  [merge(): pl.pallas_call(functools.partial(merge_kernel, heads), out_shape=jax.Shap...]
    unnamed x36 -> x16, local copies, waits for them, and re-layouts: 5.87 us -> 5.81 us
  transfers between devices with their start and end apart: 18 -> 18, of which waited for: 8 -> 8; matrix products, arithmetic and copies ran while one was open for 4% -> 4% of each run, Pallas kernels for 15% -> 2%
where the time goes in v2:
time: 49.8 us; the launch traced here: 49.5 us
  starting transfers between devices  22 us (44%)
  waiting for transfers between devices  17.7 us (36%)
  local copies, waits for them, and re-layouts  5.81 us (12%)
  Pallas kernels  3.92 us (8%)
    ppermute x18, starting transfers between devices, swapped(): return lax.ppermute(array, 'patch', [(i, i ^ mask) for i in range(size)])  22 us
    ppermute x18, waiting for transfers between devices, swapped(): return lax.ppermute(array, 'patch', [(i, i ^ mask) for i in range(size)])  17.7 us
    unnamed x16, local copies, waits for them, and re-layouts  5.81 us
    pallas_call x2, Pallas kernels, attend(): pl.pallas_call(functools.partial(attend_kernel, heads), out_shape=[out] *...  1.71 us
    pallas_call x1, Pallas kernels, merge(): pl.pallas_call(functools.partial(merge_kernel, heads), out_shape=jax.Shap...  1.21 us
  transfers between devices with their start and end apart: 18, of which 8 were waited for; matrix products, arithmetic and copies ran while one was open for 4% of the time, Pallas kernels for 2%

profile of v2, /device:TPU:0, one launch (start us, length us, event | category | flops | bytes accessed | tf_op | source)
XLA Modules:
  0.0 49.5 jit_solution(10367341727284717629)
XLA Ops:
  0.0 1.0 %copy-done.3 = bf16[32,2560]{1,0:T(8,128)(2,1)S(1)} copy-done((bf16[32,2560]{1,0:T(8,128)(2,1)S(1)}, bf16[32,2560]{1,0:T(8,128)(2,1)}, u32[]{:S(2)}) %copy-start.3) | copy-done | bytes 163864
  1.0 0.9 %copy-done.5 = bf16[32,2560]{1,0:T(8,128)(2,1)S(1)} copy-done((bf16[32,2560]{1,0:T(8,128)(2,1)S(1)}, bf16[32,2560]{1,0:T(8,128)(2,1)}, u32[]{:S(2)}) %copy-start.5) | copy-done | bytes 163864
  2.4 2.6 %collective-permute-start.4 = (bf16[2,32,640]{2,1,0:T(8,128)(2,1)S(1)}, bf16[2,32,640]{2,1,0:T(8,128)(2,1)S(1)}, u32[]{:S(2)}, u32[]{:S(2)}) collective-permute-start(bf16[2,32,640]{2,1,0:T(8,128)(2,1)S(1)} %get-tuple-element.26), channel_id=1, source_target_pairs={{0,2},{1,3},{2,0},{3,1},{4,6},{5,7},{6,4},{7,5},{8,10},{9,11},{10,... | collective-permute-start | bytes 245768 | tf_op jit(solution)/shard_map/ppermute | solution.py:30
  5.1 0.9 %copy.8.kb = f32[512,20]{1,0:T(8,128)S(1)} copy(f32[512,20]{0,1:T(8,128)} %param.12) | data formatting | bytes 81920 | tf_op args[5]
  6.0 1.0 %copy.9.vb = f32[512,20]{1,0:T(8,128)S(1)} copy(f32[512,20]{0,1:T(8,128)} %param.13) | data formatting | bytes 81920 | tf_op args[6]
  7.0 1.0 %collective-permute-done.4.a2 = bf16[2,32,640]{2,1,0:T(8,128)(2,1)S(1)} collective-permute-done((bf16[2,32,640]{2,1,0:T(8,128)(2,1)S(1)}, bf16[2,32,640]{2,1,0:T(8,128)(2,1)S(1)}, u32[]{:S(2)}, u32[]{:S(2)}) %collective-permute-start.4) | collective-permute-done | bytes 81952 | tf_op jit(solution)/shard_map/ppermute | solution.py:30
  8.0 1.5 %collective-permute-done.5.a3 = bf16[2,32,640]{2,1,0:T(8,128)(2,1)S(1)} collective-permute-done((bf16[2,32,640]{2,1,0:T(8,128)(2,1)S(1)}, bf16[2,32,640]{2,1,0:T(8,128)(2,1)S(1)}, u32[]{:S(2)}, u32[]{:S(2)}) %collective-permute-start.5) | collective-permute-done | bytes 81952 | tf_op jit(solution)/shard_map/ppermute | solution.py:30
  9.5 1.1 %copy-done.2 = bf16[1,512,640]{2,1,0:T(8,128)(2,1)S(1)} copy-done((bf16[1,512,640]{2,1,0:T(8,128)(2,1)S(1)}, bf16[1,512,640]{2,1,0:T(8,128)(2,1)}, u32[]{:S(2)}) %copy-start.2) | copy-done | bytes 655384
  11.5 0.9 %rebuild.1.near = bf16[2,128,640]{2,1,0:T(8,128)(2,1)S(1)} custom-call(bf16[32,2560]{1,0:T(8,128)(2,1)S(1)} %copy-done.4, bf16[32,2560]{1,0:T(8,128)(2,1)S(1)} %copy-done.6, bf16[2,32,640]{2,1,0:T(8,128)(2,1)S(1)} %collective-permute-done.3.a1, bf16[2,32,640]{2,1,0:T(8,128)(2,1)S(1)} %collective-permute-done.4.a2, ...), custom_call_target="tpu_custom_call" | custom-call | bytes 1000 | tf_op jit(solution)/shard_map/rebuild/pallas_call | solution.py:106
  12.5 1.9 %collective-permute-start.6 = (bf16[2,128,640]{2,1,0:T(8,128)(2,1)S(1)}, bf16[2,128,640]{2,1,0:T(8,128)(2,1)S(1)}, u32[]{:S(2)}, u32[]{:S(2)}) collective-permute-start(bf16[2,128,640]{2,1,0:T(8,128)(2,1)S(1)} %rebuild.1.near), channel_id=1, source_target_pairs={{0,4},{1,5},{2,6},{3,7},{4,0},{5,1},{6,2},{7,3},{8,12},{9,13},{10,... | collective-permute-start | bytes 983048 | tf_op jit(solution)/shard_map/ppermute | solution.py:30
  14.3 2.6 %collective-permute-start.10 = (bf16[32,2560]{1,0:T(8,128)(2,1)S(1)}, bf16[32,2560]{1,0:T(8,128)(2,1)S(1)}, u32[]{:S(2)}, u32[]{:S(2)}) collective-permute-start(bf16[32,2560]{1,0:T(8,128)(2,1)S(1)} %copy-done), channel_id=1, source_target_pairs={{0,8},{1,9},{2,10},{3,11},{4,12},{5,13},{6,14},{7,15},{8,0},{9,1},... | collective-permute-start | bytes 491528 | tf_op jit(solution)/shard_map/ppermute | solution.py:30
  16.9 8.2 %collective-permute-done.10.refs_0_.slab = bf16[32,2560]{1,0:T(8,128)(2,1)S(1)} collective-permute-done((bf16[32,2560]{1,0:T(8,128)(2,1)S(1)}, bf16[32,2560]{1,0:T(8,128)(2,1)S(1)}, u32[]{:S(2)}, u32[]{:S(2)}) %collective-permute-start.10) | collective-permute-done | bytes 163872 | tf_op jit(solution)/shard_map/ppermute | solution.py:30
  25.2 1.6 %collective-permute-start.12 = (bf16[1,32,640]{2,1,0:T(8,128)(2,1)S(1)}, bf16[1,32,640]{2,1,0:T(8,128)(2,1)S(1)}, u32[]{:S(2)}, u32[]{:S(2)}) collective-permute-start(bf16[1,32,640]{2,1,0:T(8,128)(2,1)S(1)} %get-tuple-element.33), channel_id=1, source_target_pairs={{0,2},{1,3},{2,0},{3,1},{4,6},{5,7},{6,4},{7,5},{8,10},{9,11},{10,... | collective-permute-start | bytes 122888 | tf_op jit(solution)/shard_map/ppermute | solution.py:30
  27.1 2.2 %collective-permute-done.12.q2 = bf16[1,32,640]{2,1,0:T(8,128)(2,1)S(1)} collective-permute-done((bf16[1,32,640]{2,1,0:T(8,128)(2,1)S(1)}, bf16[1,32,640]{2,1,0:T(8,128)(2,1)S(1)}, u32[]{:S(2)}, u32[]{:S(2)}) %collective-permute-start.12) | collective-permute-done | bytes 40992 | tf_op jit(solution)/shard_map/ppermute | solution.py:30
  29.3 1.0 %collective-permute-done.13.q3 = bf16[1,32,640]{2,1,0:T(8,128)(2,1)S(1)} collective-permute-done((bf16[1,32,640]{2,1,0:T(8,128)(2,1)S(1)}, bf16[1,32,640]{2,1,0:T(8,128)(2,1)S(1)}, u32[]{:S(2)}, u32[]{:S(2)}) %collective-permute-start.13) | collective-permute-done | bytes 40992 | tf_op jit(solution)/shard_map/ppermute | solution.py:30
  31.2 3.4 %collective-permute-start.14 = (bf16[176,128]{1,0:T(8,128)(2,1)S(1)}, bf16[176,128]{1,0:T(8,128)(2,1)S(1)}, u32[]{:S(2)}, u32[]{:S(2)}) collective-permute-start(bf16[176,128]{1,0:T(8,128)(2,1)S(1)} %get-tuple-element.35), channel_id=1, source_target_pairs={{0,8},{1,9},{2,10},{3,11},{4,12},{5,13},{6,14},{7,15},{8,0},{9,1},... | collective-permute-start | bytes 135176 | tf_op jit(solution)/shard_map/ppermute | solution.py:30
  36.6 2.9 %collective-permute-start.16 = (bf16[176,128]{1,0:T(8,128)(2,1)S(1)}, bf16[176,128]{1,0:T(8,128)(2,1)S(1)}, u32[]{:S(2)}, u32[]{:S(2)}) collective-permute-start(bf16[176,128]{1,0:T(8,128)(2,1)S(1)} %get-tuple-element.37), channel_id=1, source_target_pairs={{0,10},{1,11},{2,8},{3,9},{4,14},{5,15},{6,12},{7,13},{8,2},{9,3},... | collective-permute-start | bytes 135176 | tf_op jit(solution)/shard_map/ppermute | solution.py:30
  39.5 1.1 %collective-permute-start.17 = (bf16[176,128]{1,0:T(8,128)(2,1)S(1)}, bf16[176,128]{1,0:T(8,128)(2,1)S(1)}, u32[]{:S(2)}, u32[]{:S(2)}) collective-permute-start(bf16[176,128]{1,0:T(8,128)(2,1)S(1)} %get-tuple-element.38), channel_id=1, source_target_pairs={{0,11},{1,10},{2,9},{3,8},{4,15},{5,14},{6,13},{7,12},{8,3},{9,2},... | collective-permute-start | bytes 135176 | tf_op jit(solution)/shard_map/ppermute | solution.py:30
  41.5 1.6 %collective-permute-start.7 = (bf16[176,128]{1,0:T(8,128)(2,1)S(1)}, bf16[176,128]{1,0:T(8,128)(2,1)S(1)}, u32[]{:S(2)}, u32[]{:S(2)}) collective-permute-start(bf16[176,128]{1,0:T(8,128)(2,1)S(1)} %get-tuple-element.29), channel_id=1, source_target_pairs={{0,1},{1,0},{2,3},{3,2},{4,5},{5,4},{6,7},{7,6},{8,9},{9,8},{10,11... | collective-permute-start | bytes 135176 | tf_op jit(solution)/shard_map/ppermute | solution.py:30
  43.1 1.3 %collective-permute-start.8 = (bf16[176,128]{1,0:T(8,128)(2,1)S(1)}, bf16[176,128]{1,0:T(8,128)(2,1)S(1)}, u32[]{:S(2)}, u32[]{:S(2)}) collective-permute-start(bf16[176,128]{1,0:T(8,128)(2,1)S(1)} %get-tuple-element.30), channel_id=1, source_target_pairs={{0,2},{1,3},{2,0},{3,1},{4,6},{5,7},{6,4},{7,5},{8,10},{9,11},{10,... | collective-permute-start | bytes 135176 | tf_op jit(solution)/shard_map/ppermute | solution.py:30
  44.6 1.6 %collective-permute-done.17.f3 = bf16[176,128]{1,0:T(8,128)(2,1)S(1)} collective-permute-done((bf16[176,128]{1,0:T(8,128)(2,1)S(1)}, bf16[176,128]{1,0:T(8,128)(2,1)S(1)}, u32[]{:S(2)}, u32[]{:S(2)}) %collective-permute-start.17) | collective-permute-done | bytes 45088 | tf_op jit(solution)/shard_map/ppermute | solution.py:30
  46.1 1.1 %collective-permute-done.8.n2 = bf16[176,128]{1,0:T(8,128)(2,1)S(1)} collective-permute-done((bf16[176,128]{1,0:T(8,128)(2,1)S(1)}, bf16[176,128]{1,0:T(8,128)(2,1)S(1)}, u32[]{:S(2)}, u32[]{:S(2)}) %collective-permute-start.8) | collective-permute-done | bytes 45088 | tf_op jit(solution)/shard_map/ppermute | solution.py:30
  47.2 1.1 %collective-permute-done.9.n3 = bf16[176,128]{1,0:T(8,128)(2,1)S(1)} collective-permute-done((bf16[176,128]{1,0:T(8,128)(2,1)S(1)}, bf16[176,128]{1,0:T(8,128)(2,1)S(1)}, u32[]{:S(2)}, u32[]{:S(2)}) %collective-permute-start.9) | collective-permute-done | bytes 45088 | tf_op jit(solution)/shard_map/ppermute | solution.py:30
  48.3 1.2 %merge.1 = bf16[32,2560]{1,0:T(8,128)(2,1)} custom-call(bf16[176,128]{1,0:T(8,128)(2,1)S(1)} %get-tuple-element.28.n0, bf16[176,128]{1,0:T(8,128)(2,1)S(1)} %collective-permute-done.7.n1, bf16[176,128]{1,0:T(8,128)(2,1)S(1)} %collective-permute-done.8.n2, bf16[176,128]{1,0:T(8,128)(2,1)S(1)} %collective-permute-done.9.n3, ...), custom_call_target="tpu_custom_call" | custom-call | bytes 1000 | tf_op jit(solution)/shard_map/merge/pallas_call | solution.py:220
  (35 shorter events, 5.8 us)
Async XLA Ops:
  0.0 9.5 %copy-start.1 = (bf16[1,512,640]{2,1,0:T(8,128)(2,1)S(1)}, bf16[1,512,640]{2,1,0:T(8,128)(2,1)}, u32[]{:S(2)}) copy-start(bf16[1,512,640]{2,1,0:T(8,128)(2,1)} %keys_copy.1) | copy-start | bytes 1966084
  0.0 1.0 %copy-start.3 = (bf16[32,2560]{1,0:T(8,128)(2,1)S(1)}, bf16[32,2560]{1,0:T(8,128)(2,1)}, u32[]{:S(2)}) copy-start(bf16[32,2560]{1,0:T(8,128)(2,1)} %keys_ref.1) | copy-start | bytes 491524
  1.0 0.9 %copy-start.5 = (bf16[32,2560]{1,0:T(8,128)(2,1)S(1)}, bf16[32,2560]{1,0:T(8,128)(2,1)}, u32[]{:S(2)}) copy-start(bf16[32,2560]{1,0:T(8,128)(2,1)} %values_ref.1) | copy-start | bytes 491524
  1.9 5.1 %collective-permute-start.3 = (bf16[2,32,640]{2,1,0:T(8,128)(2,1)S(1)}, bf16[2,32,640]{2,1,0:T(8,128)(2,1)S(1)}, u32[]{:S(2)}, u32[]{:S(2)}) collective-permute-start(bf16[2,32,640]{2,1,0:T(8,128)(2,1)S(1)} %get-tuple-element.25), channel_id=1, source_target_pairs={{0,1},{1,0},{2,3},{3,2},{4,5},{5,4},{6,7},{7,6},{8,9},{9,8},{10,11... | collective-permute-start | bytes 245768 | tf_op jit(solution)/shard_map/ppermute | solution.py:30
  2.4 5.6 %collective-permute-start.4 = (bf16[2,32,640]{2,1,0:T(8,128)(2,1)S(1)}, bf16[2,32,640]{2,1,0:T(8,128)(2,1)S(1)}, u32[]{:S(2)}, u32[]{:S(2)}) collective-permute-start(bf16[2,32,640]{2,1,0:T(8,128)(2,1)S(1)} %get-tuple-element.26), channel_id=1, source_target_pairs={{0,2},{1,3},{2,0},{3,1},{4,6},{5,7},{6,4},{7,5},{8,10},{9,11},{10,... | collective-permute-start | bytes 245768 | tf_op jit(solution)/shard_map/ppermute | solution.py:30
  5.0 4.5 %collective-permute-start.5 = (bf16[2,32,640]{2,1,0:T(8,128)(2,1)S(1)}, bf16[2,32,640]{2,1,0:T(8,128)(2,1)S(1)}, u32[]{:S(2)}, u32[]{:S(2)}) collective-permute-start(bf16[2,32,640]{2,1,0:T(8,128)(2,1)S(1)} %get-tuple-element.27), channel_id=1, source_target_pairs={{0,3},{1,2},{2,1},{3,0},{4,7},{5,6},{6,5},{7,4},{8,11},{9,10},{10,... | collective-permute-start | bytes 245768 | tf_op jit(solution)/shard_map/ppermute | solution.py:30
  6.0 3.5 %copy-start.4 = (bf16[32,2560]{1,0:T(8,128)(2,1)S(1)}, bf16[32,2560]{1,0:T(8,128)(2,1)}, u32[]{:S(2)}) copy-start(bf16[32,2560]{1,0:T(8,128)(2,1)} %keys_ref.1) | copy-start | bytes 491524
  7.0 7.3 %copy-start = (bf16[32,2560]{1,0:T(8,128)(2,1)S(1)}, bf16[32,2560]{1,0:T(8,128)(2,1)}, u32[]{:S(2)}) copy-start(bf16[32,2560]{1,0:T(8,128)(2,1)} %slab.1) | copy-start | bytes 491524
  9.5 1.1 %copy-start.2 = (bf16[1,512,640]{2,1,0:T(8,128)(2,1)S(1)}, bf16[1,512,640]{2,1,0:T(8,128)(2,1)}, u32[]{:S(2)}) copy-start(bf16[1,512,640]{2,1,0:T(8,128)(2,1)} %values_copy.1) | copy-start | bytes 1966084
  12.5 17.8 %collective-permute-start.6 = (bf16[2,128,640]{2,1,0:T(8,128)(2,1)S(1)}, bf16[2,128,640]{2,1,0:T(8,128)(2,1)S(1)}, u32[]{:S(2)}, u32[]{:S(2)}) collective-permute-start(bf16[2,128,640]{2,1,0:T(8,128)(2,1)S(1)} %rebuild.1.near), channel_id=1, source_target_pairs={{0,4},{1,5},{2,6},{3,7},{4,0},{5,1},{6,2},{7,3},{8,12},{9,13},{10,... | collective-permute-start | bytes 983048 | tf_op jit(solution)/shard_map/ppermute | solution.py:30
  14.3 10.8 %collective-permute-start.10 = (bf16[32,2560]{1,0:T(8,128)(2,1)S(1)}, bf16[32,2560]{1,0:T(8,128)(2,1)S(1)}, u32[]{:S(2)}, u32[]{:S(2)}) collective-permute-start(bf16[32,2560]{1,0:T(8,128)(2,1)S(1)} %copy-done), channel_id=1, source_target_pairs={{0,8},{1,9},{2,10},{3,11},{4,12},{5,13},{6,14},{7,15},{8,0},{9,1},... | collective-permute-start | bytes 491528 | tf_op jit(solution)/shard_map/ppermute | solution.py:30
  25.2 1.9 %collective-permute-start.11 = (bf16[1,32,640]{2,1,0:T(8,128)(2,1)S(1)}, bf16[1,32,640]{2,1,0:T(8,128)(2,1)S(1)}, u32[]{:S(2)}, u32[]{:S(2)}) collective-permute-start(bf16[1,32,640]{2,1,0:T(8,128)(2,1)S(1)} %get-tuple-element.32), channel_id=1, source_target_pairs={{0,1},{1,0},{2,3},{3,2},{4,5},{5,4},{6,7},{7,6},{8,9},{9,8},{10,11... | collective-permute-start | bytes 122888 | tf_op jit(solution)/shard_map/ppermute | solution.py:30
  25.2 4.1 %collective-permute-start.12 = (bf16[1,32,640]{2,1,0:T(8,128)(2,1)S(1)}, bf16[1,32,640]{2,1,0:T(8,128)(2,1)S(1)}, u32[]{:S(2)}, u32[]{:S(2)}) collective-permute-start(bf16[1,32,640]{2,1,0:T(8,128)(2,1)S(1)} %get-tuple-element.33), channel_id=1, source_target_pairs={{0,2},{1,3},{2,0},{3,1},{4,6},{5,7},{6,4},{7,5},{8,10},{9,11},{10,... | collective-permute-start | bytes 122888 | tf_op jit(solution)/shard_map/ppermute | solution.py:30
  26.8 3.5 %collective-permute-start.13 = (bf16[1,32,640]{2,1,0:T(8,128)(2,1)S(1)}, bf16[1,32,640]{2,1,0:T(8,128)(2,1)S(1)}, u32[]{:S(2)}, u32[]{:S(2)}) collective-permute-start(bf16[1,32,640]{2,1,0:T(8,128)(2,1)S(1)} %get-tuple-element.34), channel_id=1, source_target_pairs={{0,3},{1,2},{2,1},{3,0},{4,7},{5,6},{6,5},{7,4},{8,11},{9,10},{10,... | collective-permute-start | bytes 122888 | tf_op jit(solution)/shard_map/ppermute | solution.py:30
  31.2 11.9 %collective-permute-start.14 = (bf16[176,128]{1,0:T(8,128)(2,1)S(1)}, bf16[176,128]{1,0:T(8,128)(2,1)S(1)}, u32[]{:S(2)}, u32[]{:S(2)}) collective-permute-start(bf16[176,128]{1,0:T(8,128)(2,1)S(1)} %get-tuple-element.35), channel_id=1, source_target_pairs={{0,8},{1,9},{2,10},{3,11},{4,12},{5,13},{6,14},{7,15},{8,0},{9,1},... | collective-permute-start | bytes 135176 | tf_op jit(solution)/shard_map/ppermute | solution.py:30
  34.6 9.8 %collective-permute-start.15 = (bf16[176,128]{1,0:T(8,128)(2,1)S(1)}, bf16[176,128]{1,0:T(8,128)(2,1)S(1)}, u32[]{:S(2)}, u32[]{:S(2)}) collective-permute-start(bf16[176,128]{1,0:T(8,128)(2,1)S(1)} %get-tuple-element.36), channel_id=1, source_target_pairs={{0,9},{1,8},{2,11},{3,10},{4,13},{5,12},{6,15},{7,14},{8,1},{9,0},... | collective-permute-start | bytes 135176 | tf_op jit(solution)/shard_map/ppermute | solution.py:30
  34.6 1.9 %collective-permute-start = (bf16[1,32,640]{2,1,0:T(8,128)(2,1)S(1)}, bf16[1,32,640]{2,1,0:T(8,128)(2,1)S(1)}, u32[]{:S(2)}, u32[]{:S(2)}) collective-permute-start(bf16[1,32,640]{2,1,0:T(8,128)(2,1)S(1)} %get-tuple-element.22), channel_id=1, source_target_pairs={{0,1},{1,0},{2,3},{3,2},{4,5},{5,4},{6,7},{7,6},{8,9},{9,8},{10,11... | collective-permute-start | bytes 122888 | tf_op jit(solution)/shard_map/ppermute | solution.py:30
  34.9 4.6 %collective-permute-start.1 = (bf16[1,32,640]{2,1,0:T(8,128)(2,1)S(1)}, bf16[1,32,640]{2,1,0:T(8,128)(2,1)S(1)}, u32[]{:S(2)}, u32[]{:S(2)}) collective-permute-start(bf16[1,32,640]{2,1,0:T(8,128)(2,1)S(1)} %get-tuple-element.23), channel_id=1, source_target_pairs={{0,2},{1,3},{2,0},{3,1},{4,6},{5,7},{6,4},{7,5},{8,10},{9,11},{10,... | collective-permute-start | bytes 122888 | tf_op jit(solution)/shard_map/ppermute | solution.py:30
  35.8 4.8 %collective-permute-start.2 = (bf16[1,32,640]{2,1,0:T(8,128)(2,1)S(1)}, bf16[1,32,640]{2,1,0:T(8,128)(2,1)S(1)}, u32[]{:S(2)}, u32[]{:S(2)}) collective-permute-start(bf16[1,32,640]{2,1,0:T(8,128)(2,1)S(1)} %get-tuple-element.24), channel_id=1, source_target_pairs={{0,3},{1,2},{2,1},{3,0},{4,7},{5,6},{6,5},{7,4},{8,11},{9,10},{10,... | collective-permute-start | bytes 122888 | tf_op jit(solution)/shard_map/ppermute | solution.py:30
  36.6 8.0 %collective-permute-start.16 = (bf16[176,128]{1,0:T(8,128)(2,1)S(1)}, bf16[176,128]{1,0:T(8,128)(2,1)S(1)}, u32[]{:S(2)}, u32[]{:S(2)}) collective-permute-start(bf16[176,128]{1,0:T(8,128)(2,1)S(1)} %get-tuple-element.37), channel_id=1, source_target_pairs={{0,10},{1,11},{2,8},{3,9},{4,14},{5,15},{6,12},{7,13},{8,2},{9,3},... | collective-permute-start | bytes 135176 | tf_op jit(solution)/shard_map/ppermute | solution.py:30
  39.5 6.6 %collective-permute-start.17 = (bf16[176,128]{1,0:T(8,128)(2,1)S(1)}, bf16[176,128]{1,0:T(8,128)(2,1)S(1)}, u32[]{:S(2)}, u32[]{:S(2)}) collective-permute-start(bf16[176,128]{1,0:T(8,128)(2,1)S(1)} %get-tuple-element.38), channel_id=1, source_target_pairs={{0,11},{1,10},{2,9},{3,8},{4,15},{5,14},{6,13},{7,12},{8,3},{9,2},... | collective-permute-start | bytes 135176 | tf_op jit(solution)/shard_map/ppermute | solution.py:30
  41.5 4.7 %collective-permute-start.7 = (bf16[176,128]{1,0:T(8,128)(2,1)S(1)}, bf16[176,128]{1,0:T(8,128)(2,1)S(1)}, u32[]{:S(2)}, u32[]{:S(2)}) collective-permute-start(bf16[176,128]{1,0:T(8,128)(2,1)S(1)} %get-tuple-element.29), channel_id=1, source_target_pairs={{0,1},{1,0},{2,3},{3,2},{4,5},{5,4},{6,7},{7,6},{8,9},{9,8},{10,11... | collective-permute-start | bytes 135176 | tf_op jit(solution)/shard_map/ppermute | solution.py:30
  43.1 4.1 %collective-permute-start.8 = (bf16[176,128]{1,0:T(8,128)(2,1)S(1)}, bf16[176,128]{1,0:T(8,128)(2,1)S(1)}, u32[]{:S(2)}, u32[]{:S(2)}) collective-permute-start(bf16[176,128]{1,0:T(8,128)(2,1)S(1)} %get-tuple-element.30), channel_id=1, source_target_pairs={{0,2},{1,3},{2,0},{3,1},{4,6},{5,7},{6,4},{7,5},{8,10},{9,11},{10,... | collective-permute-start | bytes 135176 | tf_op jit(solution)/shard_map/ppermute | solution.py:30
  44.4 3.9 %collective-permute-start.9 = (bf16[176,128]{1,0:T(8,128)(2,1)S(1)}, bf16[176,128]{1,0:T(8,128)(2,1)S(1)}, u32[]{:S(2)}, u32[]{:S(2)}) collective-permute-start(bf16[176,128]{1,0:T(8,128)(2,1)S(1)} %get-tuple-element.31), channel_id=1, source_target_pairs={{0,3},{1,2},{2,1},{3,0},{4,7},{5,6},{6,5},{7,4},{8,11},{9,10},{10,... | collective-permute-start | bytes 135176 | tf_op jit(solution)/shard_map/ppermute | solution.py:30
  (1 other events, 0.9 us)

commit v3 on v2

v3 whole, which is shorter than its diff:
```python
import functools

import jax
import jax.numpy as jnp
from jax import lax
from jax.experimental import pallas as pl
from jax.experimental.pallas import tpu as pltpu
from jax.sharding import PartitionSpec as P

GROUP = 4
LOG2E = 1.4426950408889634
MB = 1 << 20
HBM = pl.BlockSpec(memory_space=pltpu.HBM)
VMEM = pl.BlockSpec(memory_space=pltpu.VMEM)


def limit(size):
    return pltpu.CompilerParams(vmem_limit_bytes=size)


def cost(size):
    return pl.CostEstimate(flops=0, bytes_accessed=size, transcendentals=0)


def swapped(array, mask):
    size = lax.axis_size("patch")
    return lax.ppermute(array, "patch", [(i, i ^ mask) for i in range(size)])


def position():
    place = lax.axis_index("patch")
    return place // GROUP, place % GROUP


def part(index, size):
    return pl.ds(pl.multiple_of(index * size, size), size)


def run_copies(pairs, sems):
    copies = [pltpu.make_async_copy(a, b, sems.at[i]) for i, (a, b) in enumerate(pairs)]
    for copy in copies:
        copy.start()
    for copy in copies:
        copy.wait()


def cut_first_kernel(keys_ref, values_ref, o1, o2, o3, sems):
    width = keys_ref.shape[1] // GROUP
    _, member = position()
    pairs = []
    for k, out in enumerate((o1, o2, o3), 1):
        for i, slab in enumerate((keys_ref, values_ref)):
            pairs.append((slab.at[:, part(member ^ k, width)], out.at[i]))
    run_copies(pairs, sems)


def cut_kernel(first_ref, second_ref, o1, o2, o3):
    width = first_ref.shape[1] // GROUP
    _, member = position()
    for k, out in enumerate((o1, o2, o3), 1):
        for i, slab in enumerate((first_ref, second_ref)):
            out[i] = slab[:, part(member ^ k, width)]


def cut(first, second, from_hbm):
    rows, features = first.shape
    shape = jax.ShapeDtypeStruct((2, rows, features // GROUP), first.dtype)
    return pl.pallas_call(
        cut_first_kernel if from_hbm else cut_kernel,
        out_shape=[shape] * (GROUP - 1),
        in_specs=[HBM if from_hbm else VMEM] * 2,
        out_specs=[VMEM] * (GROUP - 1),
        scratch_shapes=[pltpu.SemaphoreType.DMA((6,))] if from_hbm else [],
        compiler_params=limit(4 * MB),
        cost_estimate=cost(1000),
        name="cut",
    )(first, second)


def fetch_kernel(
    heads, keys_ref, values_ref, keys_copy, values_copy, kb, vb, own, old, limits, lines, turned, sems
):
    rows, features = keys_ref.shape
    width = features // GROUP
    group, member = position()
    block = part(group, GROUP * rows)
    pairs = []
    for i, (slab, copy, bound) in enumerate(((keys_ref, keys_copy, kb), (values_ref, values_copy, vb))):
        pairs.append((bound.at[:, block], lines.at[i]))
        pairs.append((slab.at[:, part(member, width)], own.at[i]))
        for k in range(GROUP):
            source = copy.at[0, part(group * GROUP + (member ^ k), rows), :]
            pairs.append((source, old.at[i, pl.ds(k * rows, rows), :]))
    run_copies(pairs, sems)
    for i in range(2):
        chosen = lines[i, pl.ds(member * heads, heads), :]
        padding = jnp.zeros((limits.shape[2] - heads, GROUP * rows), chosen.dtype)
        turned[...] = jnp.concatenate([chosen, padding], axis=0).T
        for k in range(GROUP):
            limits[i, pl.ds(k * rows, rows), :] = turned[part(member ^ k, rows), :]


def fetch(heads, keys_new, values_new, keys_copy, values_copy, key_bounds, value_bounds):
    rows, features = keys_new.shape
    width = features // GROUP
    kind = keys_new.dtype
    return pl.pallas_call(
        functools.partial(fetch_kernel, heads),
        out_shape=[
            jax.ShapeDtypeStruct((2, rows, width), kind),
            jax.ShapeDtypeStruct((2, GROUP * rows, width), kind),
            jax.ShapeDtypeStruct((2, GROUP * rows, 128), key_bounds.dtype),
        ],
        in_specs=[HBM] * 6,
        out_specs=[VMEM] * 3,
        scratch_shapes=[
            pltpu.VMEM((2, key_bounds.shape[1], GROUP * rows), key_bounds.dtype),
            pltpu.VMEM((GROUP * rows, 128), key_bounds.dtype),
            pltpu.SemaphoreType.DMA((12,)),
        ],
        compiler_params=limit(4 * MB),
        cost_estimate=cost(1000),
        name="fetch",
    )(keys_new, values_new, keys_copy, values_copy, key_bounds.T, value_bounds.T)


def rebuild_kernel(heads, own, a1, a2, a3, old, limits, *outs):
    rows = own.shape[1]
    head = own.shape[2] // heads
    for k, piece in enumerate((own, a1, a2, a3)):
        place = slice(k * rows, (k + 1) * rows)
        for i in range(2):
            for h in range(heads):
                lanes = slice(h * head, (h + 1) * head)
                bound = limits[i, place, h : h + 1]
                previous = old[i, place, lanes].astype(jnp.float32)
                change = jnp.clip(piece[i, :, lanes].astype(jnp.float32) - previous, -bound, bound)
                change = change.astype(jnp.bfloat16).astype(jnp.float32)
                outs[i][place, lanes] = (previous + change).astype(outs[i].dtype)


def rebuild(heads, own, arrived, old, limits):
    return pl.pallas_call(
        functools.partial(rebuild_kernel, heads),
        out_shape=[jax.ShapeDtypeStruct(old.shape[1:], old.dtype)] * 2,
        in_specs=[VMEM] * 6,
        out_specs=[VMEM] * 2,
        compiler_params=limit(4 * MB),
        cost_estimate=cost(1000),
        name="rebuild",
    )(own, *arrived, old, limits)


def attend_kernel(heads, which, slab, q1, q2, q3, near_keys, near_values, far_keys, far_values, o0, o1, o2, o3):
    rows, features = slab.shape
    width = features // GROUP
    head = width // heads
    _, member = position()
    scale = head ** (-0.5) * LOG2E
    lane = lax.broadcasted_iota(jnp.int32, (GROUP * rows, head), 1)
    stats = jnp.zeros((GROUP * rows, head), jnp.float32)
    contract = (((1,), (1,)), ((), ()))
    outs = (o0, o1, o2, o3)
    for h in range(heads):
        lanes = slice(h * head, (h + 1) * head)
        own = slab[:, pl.ds(pl.multiple_of(member * width + h * head, head), head)]
        query = jnp.concatenate([own] + [q[which, :, lanes] for q in (q1, q2, q3)], axis=0)
        scores = [
            lax.dot_general(query, keys[:, lanes], contract, preferred_element_type=jnp.float32)
            for keys in (near_keys, far_keys)
        ]
        peak = jnp.maximum(
            jnp.max(scores[0], axis=1, keepdims=True), jnp.max(scores[1], axis=1, keepdims=True)
        )
        level = (peak * scale).astype(jnp.bfloat16).astype(jnp.float32)
        total = None
        for values, score in zip((near_values, far_values), scores):
            probs = jnp.exp2(score * scale - level).astype(jnp.bfloat16)
            value = values[:, lanes]
            joined = jnp.concatenate([value, jnp.ones_like(value)], axis=1)
            product = jnp.dot(probs, joined, preferred_element_type=jnp.float32)
            total = product if total is None else total + product
        weighted = total[:, :head].astype(jnp.bfloat16)
        weight = total[:, head:]
        high = weight.astype(jnp.bfloat16).astype(jnp.float32)
        stats = jnp.where(lane == h, level, stats)
        stats = jnp.where(lane == heads + h, high, stats)
        stats = jnp.where(lane == 2 * heads + h, weight - high, stats)
        for k, out in enumerate(outs):
            out[h * rows : (h + 1) * rows, :] = weighted[k * rows : (k + 1) * rows]
    half = rows // 2
    for k, out in enumerate(outs):
        first = stats[k * rows : k * rows + half]
        second = stats[k * rows + half : (k + 1) * rows]
        packed = first + pltpu.roll(second, 16, 1)
        out[heads * rows :, :] = packed.astype(out.dtype)


def attend(heads, which, slab, pieces, near, far):
    rows, features = slab.shape
    width = features // GROUP
    head = width // heads
    out = jax.ShapeDtypeStruct((heads * rows + rows // 2, head), slab.dtype)
    room = 4 * MB + 8 * near[0].size * near[0].dtype.itemsize + 32 * GROUP * rows * near[0].shape[0]
    return pl.pallas_call(
        functools.partial(attend_kernel, heads, which),
        out_shape=[out] * GROUP,
        in_specs=[VMEM] * 8,
        out_specs=[VMEM] * GROUP,
        compiler_params=limit(room),
        cost_estimate=cost(1000),
        name="attend",
    )(slab, *pieces, *near, *far)


def merge_kernel(heads, n0, n1, n2, n3, f0, f1, f2, f3, out):
    rows = out.shape[0]
    head = n0.shape[1]
    width = heads * head
    _, member = position()

    def unpack(ref):
        packed = ref[heads * rows :, :].astype(jnp.float32)
        stats = jnp.concatenate([packed, pltpu.roll(packed, head - 16, 1)], axis=0)
        weight = pltpu.roll(stats, head - heads, 1) + pltpu.roll(stats, head - 2 * heads, 1)
        return stats, weight

    for k, (near, far) in enumerate(((n0, f0), (n1, f1), (n2, f2), (n3, f3))):
        near_level, near_weight = unpack(near)
        far_level, far_weight = unpack(far)
        top = jnp.maximum(near_level, far_level)
        near_scale = jnp.exp2(near_level - top)
        far_scale = jnp.exp2(far_level - top)
        total = near_scale * near_weight + far_scale * far_weight
        near_scale = near_scale / total
        far_scale = far_scale / total
        for h in range(heads):
            place = slice(h * rows, (h + 1) * rows)
            mixed = near[place, :].astype(jnp.float32) * near_scale[:, h : h + 1]
            mixed = mixed + far[place, :].astype(jnp.float32) * far_scale[:, h : h + 1]
            start = pl.multiple_of((member ^ k) * width + h * head, head)
            out[:, pl.ds(start, head)] = mixed.astype(out.dtype)


def merge(heads, near, far, rows):
    head = near[0].shape[1]
    return pl.pallas_call(
        functools.partial(merge_kernel, heads),
        out_shape=jax.ShapeDtypeStruct((rows, GROUP * heads * head), near[0].dtype),
        in_specs=[VMEM] * 8,
        out_specs=VMEM,
        compiler_params=limit(4 * MB),
        cost_estimate=cost(1000),
        name="merge",
    )(*near, *far)


def shards(queries, keys_new, values_new, keys_copy, values_copy, key_bounds, value_bounds):
    rows = queries.shape[0]
    heads = key_bounds.shape[1] // GROUP
    levels = lax.axis_size("patch").bit_length() - 1
    across = 1 << levels - 1
    others = range(1, GROUP)

    far_slab = swapped(queries, across)
    sent = cut(keys_new, values_new, True)
    arrived = [swapped(sent[k - 1], k) for k in others]
    own, old, limits = fetch(
        heads, keys_new, values_new, keys_copy, values_copy, key_bounds, value_bounds
    )
    near = rebuild(heads, own, arrived, old, limits)
    for bit in range(2, levels - 2):
        near = [jnp.concatenate([a, swapped(a, 1 << bit)], axis=0) for a in near]
    far = [swapped(a, 1 << levels - 2) for a in near]
    sent = cut(queries, far_slab, False)
    pieces = [swapped(sent[k - 1], k) for k in others]
    far_out = attend(heads, 1, far_slab, pieces, near, far)
    far_back = [swapped(far_out[k], across + k) for k in range(GROUP)]
    own_out = attend(heads, 0, queries, pieces, near, far)
    own_back = [own_out[0]] + [swapped(own_out[k], k) for k in others]
    return merge(heads, own_back, far_back, rows)


def solution(mesh):
    rows = P(("clips", "patch"), None)
    copies = P(("clips", "patch"), None, None)
    bounds = P("clips", None)
    return jax.shard_map(
        shards,
        mesh=mesh,
        in_specs=(rows, rows, rows, copies, copies, bounds, bounds),
        out_specs=rows,
        check_vma=False,
    )
```

time: 49.8 us -> 38.3 us (0.77)
  waiting for transfers between devices: 17.7 us -> 11.4 us
  starting transfers between devices: 22 us -> 18.4 us
  local copies, waits for them, and re-layouts: 5.81 us -> 4.02 us
    ppermute x18 -> x16, waiting for transfers between devices: 17.7 us -> 11.4 us  [swapped(): return lax.ppermute(array, 'patch', [(i, i ^ mask) for i in range(size)])]
    ppermute x18 -> x16, starting transfers between devices: 22 us -> 18.4 us  [swapped(): return lax.ppermute(array, 'patch', [(i, i ^ mask) for i in range(size)])]
    unnamed x16 -> x14, local copies, waits for them, and re-layouts: 5.81 us -> 4.02 us
  transfers between devices with their start and end apart: 18 -> 16, of which waited for: 8 -> 7; matrix products, arithmetic and copies ran while one was open for 4% -> 0% of each run, Pallas kernels for 2% -> 5%
where the time goes in v3:
time: 38.3 us; the launch traced here: 38 us
  starting transfers between devices  18.4 us (48%)
  waiting for transfers between devices  11.4 us (30%)
  Pallas kernels  4.06 us (11%)
  local copies, waits for them, and re-layouts  4.02 us (10%)
    ppermute x16, starting transfers between devices, swapped(): return lax.ppermute(array, 'patch', [(i, i ^ mask) for i in range(size)])  18.4 us
    ppermute x16, waiting for transfers between devices, swapped(): return lax.ppermute(array, 'patch', [(i, i ^ mask) for i in range(size)])  11.4 us
    unnamed x14, local copies, waits for them, and re-layouts  4.02 us
    pallas_call x2, Pallas kernels, attend(): pl.pallas_call(functools.partial(attend_kernel, heads, which), out_shape=...  1.66 us
    pallas_call x1, Pallas kernels, merge(): pl.pallas_call(functools.partial(merge_kernel, heads), out_shape=jax.Shap...  1.22 us
  transfers between devices with their start and end apart: 16, of which 7 were waited for; matrix products, arithmetic and copies ran while one was open for 0% of the time, Pallas kernels for 5%

profile of v3, /device:TPU:0, one launch (start us, length us, event | category | flops | bytes accessed | tf_op | source)
XLA Modules:
  0.0 38.0 jit_solution(14918495301795104240)
XLA Ops:
  0.0 0.9 %copy-done.2 = bf16[32,2560]{1,0:T(8,128)(2,1)S(1)} copy-done((bf16[32,2560]{1,0:T(8,128)(2,1)S(1)}, bf16[32,2560]{1,0:T(8,128)(2,1)}, u32[]{:S(2)}) %copy-start.2) | copy-done | bytes 163864
  0.9 0.9 %copy-done.3 = bf16[32,2560]{1,0:T(8,128)(2,1)S(1)} copy-done((bf16[32,2560]{1,0:T(8,128)(2,1)S(1)}, bf16[32,2560]{1,0:T(8,128)(2,1)}, u32[]{:S(2)}) %copy-start.3) | copy-done | bytes 163864
  2.0 0.5 %collective-permute-start.4 = (bf16[2,32,640]{2,1,0:T(8,128)(2,1)S(1)}, bf16[2,32,640]{2,1,0:T(8,128)(2,1)S(1)}, u32[]{:S(2)}, u32[]{:S(2)}) collective-permute-start(bf16[2,32,640]{2,1,0:T(8,128)(2,1)S(1)} %get-tuple-element.28), channel_id=1, source_target_pairs={{0,1},{1,0},{2,3},{3,2},{4,5},{5,4},{6,7},{7,6},{8,9},{9,8},{10,11... | collective-permute-start | bytes 245768 | tf_op jit(solution)/shard_map/ppermute | solution.py:27
  2.5 2.6 %collective-permute-start.5 = (bf16[2,32,640]{2,1,0:T(8,128)(2,1)S(1)}, bf16[2,32,640]{2,1,0:T(8,128)(2,1)S(1)}, u32[]{:S(2)}, u32[]{:S(2)}) collective-permute-start(bf16[2,32,640]{2,1,0:T(8,128)(2,1)S(1)} %get-tuple-element.29), channel_id=1, source_target_pairs={{0,2},{1,3},{2,0},{3,1},{4,6},{5,7},{6,4},{7,5},{8,10},{9,11},{10,... | collective-permute-start | bytes 245768 | tf_op jit(solution)/shard_map/ppermute | solution.py:27
  5.1 2.8 %collective-permute-start = (bf16[32,2560]{1,0:T(8,128)(2,1)S(1)}, bf16[32,2560]{1,0:T(8,128)(2,1)S(1)}, u32[]{:S(2)}, u32[]{:S(2)}) collective-permute-start(bf16[32,2560]{1,0:T(8,128)(2,1)S(1)} %copy-done.4), channel_id=1, source_target_pairs={{0,8},{1,9},{2,10},{3,11},{4,12},{5,13},{6,14},{7,15},{8,0},{9,1},... | collective-permute-start | bytes 491528 | tf_op jit(solution)/shard_map/ppermute | solution.py:27
  8.0 1.1 %copy-done = bf16[1,512,640]{2,1,0:T(8,128)(2,1)S(1)} copy-done((bf16[1,512,640]{2,1,0:T(8,128)(2,1)S(1)}, bf16[1,512,640]{2,1,0:T(8,128)(2,1)}, u32[]{:S(2)}) %copy-start) | copy-done | bytes 655384
  9.1 1.1 %copy-done.1 = bf16[1,512,640]{2,1,0:T(8,128)(2,1)S(1)} copy-done((bf16[1,512,640]{2,1,0:T(8,128)(2,1)S(1)}, bf16[1,512,640]{2,1,0:T(8,128)(2,1)}, u32[]{:S(2)}) %copy-start.1) | copy-done | bytes 655384
  10.1 0.7 %fetch.1 = (bf16[2,32,640]{2,1,0:T(8,128)(2,1)S(1)}, bf16[2,128,640]{2,1,0:T(8,128)(2,1)S(1)}, f32[2,128,128]{2,1,0:T(8,128)S(1)}) custom-call(bf16[32,2560]{1,0:T(8,128)(2,1)S(1)} %copy-done.2, bf16[32,2560]{1,0:T(8,128)(2,1)S(1)} %copy-done.3, bf16[1,512,640]{2,1,0:T(8,128)(2,1)S(1)} %copy-done, bf16[1,512,640]{2,1,0:T(8,128)(2,1)S(1)} %copy-done.1, ...), custom_call_target="tpu_custom_call" | custom-call | bytes 1000 | tf_op jit(solution)/shard_map/fetch/pallas_call | solution.py:107
  11.2 1.6 %collective-permute-start.7 = (bf16[128,640]{1,0:T(8,128)(2,1)S(1)}, bf16[128,640]{1,0:T(8,128)(2,1)S(1)}, u32[]{:S(2)}, u32[]{:S(2)}) collective-permute-start(bf16[128,640]{1,0:T(8,128)(2,1)S(1)} %get-tuple-element.33.near_keys), channel_id=1, source_target_pairs={{0,4},{1,5},{2,6},{3,7},{4,0},{5,1},{6,2},{7,3},{8,12},{9,13},{10,... | collective-permute-start | bytes 491528 | tf_op jit(solution)/shard_map/ppermute | solution.py:27
  13.3 3.0 %collective-permute-done.second_ref.slab = bf16[32,2560]{1,0:T(8,128)(2,1)S(1)} collective-permute-done((bf16[32,2560]{1,0:T(8,128)(2,1)S(1)}, bf16[32,2560]{1,0:T(8,128)(2,1)S(1)}, u32[]{:S(2)}, u32[]{:S(2)}) %collective-permute-start) | collective-permute-done | bytes 163872 | tf_op jit(solution)/shard_map/ppermute | solution.py:27
  16.4 1.6 %collective-permute-start.2 = (bf16[2,32,640]{2,1,0:T(8,128)(2,1)S(1)}, bf16[2,32,640]{2,1,0:T(8,128)(2,1)S(1)}, u32[]{:S(2)}, u32[]{:S(2)}) collective-permute-start(bf16[2,32,640]{2,1,0:T(8,128)(2,1)S(1)} %get-tuple-element.25), channel_id=1, source_target_pairs={{0,2},{1,3},{2,0},{3,1},{4,6},{5,7},{6,4},{7,5},{8,10},{9,11},{10,... | collective-permute-start | bytes 245768 | tf_op jit(solution)/shard_map/ppermute | solution.py:27
  18.2 1.5 %collective-permute-done.7.far_keys = bf16[128,640]{1,0:T(8,128)(2,1)S(1)} collective-permute-done((bf16[128,640]{1,0:T(8,128)(2,1)S(1)}, bf16[128,640]{1,0:T(8,128)(2,1)S(1)}, u32[]{:S(2)}, u32[]{:S(2)}) %collective-permute-start.7) | collective-permute-done | bytes 163872 | tf_op jit(solution)/shard_map/ppermute | solution.py:27
  19.8 3.4 %collective-permute-done.8.far_values = bf16[128,640]{1,0:T(8,128)(2,1)S(1)} collective-permute-done((bf16[128,640]{1,0:T(8,128)(2,1)S(1)}, bf16[128,640]{1,0:T(8,128)(2,1)S(1)}, u32[]{:S(2)}, u32[]{:S(2)}) %collective-permute-start.8) | collective-permute-done | bytes 163872 | tf_op jit(solution)/shard_map/ppermute | solution.py:27
  23.2 0.8 %attend.3 = (bf16[176,128]{1,0:T(8,128)(2,1)S(1)}, bf16[176,128]{1,0:T(8,128)(2,1)S(1)}, bf16[176,128]{1,0:T(8,128)(2,1)S(1)}, bf16[176,128]{1,0:T(8,128)(2,1)S(1)}) custom-call(bf16[32,2560]{1,0:T(8,128)(2,1)S(1)} %collective-permute-done.second_ref.slab, bf16[2,32,640]{2,1,0:T(8,128)(2,1)S(1)} %collective-permute-done.1.q1, ...), custom_call_target="tpu_custom_call" | custom-call | bytes 1000 | tf_op jit(solution)/shard_map/attend/pallas_call | solution.py:205
  24.0 1.7 %collective-permute-start.12 = (bf16[176,128]{1,0:T(8,128)(2,1)S(1)}, bf16[176,128]{1,0:T(8,128)(2,1)S(1)}, u32[]{:S(2)}, u32[]{:S(2)}) collective-permute-start(bf16[176,128]{1,0:T(8,128)(2,1)S(1)} %get-tuple-element.39), channel_id=1, source_target_pairs={{0,8},{1,9},{2,10},{3,11},{4,12},{5,13},{6,14},{7,15},{8,0},{9,1},... | collective-permute-start | bytes 135176 | tf_op jit(solution)/shard_map/ppermute | solution.py:27
  25.7 0.6 %collective-permute-start.13 = (bf16[176,128]{1,0:T(8,128)(2,1)S(1)}, bf16[176,128]{1,0:T(8,128)(2,1)S(1)}, u32[]{:S(2)}, u32[]{:S(2)}) collective-permute-start(bf16[176,128]{1,0:T(8,128)(2,1)S(1)} %get-tuple-element.40), channel_id=1, source_target_pairs={{0,9},{1,8},{2,11},{3,10},{4,13},{5,12},{6,15},{7,14},{8,1},{9,0},... | collective-permute-start | bytes 135176 | tf_op jit(solution)/shard_map/ppermute | solution.py:27
  26.4 2.6 %collective-permute-start.14 = (bf16[176,128]{1,0:T(8,128)(2,1)S(1)}, bf16[176,128]{1,0:T(8,128)(2,1)S(1)}, u32[]{:S(2)}, u32[]{:S(2)}) collective-permute-start(bf16[176,128]{1,0:T(8,128)(2,1)S(1)} %get-tuple-element.41), channel_id=1, source_target_pairs={{0,10},{1,11},{2,8},{3,9},{4,14},{5,15},{6,12},{7,13},{8,2},{9,3},... | collective-permute-start | bytes 135176 | tf_op jit(solution)/shard_map/ppermute | solution.py:27
  29.0 1.3 %collective-permute-start.15 = (bf16[176,128]{1,0:T(8,128)(2,1)S(1)}, bf16[176,128]{1,0:T(8,128)(2,1)S(1)}, u32[]{:S(2)}, u32[]{:S(2)}) collective-permute-start(bf16[176,128]{1,0:T(8,128)(2,1)S(1)} %get-tuple-element.42), channel_id=1, source_target_pairs={{0,11},{1,10},{2,9},{3,8},{4,15},{5,14},{6,13},{7,12},{8,3},{9,2},... | collective-permute-start | bytes 135176 | tf_op jit(solution)/shard_map/ppermute | solution.py:27
  30.3 0.8 %attend.2 = (bf16[176,128]{1,0:T(8,128)(2,1)S(1)}, bf16[176,128]{1,0:T(8,128)(2,1)S(1)}, bf16[176,128]{1,0:T(8,128)(2,1)S(1)}, bf16[176,128]{1,0:T(8,128)(2,1)S(1)}) custom-call(bf16[32,2560]{1,0:T(8,128)(2,1)S(1)} %copy-done.4, bf16[2,32,640]{2,1,0:T(8,128)(2,1)S(1)} %collective-permute-done.1.q1, bf16[2,32,640]{2,1,0:T(8,128)(2,1)S(1)} %collective-permute-done.2.q2, ...), custom_call_target="tpu_custom_call" | custom-call | bytes 1000 | tf_op jit(solution)/shard_map/attend/pallas_call | solution.py:205
  31.1 1.6 %collective-permute-start.10 = (bf16[176,128]{1,0:T(8,128)(2,1)S(1)}, bf16[176,128]{1,0:T(8,128)(2,1)S(1)}, u32[]{:S(2)}, u32[]{:S(2)}) collective-permute-start(bf16[176,128]{1,0:T(8,128)(2,1)S(1)} %get-tuple-element.37), channel_id=1, source_target_pairs={{0,2},{1,3},{2,0},{3,1},{4,6},{5,7},{6,4},{7,5},{8,10},{9,11},{10,... | collective-permute-start | bytes 135176 | tf_op jit(solution)/shard_map/ppermute | solution.py:27
  32.7 0.6 %collective-permute-start.9 = (bf16[176,128]{1,0:T(8,128)(2,1)S(1)}, bf16[176,128]{1,0:T(8,128)(2,1)S(1)}, u32[]{:S(2)}, u32[]{:S(2)}) collective-permute-start(bf16[176,128]{1,0:T(8,128)(2,1)S(1)} %get-tuple-element.36), channel_id=1, source_target_pairs={{0,1},{1,0},{2,3},{3,2},{4,5},{5,4},{6,7},{7,6},{8,9},{9,8},{10,11... | collective-permute-start | bytes 135176 | tf_op jit(solution)/shard_map/ppermute | solution.py:27
  33.3 1.8 %collective-permute-done.14.f2 = bf16[176,128]{1,0:T(8,128)(2,1)S(1)} collective-permute-done((bf16[176,128]{1,0:T(8,128)(2,1)S(1)}, bf16[176,128]{1,0:T(8,128)(2,1)S(1)}, u32[]{:S(2)}, u32[]{:S(2)}) %collective-permute-start.14) | collective-permute-done | bytes 45088 | tf_op jit(solution)/shard_map/ppermute | solution.py:27
  35.6 1.1 %collective-permute-done.10.n2 = bf16[176,128]{1,0:T(8,128)(2,1)S(1)} collective-permute-done((bf16[176,128]{1,0:T(8,128)(2,1)S(1)}, bf16[176,128]{1,0:T(8,128)(2,1)S(1)}, u32[]{:S(2)}, u32[]{:S(2)}) %collective-permute-start.10) | collective-permute-done | bytes 45088 | tf_op jit(solution)/shard_map/ppermute | solution.py:27
  36.8 1.2 %merge.1 = bf16[32,2560]{1,0:T(8,128)(2,1)} custom-call(bf16[176,128]{1,0:T(8,128)(2,1)S(1)} %get-tuple-element.35.n0, bf16[176,128]{1,0:T(8,128)(2,1)S(1)} %collective-permute-done.9.n1, bf16[176,128]{1,0:T(8,128)(2,1)S(1)} %collective-permute-done.10.n2, bf16[176,128]{1,0:T(8,128)(2,1)S(1)} %collective-permute-done.11.n3, ...), custom_call_target="tpu_custom_call" | custom-call | bytes 1000 | tf_op jit(solution)/shard_map/merge/pallas_call | solution.py:247
  (29 shorter events, 2.0 us)
Async XLA Ops:
  0.0 0.9 %copy-start.2 = (bf16[32,2560]{1,0:T(8,128)(2,1)S(1)}, bf16[32,2560]{1,0:T(8,128)(2,1)}, u32[]{:S(2)}) copy-start(bf16[32,2560]{1,0:T(8,128)(2,1)} %keys_ref.3) | copy-start | bytes 491524
  0.9 0.9 %copy-start.3 = (bf16[32,2560]{1,0:T(8,128)(2,1)S(1)}, bf16[32,2560]{1,0:T(8,128)(2,1)}, u32[]{:S(2)}) copy-start(bf16[32,2560]{1,0:T(8,128)(2,1)} %values_ref.3) | copy-start | bytes 491524
  1.8 3.3 %copy-start.4 = (bf16[32,2560]{1,0:T(8,128)(2,1)S(1)}, bf16[32,2560]{1,0:T(8,128)(2,1)}, u32[]{:S(2)}) copy-start(bf16[32,2560]{1,0:T(8,128)(2,1)} %slab.1) | copy-start | bytes 491524
  1.8 6.1 %copy-start.5 = (f32[512,20]{0,1:T(8,128)S(1)}, f32[512,20]{0,1:T(8,128)}, u32[]{:S(2)}) copy-start(f32[512,20]{0,1:T(8,128)} %param.12) | copy-start | bytes 122884
  1.8 6.1 %copy-start.6 = (f32[512,20]{0,1:T(8,128)S(1)}, f32[512,20]{0,1:T(8,128)}, u32[]{:S(2)}) copy-start(f32[512,20]{0,1:T(8,128)} %param.13) | copy-start | bytes 122884
  2.0 8.9 %collective-permute-start.4 = (bf16[2,32,640]{2,1,0:T(8,128)(2,1)S(1)}, bf16[2,32,640]{2,1,0:T(8,128)(2,1)S(1)}, u32[]{:S(2)}, u32[]{:S(2)}) collective-permute-start(bf16[2,32,640]{2,1,0:T(8,128)(2,1)S(1)} %get-tuple-element.28), channel_id=1, source_target_pairs={{0,1},{1,0},{2,3},{3,2},{4,5},{5,4},{6,7},{7,6},{8,9},{9,8},{10,11... | collective-permute-start | bytes 245768 | tf_op jit(solution)/shard_map/ppermute | solution.py:27
  2.5 8.4 %collective-permute-start.5 = (bf16[2,32,640]{2,1,0:T(8,128)(2,1)S(1)}, bf16[2,32,640]{2,1,0:T(8,128)(2,1)S(1)}, u32[]{:S(2)}, u32[]{:S(2)}) collective-permute-start(bf16[2,32,640]{2,1,0:T(8,128)(2,1)S(1)} %get-tuple-element.29), channel_id=1, source_target_pairs={{0,2},{1,3},{2,0},{3,1},{4,6},{5,7},{6,4},{7,5},{8,10},{9,11},{10,... | collective-permute-start | bytes 245768 | tf_op jit(solution)/shard_map/ppermute | solution.py:27
  5.1 5.8 %collective-permute-start.6 = (bf16[2,32,640]{2,1,0:T(8,128)(2,1)S(1)}, bf16[2,32,640]{2,1,0:T(8,128)(2,1)S(1)}, u32[]{:S(2)}, u32[]{:S(2)}) collective-permute-start(bf16[2,32,640]{2,1,0:T(8,128)(2,1)S(1)} %get-tuple-element.30), channel_id=1, source_target_pairs={{0,3},{1,2},{2,1},{3,0},{4,7},{5,6},{6,5},{7,4},{8,11},{9,10},{10,... | collective-permute-start | bytes 245768 | tf_op jit(solution)/shard_map/ppermute | solution.py:27
  5.1 11.1 %collective-permute-start = (bf16[32,2560]{1,0:T(8,128)(2,1)S(1)}, bf16[32,2560]{1,0:T(8,128)(2,1)S(1)}, u32[]{:S(2)}, u32[]{:S(2)}) collective-permute-start(bf16[32,2560]{1,0:T(8,128)(2,1)S(1)} %copy-done.4), channel_id=1, source_target_pairs={{0,8},{1,9},{2,10},{3,11},{4,12},{5,13},{6,14},{7,15},{8,0},{9,1},... | collective-permute-start | bytes 491528 | tf_op jit(solution)/shard_map/ppermute | solution.py:27
  8.0 1.1 %copy-start = (bf16[1,512,640]{2,1,0:T(8,128)(2,1)S(1)}, bf16[1,512,640]{2,1,0:T(8,128)(2,1)}, u32[]{:S(2)}) copy-start(bf16[1,512,640]{2,1,0:T(8,128)(2,1)} %keys_copy.1) | copy-start | bytes 1966084
  9.0 1.1 %copy-start.1 = (bf16[1,512,640]{2,1,0:T(8,128)(2,1)S(1)}, bf16[1,512,640]{2,1,0:T(8,128)(2,1)}, u32[]{:S(2)}) copy-start(bf16[1,512,640]{2,1,0:T(8,128)(2,1)} %values_copy.1) | copy-start | bytes 1966084
  11.2 8.5 %collective-permute-start.7 = (bf16[128,640]{1,0:T(8,128)(2,1)S(1)}, bf16[128,640]{1,0:T(8,128)(2,1)S(1)}, u32[]{:S(2)}, u32[]{:S(2)}) collective-permute-start(bf16[128,640]{1,0:T(8,128)(2,1)S(1)} %get-tuple-element.33.near_keys), channel_id=1, source_target_pairs={{0,4},{1,5},{2,6},{3,7},{4,0},{5,1},{6,2},{7,3},{8,12},{9,13},{10,... | collective-permute-start | bytes 491528 | tf_op jit(solution)/shard_map/ppermute | solution.py:27
  12.9 10.3 %collective-permute-start.8 = (bf16[128,640]{1,0:T(8,128)(2,1)S(1)}, bf16[128,640]{1,0:T(8,128)(2,1)S(1)}, u32[]{:S(2)}, u32[]{:S(2)}) collective-permute-start(bf16[128,640]{1,0:T(8,128)(2,1)S(1)} %get-tuple-element.34.near_values), channel_id=1, source_target_pairs={{0,4},{1,5},{2,6},{3,7},{4,0},{5,1},{6,2},{7,3},{8,12},{9,13},{10,... | collective-permute-start | bytes 491528 | tf_op jit(solution)/shard_map/ppermute | solution.py:27
  16.3 6.9 %collective-permute-start.1 = (bf16[2,32,640]{2,1,0:T(8,128)(2,1)S(1)}, bf16[2,32,640]{2,1,0:T(8,128)(2,1)S(1)}, u32[]{:S(2)}, u32[]{:S(2)}) collective-permute-start(bf16[2,32,640]{2,1,0:T(8,128)(2,1)S(1)} %get-tuple-element.24), channel_id=1, source_target_pairs={{0,1},{1,0},{2,3},{3,2},{4,5},{5,4},{6,7},{7,6},{8,9},{9,8},{10,11... | collective-permute-start | bytes 245768 | tf_op jit(solution)/shard_map/ppermute | solution.py:27
  16.4 6.8 %collective-permute-start.2 = (bf16[2,32,640]{2,1,0:T(8,128)(2,1)S(1)}, bf16[2,32,640]{2,1,0:T(8,128)(2,1)S(1)}, u32[]{:S(2)}, u32[]{:S(2)}) collective-permute-start(bf16[2,32,640]{2,1,0:T(8,128)(2,1)S(1)} %get-tuple-element.25), channel_id=1, source_target_pairs={{0,2},{1,3},{2,0},{3,1},{4,6},{5,7},{6,4},{7,5},{8,10},{9,11},{10,... | collective-permute-start | bytes 245768 | tf_op jit(solution)/shard_map/ppermute | solution.py:27
  18.0 5.2 %collective-permute-start.3 = (bf16[2,32,640]{2,1,0:T(8,128)(2,1)S(1)}, bf16[2,32,640]{2,1,0:T(8,128)(2,1)S(1)}, u32[]{:S(2)}, u32[]{:S(2)}) collective-permute-start(bf16[2,32,640]{2,1,0:T(8,128)(2,1)S(1)} %get-tuple-element.26), channel_id=1, source_target_pairs={{0,3},{1,2},{2,1},{3,0},{4,7},{5,6},{6,5},{7,4},{8,11},{9,10},{10,... | collective-permute-start | bytes 245768 | tf_op jit(solution)/shard_map/ppermute | solution.py:27
  24.0 8.7 %collective-permute-start.12 = (bf16[176,128]{1,0:T(8,128)(2,1)S(1)}, bf16[176,128]{1,0:T(8,128)(2,1)S(1)}, u32[]{:S(2)}, u32[]{:S(2)}) collective-permute-start(bf16[176,128]{1,0:T(8,128)(2,1)S(1)} %get-tuple-element.39), channel_id=1, source_target_pairs={{0,8},{1,9},{2,10},{3,11},{4,12},{5,13},{6,14},{7,15},{8,0},{9,1},... | collective-permute-start | bytes 135176 | tf_op jit(solution)/shard_map/ppermute | solution.py:27
  25.7 7.0 %collective-permute-start.13 = (bf16[176,128]{1,0:T(8,128)(2,1)S(1)}, bf16[176,128]{1,0:T(8,128)(2,1)S(1)}, u32[]{:S(2)}, u32[]{:S(2)}) collective-permute-start(bf16[176,128]{1,0:T(8,128)(2,1)S(1)} %get-tuple-element.40), channel_id=1, source_target_pairs={{0,9},{1,8},{2,11},{3,10},{4,13},{5,12},{6,15},{7,14},{8,1},{9,0},... | collective-permute-start | bytes 135176 | tf_op jit(solution)/shard_map/ppermute | solution.py:27
  26.4 8.7 %collective-permute-start.14 = (bf16[176,128]{1,0:T(8,128)(2,1)S(1)}, bf16[176,128]{1,0:T(8,128)(2,1)S(1)}, u32[]{:S(2)}, u32[]{:S(2)}) collective-permute-start(bf16[176,128]{1,0:T(8,128)(2,1)S(1)} %get-tuple-element.41), channel_id=1, source_target_pairs={{0,10},{1,11},{2,8},{3,9},{4,14},{5,15},{6,12},{7,13},{8,2},{9,3},... | collective-permute-start | bytes 135176 | tf_op jit(solution)/shard_map/ppermute | solution.py:27
  29.0 6.6 %collective-permute-start.15 = (bf16[176,128]{1,0:T(8,128)(2,1)S(1)}, bf16[176,128]{1,0:T(8,128)(2,1)S(1)}, u32[]{:S(2)}, u32[]{:S(2)}) collective-permute-start(bf16[176,128]{1,0:T(8,128)(2,1)S(1)} %get-tuple-element.42), channel_id=1, source_target_pairs={{0,11},{1,10},{2,9},{3,8},{4,15},{5,14},{6,13},{7,12},{8,3},{9,2},... | collective-permute-start | bytes 135176 | tf_op jit(solution)/shard_map/ppermute | solution.py:27
  31.1 5.5 %collective-permute-start.10 = (bf16[176,128]{1,0:T(8,128)(2,1)S(1)}, bf16[176,128]{1,0:T(8,128)(2,1)S(1)}, u32[]{:S(2)}, u32[]{:S(2)}) collective-permute-start(bf16[176,128]{1,0:T(8,128)(2,1)S(1)} %get-tuple-element.37), channel_id=1, source_target_pairs={{0,2},{1,3},{2,0},{3,1},{4,6},{5,7},{6,4},{7,5},{8,10},{9,11},{10,... | collective-permute-start | bytes 135176 | tf_op jit(solution)/shard_map/ppermute | solution.py:27
  32.7 4.1 %collective-permute-start.11 = (bf16[176,128]{1,0:T(8,128)(2,1)S(1)}, bf16[176,128]{1,0:T(8,128)(2,1)S(1)}, u32[]{:S(2)}, u32[]{:S(2)}) collective-permute-start(bf16[176,128]{1,0:T(8,128)(2,1)S(1)} %get-tuple-element.38), channel_id=1, source_target_pairs={{0,3},{1,2},{2,1},{3,0},{4,7},{5,6},{6,5},{7,4},{8,11},{9,10},{10,... | collective-permute-start | bytes 135176 | tf_op jit(solution)/shard_map/ppermute | solution.py:27
  32.7 4.1 %collective-permute-start.9 = (bf16[176,128]{1,0:T(8,128)(2,1)S(1)}, bf16[176,128]{1,0:T(8,128)(2,1)S(1)}, u32[]{:S(2)}, u32[]{:S(2)}) collective-permute-start(bf16[176,128]{1,0:T(8,128)(2,1)S(1)} %get-tuple-element.36), channel_id=1, source_target_pairs={{0,1},{1,0},{2,3},{3,2},{4,5},{5,4},{6,7},{7,6},{8,9},{9,8},{10,11... | collective-permute-start | bytes 135176 | tf_op jit(solution)/shard_map/ppermute | solution.py:27

commit v4 on v3

v4 whole, which is shorter than its diff:
```python
import functools

import jax
import jax.numpy as jnp
from jax import lax
from jax.experimental import pallas as pl
from jax.experimental.pallas import tpu as pltpu
from jax.sharding import PartitionSpec as P

GROUP = 4
LOG2E = 1.4426950408889634
MB = 1 << 20
HBM = pl.BlockSpec(memory_space=pltpu.HBM)
VMEM = pl.BlockSpec(memory_space=pltpu.VMEM)


def limit(size):
    return pltpu.CompilerParams(vmem_limit_bytes=size)


def cost(size):
    return pl.CostEstimate(flops=0, bytes_accessed=size, transcendentals=0)


def swapped(array, mask):
    size = lax.axis_size("patch")
    return lax.ppermute(array, "patch", [(i, i ^ mask) for i in range(size)])


def position():
    place = lax.axis_index("patch")
    return place // GROUP, place % GROUP


def part(index, size):
    return pl.ds(pl.multiple_of(index * size, size), size)


def run_copies(pairs, sems):
    copies = [pltpu.make_async_copy(a, b, sems.at[i]) for i, (a, b) in enumerate(pairs)]
    for copy in copies:
        copy.start()
    for copy in copies:
        copy.wait()


def cut_kernel(count, *refs):
    slabs, sent, kept, sems = refs[:count], refs[-3], refs[-2], refs[-1]
    width = slabs[0].shape[1] // GROUP
    _, member = position()
    pairs = []
    for i, slab in enumerate(slabs):
        for k in range(2):
            pairs.append((slab.at[:, part(member ^ (1 + 2 * k), width)], sent.at[i, k]))
            pairs.append((slab.at[:, part(member ^ (2 * k), width)], kept.at[i, k]))
    run_copies(pairs, sems)


def cut(*slabs):
    rows, features = slabs[0].shape
    shape = jax.ShapeDtypeStruct((len(slabs), 2, rows, features // GROUP), slabs[0].dtype)
    return pl.pallas_call(
        functools.partial(cut_kernel, len(slabs)),
        out_shape=[shape] * 2,
        in_specs=[HBM] * len(slabs),
        out_specs=[VMEM] * 2,
        scratch_shapes=[pltpu.SemaphoreType.DMA((4 * len(slabs),))],
        compiler_params=limit(4 * MB),
        cost_estimate=cost(1000),
        name="cut",
    )(*slabs)


def join_kernel(kept, arrived, keys, values, query, crossing):
    rows = kept.shape[2]
    for i, out in enumerate((keys, values, query)):
        out[:rows] = kept[i, 1]
        out[rows:] = arrived[i, 1]
    for k in range(2):
        crossing[k, :rows] = kept[2, k]
        crossing[k, rows:] = arrived[2, k]


def join(kept, arrived):
    _, _, rows, width = kept.shape
    shape = jax.ShapeDtypeStruct((2 * rows, width), kept.dtype)
    return pl.pallas_call(
        join_kernel,
        out_shape=[shape] * 3 + [jax.ShapeDtypeStruct((2, 2 * rows, width), kept.dtype)],
        in_specs=[VMEM] * 2,
        out_specs=[VMEM] * 4,
        compiler_params=limit(4 * MB),
        cost_estimate=cost(1000),
        name="join",
    )(kept, arrived)


def pair_kernel(query, far_query, *refs):
    out = refs[-1]
    out[0] = query[...]
    out[1] = far_query[1]


def pair(query, far_query, *earlier):
    return pl.pallas_call(
        pair_kernel,
        out_shape=jax.ShapeDtypeStruct(far_query.shape, far_query.dtype),
        in_specs=[VMEM] * 2 + [HBM] * len(earlier),
        out_specs=VMEM,
        compiler_params=limit(4 * MB),
        cost_estimate=cost(1000),
        name="pair",
    )(query, far_query, *earlier)


def fetch_kernel(heads, keys_copy, values_copy, kb, vb, old, limits, lines, turned, sems):
    rows = old.shape[1] // GROUP
    group, member = position()
    block = part(group, GROUP * rows)
    pairs = []
    for i, (copy, bound) in enumerate(((keys_copy, kb), (values_copy, vb))):
        pairs.append((bound.at[:, block], lines.at[i]))
        for k in range(GROUP):
            source = copy.at[0, part(group * GROUP + (member ^ k), rows), :]
            pairs.append((source, old.at[i, pl.ds(k * rows, rows), :]))
    run_copies(pairs, sems)
    for i in range(2):
        chosen = lines[i, pl.ds(member * heads, heads), :]
        padding = jnp.zeros((limits.shape[2] - heads, GROUP * rows), chosen.dtype)
        turned[...] = jnp.concatenate([chosen, padding], axis=0).T
        for k in range(GROUP):
            limits[i, pl.ds(k * rows, rows), :] = turned[part(member ^ k, rows), :]


def fetch(heads, rows, keys_copy, values_copy, key_bounds, value_bounds):
    width = keys_copy.shape[2]
    return pl.pallas_call(
        functools.partial(fetch_kernel, heads),
        out_shape=[
            jax.ShapeDtypeStruct((2, GROUP * rows, width), keys_copy.dtype),
            jax.ShapeDtypeStruct((2, GROUP * rows, 128), key_bounds.dtype),
        ],
        in_specs=[HBM] * 4,
        out_specs=[VMEM] * 2,
        scratch_shapes=[
            pltpu.VMEM((2, key_bounds.shape[1], GROUP * rows), key_bounds.dtype),
            pltpu.VMEM((GROUP * rows, 128), key_bounds.dtype),
            pltpu.SemaphoreType.DMA((10,)),
        ],
        compiler_params=limit(4 * MB),
        cost_estimate=cost(1000),
        name="fetch",
    )(keys_copy, values_copy, key_bounds.T, value_bounds.T)


def rebuild_kernel(heads, i, kept, beside, opposite, old, limits, out):
    rows = kept.shape[2]
    head = kept.shape[3] // heads
    pieces = (kept.at[i, 0], beside.at[i, 0], opposite.at[pl.ds(0, rows)], opposite.at[pl.ds(rows, rows)])
    for k, piece in enumerate(pieces):
        place = slice(k * rows, (k + 1) * rows)
        for h in range(heads):
            lanes = slice(h * head, (h + 1) * head)
            bound = limits[i, place, h : h + 1]
            previous = old[i, place, lanes].astype(jnp.float32)
            change = jnp.clip(piece[:, lanes].astype(jnp.float32) - previous, -bound, bound)
            change = change.astype(jnp.bfloat16).astype(jnp.float32)
            out[place, lanes] = (previous + change).astype(out.dtype)


def rebuild(heads, i, kept, beside, opposite, old, limits):
    return pl.pallas_call(
        functools.partial(rebuild_kernel, heads, i),
        out_shape=jax.ShapeDtypeStruct(old.shape[1:], old.dtype),
        in_specs=[VMEM] * 5,
        out_specs=VMEM,
        compiler_params=limit(4 * MB),
        cost_estimate=cost(1000),
        name="rebuild",
    )(kept, beside, opposite, old, limits)


def attend_kernel(heads, parts, count, *refs):
    queries, (near_keys, near_values, far_keys, far_values) = refs[:count], refs[count : count + 4]
    refs = refs[-len(parts) :]
    width = near_keys.shape[1]
    rows = sum(query.shape[0] for query in queries) // GROUP
    head = width // heads
    outs = [ref.at[j] for ref, group in zip(refs, parts) for j in range(len(group))]
    scale = head ** (-0.5) * LOG2E
    lane = lax.broadcasted_iota(jnp.int32, (GROUP * rows, head), 1)
    stats = jnp.zeros((GROUP * rows, head), jnp.float32)
    contract = (((1,), (1,)), ((), ()))
    for h in range(heads):
        lanes = slice(h * head, (h + 1) * head)
        query = jnp.concatenate([q[:, lanes] for q in queries], axis=0)
        scores = [
            lax.dot_general(query, keys[:, lanes], contract, preferred_element_type=jnp.float32)
            for keys in (near_keys, far_keys)
        ]
        peak = jnp.maximum(
            jnp.max(scores[0], axis=1, keepdims=True), jnp.max(scores[1], axis=1, keepdims=True)
        )
        level = (peak * scale).astype(jnp.bfloat16).astype(jnp.float32)
        total = None
        for values, score in zip((near_values, far_values), scores):
            probs = jnp.exp2(score * scale - level).astype(jnp.bfloat16)
            value = values[:, lanes]
            joined = jnp.concatenate([value, jnp.ones_like(value)], axis=1)
            product = jnp.dot(probs, joined, preferred_element_type=jnp.float32)
            total = product if total is None else total + product
        weighted = total[:, :head].astype(jnp.bfloat16)
        weight = total[:, head:]
        high = weight.astype(jnp.bfloat16).astype(jnp.float32)
        stats = jnp.where(lane == h, level, stats)
        stats = jnp.where(lane == heads + h, high, stats)
        stats = jnp.where(lane == 2 * heads + h, weight - high, stats)
        for k, out in enumerate(outs):
            out[h * rows : (h + 1) * rows, :] = weighted[k * rows : (k + 1) * rows]
    half = rows // 2
    for k, out in enumerate(outs):
        first = stats[k * rows : k * rows + half]
        second = stats[k * rows + half : (k + 1) * rows]
        packed = first + pltpu.roll(second, 16, 1)
        out[heads * rows :, :] = packed.astype(out.dtype)


def far_kernel(heads, parts, far_query, opposite, *refs):
    attend_kernel(heads, parts, 2, far_query.at[0], opposite.at[1], *refs)


def own_kernel(heads, parts, kept, beside, opposite, *refs):
    attend_kernel(heads, parts, 3, kept.at[2, 0], beside.at[2, 0], opposite.at[0], *refs)


def attend(kernel, heads, parts, rows, queries, near, far, *earlier):
    tokens, width = near[0].shape
    shape = (heads * rows + rows // 2, width // heads)
    outs = [jax.ShapeDtypeStruct((len(group),) + shape, near[0].dtype) for group in parts]
    room = 4 * MB + 8 * near[0].size * near[0].dtype.itemsize + 32 * GROUP * rows * tokens
    return pl.pallas_call(
        functools.partial(kernel, heads, parts),
        out_shape=outs,
        in_specs=[VMEM] * (len(queries) + 4) + [HBM] * len(earlier),
        out_specs=[VMEM] * len(outs),
        compiler_params=limit(room),
        cost_estimate=cost(1000),
        name="attend",
    )(*queries, *near, *far, *earlier)


def merge_kernel(heads, n0, n1, n2, n3, f0, f1, f2, f3, out):
    rows = out.shape[0]
    head = n0.shape[2]
    width = heads * head
    _, member = position()

    def unpack(ref):
        packed = ref[0, heads * rows :, :].astype(jnp.float32)
        stats = jnp.concatenate([packed, pltpu.roll(packed, head - 16, 1)], axis=0)
        weight = pltpu.roll(stats, head - heads, 1) + pltpu.roll(stats, head - 2 * heads, 1)
        return stats, weight

    for k, (near, far) in enumerate(((n0, f0), (n1, f1), (n2, f2), (n3, f3))):
        near_level, near_weight = unpack(near)
        far_level, far_weight = unpack(far)
        top = jnp.maximum(near_level, far_level)
        near_scale = jnp.exp2(near_level - top)
        far_scale = jnp.exp2(far_level - top)
        total = near_scale * near_weight + far_scale * far_weight
        near_scale = near_scale / total
        far_scale = far_scale / total
        for h in range(heads):
            place = slice(h * rows, (h + 1) * rows)
            mixed = near[0, place, :].astype(jnp.float32) * near_scale[:, h : h + 1]
            mixed = mixed + far[0, place, :].astype(jnp.float32) * far_scale[:, h : h + 1]
            start = pl.multiple_of((member ^ k) * width + h * head, head)
            out[:, pl.ds(start, head)] = mixed.astype(out.dtype)


def merge(heads, near, far, rows):
    head = near[0].shape[2]
    return pl.pallas_call(
        functools.partial(merge_kernel, heads),
        out_shape=jax.ShapeDtypeStruct((rows, GROUP * heads * head), near[0].dtype),
        in_specs=[VMEM] * 8,
        out_specs=VMEM,
        compiler_params=limit(4 * MB),
        cost_estimate=cost(1000),
        name="merge",
    )(*near, *far)


def shards(queries, keys_new, values_new, keys_copy, values_copy, key_bounds, value_bounds):
    rows = queries.shape[0]
    heads = key_bounds.shape[1] // GROUP
    levels = lax.axis_size("patch").bit_length() - 1
    across = 1 << levels - 1

    pinned = [pltpu.with_memory_space_constraint(a, pltpu.HBM) for a in (keys_new, values_new, queries)]
    copies = [pltpu.with_memory_space_constraint(a, pltpu.HBM) for a in (keys_copy, values_copy)]
    sent, kept = cut(*pinned)
    beside = swapped(sent, 1)
    x_keys, x_values, x_query, crossing = join(kept, beside)
    far_query = swapped(crossing, across)
    opposite = [swapped(a, 2) for a in (x_keys, x_values)]
    old, limits = fetch(heads, rows, *copies, key_bounds, value_bounds)
    near = [rebuild(heads, i, kept, beside, opposite[i], old, limits) for i in range(2)]
    for bit in range(2, levels - 2):
        near = [jnp.concatenate([a, swapped(a, 1 << bit)], axis=0) for a in near]
    far = [swapped(a, 1 << levels - 2) for a in near]
    q_opposite = swapped(pair(x_query, far_query, *near), 2)
    parts = ((0, 1), (2,), (3,))
    far_out = attend(far_kernel, heads, parts, rows, (far_query, q_opposite), near, far)
    f01, f2, f3 = [swapped(a, across + group[0]) for a, group in zip(far_out, parts)]
    parts = ((0,), (1,), (2, 3))
    own_query = (kept, beside, q_opposite)
    n0, n1, n23 = attend(own_kernel, heads, parts, rows, own_query, near, far, far_out[2])
    n1, n23 = swapped(n1, 1), swapped(n23, 2)
    near_parts = (n0, n1, n23, swapped(n23[1:], 1))
    far_parts = (f01, swapped(f01[1:], 1), f2, f3)
    return merge(heads, near_parts, far_parts, rows)


def solution(mesh):
    rows = P(("clips", "patch"), None)
    copies = P(("clips", "patch"), None, None)
    bounds = P("clips", None)
    return jax.shard_map(
        shards,
        mesh=mesh,
        in_specs=(rows, rows, rows, copies, copies, bounds, bounds),
        out_specs=rows,
        check_vma=False,
    )
```

time: 38.3 us -> 35.3 us (0.922)
  the two profiles are of different devices: /device:TPU:0 before, /device:TPU:1 now
where the time goes in v4:
time: 35.3 us; the launch traced here: 35.1 us
  starting transfers between devices  16.6 us (47%)
  waiting for transfers between devices  12.8 us (36%)
  Pallas kernels  5.57 us (16%)
    ppermute x14, starting transfers between devices, swapped(): return lax.ppermute(array, 'patch', [(i, i ^ mask) for i in range(size)])  16.6 us
    ppermute x14, waiting for transfers between devices, swapped(): return lax.ppermute(array, 'patch', [(i, i ^ mask) for i in range(size)])  12.8 us
    pallas_call x2, Pallas kernels, attend(): pl.pallas_call(functools.partial(kernel, heads, parts), out_shape=outs, i...  1.67 us
    pallas_call x1, Pallas kernels, merge(): pl.pallas_call(functools.partial(merge_kernel, heads), out_shape=jax.Shap...  1.22 us
    pallas_call x1, Pallas kernels, fetch(): pl.pallas_call(functools.partial(fetch_kernel, heads), out_shape=[jax.Sha...  1.15 us
    pallas_call x1, Pallas kernels, cut(): pl.pallas_call(functools.partial(cut_kernel, len(slabs)), out_shape=[shap...  1.11 us
  transfers between devices with their start and end apart: 14, of which 7 were waited for; matrix products, arithmetic and copies ran while one was open for 0% of the time, Pallas kernels for 7%

profile of v4, /device:TPU:1, one launch (start us, length us, event | category | flops | bytes accessed | tf_op | source)
XLA Modules:
  0.0 35.1 jit_solution(5660590455141545400)
XLA Ops:
  0.0 1.1 %cut.1 = (bf16[3,2,32,640]{3,2,1,0:T(8,128)(2,1)S(1)}, bf16[3,2,32,640]{3,2,1,0:T(8,128)(2,1)S(1)}) custom-call(bf16[32,2560]{1,0:T(8,128)(2,1)} %refs_0_.1, bf16[32,2560]{1,0:T(8,128)(2,1)} %refs_1_.1, bf16[32,2560]{1,0:T(8,128)(2,1)} %refs_2_.1), custom_call_target="tpu_custom_call" | custom-call | bytes 1000 | tf_op jit(solution)/shard_map/cut/pallas_call | solution.py:62
  1.2 1.5 %collective-permute-done.arrived.beside = bf16[3,2,32,640]{3,2,1,0:T(8,128)(2,1)S(1)} collective-permute-done((bf16[3,2,32,640]{3,2,1,0:T(8,128)(2,1)S(1)}, bf16[3,2,32,640]{3,2,1,0:T(8,128)(2,1)S(1)}, u32[]{:S(2)}, u32[]{:S(2)}) %collective-permute-start) | collective-permute-done | bytes 245792 | tf_op jit(solution)/shard_map/ppermute | solution.py:27
  2.7 3.5 %collective-permute-start.1 = (bf16[2,64,640]{2,1,0:T(8,128)(2,1)S(1)}, bf16[2,64,640]{2,1,0:T(8,128)(2,1)S(1)}, u32[]{:S(2)}, u32[]{:S(2)}) collective-permute-start(bf16[2,64,640]{2,1,0:T(8,128)(2,1)S(1)} %get-tuple-element.22), channel_id=1, source_target_pairs={{0,8},{1,9},{2,10},{3,11},{4,12},{5,13},{6,14},{7,15},{8,0},{9,1},... | collective-permute-start | bytes 491528 | tf_op jit(solution)/shard_map/ppermute | solution.py:27
  6.2 1.2 %collective-permute-start.3 = (bf16[64,640]{1,0:T(8,128)(2,1)S(1)}, bf16[64,640]{1,0:T(8,128)(2,1)S(1)}, u32[]{:S(2)}, u32[]{:S(2)}) collective-permute-start(bf16[64,640]{1,0:T(8,128)(2,1)S(1)} %get-tuple-element.26), channel_id=1, source_target_pairs={{0,2},{1,3},{2,0},{3,1},{4,6},{5,7},{6,4},{7,5},{8,10},{9,11},{10,... | collective-permute-start | bytes 245768 | tf_op jit(solution)/shard_map/ppermute | solution.py:27
  7.4 0.3 collective-permute-start.2
  7.7 1.2 %fetch.1 = (bf16[2,128,640]{2,1,0:T(8,128)(2,1)S(1)}, f32[2,128,128]{2,1,0:T(8,128)S(1)}) custom-call(bf16[1,512,640]{2,1,0:T(8,128)(2,1)} %keys_copy.1, bf16[1,512,640]{2,1,0:T(8,128)(2,1)} %values_copy.1, f32[20,512]{1,0:T(8,128)S(1)} %bitcast.2, f32[20,512]{1,0:T(8,128)S(1)} %bitcast.3), custom_call_target="tpu_custom_call" | custom-call | bytes 1000 | tf_op jit(solution)/shard_map/fetch/pallas_call | solution.py:137
  8.9 1.0 %collective-permute-done.3.opposite = bf16[64,640]{1,0:T(8,128)(2,1)S(1)} collective-permute-done((bf16[64,640]{1,0:T(8,128)(2,1)S(1)}, bf16[64,640]{1,0:T(8,128)(2,1)S(1)}, u32[]{:S(2)}, u32[]{:S(2)}) %collective-permute-start.3) | collective-permute-done | bytes 81952 | tf_op jit(solution)/shard_map/ppermute | solution.py:27
  9.8 0.2 rebuild.3.refs_1_
  10.0 1.4 %collective-permute-start.6 = (bf16[128,640]{1,0:T(8,128)(2,1)S(1)}, bf16[128,640]{1,0:T(8,128)(2,1)S(1)}, u32[]{:S(2)}, u32[]{:S(2)}) collective-permute-start(bf16[128,640]{1,0:T(8,128)(2,1)S(1)} %rebuild.3.refs_1_), channel_id=1, source_target_pairs={{0,4},{1,5},{2,6},{3,7},{4,0},{5,1},{6,2},{7,3},{8,12},{9,13},{10,... | collective-permute-start | bytes 491528 | tf_op jit(solution)/shard_map/ppermute | solution.py:27
  11.4 0.5 %collective-permute-done.2.opposite = bf16[64,640]{1,0:T(8,128)(2,1)S(1)} collective-permute-done((bf16[64,640]{1,0:T(8,128)(2,1)S(1)}, bf16[64,640]{1,0:T(8,128)(2,1)S(1)}, u32[]{:S(2)}, u32[]{:S(2)}) %collective-permute-start.2) | collective-permute-done | bytes 81952 | tf_op jit(solution)/shard_map/ppermute | solution.py:27
  12.1 1.4 %collective-permute-start.5 = (bf16[128,640]{1,0:T(8,128)(2,1)S(1)}, bf16[128,640]{1,0:T(8,128)(2,1)S(1)}, u32[]{:S(2)}, u32[]{:S(2)}) collective-permute-start(bf16[128,640]{1,0:T(8,128)(2,1)S(1)} %rebuild.2.refs_0_), channel_id=1, source_target_pairs={{0,4},{1,5},{2,6},{3,7},{4,0},{5,1},{6,2},{7,3},{8,12},{9,13},{10,... | collective-permute-start | bytes 491528 | tf_op jit(solution)/shard_map/ppermute | solution.py:27
  13.5 0.6 %collective-permute-done.1.far_query = bf16[2,64,640]{2,1,0:T(8,128)(2,1)S(1)} collective-permute-done((bf16[2,64,640]{2,1,0:T(8,128)(2,1)S(1)}, bf16[2,64,640]{2,1,0:T(8,128)(2,1)S(1)}, u32[]{:S(2)}, u32[]{:S(2)}) %collective-permute-start.1) | collective-permute-done | bytes 163872 | tf_op jit(solution)/shard_map/ppermute | solution.py:27
  14.0 1.0 %collective-permute-start.4 = (bf16[2,64,640]{2,1,0:T(8,128)(2,1)S(1)}, bf16[2,64,640]{2,1,0:T(8,128)(2,1)S(1)}, u32[]{:S(2)}, u32[]{:S(2)}) collective-permute-start(bf16[2,64,640]{2,1,0:T(8,128)(2,1)S(1)} %pair.1), channel_id=1, source_target_pairs={{0,2},{1,3},{2,0},{3,1},{4,6},{5,7},{6,4},{7,5},{8,10},{9,11},{10,... | collective-permute-start | bytes 491528 | tf_op jit(solution)/shard_map/ppermute | solution.py:27
  15.0 1.9 %collective-permute-done.6.refs_3_ = bf16[128,640]{1,0:T(8,128)(2,1)S(1)} collective-permute-done((bf16[128,640]{1,0:T(8,128)(2,1)S(1)}, bf16[128,640]{1,0:T(8,128)(2,1)S(1)}, u32[]{:S(2)}, u32[]{:S(2)}) %collective-permute-start.6) | collective-permute-done | bytes 163872 | tf_op jit(solution)/shard_map/ppermute | solution.py:27
  16.9 3.5 %collective-permute-done.5.refs_2_ = bf16[128,640]{1,0:T(8,128)(2,1)S(1)} collective-permute-done((bf16[128,640]{1,0:T(8,128)(2,1)S(1)}, bf16[128,640]{1,0:T(8,128)(2,1)S(1)}, u32[]{:S(2)}, u32[]{:S(2)}) %collective-permute-start.5) | collective-permute-done | bytes 163872 | tf_op jit(solution)/shard_map/ppermute | solution.py:27
  20.4 0.8 %attend.2 = (bf16[2,176,128]{2,1,0:T(8,128)(2,1)S(1)}, bf16[1,176,128]{2,1,0:T(8,128)(2,1)S(1)}, bf16[1,176,128]{2,1,0:T(8,128)(2,1)S(1)}) custom-call(bf16[2,64,640]{2,1,0:T(8,128)(2,1)S(1)} %collective-permute-done.1.far_query, bf16[2,64,640]{2,1,0:T(8,128)(2,1)S(1)} %collective-permute-done.4.opposite, bf16[128,640]{1,0:T(8,128)(2,1)S(1)} %rebuild.2.refs_0_, ...), custom_call_target="tpu_custom_call" | custom-call | bytes 1000 | tf_op jit(solution)/shard_map/attend/pallas_call | solution.py:241
  21.3 0.8 %collective-permute-start.10 = (bf16[2,176,128]{2,1,0:T(8,128)(2,1)S(1)}, bf16[2,176,128]{2,1,0:T(8,128)(2,1)S(1)}, u32[]{:S(2)}, u32[]{:S(2)}) collective-permute-start(bf16[2,176,128]{2,1,0:T(8,128)(2,1)S(1)} %get-tuple-element.31), channel_id=1, source_target_pairs={{0,8},{1,9},{2,10},{3,11},{4,12},{5,13},{6,14},{7,15},{8,0},{9,1},... | collective-permute-start | bytes 270344 | tf_op jit(solution)/shard_map/ppermute | solution.py:27
  22.1 0.8 %attend.3 = (bf16[1,176,128]{2,1,0:T(8,128)(2,1)S(1)}, bf16[1,176,128]{2,1,0:T(8,128)(2,1)S(1)}, bf16[2,176,128]{2,1,0:T(8,128)(2,1)S(1)}) custom-call(bf16[3,2,32,640]{3,2,1,0:T(8,128)(2,1)S(1)} %get-tuple-element.19.kept, bf16[3,2,32,640]{3,2,1,0:T(8,128)(2,1)S(1)} %collective-permute-done.arrived.beside, ...), custom_call_target="tpu_custom_call" | custom-call | bytes 1000 | tf_op jit(solution)/shard_map/attend/pallas_call | solution.py:241
  22.9 1.3 %collective-permute-start.8 = (bf16[2,176,128]{2,1,0:T(8,128)(2,1)S(1)}, bf16[2,176,128]{2,1,0:T(8,128)(2,1)S(1)}, u32[]{:S(2)}, u32[]{:S(2)}) collective-permute-start(bf16[2,176,128]{2,1,0:T(8,128)(2,1)S(1)} %get-tuple-element.30), channel_id=1, source_target_pairs={{0,2},{1,3},{2,0},{3,1},{4,6},{5,7},{6,4},{7,5},{8,10},{9,11},{10,... | collective-permute-start | bytes 270344 | tf_op jit(solution)/shard_map/ppermute | solution.py:27
  24.2 3.5 %collective-permute-start.13 = (bf16[1,176,128]{2,1,0:T(8,128)(2,1)S(1)}, bf16[1,176,128]{2,1,0:T(8,128)(2,1)S(1)}, u32[]{:S(2)}, u32[]{:S(2)}) collective-permute-start(bf16[1,176,128]{2,1,0:T(8,128)(2,1)S(1)} %get-tuple-element.27.refs_4_), channel_id=1, source_target_pairs={{0,11},{1,10},{2,9},{3,8},{4,15},{5,14},{6,13},{7,12},{8,3},{9,2},... | collective-permute-start | bytes 135176 | tf_op jit(solution)/shard_map/ppermute | solution.py:27
  27.7 1.5 %collective-permute-start.12 = (bf16[1,176,128]{2,1,0:T(8,128)(2,1)S(1)}, bf16[1,176,128]{2,1,0:T(8,128)(2,1)S(1)}, u32[]{:S(2)}, u32[]{:S(2)}) collective-permute-start(bf16[1,176,128]{2,1,0:T(8,128)(2,1)S(1)} %get-tuple-element.32), channel_id=1, source_target_pairs={{0,10},{1,11},{2,8},{3,9},{4,14},{5,15},{6,12},{7,13},{8,2},{9,3},... | collective-permute-start | bytes 135176 | tf_op jit(solution)/shard_map/ppermute | solution.py:27
  29.2 0.6 %collective-permute-start.11 = (bf16[1,176,128]{2,1,0:T(8,128)(2,1)S(1)}, bf16[1,176,128]{2,1,0:T(8,128)(2,1)S(1)}, u32[]{:S(2)}, u32[]{:S(2)}) collective-permute-start(bf16[1,176,128]{2,1,0:T(8,128)(2,1)S(1)} %slice.9), channel_id=1, source_target_pairs={{0,1},{1,0},{2,3},{3,2},{4,5},{5,4},{6,7},{7,6},{8,9},{9,8},{10,11... | collective-permute-start | bytes 135176 | tf_op jit(solution)/shard_map/ppermute | solution.py:27
  29.9 4.0 %collective-permute-done.12.f2 = bf16[1,176,128]{2,1,0:T(8,128)(2,1)S(1)} collective-permute-done((bf16[1,176,128]{2,1,0:T(8,128)(2,1)S(1)}, bf16[1,176,128]{2,1,0:T(8,128)(2,1)S(1)}, u32[]{:S(2)}, u32[]{:S(2)}) %collective-permute-start.12) | collective-permute-done | bytes 45088 | tf_op jit(solution)/shard_map/ppermute | solution.py:27
  33.9 1.2 %merge.1 = bf16[32,2560]{1,0:T(8,128)(2,1)} custom-call(bf16[1,176,128]{2,1,0:T(8,128)(2,1)S(1)} %get-tuple-element.28.n0, bf16[1,176,128]{2,1,0:T(8,128)(2,1)S(1)} %collective-permute-done.7.n1, bf16[2,176,128]{2,1,0:T(8,128)(2,1)S(1)} %collective-permute-done.8.n2, bf16[1,176,128]{2,1,0:T(8,128)(2,1)S(1)} %collective-permute-done.9.n3, ...), custom_call_target="tpu_custom_call" | custom-call | bytes 1000 | tf_op jit(solution)/shard_map/merge/pallas_call | solution.py:283
  (19 shorter events, 0.5 us)
Async XLA Ops:
  1.1 1.6 %collective-permute-start = (bf16[3,2,32,640]{3,2,1,0:T(8,128)(2,1)S(1)}, bf16[3,2,32,640]{3,2,1,0:T(8,128)(2,1)S(1)}, u32[]{:S(2)}, u32[]{:S(2)}) collective-permute-start(bf16[3,2,32,640]{3,2,1,0:T(8,128)(2,1)S(1)} %get-tuple-element.20), channel_id=1, source_target_pairs={{0,1},{1,0},{2,3},{3,2},{4,5},{5,4},{6,7},{7,6},{8,9},{9,8},{10,11... | collective-permute-start | bytes 737288 | tf_op jit(solution)/shard_map/ppermute | solution.py:27
  2.7 5.0 %copy-start = (f32[512,20]{0,1:T(8,128)S(1)}, f32[512,20]{0,1:T(8,128)}, u32[]{:S(2)}) copy-start(f32[512,20]{0,1:T(8,128)} %param.12) | copy-start | bytes 122884
  2.7 5.0 %copy-start.1 = (f32[512,20]{0,1:T(8,128)S(1)}, f32[512,20]{0,1:T(8,128)}, u32[]{:S(2)}) copy-start(f32[512,20]{0,1:T(8,128)} %param.13) | copy-start | bytes 122884
  2.7 11.3 %collective-permute-start.1 = (bf16[2,64,640]{2,1,0:T(8,128)(2,1)S(1)}, bf16[2,64,640]{2,1,0:T(8,128)(2,1)S(1)}, u32[]{:S(2)}, u32[]{:S(2)}) collective-permute-start(bf16[2,64,640]{2,1,0:T(8,128)(2,1)S(1)} %get-tuple-element.22), channel_id=1, source_target_pairs={{0,8},{1,9},{2,10},{3,11},{4,12},{5,13},{6,14},{7,15},{8,0},{9,1},... | collective-permute-start | bytes 491528 | tf_op jit(solution)/shard_map/ppermute | solution.py:27
  6.2 3.6 %collective-permute-start.3 = (bf16[64,640]{1,0:T(8,128)(2,1)S(1)}, bf16[64,640]{1,0:T(8,128)(2,1)S(1)}, u32[]{:S(2)}, u32[]{:S(2)}) collective-permute-start(bf16[64,640]{1,0:T(8,128)(2,1)S(1)} %get-tuple-element.26), channel_id=1, source_target_pairs={{0,2},{1,3},{2,0},{3,1},{4,6},{5,7},{6,4},{7,5},{8,10},{9,11},{10,... | collective-permute-start | bytes 245768 | tf_op jit(solution)/shard_map/ppermute | solution.py:27
  7.4 4.5 %collective-permute-start.2 = (bf16[64,640]{1,0:T(8,128)(2,1)S(1)}, bf16[64,640]{1,0:T(8,128)(2,1)S(1)}, u32[]{:S(2)}, u32[]{:S(2)}) collective-permute-start(bf16[64,640]{1,0:T(8,128)(2,1)S(1)} %get-tuple-element.23), channel_id=1, source_target_pairs={{0,2},{1,3},{2,0},{3,1},{4,6},{5,7},{6,4},{7,5},{8,10},{9,11},{10,... | collective-permute-start | bytes 245768 | tf_op jit(solution)/shard_map/ppermute | solution.py:27
  10.0 6.9 %collective-permute-start.6 = (bf16[128,640]{1,0:T(8,128)(2,1)S(1)}, bf16[128,640]{1,0:T(8,128)(2,1)S(1)}, u32[]{:S(2)}, u32[]{:S(2)}) collective-permute-start(bf16[128,640]{1,0:T(8,128)(2,1)S(1)} %rebuild.3.refs_1_), channel_id=1, source_target_pairs={{0,4},{1,5},{2,6},{3,7},{4,0},{5,1},{6,2},{7,3},{8,12},{9,13},{10,... | collective-permute-start | bytes 491528 | tf_op jit(solution)/shard_map/ppermute | solution.py:27
  12.1 8.3 %collective-permute-start.5 = (bf16[128,640]{1,0:T(8,128)(2,1)S(1)}, bf16[128,640]{1,0:T(8,128)(2,1)S(1)}, u32[]{:S(2)}, u32[]{:S(2)}) collective-permute-start(bf16[128,640]{1,0:T(8,128)(2,1)S(1)} %rebuild.2.refs_0_), channel_id=1, source_target_pairs={{0,4},{1,5},{2,6},{3,7},{4,0},{5,1},{6,2},{7,3},{8,12},{9,13},{10,... | collective-permute-start | bytes 491528 | tf_op jit(solution)/shard_map/ppermute | solution.py:27
  14.0 6.4 %collective-permute-start.4 = (bf16[2,64,640]{2,1,0:T(8,128)(2,1)S(1)}, bf16[2,64,640]{2,1,0:T(8,128)(2,1)S(1)}, u32[]{:S(2)}, u32[]{:S(2)}) collective-permute-start(bf16[2,64,640]{2,1,0:T(8,128)(2,1)S(1)} %pair.1), channel_id=1, source_target_pairs={{0,2},{1,3},{2,0},{3,1},{4,6},{5,7},{6,4},{7,5},{8,10},{9,11},{10,... | collective-permute-start | bytes 491528 | tf_op jit(solution)/shard_map/ppermute | solution.py:27
  21.3 7.9 %collective-permute-start.10 = (bf16[2,176,128]{2,1,0:T(8,128)(2,1)S(1)}, bf16[2,176,128]{2,1,0:T(8,128)(2,1)S(1)}, u32[]{:S(2)}, u32[]{:S(2)}) collective-permute-start(bf16[2,176,128]{2,1,0:T(8,128)(2,1)S(1)} %get-tuple-element.31), channel_id=1, source_target_pairs={{0,8},{1,9},{2,10},{3,11},{4,12},{5,13},{6,14},{7,15},{8,0},{9,1},... | collective-permute-start | bytes 270344 | tf_op jit(solution)/shard_map/ppermute | solution.py:27
  22.9 6.9 %collective-permute-start.8 = (bf16[2,176,128]{2,1,0:T(8,128)(2,1)S(1)}, bf16[2,176,128]{2,1,0:T(8,128)(2,1)S(1)}, u32[]{:S(2)}, u32[]{:S(2)}) collective-permute-start(bf16[2,176,128]{2,1,0:T(8,128)(2,1)S(1)} %get-tuple-element.30), channel_id=1, source_target_pairs={{0,2},{1,3},{2,0},{3,1},{4,6},{5,7},{6,4},{7,5},{8,10},{9,11},{10,... | collective-permute-start | bytes 270344 | tf_op jit(solution)/shard_map/ppermute | solution.py:27
  24.2 9.7 %collective-permute-start.13 = (bf16[1,176,128]{2,1,0:T(8,128)(2,1)S(1)}, bf16[1,176,128]{2,1,0:T(8,128)(2,1)S(1)}, u32[]{:S(2)}, u32[]{:S(2)}) collective-permute-start(bf16[1,176,128]{2,1,0:T(8,128)(2,1)S(1)} %get-tuple-element.27.refs_4_), channel_id=1, source_target_pairs={{0,11},{1,10},{2,9},{3,8},{4,15},{5,14},{6,13},{7,12},{8,3},{9,2},... | collective-permute-start | bytes 135176 | tf_op jit(solution)/shard_map/ppermute | solution.py:27
  27.7 6.1 %collective-permute-start.12 = (bf16[1,176,128]{2,1,0:T(8,128)(2,1)S(1)}, bf16[1,176,128]{2,1,0:T(8,128)(2,1)S(1)}, u32[]{:S(2)}, u32[]{:S(2)}) collective-permute-start(bf16[1,176,128]{2,1,0:T(8,128)(2,1)S(1)} %get-tuple-element.32), channel_id=1, source_target_pairs={{0,10},{1,11},{2,8},{3,9},{4,14},{5,15},{6,12},{7,13},{8,2},{9,3},... | collective-permute-start | bytes 135176 | tf_op jit(solution)/shard_map/ppermute | solution.py:27
  29.2 4.6 %collective-permute-start.7 = (bf16[1,176,128]{2,1,0:T(8,128)(2,1)S(1)}, bf16[1,176,128]{2,1,0:T(8,128)(2,1)S(1)}, u32[]{:S(2)}, u32[]{:S(2)}) collective-permute-start(bf16[1,176,128]{2,1,0:T(8,128)(2,1)S(1)} %get-tuple-element.29), channel_id=1, source_target_pairs={{0,1},{1,0},{2,3},{3,2},{4,5},{5,4},{6,7},{7,6},{8,9},{9,8},{10,11... | collective-permute-start | bytes 135176 | tf_op jit(solution)/shard_map/ppermute | solution.py:27
  29.2 4.6 %collective-permute-start.11 = (bf16[1,176,128]{2,1,0:T(8,128)(2,1)S(1)}, bf16[1,176,128]{2,1,0:T(8,128)(2,1)S(1)}, u32[]{:S(2)}, u32[]{:S(2)}) collective-permute-start(bf16[1,176,128]{2,1,0:T(8,128)(2,1)S(1)} %slice.9), channel_id=1, source_target_pairs={{0,1},{1,0},{2,3},{3,2},{4,5},{5,4},{6,7},{7,6},{8,9},{9,8},{10,11... | collective-permute-start | bytes 135176 | tf_op jit(solution)/shard_map/ppermute | solution.py:27
  29.8 4.1 %collective-permute-start.9 = (bf16[1,176,128]{2,1,0:T(8,128)(2,1)S(1)}, bf16[1,176,128]{2,1,0:T(8,128)(2,1)S(1)}, u32[]{:S(2)}, u32[]{:S(2)}) collective-permute-start(bf16[1,176,128]{2,1,0:T(8,128)(2,1)S(1)} %slice.8), channel_id=1, source_target_pairs={{0,1},{1,0},{2,3},{3,2},{4,5},{5,4},{6,7},{7,6},{8,9},{9,8},{10,11... | collective-permute-start | bytes 135176 | tf_op jit(solution)/shard_map/ppermute | solution.py:27

commit v5 on v4

--- a/solution.py
+++ b/solution.py
@@ -186,7 +186,7 @@
     width = near_keys.shape[1]
     rows = sum(query.shape[0] for query in queries) // GROUP
     head = width // heads
-    outs = [ref.at[j] for ref, group in zip(refs, parts) for j in range(len(group))]
+    outs = {k: ref.at[j] for ref, group in zip(refs, parts) for j, k in enumerate(group)}
     scale = head ** (-0.5) * LOG2E
     lane = lax.broadcasted_iota(jnp.int32, (GROUP * rows, head), 1)
     stats = jnp.zeros((GROUP * rows, head), jnp.float32)
@@ -215,10 +215,10 @@
         stats = jnp.where(lane == h, level, stats)
         stats = jnp.where(lane == heads + h, high, stats)
         stats = jnp.where(lane == 2 * heads + h, weight - high, stats)
-        for k, out in enumerate(outs):
+        for k, out in sorted(outs.items()):
             out[h * rows : (h + 1) * rows, :] = weighted[k * rows : (k + 1) * rows]
     half = rows // 2
-    for k, out in enumerate(outs):
+    for k, out in sorted(outs.items()):
         first = stats[k * rows : k * rows + half]
         second = stats[k * rows + half : (k + 1) * rows]
         packed = first + pltpu.roll(second, 16, 1)
@@ -310,15 +310,15 @@
         near = [jnp.concatenate([a, swapped(a, 1 << bit)], axis=0) for a in near]
     far = [swapped(a, 1 << levels - 2) for a in near]
     q_opposite = swapped(pair(x_query, far_query, *near), 2)
-    parts = ((0, 1), (2,), (3,))
+    parts = ((2, 3), (0,), (1,))
     far_out = attend(far_kernel, heads, parts, rows, (far_query, q_opposite), near, far)
-    f01, f2, f3 = [swapped(a, across + group[0]) for a, group in zip(far_out, parts)]
+    f23, f0, f1 = [swapped(a, across + group[0]) for a, group in zip(far_out, parts)]
     parts = ((0,), (1,), (2, 3))
     own_query = (kept, beside, q_opposite)
     n0, n1, n23 = attend(own_kernel, heads, parts, rows, own_query, near, far, far_out[2])
     n1, n23 = swapped(n1, 1), swapped(n23, 2)
     near_parts = (n0, n1, n23, swapped(n23[1:], 1))
-    far_parts = (f01, swapped(f01[1:], 1), f2, f3)
+    far_parts = (f0, f1, f23, swapped(f23[1:], 1))
     return merge(heads, near_parts, far_parts, rows)
 
 

time: 35.3 us -> 34.4 us (0.975)
  waiting for transfers between devices: 12.8 us -> 11.2 us
  starting transfers between devices: 16.6 us -> 17.3 us
    ppermute x14, waiting for transfers between devices: 12.8 us -> 11.2 us  [swapped(): return lax.ppermute(array, 'patch', [(i, i ^ mask) for i in range(size)])]
    ppermute x14, starting transfers between devices: 16.6 us -> 17.3 us  [swapped(): return lax.ppermute(array, 'patch', [(i, i ^ mask) for i in range(size)])]
  transfers between devices with their start and end apart: 14 -> 14, of which waited for: 7 -> 8; matrix products, arithmetic and copies ran while one was open for 0% -> 0% of each run, Pallas kernels for 7% -> 7%
where the time goes in v5:
time: 34.4 us; the launch traced here: 34.2 us
  starting transfers between devices  17.3 us (50%)
  waiting for transfers between devices  11.2 us (33%)
  Pallas kernels  5.58 us (16%)
    ppermute x14, starting transfers between devices, swapped(): return lax.ppermute(array, 'patch', [(i, i ^ mask) for i in range(size)])  17.3 us
    ppermute x14, waiting for transfers between devices, swapped(): return lax.ppermute(array, 'patch', [(i, i ^ mask) for i in range(size)])  11.2 us
    pallas_call x2, Pallas kernels, attend(): pl.pallas_call(functools.partial(kernel, heads, parts), out_shape=outs, i...  1.67 us
    pallas_call x1, Pallas kernels, merge(): pl.pallas_call(functools.partial(merge_kernel, heads), out_shape=jax.Shap...  1.22 us
    pallas_call x1, Pallas kernels, fetch(): pl.pallas_call(functools.partial(fetch_kernel, heads), out_shape=[jax.Sha...  1.15 us
    pallas_call x1, Pallas kernels, cut(): pl.pallas_call(functools.partial(cut_kernel, len(slabs)), out_shape=[shap...  1.11 us
  transfers between devices with their start and end apart: 14, of which 8 were waited for; matrix products, arithmetic and copies ran while one was open for 0% of the time, Pallas kernels for 7%

profile of v5, /device:TPU:1, one launch (start us, length us, event | category | flops | bytes accessed | tf_op | source)
XLA Modules:
  0.0 34.2 jit_solution(8269492812825832539)
XLA Ops:
  0.0 1.1 %cut.1 = (bf16[3,2,32,640]{3,2,1,0:T(8,128)(2,1)S(1)}, bf16[3,2,32,640]{3,2,1,0:T(8,128)(2,1)S(1)}) custom-call(bf16[32,2560]{1,0:T(8,128)(2,1)} %refs_0_.1, bf16[32,2560]{1,0:T(8,128)(2,1)} %refs_1_.1, bf16[32,2560]{1,0:T(8,128)(2,1)} %refs_2_.1), custom_call_target="tpu_custom_call" | custom-call | bytes 1000 | tf_op jit(solution)/shard_map/cut/pallas_call | solution.py:62
  1.2 1.5 %collective-permute-done.arrived.beside = bf16[3,2,32,640]{3,2,1,0:T(8,128)(2,1)S(1)} collective-permute-done((bf16[3,2,32,640]{3,2,1,0:T(8,128)(2,1)S(1)}, bf16[3,2,32,640]{3,2,1,0:T(8,128)(2,1)S(1)}, u32[]{:S(2)}, u32[]{:S(2)}) %collective-permute-start) | collective-permute-done | bytes 245792 | tf_op jit(solution)/shard_map/ppermute | solution.py:27
  2.7 3.5 %collective-permute-start.1 = (bf16[2,64,640]{2,1,0:T(8,128)(2,1)S(1)}, bf16[2,64,640]{2,1,0:T(8,128)(2,1)S(1)}, u32[]{:S(2)}, u32[]{:S(2)}) collective-permute-start(bf16[2,64,640]{2,1,0:T(8,128)(2,1)S(1)} %get-tuple-element.22), channel_id=1, source_target_pairs={{0,8},{1,9},{2,10},{3,11},{4,12},{5,13},{6,14},{7,15},{8,0},{9,1},... | collective-permute-start | bytes 491528 | tf_op jit(solution)/shard_map/ppermute | solution.py:27
  6.2 1.2 %collective-permute-start.3 = (bf16[64,640]{1,0:T(8,128)(2,1)S(1)}, bf16[64,640]{1,0:T(8,128)(2,1)S(1)}, u32[]{:S(2)}, u32[]{:S(2)}) collective-permute-start(bf16[64,640]{1,0:T(8,128)(2,1)S(1)} %get-tuple-element.26), channel_id=1, source_target_pairs={{0,2},{1,3},{2,0},{3,1},{4,6},{5,7},{6,4},{7,5},{8,10},{9,11},{10,... | collective-permute-start | bytes 245768 | tf_op jit(solution)/shard_map/ppermute | solution.py:27
  7.7 1.2 %fetch.1 = (bf16[2,128,640]{2,1,0:T(8,128)(2,1)S(1)}, f32[2,128,128]{2,1,0:T(8,128)S(1)}) custom-call(bf16[1,512,640]{2,1,0:T(8,128)(2,1)} %keys_copy.1, bf16[1,512,640]{2,1,0:T(8,128)(2,1)} %values_copy.1, f32[20,512]{1,0:T(8,128)S(1)} %bitcast.2, f32[20,512]{1,0:T(8,128)S(1)} %bitcast.3), custom_call_target="tpu_custom_call" | custom-call | bytes 1000 | tf_op jit(solution)/shard_map/fetch/pallas_call | solution.py:137
  8.9 1.0 %collective-permute-done.3.opposite = bf16[64,640]{1,0:T(8,128)(2,1)S(1)} collective-permute-done((bf16[64,640]{1,0:T(8,128)(2,1)S(1)}, bf16[64,640]{1,0:T(8,128)(2,1)S(1)}, u32[]{:S(2)}, u32[]{:S(2)}) %collective-permute-start.3) | collective-permute-done | bytes 81952 | tf_op jit(solution)/shard_map/ppermute | solution.py:27
  10.0 1.4 %collective-permute-start.6 = (bf16[128,640]{1,0:T(8,128)(2,1)S(1)}, bf16[128,640]{1,0:T(8,128)(2,1)S(1)}, u32[]{:S(2)}, u32[]{:S(2)}) collective-permute-start(bf16[128,640]{1,0:T(8,128)(2,1)S(1)} %rebuild.3.refs_1_), channel_id=1, source_target_pairs={{0,4},{1,5},{2,6},{3,7},{4,0},{5,1},{6,2},{7,3},{8,12},{9,13},{10,... | collective-permute-start | bytes 491528 | tf_op jit(solution)/shard_map/ppermute | solution.py:27
  11.4 0.5 %collective-permute-done.2.opposite = bf16[64,640]{1,0:T(8,128)(2,1)S(1)} collective-permute-done((bf16[64,640]{1,0:T(8,128)(2,1)S(1)}, bf16[64,640]{1,0:T(8,128)(2,1)S(1)}, u32[]{:S(2)}, u32[]{:S(2)}) %collective-permute-start.2) | collective-permute-done | bytes 81952 | tf_op jit(solution)/shard_map/ppermute | solution.py:27
  12.1 1.4 %collective-permute-start.5 = (bf16[128,640]{1,0:T(8,128)(2,1)S(1)}, bf16[128,640]{1,0:T(8,128)(2,1)S(1)}, u32[]{:S(2)}, u32[]{:S(2)}) collective-permute-start(bf16[128,640]{1,0:T(8,128)(2,1)S(1)} %rebuild.2.refs_0_), channel_id=1, source_target_pairs={{0,4},{1,5},{2,6},{3,7},{4,0},{5,1},{6,2},{7,3},{8,12},{9,13},{10,... | collective-permute-start | bytes 491528 | tf_op jit(solution)/shard_map/ppermute | solution.py:27
  13.5 0.6 %collective-permute-done.1.far_query = bf16[2,64,640]{2,1,0:T(8,128)(2,1)S(1)} collective-permute-done((bf16[2,64,640]{2,1,0:T(8,128)(2,1)S(1)}, bf16[2,64,640]{2,1,0:T(8,128)(2,1)S(1)}, u32[]{:S(2)}, u32[]{:S(2)}) %collective-permute-start.1) | collective-permute-done | bytes 163872 | tf_op jit(solution)/shard_map/ppermute | solution.py:27
  14.0 1.0 %collective-permute-start.4 = (bf16[2,64,640]{2,1,0:T(8,128)(2,1)S(1)}, bf16[2,64,640]{2,1,0:T(8,128)(2,1)S(1)}, u32[]{:S(2)}, u32[]{:S(2)}) collective-permute-start(bf16[2,64,640]{2,1,0:T(8,128)(2,1)S(1)} %pair.1), channel_id=1, source_target_pairs={{0,2},{1,3},{2,0},{3,1},{4,6},{5,7},{6,4},{7,5},{8,10},{9,11},{10,... | collective-permute-start | bytes 491528 | tf_op jit(solution)/shard_map/ppermute | solution.py:27
  15.0 1.9 %collective-permute-done.6.refs_3_ = bf16[128,640]{1,0:T(8,128)(2,1)S(1)} collective-permute-done((bf16[128,640]{1,0:T(8,128)(2,1)S(1)}, bf16[128,640]{1,0:T(8,128)(2,1)S(1)}, u32[]{:S(2)}, u32[]{:S(2)}) %collective-permute-start.6) | collective-permute-done | bytes 163872 | tf_op jit(solution)/shard_map/ppermute | solution.py:27
  16.9 3.5 %collective-permute-done.5.refs_2_ = bf16[128,640]{1,0:T(8,128)(2,1)S(1)} collective-permute-done((bf16[128,640]{1,0:T(8,128)(2,1)S(1)}, bf16[128,640]{1,0:T(8,128)(2,1)S(1)}, u32[]{:S(2)}, u32[]{:S(2)}) %collective-permute-start.5) | collective-permute-done | bytes 163872 | tf_op jit(solution)/shard_map/ppermute | solution.py:27
  20.4 0.8 %attend.2 = (bf16[2,176,128]{2,1,0:T(8,128)(2,1)S(1)}, bf16[1,176,128]{2,1,0:T(8,128)(2,1)S(1)}, bf16[1,176,128]{2,1,0:T(8,128)(2,1)S(1)}) custom-call(bf16[2,64,640]{2,1,0:T(8,128)(2,1)S(1)} %collective-permute-done.1.far_query, bf16[2,64,640]{2,1,0:T(8,128)(2,1)S(1)} %collective-permute-done.4.opposite, bf16[128,640]{1,0:T(8,128)(2,1)S(1)} %rebuild.2.refs_0_, ...), custom_call_target="tpu_custom_call" | custom-call | bytes 1000 | tf_op jit(solution)/shard_map/attend/pallas_call | solution.py:241
  21.3 1.7 %collective-permute-start.12 = (bf16[2,176,128]{2,1,0:T(8,128)(2,1)S(1)}, bf16[2,176,128]{2,1,0:T(8,128)(2,1)S(1)}, u32[]{:S(2)}, u32[]{:S(2)}) collective-permute-start(bf16[2,176,128]{2,1,0:T(8,128)(2,1)S(1)} %get-tuple-element.32), channel_id=1, source_target_pairs={{0,10},{1,11},{2,8},{3,9},{4,14},{5,15},{6,12},{7,13},{8,2},{9,3},... | collective-permute-start | bytes 270344 | tf_op jit(solution)/shard_map/ppermute | solution.py:27
  23.0 0.8 %attend.3 = (bf16[1,176,128]{2,1,0:T(8,128)(2,1)S(1)}, bf16[1,176,128]{2,1,0:T(8,128)(2,1)S(1)}, bf16[2,176,128]{2,1,0:T(8,128)(2,1)S(1)}) custom-call(bf16[3,2,32,640]{3,2,1,0:T(8,128)(2,1)S(1)} %get-tuple-element.19.kept, bf16[3,2,32,640]{3,2,1,0:T(8,128)(2,1)S(1)} %collective-permute-done.arrived.beside, ...), custom_call_target="tpu_custom_call" | custom-call | bytes 1000 | tf_op jit(solution)/shard_map/attend/pallas_call | solution.py:241
  23.8 0.3 collective-permute-start.8
  24.1 3.6 %collective-permute-start.11 = (bf16[1,176,128]{2,1,0:T(8,128)(2,1)S(1)}, bf16[1,176,128]{2,1,0:T(8,128)(2,1)S(1)}, u32[]{:S(2)}, u32[]{:S(2)}) collective-permute-start(bf16[1,176,128]{2,1,0:T(8,128)(2,1)S(1)} %get-tuple-element.27.refs_4_), channel_id=1, source_target_pairs={{0,9},{1,8},{2,11},{3,10},{4,13},{5,12},{6,15},{7,14},{8,1},{9,0},... | collective-permute-start | bytes 135176 | tf_op jit(solution)/shard_map/ppermute | solution.py:27
  27.7 0.6 %collective-permute-start.10 = (bf16[1,176,128]{2,1,0:T(8,128)(2,1)S(1)}, bf16[1,176,128]{2,1,0:T(8,128)(2,1)S(1)}, u32[]{:S(2)}, u32[]{:S(2)}) collective-permute-start(bf16[1,176,128]{2,1,0:T(8,128)(2,1)S(1)} %get-tuple-element.31), channel_id=1, source_target_pairs={{0,8},{1,9},{2,10},{3,11},{4,12},{5,13},{6,14},{7,15},{8,0},{9,1},... | collective-permute-start | bytes 135176 | tf_op jit(solution)/shard_map/ppermute | solution.py:27
  28.3 0.5 %collective-permute-done.12.f2 = bf16[2,176,128]{2,1,0:T(8,128)(2,1)S(1)} collective-permute-done((bf16[2,176,128]{2,1,0:T(8,128)(2,1)S(1)}, bf16[2,176,128]{2,1,0:T(8,128)(2,1)S(1)}, u32[]{:S(2)}, u32[]{:S(2)}) %collective-permute-start.12) | collective-permute-done | bytes 90144 | tf_op jit(solution)/shard_map/ppermute | solution.py:27
  28.8 1.4 %collective-permute-start.13 = (bf16[1,176,128]{2,1,0:T(8,128)(2,1)S(1)}, bf16[1,176,128]{2,1,0:T(8,128)(2,1)S(1)}, u32[]{:S(2)}, u32[]{:S(2)}) collective-permute-start(bf16[1,176,128]{2,1,0:T(8,128)(2,1)S(1)} %slice.9), channel_id=1, source_target_pairs={{0,1},{1,0},{2,3},{3,2},{4,5},{5,4},{6,7},{7,6},{8,9},{9,8},{10,11... | collective-permute-start | bytes 135176 | tf_op jit(solution)/shard_map/ppermute | solution.py:27
  30.2 0.9 %collective-permute-start.9 = (bf16[1,176,128]{2,1,0:T(8,128)(2,1)S(1)}, bf16[1,176,128]{2,1,0:T(8,128)(2,1)S(1)}, u32[]{:S(2)}, u32[]{:S(2)}) collective-permute-start(bf16[1,176,128]{2,1,0:T(8,128)(2,1)S(1)} %slice.8), channel_id=1, source_target_pairs={{0,1},{1,0},{2,3},{3,2},{4,5},{5,4},{6,7},{7,6},{8,9},{9,8},{10,11... | collective-permute-start | bytes 135176 | tf_op jit(solution)/shard_map/ppermute | solution.py:27
  31.1 1.9 %collective-permute-done.10.f0 = bf16[1,176,128]{2,1,0:T(8,128)(2,1)S(1)} collective-permute-done((bf16[1,176,128]{2,1,0:T(8,128)(2,1)S(1)}, bf16[1,176,128]{2,1,0:T(8,128)(2,1)S(1)}, u32[]{:S(2)}, u32[]{:S(2)}) %collective-permute-start.10) | collective-permute-done | bytes 45088 | tf_op jit(solution)/shard_map/ppermute | solution.py:27
  33.0 1.2 %merge.1 = bf16[32,2560]{1,0:T(8,128)(2,1)} custom-call(bf16[1,176,128]{2,1,0:T(8,128)(2,1)S(1)} %get-tuple-element.28.n0, bf16[1,176,128]{2,1,0:T(8,128)(2,1)S(1)} %collective-permute-done.7.n1, bf16[2,176,128]{2,1,0:T(8,128)(2,1)S(1)} %collective-permute-done.8.n2, bf16[1,176,128]{2,1,0:T(8,128)(2,1)S(1)} %collective-permute-done.9.n3, ...), custom_call_target="tpu_custom_call" | custom-call | bytes 1000 | tf_op jit(solution)/shard_map/merge/pallas_call | solution.py:283
  (19 shorter events, 0.8 us)
Async XLA Ops:
  1.1 1.6 %collective-permute-start = (bf16[3,2,32,640]{3,2,1,0:T(8,128)(2,1)S(1)}, bf16[3,2,32,640]{3,2,1,0:T(8,128)(2,1)S(1)}, u32[]{:S(2)}, u32[]{:S(2)}) collective-permute-start(bf16[3,2,32,640]{3,2,1,0:T(8,128)(2,1)S(1)} %get-tuple-element.20), channel_id=1, source_target_pairs={{0,1},{1,0},{2,3},{3,2},{4,5},{5,4},{6,7},{7,6},{8,9},{9,8},{10,11... | collective-permute-start | bytes 737288 | tf_op jit(solution)/shard_map/ppermute | solution.py:27
  2.7 5.0 %copy-start = (f32[512,20]{0,1:T(8,128)S(1)}, f32[512,20]{0,1:T(8,128)}, u32[]{:S(2)}) copy-start(f32[512,20]{0,1:T(8,128)} %param.12) | copy-start | bytes 122884
  2.7 5.0 %copy-start.1 = (f32[512,20]{0,1:T(8,128)S(1)}, f32[512,20]{0,1:T(8,128)}, u32[]{:S(2)}) copy-start(f32[512,20]{0,1:T(8,128)} %param.13) | copy-start | bytes 122884
  2.7 11.3 %collective-permute-start.1 = (bf16[2,64,640]{2,1,0:T(8,128)(2,1)S(1)}, bf16[2,64,640]{2,1,0:T(8,128)(2,1)S(1)}, u32[]{:S(2)}, u32[]{:S(2)}) collective-permute-start(bf16[2,64,640]{2,1,0:T(8,128)(2,1)S(1)} %get-tuple-element.22), channel_id=1, source_target_pairs={{0,8},{1,9},{2,10},{3,11},{4,12},{5,13},{6,14},{7,15},{8,0},{9,1},... | collective-permute-start | bytes 491528 | tf_op jit(solution)/shard_map/ppermute | solution.py:27
  6.2 3.6 %collective-permute-start.3 = (bf16[64,640]{1,0:T(8,128)(2,1)S(1)}, bf16[64,640]{1,0:T(8,128)(2,1)S(1)}, u32[]{:S(2)}, u32[]{:S(2)}) collective-permute-start(bf16[64,640]{1,0:T(8,128)(2,1)S(1)} %get-tuple-element.26), channel_id=1, source_target_pairs={{0,2},{1,3},{2,0},{3,1},{4,6},{5,7},{6,4},{7,5},{8,10},{9,11},{10,... | collective-permute-start | bytes 245768 | tf_op jit(solution)/shard_map/ppermute | solution.py:27
  7.4 4.5 %collective-permute-start.2 = (bf16[64,640]{1,0:T(8,128)(2,1)S(1)}, bf16[64,640]{1,0:T(8,128)(2,1)S(1)}, u32[]{:S(2)}, u32[]{:S(2)}) collective-permute-start(bf16[64,640]{1,0:T(8,128)(2,1)S(1)} %get-tuple-element.23), channel_id=1, source_target_pairs={{0,2},{1,3},{2,0},{3,1},{4,6},{5,7},{6,4},{7,5},{8,10},{9,11},{10,... | collective-permute-start | bytes 245768 | tf_op jit(solution)/shard_map/ppermute | solution.py:27
  10.0 6.9 %collective-permute-start.6 = (bf16[128,640]{1,0:T(8,128)(2,1)S(1)}, bf16[128,640]{1,0:T(8,128)(2,1)S(1)}, u32[]{:S(2)}, u32[]{:S(2)}) collective-permute-start(bf16[128,640]{1,0:T(8,128)(2,1)S(1)} %rebuild.3.refs_1_), channel_id=1, source_target_pairs={{0,4},{1,5},{2,6},{3,7},{4,0},{5,1},{6,2},{7,3},{8,12},{9,13},{10,... | collective-permute-start | bytes 491528 | tf_op jit(solution)/shard_map/ppermute | solution.py:27
  12.1 8.3 %collective-permute-start.5 = (bf16[128,640]{1,0:T(8,128)(2,1)S(1)}, bf16[128,640]{1,0:T(8,128)(2,1)S(1)}, u32[]{:S(2)}, u32[]{:S(2)}) collective-permute-start(bf16[128,640]{1,0:T(8,128)(2,1)S(1)} %rebuild.2.refs_0_), channel_id=1, source_target_pairs={{0,4},{1,5},{2,6},{3,7},{4,0},{5,1},{6,2},{7,3},{8,12},{9,13},{10,... | collective-permute-start | bytes 491528 | tf_op jit(solution)/shard_map/ppermute | solution.py:27
  14.0 6.4 %collective-permute-start.4 = (bf16[2,64,640]{2,1,0:T(8,128)(2,1)S(1)}, bf16[2,64,640]{2,1,0:T(8,128)(2,1)S(1)}, u32[]{:S(2)}, u32[]{:S(2)}) collective-permute-start(bf16[2,64,640]{2,1,0:T(8,128)(2,1)S(1)} %pair.1), channel_id=1, source_target_pairs={{0,2},{1,3},{2,0},{3,1},{4,6},{5,7},{6,4},{7,5},{8,10},{9,11},{10,... | collective-permute-start | bytes 491528 | tf_op jit(solution)/shard_map/ppermute | solution.py:27
  21.3 7.5 %collective-permute-start.12 = (bf16[2,176,128]{2,1,0:T(8,128)(2,1)S(1)}, bf16[2,176,128]{2,1,0:T(8,128)(2,1)S(1)}, u32[]{:S(2)}, u32[]{:S(2)}) collective-permute-start(bf16[2,176,128]{2,1,0:T(8,128)(2,1)S(1)} %get-tuple-element.32), channel_id=1, source_target_pairs={{0,10},{1,11},{2,8},{3,9},{4,14},{5,15},{6,12},{7,13},{8,2},{9,3},... | collective-permute-start | bytes 270344 | tf_op jit(solution)/shard_map/ppermute | solution.py:27
  23.8 6.4 %collective-permute-start.8 = (bf16[2,176,128]{2,1,0:T(8,128)(2,1)S(1)}, bf16[2,176,128]{2,1,0:T(8,128)(2,1)S(1)}, u32[]{:S(2)}, u32[]{:S(2)}) collective-permute-start(bf16[2,176,128]{2,1,0:T(8,128)(2,1)S(1)} %get-tuple-element.30), channel_id=1, source_target_pairs={{0,2},{1,3},{2,0},{3,1},{4,6},{5,7},{6,4},{7,5},{8,10},{9,11},{10,... | collective-permute-start | bytes 270344 | tf_op jit(solution)/shard_map/ppermute | solution.py:27
  24.1 8.8 %collective-permute-start.11 = (bf16[1,176,128]{2,1,0:T(8,128)(2,1)S(1)}, bf16[1,176,128]{2,1,0:T(8,128)(2,1)S(1)}, u32[]{:S(2)}, u32[]{:S(2)}) collective-permute-start(bf16[1,176,128]{2,1,0:T(8,128)(2,1)S(1)} %get-tuple-element.27.refs_4_), channel_id=1, source_target_pairs={{0,9},{1,8},{2,11},{3,10},{4,13},{5,12},{6,15},{7,14},{8,1},{9,0},... | collective-permute-start | bytes 135176 | tf_op jit(solution)/shard_map/ppermute | solution.py:27
  27.7 5.2 %collective-permute-start.10 = (bf16[1,176,128]{2,1,0:T(8,128)(2,1)S(1)}, bf16[1,176,128]{2,1,0:T(8,128)(2,1)S(1)}, u32[]{:S(2)}, u32[]{:S(2)}) collective-permute-start(bf16[1,176,128]{2,1,0:T(8,128)(2,1)S(1)} %get-tuple-element.31), channel_id=1, source_target_pairs={{0,8},{1,9},{2,10},{3,11},{4,12},{5,13},{6,14},{7,15},{8,0},{9,1},... | collective-permute-start | bytes 135176 | tf_op jit(solution)/shard_map/ppermute | solution.py:27
  28.3 4.7 %collective-permute-start.7 = (bf16[1,176,128]{2,1,0:T(8,128)(2,1)S(1)}, bf16[1,176,128]{2,1,0:T(8,128)(2,1)S(1)}, u32[]{:S(2)}, u32[]{:S(2)}) collective-permute-start(bf16[1,176,128]{2,1,0:T(8,128)(2,1)S(1)} %get-tuple-element.29), channel_id=1, source_target_pairs={{0,1},{1,0},{2,3},{3,2},{4,5},{5,4},{6,7},{7,6},{8,9},{9,8},{10,11... | collective-permute-start | bytes 135176 | tf_op jit(solution)/shard_map/ppermute | solution.py:27
  28.8 4.2 %collective-permute-start.13 = (bf16[1,176,128]{2,1,0:T(8,128)(2,1)S(1)}, bf16[1,176,128]{2,1,0:T(8,128)(2,1)S(1)}, u32[]{:S(2)}, u32[]{:S(2)}) collective-permute-start(bf16[1,176,128]{2,1,0:T(8,128)(2,1)S(1)} %slice.9), channel_id=1, source_target_pairs={{0,1},{1,0},{2,3},{3,2},{4,5},{5,4},{6,7},{7,6},{8,9},{9,8},{10,11... | collective-permute-start | bytes 135176 | tf_op jit(solution)/shard_map/ppermute | solution.py:27
  30.2 2.8 %collective-permute-start.9 = (bf16[1,176,128]{2,1,0:T(8,128)(2,1)S(1)}, bf16[1,176,128]{2,1,0:T(8,128)(2,1)S(1)}, u32[]{:S(2)}, u32[]{:S(2)}) collective-permute-start(bf16[1,176,128]{2,1,0:T(8,128)(2,1)S(1)} %slice.8), channel_id=1, source_target_pairs={{0,1},{1,0},{2,3},{3,2},{4,5},{5,4},{6,7},{7,6},{8,9},{9,8},{10,11... | collective-permute-start | bytes 135176 | tf_op jit(solution)/shard_map/ppermute | solution.py:27

commit v6 on v5

--- a/solution.py
+++ b/solution.py
@@ -71,22 +71,22 @@
     )(*slabs)
 
 
-def join_kernel(kept, arrived, keys, values, query, crossing):
+def join_kernel(kept, arrived, x_query, x_keys, x_values, z_values):
     rows = kept.shape[2]
-    for i, out in enumerate((keys, values, query)):
+    for i, out in ((0, x_keys), (1, x_values), (2, x_query)):
         out[:rows] = kept[i, 1]
         out[rows:] = arrived[i, 1]
     for k in range(2):
-        crossing[k, :rows] = kept[2, k]
-        crossing[k, rows:] = arrived[2, k]
+        z_values[k, :rows] = kept[1, k]
+        z_values[k, rows:] = arrived[1, k]
 
 
 def join(kept, arrived):
     _, _, rows, width = kept.shape
-    shape = jax.ShapeDtypeStruct((2 * rows, width), kept.dtype)
+    shape = (2 * rows, width)
     return pl.pallas_call(
         join_kernel,
-        out_shape=[shape] * 3 + [jax.ShapeDtypeStruct((2, 2 * rows, width), kept.dtype)],
+        out_shape=[jax.ShapeDtypeStruct(shape, kept.dtype)] * 3 + [jax.ShapeDtypeStruct((2,) + shape, kept.dtype)],
         in_specs=[VMEM] * 2,
         out_specs=[VMEM] * 4,
         compiler_params=limit(4 * MB),
@@ -95,36 +95,54 @@
     )(kept, arrived)
 
 
-def pair_kernel(query, far_query, *refs):
-    out = refs[-1]
-    out[0] = query[...]
-    out[1] = far_query[1]
-
-
-def pair(query, far_query, *earlier):
-    return pl.pallas_call(
-        pair_kernel,
-        out_shape=jax.ShapeDtypeStruct(far_query.shape, far_query.dtype),
-        in_specs=[VMEM] * 2 + [HBM] * len(earlier),
+def assemble_kernel(kept, beside, opposite, out):
+    rows = kept.shape[2]
+    out[:rows] = kept[2, 0]
+    out[rows : 2 * rows] = beside[2, 0]
+    out[2 * rows :] = opposite[...]
+
+
+def assemble(kept, beside, opposite):
+    _, _, rows, width = kept.shape
+    return pl.pallas_call(
+        assemble_kernel,
+        out_shape=jax.ShapeDtypeStruct((GROUP * rows, width), kept.dtype),
+        in_specs=[VMEM] * 3,
         out_specs=VMEM,
         compiler_params=limit(4 * MB),
         cost_estimate=cost(1000),
-        name="pair",
-    )(query, far_query, *earlier)
-
-
-def fetch_kernel(heads, keys_copy, values_copy, kb, vb, old, limits, lines, turned, sems):
+        name="assemble",
+    )(kept, beside, opposite)
+
+
+def pick_kernel(both, *refs):
+    refs[-1][...] = both[1]
+
+
+def pick(both, *earlier):
+    return pl.pallas_call(
+        pick_kernel,
+        out_shape=jax.ShapeDtypeStruct(both.shape[1:], both.dtype),
+        in_specs=[VMEM] + [HBM] * len(earlier),
+        out_specs=VMEM,
+        compiler_params=limit(4 * MB + 2 * both.size * both.dtype.itemsize),
+        cost_estimate=cost(1000),
+        name="pick",
+    )(both, *earlier)
+
+
+def fetch_kernel(heads, count, keys_copy, values_copy, kb, vb, old, limits, lines, turned, sems):
     rows = old.shape[1] // GROUP
     group, member = position()
-    block = part(group, GROUP * rows)
+    sources = [(keys_copy, kb, group)] + [(values_copy, vb, group ^ j) for j in range(count)]
     pairs = []
-    for i, (copy, bound) in enumerate(((keys_copy, kb), (values_copy, vb))):
-        pairs.append((bound.at[:, block], lines.at[i]))
+    for i, (copy, bound, block) in enumerate(sources):
+        pairs.append((bound.at[:, part(block, GROUP * rows)], lines.at[i]))
         for k in range(GROUP):
-            source = copy.at[0, part(group * GROUP + (member ^ k), rows), :]
+            source = copy.at[0, part(block * GROUP + (member ^ k), rows), :]
             pairs.append((source, old.at[i, pl.ds(k * rows, rows), :]))
     run_copies(pairs, sems)
-    for i in range(2):
+    for i in range(len(sources)):
         chosen = lines[i, pl.ds(member * heads, heads), :]
         padding = jnp.zeros((limits.shape[2] - heads, GROUP * rows), chosen.dtype)
         turned[...] = jnp.concatenate([chosen, padding], axis=0).T
@@ -132,59 +150,73 @@
             limits[i, pl.ds(k * rows, rows), :] = turned[part(member ^ k, rows), :]
 
 
-def fetch(heads, rows, keys_copy, values_copy, key_bounds, value_bounds):
+def fetch(heads, rows, count, keys_copy, values_copy, key_bounds, value_bounds):
     width = keys_copy.shape[2]
     return pl.pallas_call(
-        functools.partial(fetch_kernel, heads),
+        functools.partial(fetch_kernel, heads, count),
         out_shape=[
-            jax.ShapeDtypeStruct((2, GROUP * rows, width), keys_copy.dtype),
-            jax.ShapeDtypeStruct((2, GROUP * rows, 128), key_bounds.dtype),
+            jax.ShapeDtypeStruct((1 + count, GROUP * rows, width), keys_copy.dtype),
+            jax.ShapeDtypeStruct((1 + count, GROUP * rows, 128), key_bounds.dtype),
         ],
         in_specs=[HBM] * 4,
         out_specs=[VMEM] * 2,
         scratch_shapes=[
-            pltpu.VMEM((2, key_bounds.shape[1], GROUP * rows), key_bounds.dtype),
+            pltpu.VMEM((1 + count, key_bounds.shape[1], GROUP * rows), key_bounds.dtype),
             pltpu.VMEM((GROUP * rows, 128), key_bounds.dtype),
-            pltpu.SemaphoreType.DMA((10,)),
+            pltpu.SemaphoreType.DMA(((1 + GROUP) * (1 + count),)),
         ],
-        compiler_params=limit(4 * MB),
+        compiler_params=limit(4 * MB + MB * count),
         cost_estimate=cost(1000),
         name="fetch",
     )(keys_copy, values_copy, key_bounds.T, value_bounds.T)
 
 
-def rebuild_kernel(heads, i, kept, beside, opposite, old, limits, out):
-    rows = kept.shape[2]
-    head = kept.shape[3] // heads
-    pieces = (kept.at[i, 0], beside.at[i, 0], opposite.at[pl.ds(0, rows)], opposite.at[pl.ds(rows, rows)])
+def restore(heads, pieces, old, limits, out, start):
+    rows, width = pieces[0].shape
+    head = width // heads
     for k, piece in enumerate(pieces):
         place = slice(k * rows, (k + 1) * rows)
         for h in range(heads):
             lanes = slice(h * head, (h + 1) * head)
-            bound = limits[i, place, h : h + 1]
-            previous = old[i, place, lanes].astype(jnp.float32)
+            bound = limits[place, h : h + 1]
+            previous = old[place, lanes].astype(jnp.float32)
             change = jnp.clip(piece[:, lanes].astype(jnp.float32) - previous, -bound, bound)
             change = change.astype(jnp.bfloat16).astype(jnp.float32)
-            out[place, lanes] = (previous + change).astype(out.dtype)
-
-
-def rebuild(heads, i, kept, beside, opposite, old, limits):
-    return pl.pallas_call(
-        functools.partial(rebuild_kernel, heads, i),
-        out_shape=jax.ShapeDtypeStruct(old.shape[1:], old.dtype),
-        in_specs=[VMEM] * 5,
+            out[start + k * rows : start + (k + 1) * rows, lanes] = (previous + change).astype(out.dtype)
+
+
+def rebuild_keys_kernel(heads, kept, beside, opposite, old, limits, _, out):
+    rows = kept.shape[2]
+    pieces = [kept.at[0, 0], beside.at[0, 0], opposite.at[pl.ds(0, rows)], opposite.at[pl.ds(rows, rows)]]
+    restore(heads, pieces, old.at[0], limits.at[0], out, 0)
+
+
+def rebuild_values_kernel(heads, first, this, opposite, old, limits, *refs):
+    out = refs[-1]
+    rows = old.shape[1] // GROUP
+    for j in range(this.shape[1] // (2 * rows)):
+        starts = [2 * j * rows, (2 * j + 1) * rows]
+        pieces = [this.at[0, pl.ds(start, rows)] for start in starts]
+        pieces += [opposite.at[pl.ds(start, rows)] for start in starts]
+        restore(heads, pieces, old.at[1 + first + j], limits.at[1 + first + j], out, j * GROUP * rows)
+
+
+def rebuild(kernel, tokens, old, *operands):
+    return pl.pallas_call(
+        kernel,
+        out_shape=jax.ShapeDtypeStruct((tokens, old.shape[2]), old.dtype),
+        in_specs=[VMEM] * len(operands),
         out_specs=VMEM,
-        compiler_params=limit(4 * MB),
+        compiler_params=limit(4 * MB + 16 * tokens * old.shape[2]),
         cost_estimate=cost(1000),
         name="rebuild",
-    )(kept, beside, opposite, old, limits)
-
-
-def attend_kernel(heads, parts, count, *refs):
-    queries, (near_keys, near_values, far_keys, far_values) = refs[:count], refs[count : count + 4]
+    )(*operands)
+
+
+def attend_kernel(heads, parts, query_ref, near_keys, near_values, far_keys, far_values, *refs):
     refs = refs[-len(parts) :]
     width = near_keys.shape[1]
-    rows = sum(query.shape[0] for query in queries) // GROUP
+    rows = query_ref.shape[0] // GROUP
     head = width // heads
     outs = {k: ref.at[j] for ref, group in zip(refs, parts) for j, k in enumerate(group)}
     scale = head ** (-0.5) * LOG2E
@@ -193,7 +225,7 @@
     contract = (((1,), (1,)), ((), ()))
     for h in range(heads):
         lanes = slice(h * head, (h + 1) * head)
-        query = jnp.concatenate([q[:, lanes] for q in queries], axis=0)
+        query = query_ref[:, lanes]
         scores = [
             lax.dot_general(query, keys[:, lanes], contract, preferred_element_type=jnp.float32)
             for keys in (near_keys, far_keys)
@@ -225,28 +257,21 @@
         out[heads * rows :, :] = packed.astype(out.dtype)
 
 
-def far_kernel(heads, parts, far_query, opposite, *refs):
-    attend_kernel(heads, parts, 2, far_query.at[0], opposite.at[1], *refs)
-
-
-def own_kernel(heads, parts, kept, beside, opposite, *refs):
-    attend_kernel(heads, parts, 3, kept.at[2, 0], beside.at[2, 0], opposite.at[0], *refs)
-
-
-def attend(kernel, heads, parts, rows, queries, near, far, *earlier):
+def attend(heads, parts, query, near, far, *earlier):
     tokens, width = near[0].shape
+    rows = query.shape[0] // GROUP
     shape = (heads * rows + rows // 2, width // heads)
     outs = [jax.ShapeDtypeStruct((len(group),) + shape, near[0].dtype) for group in parts]
     room = 4 * MB + 8 * near[0].size * near[0].dtype.itemsize + 32 * GROUP * rows * tokens
     return pl.pallas_call(
-        functools.partial(kernel, heads, parts),
+        functools.partial(attend_kernel, heads, parts),
         out_shape=outs,
-        in_specs=[VMEM] * (len(queries) + 4) + [HBM] * len(earlier),
+        in_specs=[VMEM] * 5 + [HBM] * len(earlier),
         out_specs=[VMEM] * len(outs),
         compiler_params=limit(room),
         cost_estimate=cost(1000),
         name="attend",
-    )(*queries, *near, *far, *earlier)
+    )(query, *near, *far, *earlier)
 
 
 def merge_kernel(heads, n0, n1, n2, n3, f0, f1, f2, f3, out):
@@ -301,24 +326,41 @@
     copies = [pltpu.with_memory_space_constraint(a, pltpu.HBM) for a in (keys_copy, values_copy)]
     sent, kept = cut(*pinned)
     beside = swapped(sent, 1)
-    x_keys, x_values, x_query, crossing = join(kept, beside)
-    far_query = swapped(crossing, across)
-    opposite = [swapped(a, 2) for a in (x_keys, x_values)]
-    old, limits = fetch(heads, rows, *copies, key_bounds, value_bounds)
-    near = [rebuild(heads, i, kept, beside, opposite[i], old, limits) for i in range(2)]
-    for bit in range(2, levels - 2):
-        near = [jnp.concatenate([a, swapped(a, 1 << bit)], axis=0) for a in near]
-    far = [swapped(a, 1 << levels - 2) for a in near]
-    q_opposite = swapped(pair(x_query, far_query, *near), 2)
+    x_query, x_keys, x_own, near_raw = join(kept, beside)
+    own_query = assemble(kept, beside, swapped(x_query, 2))
+    far_query = swapped(own_query, across)
+    bits = [1 << bit for bit in range(2, levels - 1)]
+    for bit in bits[:-1]:
+        near_raw = jnp.concatenate([near_raw, swapped(near_raw, bit)], axis=1)
+    far_raw = swapped(near_raw, bits[-1])
+    if len(bits) > 1:
+        x_own = near_raw[1]
+    x_keys, x_own = swapped(x_keys, 2), swapped(x_own, 2)
+    count = 1 << len(bits)
+    old, limits = fetch(heads, rows, count, *copies, key_bounds, value_bounds)
+    block = GROUP * rows
+    rebuild_keys = functools.partial(rebuild_keys_kernel, heads)
+    near_keys = rebuild(rebuild_keys, block, old, kept, beside, x_keys, old, limits, own_query)
+    picked = pick(far_raw, near_keys)
+    for bit in bits[:-1]:
+        near_keys = jnp.concatenate([near_keys, swapped(near_keys, bit)], axis=0)
+    far_keys = swapped(near_keys, bits[-1])
+    halves = []
+    sides = ((0, near_raw, x_own, own_query), (count // 2, far_raw, swapped(picked, 2), far_query))
+    for first, this, opposite, earlier in sides:
+        kernel = functools.partial(rebuild_values_kernel, heads, first)
+        halves.append(rebuild(kernel, block * count // 2, old, this, opposite, old, limits, earlier))
+    near, far = (near_keys, halves[0]), (far_keys, halves[1])
     parts = ((2, 3), (0,), (1,))
-    far_out = attend(far_kernel, heads, parts, rows, (far_query, q_opposite), near, far)
+    far_out = attend(heads, parts, far_query, near, far)
     f23, f0, f1 = [swapped(a, across + group[0]) for a, group in zip(far_out, parts)]
     parts = ((0,), (1,), (2, 3))
-    own_query = (kept, beside, q_opposite)
-    n0, n1, n23 = attend(own_kernel, heads, parts, rows, own_query, near, far, far_out[2])
+    n0, n1, n23 = attend(heads, parts, own_query, near, far, far_out[2])
     n1, n23 = swapped(n1, 1), swapped(n23, 2)
-    near_parts = (n0, n1, n23, swapped(n23[1:], 1))
-    far_parts = (f0, f1, f23, swapped(f23[1:], 1))
+    f3 = pick(f23)
+    n3 = pick(n23, f3)
+    near_parts = (n0, n1, n23, swapped(n3, 1)[None])
+    far_parts = (f0, f1, f23, swapped(f3, 1)[None])
     return merge(heads, near_parts, far_parts, rows)
 
 

time: 34.4 us -> 33.8 us (0.983)
  the two profiles are of different devices: /device:TPU:1 before, /device:TPU:0 now
where the time goes in v6:
time: 33.8 us; the launch traced here: 33.5 us
  starting transfers between devices  18.1 us (54%)
  waiting for transfers between devices  9.4 us (28%)
  Pallas kernels  5.91 us (17%)
    ppermute x15, starting transfers between devices, swapped(): return lax.ppermute(array, 'patch', [(i, i ^ mask) for i in range(size)])  18.1 us
    ppermute x15, waiting for transfers between devices, swapped(): return lax.ppermute(array, 'patch', [(i, i ^ mask) for i in range(size)])  9.4 us
    pallas_call x2, Pallas kernels, attend(): pl.pallas_call(functools.partial(attend_kernel, heads, parts), out_shape=...  1.66 us
    pallas_call x1, Pallas kernels, fetch(): pl.pallas_call(functools.partial(fetch_kernel, heads, count), out_shape=[...  1.29 us
    pallas_call x1, Pallas kernels, merge(): pl.pallas_call(functools.partial(merge_kernel, heads), out_shape=jax.Shap...  1.22 us
    pallas_call x1, Pallas kernels, cut(): pl.pallas_call(functools.partial(cut_kernel, len(slabs)), out_shape=[shap...  1.11 us
  transfers between devices with their start and end apart: 15, of which 6 were waited for; matrix products, arithmetic and copies ran while one was open for 0% of the time, Pallas kernels for 8%

profile of v6, /device:TPU:0, one launch (start us, length us, event | category | flops | bytes accessed | tf_op | source)
XLA Modules:
  0.0 33.5 jit_solution(2916159192152734093)
XLA Ops:
  0.0 1.1 %cut.1 = (bf16[3,2,32,640]{3,2,1,0:T(8,128)(2,1)S(1)}, bf16[3,2,32,640]{3,2,1,0:T(8,128)(2,1)S(1)}) custom-call(bf16[32,2560]{1,0:T(8,128)(2,1)} %refs_0_.1, bf16[32,2560]{1,0:T(8,128)(2,1)} %refs_1_.1, bf16[32,2560]{1,0:T(8,128)(2,1)} %refs_2_.1), custom_call_target="tpu_custom_call" | custom-call | bytes 1000 | tf_op jit(solution)/shard_map/cut/pallas_call | solution.py:62
  1.1 0.5 %collective-permute-start = (bf16[3,2,32,640]{3,2,1,0:T(8,128)(2,1)S(1)}, bf16[3,2,32,640]{3,2,1,0:T(8,128)(2,1)S(1)}, u32[]{:S(2)}, u32[]{:S(2)}) collective-permute-start(bf16[3,2,32,640]{3,2,1,0:T(8,128)(2,1)S(1)} %get-tuple-element.20), channel_id=1, source_target_pairs={{0,1},{1,0},{2,3},{3,2},{4,5},{5,4},{6,7},{7,6},{8,9},{9,8},{10,11... | collective-permute-start | bytes 737288 | tf_op jit(solution)/shard_map/ppermute | solution.py:27
  1.6 1.1 %collective-permute-done.arrived.beside = bf16[3,2,32,640]{3,2,1,0:T(8,128)(2,1)S(1)} collective-permute-done((bf16[3,2,32,640]{3,2,1,0:T(8,128)(2,1)S(1)}, bf16[3,2,32,640]{3,2,1,0:T(8,128)(2,1)S(1)}, u32[]{:S(2)}, u32[]{:S(2)}) %collective-permute-start) | collective-permute-done | bytes 245792 | tf_op jit(solution)/shard_map/ppermute | solution.py:27
  2.8 2.9 %collective-permute-start.1 = (bf16[64,640]{1,0:T(8,128)(2,1)S(1)}, bf16[64,640]{1,0:T(8,128)(2,1)S(1)}, u32[]{:S(2)}, u32[]{:S(2)}) collective-permute-start(bf16[64,640]{1,0:T(8,128)(2,1)S(1)} %get-tuple-element.21), channel_id=1, source_target_pairs={{0,2},{1,3},{2,0},{3,1},{4,6},{5,7},{6,4},{7,5},{8,10},{9,11},{10,... | collective-permute-start | bytes 245768 | tf_op jit(solution)/shard_map/ppermute | solution.py:27
  5.7 1.6 %collective-permute-start.5 = (bf16[2,64,640]{2,1,0:T(8,128)(2,1)S(1)}, bf16[2,64,640]{2,1,0:T(8,128)(2,1)S(1)}, u32[]{:S(2)}, u32[]{:S(2)}) collective-permute-start(bf16[2,64,640]{2,1,0:T(8,128)(2,1)S(1)} %get-tuple-element.25.this), channel_id=1, source_target_pairs={{0,4},{1,5},{2,6},{3,7},{4,0},{5,1},{6,2},{7,3},{8,12},{9,13},{10,... | collective-permute-start | bytes 491528 | tf_op jit(solution)/shard_map/ppermute | solution.py:27
  7.3 0.5 %collective-permute-start.2 = (bf16[64,640]{1,0:T(8,128)(2,1)S(1)}, bf16[64,640]{1,0:T(8,128)(2,1)S(1)}, u32[]{:S(2)}, u32[]{:S(2)}) collective-permute-start(bf16[64,640]{1,0:T(8,128)(2,1)S(1)} %get-tuple-element.22), channel_id=1, source_target_pairs={{0,2},{1,3},{2,0},{3,1},{4,6},{5,7},{6,4},{7,5},{8,10},{9,11},{10,... | collective-permute-start | bytes 245768 | tf_op jit(solution)/shard_map/ppermute | solution.py:27
  7.9 1.3 %fetch.1 = (bf16[3,128,640]{2,1,0:T(8,128)(2,1)S(1)}, f32[3,128,128]{2,1,0:T(8,128)S(1)}) custom-call(bf16[1,512,640]{2,1,0:T(8,128)(2,1)} %keys_copy.1, bf16[1,512,640]{2,1,0:T(8,128)(2,1)} %values_copy.1, f32[20,512]{1,0:T(8,128)S(1)} %bitcast.4, f32[20,512]{1,0:T(8,128)S(1)} %bitcast.5), custom_call_target="tpu_custom_call" | custom-call | bytes 1000 | tf_op jit(solution)/shard_map/fetch/pallas_call | solution.py:155
  9.2 2.7 %collective-permute-start.7 = (bf16[128,640]{1,0:T(8,128)(2,1)S(1)}, bf16[128,640]{1,0:T(8,128)(2,1)S(1)}, u32[]{:S(2)}, u32[]{:S(2)}) collective-permute-start(bf16[128,640]{1,0:T(8,128)(2,1)S(1)} %assemble.1._.refs_0_.query_ref), channel_id=1, source_target_pairs={{0,8},{1,9},{2,10},{3,11},{4,12},{5,13},{6,14},{7,15},{8,0},{9,1},... | collective-permute-start | bytes 491528 | tf_op jit(solution)/shard_map/ppermute | solution.py:27
  12.0 1.6 %collective-permute-start.4 = (bf16[128,640]{1,0:T(8,128)(2,1)S(1)}, bf16[128,640]{1,0:T(8,128)(2,1)S(1)}, u32[]{:S(2)}, u32[]{:S(2)}) collective-permute-start(bf16[128,640]{1,0:T(8,128)(2,1)S(1)} %rebuild.3.refs_0_.near_keys), channel_id=1, source_target_pairs={{0,4},{1,5},{2,6},{3,7},{4,0},{5,1},{6,2},{7,3},{8,12},{9,13},{10,... | collective-permute-start | bytes 491528 | tf_op jit(solution)/shard_map/ppermute | solution.py:27
  13.7 1.9 %collective-permute-start.3 = (bf16[64,640]{1,0:T(8,128)(2,1)S(1)}, bf16[64,640]{1,0:T(8,128)(2,1)S(1)}, u32[]{:S(2)}, u32[]{:S(2)}) collective-permute-start(bf16[64,640]{1,0:T(8,128)(2,1)S(1)} %get-tuple-element.26), channel_id=1, source_target_pairs={{0,2},{1,3},{2,0},{3,1},{4,6},{5,7},{6,4},{7,5},{8,10},{9,11},{10,... | collective-permute-start | bytes 245768 | tf_op jit(solution)/shard_map/ppermute | solution.py:27
  15.6 0.2 collective-permute-start.6
  15.8 2.3 %collective-permute-done.3.opposite = bf16[64,640]{1,0:T(8,128)(2,1)S(1)} collective-permute-done((bf16[64,640]{1,0:T(8,128)(2,1)S(1)}, bf16[64,640]{1,0:T(8,128)(2,1)S(1)}, u32[]{:S(2)}, u32[]{:S(2)}) %collective-permute-start.3) | collective-permute-done | bytes 81952 | tf_op jit(solution)/shard_map/ppermute | solution.py:27
  18.3 1.7 %collective-permute-done.6.opposite = bf16[64,640]{1,0:T(8,128)(2,1)S(1)} collective-permute-done((bf16[64,640]{1,0:T(8,128)(2,1)S(1)}, bf16[64,640]{1,0:T(8,128)(2,1)S(1)}, u32[]{:S(2)}, u32[]{:S(2)}) %collective-permute-start.6) | collective-permute-done | bytes 81952 | tf_op jit(solution)/shard_map/ppermute | solution.py:27
  20.3 0.8 %attend.2 = (bf16[2,176,128]{2,1,0:T(8,128)(2,1)S(1)}, bf16[1,176,128]{2,1,0:T(8,128)(2,1)S(1)}, bf16[1,176,128]{2,1,0:T(8,128)(2,1)S(1)}) custom-call(bf16[128,640]{1,0:T(8,128)(2,1)S(1)} %collective-permute-done.7.refs_0_.query_ref, bf16[128,640]{1,0:T(8,128)(2,1)S(1)} %rebuild.3.refs_0_.near_keys, bf16[128,640]{1,0:T(8,128)(2,1)S(1)} %rebuild.4.near_values, ...), custom_call_target="tpu_custom_call" | custom-call | bytes 1000 | tf_op jit(solution)/shard_map/attend/pallas_call | solution.py:266
  21.1 1.7 %collective-permute-start.10 = (bf16[2,176,128]{2,1,0:T(8,128)(2,1)S(1)}, bf16[2,176,128]{2,1,0:T(8,128)(2,1)S(1)}, u32[]{:S(2)}, u32[]{:S(2)}) collective-permute-start(bf16[2,176,128]{2,1,0:T(8,128)(2,1)S(1)} %get-tuple-element.31), channel_id=1, source_target_pairs={{0,10},{1,11},{2,8},{3,9},{4,14},{5,15},{6,12},{7,13},{8,2},{9,3},... | collective-permute-start | bytes 270344 | tf_op jit(solution)/shard_map/ppermute | solution.py:27
  22.8 0.8 %attend.3 = (bf16[1,176,128]{2,1,0:T(8,128)(2,1)S(1)}, bf16[1,176,128]{2,1,0:T(8,128)(2,1)S(1)}, bf16[2,176,128]{2,1,0:T(8,128)(2,1)S(1)}) custom-call(bf16[128,640]{1,0:T(8,128)(2,1)S(1)} %assemble.1._.refs_0_.query_ref, bf16[128,640]{1,0:T(8,128)(2,1)S(1)} %rebuild.3.refs_0_.near_keys, bf16[128,640]{1,0:T(8,128)(2,1)S(1)} %rebuild.4.near_values, ...), custom_call_target="tpu_custom_call" | custom-call | bytes 1000 | tf_op jit(solution)/shard_map/attend/pallas_call | solution.py:266
  23.6 1.0 %collective-permute-start.9 = (bf16[2,176,128]{2,1,0:T(8,128)(2,1)S(1)}, bf16[2,176,128]{2,1,0:T(8,128)(2,1)S(1)}, u32[]{:S(2)}, u32[]{:S(2)}) collective-permute-start(bf16[2,176,128]{2,1,0:T(8,128)(2,1)S(1)} %get-tuple-element.30), channel_id=1, source_target_pairs={{0,2},{1,3},{2,0},{3,1},{4,6},{5,7},{6,4},{7,5},{8,10},{9,11},{10,... | collective-permute-start | bytes 270344 | tf_op jit(solution)/shard_map/ppermute | solution.py:27
  24.6 2.0 %collective-permute-start.8 = (bf16[1,176,128]{2,1,0:T(8,128)(2,1)S(1)}, bf16[1,176,128]{2,1,0:T(8,128)(2,1)S(1)}, u32[]{:S(2)}, u32[]{:S(2)}) collective-permute-start(bf16[1,176,128]{2,1,0:T(8,128)(2,1)S(1)} %get-tuple-element.29), channel_id=1, source_target_pairs={{0,1},{1,0},{2,3},{3,2},{4,5},{5,4},{6,7},{7,6},{8,9},{9,8},{10,11... | collective-permute-start | bytes 135176 | tf_op jit(solution)/shard_map/ppermute | solution.py:27
  26.5 1.1 %collective-permute-start.12 = (bf16[1,176,128]{2,1,0:T(8,128)(2,1)S(1)}, bf16[1,176,128]{2,1,0:T(8,128)(2,1)S(1)}, u32[]{:S(2)}, u32[]{:S(2)}) collective-permute-start(bf16[1,176,128]{2,1,0:T(8,128)(2,1)S(1)} %get-tuple-element.32), channel_id=1, source_target_pairs={{0,8},{1,9},{2,10},{3,11},{4,12},{5,13},{6,14},{7,15},{8,0},{9,1},... | collective-permute-start | bytes 135176 | tf_op jit(solution)/shard_map/ppermute | solution.py:27
  27.6 0.9 %collective-permute-done.10.both.f2 = bf16[2,176,128]{2,1,0:T(8,128)(2,1)S(1)} collective-permute-done((bf16[2,176,128]{2,1,0:T(8,128)(2,1)S(1)}, bf16[2,176,128]{2,1,0:T(8,128)(2,1)S(1)}, u32[]{:S(2)}, u32[]{:S(2)}) %collective-permute-start.10) | collective-permute-done | bytes 90144 | tf_op jit(solution)/shard_map/ppermute | solution.py:27
  28.5 0.6 %collective-permute-done.9.both.n2 = bf16[2,176,128]{2,1,0:T(8,128)(2,1)S(1)} collective-permute-done((bf16[2,176,128]{2,1,0:T(8,128)(2,1)S(1)}, bf16[2,176,128]{2,1,0:T(8,128)(2,1)S(1)}, u32[]{:S(2)}, u32[]{:S(2)}) %collective-permute-start.9) | collective-permute-done | bytes 90144 | tf_op jit(solution)/shard_map/ppermute | solution.py:27
  29.1 0.5 %collective-permute-start.14 = (bf16[176,128]{1,0:T(8,128)(2,1)S(1)}, bf16[176,128]{1,0:T(8,128)(2,1)S(1)}, u32[]{:S(2)}, u32[]{:S(2)}) collective-permute-start(bf16[176,128]{1,0:T(8,128)(2,1)S(1)} %pick.4.refs_0_), channel_id=1, source_target_pairs={{0,1},{1,0},{2,3},{3,2},{4,5},{5,4},{6,7},{7,6},{8,9},{9,8},{10,11... | collective-permute-start | bytes 135176 | tf_op jit(solution)/shard_map/ppermute | solution.py:27
  29.6 2.7 %collective-permute-done.12.f0 = bf16[1,176,128]{2,1,0:T(8,128)(2,1)S(1)} collective-permute-done((bf16[1,176,128]{2,1,0:T(8,128)(2,1)S(1)}, bf16[1,176,128]{2,1,0:T(8,128)(2,1)S(1)}, u32[]{:S(2)}, u32[]{:S(2)}) %collective-permute-start.12) | collective-permute-done | bytes 45088 | tf_op jit(solution)/shard_map/ppermute | solution.py:27
  32.3 1.2 %merge.1 = bf16[32,2560]{1,0:T(8,128)(2,1)} custom-call(bf16[1,176,128]{2,1,0:T(8,128)(2,1)S(1)} %get-tuple-element.28.n0, bf16[1,176,128]{2,1,0:T(8,128)(2,1)S(1)} %collective-permute-done.8.n1, bf16[2,176,128]{2,1,0:T(8,128)(2,1)S(1)} %collective-permute-done.9.both.n2, bf16[1,176,128]{2,1,0:T(8,128)(2,1)S(1)} %bitcast.6, ...), custom_call_target="tpu_custom_call" | custom-call | bytes 1000 | tf_op jit(solution)/shard_map/merge/pallas_call | solution.py:308
  (23 shorter events, 0.7 us)
Async XLA Ops:
  1.1 1.7 %collective-permute-start = (bf16[3,2,32,640]{3,2,1,0:T(8,128)(2,1)S(1)}, bf16[3,2,32,640]{3,2,1,0:T(8,128)(2,1)S(1)}, u32[]{:S(2)}, u32[]{:S(2)}) collective-permute-start(bf16[3,2,32,640]{3,2,1,0:T(8,128)(2,1)S(1)} %get-tuple-element.20), channel_id=1, source_target_pairs={{0,1},{1,0},{2,3},{3,2},{4,5},{5,4},{6,7},{7,6},{8,9},{9,8},{10,11... | collective-permute-start | bytes 737288 | tf_op jit(solution)/shard_map/ppermute | solution.py:27
  2.8 5.1 %copy-start = (f32[512,20]{0,1:T(8,128)S(1)}, f32[512,20]{0,1:T(8,128)}, u32[]{:S(2)}) copy-start(f32[512,20]{0,1:T(8,128)} %param.12) | copy-start | bytes 122884
  2.8 5.1 %copy-start.1 = (f32[512,20]{0,1:T(8,128)S(1)}, f32[512,20]{0,1:T(8,128)}, u32[]{:S(2)}) copy-start(f32[512,20]{0,1:T(8,128)} %param.13) | copy-start | bytes 122884
  2.8 6.3 %collective-permute-start.1 = (bf16[64,640]{1,0:T(8,128)(2,1)S(1)}, bf16[64,640]{1,0:T(8,128)(2,1)S(1)}, u32[]{:S(2)}, u32[]{:S(2)}) collective-permute-start(bf16[64,640]{1,0:T(8,128)(2,1)S(1)} %get-tuple-element.21), channel_id=1, source_target_pairs={{0,2},{1,3},{2,0},{3,1},{4,6},{5,7},{6,4},{7,5},{8,10},{9,11},{10,... | collective-permute-start | bytes 245768 | tf_op jit(solution)/shard_map/ppermute | solution.py:27
  5.7 9.8 %collective-permute-start.5 = (bf16[2,64,640]{2,1,0:T(8,128)(2,1)S(1)}, bf16[2,64,640]{2,1,0:T(8,128)(2,1)S(1)}, u32[]{:S(2)}, u32[]{:S(2)}) collective-permute-start(bf16[2,64,640]{2,1,0:T(8,128)(2,1)S(1)} %get-tuple-element.25.this), channel_id=1, source_target_pairs={{0,4},{1,5},{2,6},{3,7},{4,0},{5,1},{6,2},{7,3},{8,12},{9,13},{10,... | collective-permute-start | bytes 491528 | tf_op jit(solution)/shard_map/ppermute | solution.py:27
  7.3 4.5 %collective-permute-start.2 = (bf16[64,640]{1,0:T(8,128)(2,1)S(1)}, bf16[64,640]{1,0:T(8,128)(2,1)S(1)}, u32[]{:S(2)}, u32[]{:S(2)}) collective-permute-start(bf16[64,640]{1,0:T(8,128)(2,1)S(1)} %get-tuple-element.22), channel_id=1, source_target_pairs={{0,2},{1,3},{2,0},{3,1},{4,6},{5,7},{6,4},{7,5},{8,10},{9,11},{10,... | collective-permute-start | bytes 245768 | tf_op jit(solution)/shard_map/ppermute | solution.py:27
  9.2 10.9 %collective-permute-start.7 = (bf16[128,640]{1,0:T(8,128)(2,1)S(1)}, bf16[128,640]{1,0:T(8,128)(2,1)S(1)}, u32[]{:S(2)}, u32[]{:S(2)}) collective-permute-start(bf16[128,640]{1,0:T(8,128)(2,1)S(1)} %assemble.1._.refs_0_.query_ref), channel_id=1, source_target_pairs={{0,8},{1,9},{2,10},{3,11},{4,12},{5,13},{6,14},{7,15},{8,0},{9,1},... | collective-permute-start | bytes 491528 | tf_op jit(solution)/shard_map/ppermute | solution.py:27
  12.0 8.2 %collective-permute-start.4 = (bf16[128,640]{1,0:T(8,128)(2,1)S(1)}, bf16[128,640]{1,0:T(8,128)(2,1)S(1)}, u32[]{:S(2)}, u32[]{:S(2)}) collective-permute-start(bf16[128,640]{1,0:T(8,128)(2,1)S(1)} %rebuild.3.refs_0_.near_keys), channel_id=1, source_target_pairs={{0,4},{1,5},{2,6},{3,7},{4,0},{5,1},{6,2},{7,3},{8,12},{9,13},{10,... | collective-permute-start | bytes 491528 | tf_op jit(solution)/shard_map/ppermute | solution.py:27
  13.7 4.4 %collective-permute-start.3 = (bf16[64,640]{1,0:T(8,128)(2,1)S(1)}, bf16[64,640]{1,0:T(8,128)(2,1)S(1)}, u32[]{:S(2)}, u32[]{:S(2)}) collective-permute-start(bf16[64,640]{1,0:T(8,128)(2,1)S(1)} %get-tuple-element.26), channel_id=1, source_target_pairs={{0,2},{1,3},{2,0},{3,1},{4,6},{5,7},{6,4},{7,5},{8,10},{9,11},{10,... | collective-permute-start | bytes 245768 | tf_op jit(solution)/shard_map/ppermute | solution.py:27
  15.6 4.5 %collective-permute-start.6 = (bf16[64,640]{1,0:T(8,128)(2,1)S(1)}, bf16[64,640]{1,0:T(8,128)(2,1)S(1)}, u32[]{:S(2)}, u32[]{:S(2)}) collective-permute-start(bf16[64,640]{1,0:T(8,128)(2,1)S(1)} %pick.3), channel_id=1, source_target_pairs={{0,2},{1,3},{2,0},{3,1},{4,6},{5,7},{6,4},{7,5},{8,10},{9,11},{10,... | collective-permute-start | bytes 245768 | tf_op jit(solution)/shard_map/ppermute | solution.py:27
  21.1 7.4 %collective-permute-start.10 = (bf16[2,176,128]{2,1,0:T(8,128)(2,1)S(1)}, bf16[2,176,128]{2,1,0:T(8,128)(2,1)S(1)}, u32[]{:S(2)}, u32[]{:S(2)}) collective-permute-start(bf16[2,176,128]{2,1,0:T(8,128)(2,1)S(1)} %get-tuple-element.31), channel_id=1, source_target_pairs={{0,10},{1,11},{2,8},{3,9},{4,14},{5,15},{6,12},{7,13},{8,2},{9,3},... | collective-permute-start | bytes 270344 | tf_op jit(solution)/shard_map/ppermute | solution.py:27
  23.6 5.5 %collective-permute-start.9 = (bf16[2,176,128]{2,1,0:T(8,128)(2,1)S(1)}, bf16[2,176,128]{2,1,0:T(8,128)(2,1)S(1)}, u32[]{:S(2)}, u32[]{:S(2)}) collective-permute-start(bf16[2,176,128]{2,1,0:T(8,128)(2,1)S(1)} %get-tuple-element.30), channel_id=1, source_target_pairs={{0,2},{1,3},{2,0},{3,1},{4,6},{5,7},{6,4},{7,5},{8,10},{9,11},{10,... | collective-permute-start | bytes 270344 | tf_op jit(solution)/shard_map/ppermute | solution.py:27
  24.6 7.7 %collective-permute-start.13 = (bf16[1,176,128]{2,1,0:T(8,128)(2,1)S(1)}, bf16[1,176,128]{2,1,0:T(8,128)(2,1)S(1)}, u32[]{:S(2)}, u32[]{:S(2)}) collective-permute-start(bf16[1,176,128]{2,1,0:T(8,128)(2,1)S(1)} %get-tuple-element.27.refs_0_), channel_id=1, source_target_pairs={{0,9},{1,8},{2,11},{3,10},{4,13},{5,12},{6,15},{7,14},{8,1},{9,0},... | collective-permute-start | bytes 135176 | tf_op jit(solution)/shard_map/ppermute | solution.py:27
  24.6 5.0 %collective-permute-start.8 = (bf16[1,176,128]{2,1,0:T(8,128)(2,1)S(1)}, bf16[1,176,128]{2,1,0:T(8,128)(2,1)S(1)}, u32[]{:S(2)}, u32[]{:S(2)}) collective-permute-start(bf16[1,176,128]{2,1,0:T(8,128)(2,1)S(1)} %get-tuple-element.29), channel_id=1, source_target_pairs={{0,1},{1,0},{2,3},{3,2},{4,5},{5,4},{6,7},{7,6},{8,9},{9,8},{10,11... | collective-permute-start | bytes 135176 | tf_op jit(solution)/shard_map/ppermute | solution.py:27
  26.5 5.8 %collective-permute-start.12 = (bf16[1,176,128]{2,1,0:T(8,128)(2,1)S(1)}, bf16[1,176,128]{2,1,0:T(8,128)(2,1)S(1)}, u32[]{:S(2)}, u32[]{:S(2)}) collective-permute-start(bf16[1,176,128]{2,1,0:T(8,128)(2,1)S(1)} %get-tuple-element.32), channel_id=1, source_target_pairs={{0,8},{1,9},{2,10},{3,11},{4,12},{5,13},{6,14},{7,15},{8,0},{9,1},... | collective-permute-start | bytes 135176 | tf_op jit(solution)/shard_map/ppermute | solution.py:27
  29.1 3.2 %collective-permute-start.11 = (bf16[176,128]{1,0:T(8,128)(2,1)S(1)}, bf16[176,128]{1,0:T(8,128)(2,1)S(1)}, u32[]{:S(2)}, u32[]{:S(2)}) collective-permute-start(bf16[176,128]{1,0:T(8,128)(2,1)S(1)} %pick.5), channel_id=1, source_target_pairs={{0,1},{1,0},{2,3},{3,2},{4,5},{5,4},{6,7},{7,6},{8,9},{9,8},{10,11... | collective-permute-start | bytes 135176 | tf_op jit(solution)/shard_map/ppermute | solution.py:27
  29.1 3.2 %collective-permute-start.14 = (bf16[176,128]{1,0:T(8,128)(2,1)S(1)}, bf16[176,128]{1,0:T(8,128)(2,1)S(1)}, u32[]{:S(2)}, u32[]{:S(2)}) collective-permute-start(bf16[176,128]{1,0:T(8,128)(2,1)S(1)} %pick.4.refs_0_), channel_id=1, source_target_pairs={{0,1},{1,0},{2,3},{3,2},{4,5},{5,4},{6,7},{7,6},{8,9},{9,8},{10,11... | collective-permute-start | bytes 135176 | tf_op jit(solution)/shard_map/ppermute | solution.py:27

commit v7 on v6

--- a/solution.py
+++ b/solution.py
@@ -126,7 +126,7 @@
         in_specs=[VMEM] + [HBM] * len(earlier),
         out_specs=VMEM,
         compiler_params=limit(4 * MB + 2 * both.size * both.dtype.itemsize),
-        cost_estimate=cost(1000),
+        cost_estimate=cost(4_000_000),
         name="pick",
     )(both, *earlier)
 
@@ -226,21 +226,14 @@
     for h in range(heads):
         lanes = slice(h * head, (h + 1) * head)
         query = query_ref[:, lanes]
-        scores = [
-            lax.dot_general(query, keys[:, lanes], contract, preferred_element_type=jnp.float32)
-            for keys in (near_keys, far_keys)
-        ]
-        peak = jnp.maximum(
-            jnp.max(scores[0], axis=1, keepdims=True), jnp.max(scores[1], axis=1, keepdims=True)
-        )
+        keys = jnp.concatenate([near_keys[:, lanes], far_keys[:, lanes]], axis=0)
+        values = jnp.concatenate([near_values[:, lanes], far_values[:, lanes]], axis=0)
+        score = lax.dot_general(query, keys, contract, preferred_element_type=jnp.float32)
+        peak = jnp.max(score, axis=1, keepdims=True)
         level = (peak * scale).astype(jnp.bfloat16).astype(jnp.float32)
-        total = None
-        for values, score in zip((near_values, far_values), scores):
-            probs = jnp.exp2(score * scale - level).astype(jnp.bfloat16)
-            value = values[:, lanes]
-            joined = jnp.concatenate([value, jnp.ones_like(value)], axis=1)
-            product = jnp.dot(probs, joined, preferred_element_type=jnp.float32)
-            total = product if total is None else total + product
+        probs = jnp.exp2(score * scale - level).astype(jnp.bfloat16)
+        joined = jnp.concatenate([values, jnp.ones_like(values)], axis=1)
+        total = jnp.dot(probs, joined, preferred_element_type=jnp.float32)
         weighted = total[:, :head].astype(jnp.bfloat16)
         weight = total[:, head:]
         high = weight.astype(jnp.bfloat16).astype(jnp.float32)
@@ -262,7 +255,7 @@
     rows = query.shape[0] // GROUP
     shape = (heads * rows + rows // 2, width // heads)
     outs = [jax.ShapeDtypeStruct((len(group),) + shape, near[0].dtype) for group in parts]
-    room = 4 * MB + 8 * near[0].size * near[0].dtype.itemsize + 32 * GROUP * rows * tokens
+    room = 4 * MB + 32 * tokens * width + 64 * GROUP * rows * tokens
     return pl.pallas_call(
         functools.partial(attend_kernel, heads, parts),
         out_shape=outs,

time: 33.8 us -> 33.3 us (0.985)
  Pallas kernels: 5.91 us -> 5.45 us
    pallas_call x2, Pallas kernels: 1.66 us -> 1.2 us  [attend(): pl.pallas_call(functools.partial(attend_kernel, heads, parts), out_shape=...]
where the time goes in v7:
time: 33.3 us; the launch traced here: 33.1 us
  starting transfers between devices  18.1 us (54%)
  waiting for transfers between devices  9.41 us (28%)
  Pallas kernels  5.45 us (16%)
    ppermute x15, starting transfers between devices, swapped(): return lax.ppermute(array, 'patch', [(i, i ^ mask) for i in range(size)])  18.1 us
    ppermute x15, waiting for transfers between devices, swapped(): return lax.ppermute(array, 'patch', [(i, i ^ mask) for i in range(size)])  9.41 us
    pallas_call x1, Pallas kernels, fetch(): pl.pallas_call(functools.partial(fetch_kernel, heads, count), out_shape=[...  1.29 us
    pallas_call x1, Pallas kernels, merge(): pl.pallas_call(functools.partial(merge_kernel, heads), out_shape=jax.Shap...  1.22 us
    pallas_call x2, Pallas kernels, attend(): pl.pallas_call(functools.partial(attend_kernel, heads, parts), out_shape=...  1.2 us
    pallas_call x1, Pallas kernels, cut(): pl.pallas_call(functools.partial(cut_kernel, len(slabs)), out_shape=[shap...  1.11 us
  transfers between devices with their start and end apart: 15, of which 6 were waited for; matrix products, arithmetic and copies ran while one was open for 0% of the time, Pallas kernels for 8%

profile of v7, /device:TPU:0, one launch (start us, length us, event | category | flops | bytes accessed | tf_op | source)
XLA Modules:
  0.0 33.1 jit_solution(7297526151441326403)
XLA Ops:
  0.0 1.1 %cut.1 = (bf16[3,2,32,640]{3,2,1,0:T(8,128)(2,1)S(1)}, bf16[3,2,32,640]{3,2,1,0:T(8,128)(2,1)S(1)}) custom-call(bf16[32,2560]{1,0:T(8,128)(2,1)} %refs_0_.1, bf16[32,2560]{1,0:T(8,128)(2,1)} %refs_1_.1, bf16[32,2560]{1,0:T(8,128)(2,1)} %refs_2_.1), custom_call_target="tpu_custom_call" | custom-call | bytes 1000 | tf_op jit(solution)/shard_map/cut/pallas_call | solution.py:62
  1.1 0.5 %collective-permute-start = (bf16[3,2,32,640]{3,2,1,0:T(8,128)(2,1)S(1)}, bf16[3,2,32,640]{3,2,1,0:T(8,128)(2,1)S(1)}, u32[]{:S(2)}, u32[]{:S(2)}) collective-permute-start(bf16[3,2,32,640]{3,2,1,0:T(8,128)(2,1)S(1)} %get-tuple-element.20), channel_id=1, source_target_pairs={{0,1},{1,0},{2,3},{3,2},{4,5},{5,4},{6,7},{7,6},{8,9},{9,8},{10,11... | collective-permute-start | bytes 737288 | tf_op jit(solution)/shard_map/ppermute | solution.py:27
  1.6 1.1 %collective-permute-done.arrived.beside = bf16[3,2,32,640]{3,2,1,0:T(8,128)(2,1)S(1)} collective-permute-done((bf16[3,2,32,640]{3,2,1,0:T(8,128)(2,1)S(1)}, bf16[3,2,32,640]{3,2,1,0:T(8,128)(2,1)S(1)}, u32[]{:S(2)}, u32[]{:S(2)}) %collective-permute-start) | collective-permute-done | bytes 245792 | tf_op jit(solution)/shard_map/ppermute | solution.py:27
  2.8 2.9 %collective-permute-start.1 = (bf16[64,640]{1,0:T(8,128)(2,1)S(1)}, bf16[64,640]{1,0:T(8,128)(2,1)S(1)}, u32[]{:S(2)}, u32[]{:S(2)}) collective-permute-start(bf16[64,640]{1,0:T(8,128)(2,1)S(1)} %get-tuple-element.21), channel_id=1, source_target_pairs={{0,2},{1,3},{2,0},{3,1},{4,6},{5,7},{6,4},{7,5},{8,10},{9,11},{10,... | collective-permute-start | bytes 245768 | tf_op jit(solution)/shard_map/ppermute | solution.py:27
  5.7 1.6 %collective-permute-start.5 = (bf16[2,64,640]{2,1,0:T(8,128)(2,1)S(1)}, bf16[2,64,640]{2,1,0:T(8,128)(2,1)S(1)}, u32[]{:S(2)}, u32[]{:S(2)}) collective-permute-start(bf16[2,64,640]{2,1,0:T(8,128)(2,1)S(1)} %get-tuple-element.25.this), channel_id=1, source_target_pairs={{0,4},{1,5},{2,6},{3,7},{4,0},{5,1},{6,2},{7,3},{8,12},{9,13},{10,... | collective-permute-start | bytes 491528 | tf_op jit(solution)/shard_map/ppermute | solution.py:27
  7.3 0.5 %collective-permute-start.2 = (bf16[64,640]{1,0:T(8,128)(2,1)S(1)}, bf16[64,640]{1,0:T(8,128)(2,1)S(1)}, u32[]{:S(2)}, u32[]{:S(2)}) collective-permute-start(bf16[64,640]{1,0:T(8,128)(2,1)S(1)} %get-tuple-element.22), channel_id=1, source_target_pairs={{0,2},{1,3},{2,0},{3,1},{4,6},{5,7},{6,4},{7,5},{8,10},{9,11},{10,... | collective-permute-start | bytes 245768 | tf_op jit(solution)/shard_map/ppermute | solution.py:27
  7.9 1.3 %fetch.1 = (bf16[3,128,640]{2,1,0:T(8,128)(2,1)S(1)}, f32[3,128,128]{2,1,0:T(8,128)S(1)}) custom-call(bf16[1,512,640]{2,1,0:T(8,128)(2,1)} %keys_copy.1, bf16[1,512,640]{2,1,0:T(8,128)(2,1)} %values_copy.1, f32[20,512]{1,0:T(8,128)S(1)} %bitcast.4, f32[20,512]{1,0:T(8,128)S(1)} %bitcast.5), custom_call_target="tpu_custom_call" | custom-call | bytes 1000 | tf_op jit(solution)/shard_map/fetch/pallas_call | solution.py:155
  9.2 2.7 %collective-permute-start.7 = (bf16[128,640]{1,0:T(8,128)(2,1)S(1)}, bf16[128,640]{1,0:T(8,128)(2,1)S(1)}, u32[]{:S(2)}, u32[]{:S(2)}) collective-permute-start(bf16[128,640]{1,0:T(8,128)(2,1)S(1)} %assemble.1._.refs_0_.query_ref), channel_id=1, source_target_pairs={{0,8},{1,9},{2,10},{3,11},{4,12},{5,13},{6,14},{7,15},{8,0},{9,1},... | collective-permute-start | bytes 491528 | tf_op jit(solution)/shard_map/ppermute | solution.py:27
  12.0 1.6 %collective-permute-start.4 = (bf16[128,640]{1,0:T(8,128)(2,1)S(1)}, bf16[128,640]{1,0:T(8,128)(2,1)S(1)}, u32[]{:S(2)}, u32[]{:S(2)}) collective-permute-start(bf16[128,640]{1,0:T(8,128)(2,1)S(1)} %rebuild.3.refs_0_.near_keys), channel_id=1, source_target_pairs={{0,4},{1,5},{2,6},{3,7},{4,0},{5,1},{6,2},{7,3},{8,12},{9,13},{10,... | collective-permute-start | bytes 491528 | tf_op jit(solution)/shard_map/ppermute | solution.py:27
  13.7 1.9 %collective-permute-start.3 = (bf16[64,640]{1,0:T(8,128)(2,1)S(1)}, bf16[64,640]{1,0:T(8,128)(2,1)S(1)}, u32[]{:S(2)}, u32[]{:S(2)}) collective-permute-start(bf16[64,640]{1,0:T(8,128)(2,1)S(1)} %get-tuple-element.26), channel_id=1, source_target_pairs={{0,2},{1,3},{2,0},{3,1},{4,6},{5,7},{6,4},{7,5},{8,10},{9,11},{10,... | collective-permute-start | bytes 245768 | tf_op jit(solution)/shard_map/ppermute | solution.py:27
  15.6 0.2 collective-permute-start.6
  15.8 2.3 %collective-permute-done.3.opposite = bf16[64,640]{1,0:T(8,128)(2,1)S(1)} collective-permute-done((bf16[64,640]{1,0:T(8,128)(2,1)S(1)}, bf16[64,640]{1,0:T(8,128)(2,1)S(1)}, u32[]{:S(2)}, u32[]{:S(2)}) %collective-permute-start.3) | collective-permute-done | bytes 81952 | tf_op jit(solution)/shard_map/ppermute | solution.py:27
  18.3 1.7 %collective-permute-done.6.opposite = bf16[64,640]{1,0:T(8,128)(2,1)S(1)} collective-permute-done((bf16[64,640]{1,0:T(8,128)(2,1)S(1)}, bf16[64,640]{1,0:T(8,128)(2,1)S(1)}, u32[]{:S(2)}, u32[]{:S(2)}) %collective-permute-start.6) | collective-permute-done | bytes 81952 | tf_op jit(solution)/shard_map/ppermute | solution.py:27
  20.3 0.6 %attend.2 = (bf16[2,176,128]{2,1,0:T(8,128)(2,1)S(1)}, bf16[1,176,128]{2,1,0:T(8,128)(2,1)S(1)}, bf16[1,176,128]{2,1,0:T(8,128)(2,1)S(1)}) custom-call(bf16[128,640]{1,0:T(8,128)(2,1)S(1)} %collective-permute-done.7.refs_0_.query_ref, bf16[128,640]{1,0:T(8,128)(2,1)S(1)} %rebuild.3.refs_0_.near_keys, bf16[128,640]{1,0:T(8,128)(2,1)S(1)} %rebuild.4.near_values, ...), custom_call_target="tpu_custom_call" | custom-call | bytes 1000 | tf_op jit(solution)/shard_map/attend/pallas_call | solution.py:259
  20.9 1.7 %collective-permute-start.10 = (bf16[2,176,128]{2,1,0:T(8,128)(2,1)S(1)}, bf16[2,176,128]{2,1,0:T(8,128)(2,1)S(1)}, u32[]{:S(2)}, u32[]{:S(2)}) collective-permute-start(bf16[2,176,128]{2,1,0:T(8,128)(2,1)S(1)} %get-tuple-element.31), channel_id=1, source_target_pairs={{0,10},{1,11},{2,8},{3,9},{4,14},{5,15},{6,12},{7,13},{8,2},{9,3},... | collective-permute-start | bytes 270344 | tf_op jit(solution)/shard_map/ppermute | solution.py:27
  22.5 0.6 %attend.3 = (bf16[1,176,128]{2,1,0:T(8,128)(2,1)S(1)}, bf16[1,176,128]{2,1,0:T(8,128)(2,1)S(1)}, bf16[2,176,128]{2,1,0:T(8,128)(2,1)S(1)}) custom-call(bf16[128,640]{1,0:T(8,128)(2,1)S(1)} %assemble.1._.refs_0_.query_ref, bf16[128,640]{1,0:T(8,128)(2,1)S(1)} %rebuild.3.refs_0_.near_keys, bf16[128,640]{1,0:T(8,128)(2,1)S(1)} %rebuild.4.near_values, ...), custom_call_target="tpu_custom_call" | custom-call | bytes 1000 | tf_op jit(solution)/shard_map/attend/pallas_call | solution.py:259
  23.1 1.0 %collective-permute-start.9 = (bf16[2,176,128]{2,1,0:T(8,128)(2,1)S(1)}, bf16[2,176,128]{2,1,0:T(8,128)(2,1)S(1)}, u32[]{:S(2)}, u32[]{:S(2)}) collective-permute-start(bf16[2,176,128]{2,1,0:T(8,128)(2,1)S(1)} %get-tuple-element.30), channel_id=1, source_target_pairs={{0,2},{1,3},{2,0},{3,1},{4,6},{5,7},{6,4},{7,5},{8,10},{9,11},{10,... | collective-permute-start | bytes 270344 | tf_op jit(solution)/shard_map/ppermute | solution.py:27
  24.1 2.0 %collective-permute-start.8 = (bf16[1,176,128]{2,1,0:T(8,128)(2,1)S(1)}, bf16[1,176,128]{2,1,0:T(8,128)(2,1)S(1)}, u32[]{:S(2)}, u32[]{:S(2)}) collective-permute-start(bf16[1,176,128]{2,1,0:T(8,128)(2,1)S(1)} %get-tuple-element.29), channel_id=1, source_target_pairs={{0,1},{1,0},{2,3},{3,2},{4,5},{5,4},{6,7},{7,6},{8,9},{9,8},{10,11... | collective-permute-start | bytes 135176 | tf_op jit(solution)/shard_map/ppermute | solution.py:27
  26.1 1.1 %collective-permute-start.12 = (bf16[1,176,128]{2,1,0:T(8,128)(2,1)S(1)}, bf16[1,176,128]{2,1,0:T(8,128)(2,1)S(1)}, u32[]{:S(2)}, u32[]{:S(2)}) collective-permute-start(bf16[1,176,128]{2,1,0:T(8,128)(2,1)S(1)} %get-tuple-element.32), channel_id=1, source_target_pairs={{0,8},{1,9},{2,10},{3,11},{4,12},{5,13},{6,14},{7,15},{8,0},{9,1},... | collective-permute-start | bytes 135176 | tf_op jit(solution)/shard_map/ppermute | solution.py:27
  27.1 1.1 %collective-permute-done.10.both.f2 = bf16[2,176,128]{2,1,0:T(8,128)(2,1)S(1)} collective-permute-done((bf16[2,176,128]{2,1,0:T(8,128)(2,1)S(1)}, bf16[2,176,128]{2,1,0:T(8,128)(2,1)S(1)}, u32[]{:S(2)}, u32[]{:S(2)}) %collective-permute-start.10) | collective-permute-done | bytes 90144 | tf_op jit(solution)/shard_map/ppermute | solution.py:27
  28.3 0.4 %collective-permute-done.9.both.n2 = bf16[2,176,128]{2,1,0:T(8,128)(2,1)S(1)} collective-permute-done((bf16[2,176,128]{2,1,0:T(8,128)(2,1)S(1)}, bf16[2,176,128]{2,1,0:T(8,128)(2,1)S(1)}, u32[]{:S(2)}, u32[]{:S(2)}) %collective-permute-start.9) | collective-permute-done | bytes 90144 | tf_op jit(solution)/shard_map/ppermute | solution.py:27
  28.7 0.5 %collective-permute-start.14 = (bf16[176,128]{1,0:T(8,128)(2,1)S(1)}, bf16[176,128]{1,0:T(8,128)(2,1)S(1)}, u32[]{:S(2)}, u32[]{:S(2)}) collective-permute-start(bf16[176,128]{1,0:T(8,128)(2,1)S(1)} %pick.4.refs_0_), channel_id=1, source_target_pairs={{0,1},{1,0},{2,3},{3,2},{4,5},{5,4},{6,7},{7,6},{8,9},{9,8},{10,11... | collective-permute-start | bytes 135176 | tf_op jit(solution)/shard_map/ppermute | solution.py:27
  29.2 2.7 %collective-permute-done.12.f0 = bf16[1,176,128]{2,1,0:T(8,128)(2,1)S(1)} collective-permute-done((bf16[1,176,128]{2,1,0:T(8,128)(2,1)S(1)}, bf16[1,176,128]{2,1,0:T(8,128)(2,1)S(1)}, u32[]{:S(2)}, u32[]{:S(2)}) %collective-permute-start.12) | collective-permute-done | bytes 45088 | tf_op jit(solution)/shard_map/ppermute | solution.py:27
  31.9 1.2 %merge.1 = bf16[32,2560]{1,0:T(8,128)(2,1)} custom-call(bf16[1,176,128]{2,1,0:T(8,128)(2,1)S(1)} %get-tuple-element.28.n0, bf16[1,176,128]{2,1,0:T(8,128)(2,1)S(1)} %collective-permute-done.8.n1, bf16[2,176,128]{2,1,0:T(8,128)(2,1)S(1)} %collective-permute-done.9.both.n2, bf16[1,176,128]{2,1,0:T(8,128)(2,1)S(1)} %bitcast.6, ...), custom_call_target="tpu_custom_call" | custom-call | bytes 1000 | tf_op jit(solution)/shard_map/merge/pallas_call | solution.py:301
  (23 shorter events, 0.7 us)
Async XLA Ops:
  1.1 1.7 %collective-permute-start = (bf16[3,2,32,640]{3,2,1,0:T(8,128)(2,1)S(1)}, bf16[3,2,32,640]{3,2,1,0:T(8,128)(2,1)S(1)}, u32[]{:S(2)}, u32[]{:S(2)}) collective-permute-start(bf16[3,2,32,640]{3,2,1,0:T(8,128)(2,1)S(1)} %get-tuple-element.20), channel_id=1, source_target_pairs={{0,1},{1,0},{2,3},{3,2},{4,5},{5,4},{6,7},{7,6},{8,9},{9,8},{10,11... | collective-permute-start | bytes 737288 | tf_op jit(solution)/shard_map/ppermute | solution.py:27
  2.8 5.1 %copy-start = (f32[512,20]{0,1:T(8,128)S(1)}, f32[512,20]{0,1:T(8,128)}, u32[]{:S(2)}) copy-start(f32[512,20]{0,1:T(8,128)} %param.12) | copy-start | bytes 122884
  2.8 5.1 %copy-start.1 = (f32[512,20]{0,1:T(8,128)S(1)}, f32[512,20]{0,1:T(8,128)}, u32[]{:S(2)}) copy-start(f32[512,20]{0,1:T(8,128)} %param.13) | copy-start | bytes 122884
  2.8 6.3 %collective-permute-start.1 = (bf16[64,640]{1,0:T(8,128)(2,1)S(1)}, bf16[64,640]{1,0:T(8,128)(2,1)S(1)}, u32[]{:S(2)}, u32[]{:S(2)}) collective-permute-start(bf16[64,640]{1,0:T(8,128)(2,1)S(1)} %get-tuple-element.21), channel_id=1, source_target_pairs={{0,2},{1,3},{2,0},{3,1},{4,6},{5,7},{6,4},{7,5},{8,10},{9,11},{10,... | collective-permute-start | bytes 245768 | tf_op jit(solution)/shard_map/ppermute | solution.py:27
  5.7 9.8 %collective-permute-start.5 = (bf16[2,64,640]{2,1,0:T(8,128)(2,1)S(1)}, bf16[2,64,640]{2,1,0:T(8,128)(2,1)S(1)}, u32[]{:S(2)}, u32[]{:S(2)}) collective-permute-start(bf16[2,64,640]{2,1,0:T(8,128)(2,1)S(1)} %get-tuple-element.25.this), channel_id=1, source_target_pairs={{0,4},{1,5},{2,6},{3,7},{4,0},{5,1},{6,2},{7,3},{8,12},{9,13},{10,... | collective-permute-start | bytes 491528 | tf_op jit(solution)/shard_map/ppermute | solution.py:27
  7.3 4.5 %collective-permute-start.2 = (bf16[64,640]{1,0:T(8,128)(2,1)S(1)}, bf16[64,640]{1,0:T(8,128)(2,1)S(1)}, u32[]{:S(2)}, u32[]{:S(2)}) collective-permute-start(bf16[64,640]{1,0:T(8,128)(2,1)S(1)} %get-tuple-element.22), channel_id=1, source_target_pairs={{0,2},{1,3},{2,0},{3,1},{4,6},{5,7},{6,4},{7,5},{8,10},{9,11},{10,... | collective-permute-start | bytes 245768 | tf_op jit(solution)/shard_map/ppermute | solution.py:27
  9.2 10.9 %collective-permute-start.7 = (bf16[128,640]{1,0:T(8,128)(2,1)S(1)}, bf16[128,640]{1,0:T(8,128)(2,1)S(1)}, u32[]{:S(2)}, u32[]{:S(2)}) collective-permute-start(bf16[128,640]{1,0:T(8,128)(2,1)S(1)} %assemble.1._.refs_0_.query_ref), channel_id=1, source_target_pairs={{0,8},{1,9},{2,10},{3,11},{4,12},{5,13},{6,14},{7,15},{8,0},{9,1},... | collective-permute-start | bytes 491528 | tf_op jit(solution)/shard_map/ppermute | solution.py:27
  12.0 8.2 %collective-permute-start.4 = (bf16[128,640]{1,0:T(8,128)(2,1)S(1)}, bf16[128,640]{1,0:T(8,128)(2,1)S(1)}, u32[]{:S(2)}, u32[]{:S(2)}) collective-permute-start(bf16[128,640]{1,0:T(8,128)(2,1)S(1)} %rebuild.3.refs_0_.near_keys), channel_id=1, source_target_pairs={{0,4},{1,5},{2,6},{3,7},{4,0},{5,1},{6,2},{7,3},{8,12},{9,13},{10,... | collective-permute-start | bytes 491528 | tf_op jit(solution)/shard_map/ppermute | solution.py:27
  13.7 4.4 %collective-permute-start.3 = (bf16[64,640]{1,0:T(8,128)(2,1)S(1)}, bf16[64,640]{1,0:T(8,128)(2,1)S(1)}, u32[]{:S(2)}, u32[]{:S(2)}) collective-permute-start(bf16[64,640]{1,0:T(8,128)(2,1)S(1)} %get-tuple-element.26), channel_id=1, source_target_pairs={{0,2},{1,3},{2,0},{3,1},{4,6},{5,7},{6,4},{7,5},{8,10},{9,11},{10,... | collective-permute-start | bytes 245768 | tf_op jit(solution)/shard_map/ppermute | solution.py:27
  15.6 4.5 %collective-permute-start.6 = (bf16[64,640]{1,0:T(8,128)(2,1)S(1)}, bf16[64,640]{1,0:T(8,128)(2,1)S(1)}, u32[]{:S(2)}, u32[]{:S(2)}) collective-permute-start(bf16[64,640]{1,0:T(8,128)(2,1)S(1)} %pick.3), channel_id=1, source_target_pairs={{0,2},{1,3},{2,0},{3,1},{4,6},{5,7},{6,4},{7,5},{8,10},{9,11},{10,... | collective-permute-start | bytes 245768 | tf_op jit(solution)/shard_map/ppermute | solution.py:27
  20.9 7.4 %collective-permute-start.10 = (bf16[2,176,128]{2,1,0:T(8,128)(2,1)S(1)}, bf16[2,176,128]{2,1,0:T(8,128)(2,1)S(1)}, u32[]{:S(2)}, u32[]{:S(2)}) collective-permute-start(bf16[2,176,128]{2,1,0:T(8,128)(2,1)S(1)} %get-tuple-element.31), channel_id=1, source_target_pairs={{0,10},{1,11},{2,8},{3,9},{4,14},{5,15},{6,12},{7,13},{8,2},{9,3},... | collective-permute-start | bytes 270344 | tf_op jit(solution)/shard_map/ppermute | solution.py:27
  23.1 5.5 %collective-permute-start.9 = (bf16[2,176,128]{2,1,0:T(8,128)(2,1)S(1)}, bf16[2,176,128]{2,1,0:T(8,128)(2,1)S(1)}, u32[]{:S(2)}, u32[]{:S(2)}) collective-permute-start(bf16[2,176,128]{2,1,0:T(8,128)(2,1)S(1)} %get-tuple-element.30), channel_id=1, source_target_pairs={{0,2},{1,3},{2,0},{3,1},{4,6},{5,7},{6,4},{7,5},{8,10},{9,11},{10,... | collective-permute-start | bytes 270344 | tf_op jit(solution)/shard_map/ppermute | solution.py:27
  24.1 7.7 %collective-permute-start.13 = (bf16[1,176,128]{2,1,0:T(8,128)(2,1)S(1)}, bf16[1,176,128]{2,1,0:T(8,128)(2,1)S(1)}, u32[]{:S(2)}, u32[]{:S(2)}) collective-permute-start(bf16[1,176,128]{2,1,0:T(8,128)(2,1)S(1)} %get-tuple-element.27.refs_0_), channel_id=1, source_target_pairs={{0,9},{1,8},{2,11},{3,10},{4,13},{5,12},{6,15},{7,14},{8,1},{9,0},... | collective-permute-start | bytes 135176 | tf_op jit(solution)/shard_map/ppermute | solution.py:27
  24.1 5.1 %collective-permute-start.8 = (bf16[1,176,128]{2,1,0:T(8,128)(2,1)S(1)}, bf16[1,176,128]{2,1,0:T(8,128)(2,1)S(1)}, u32[]{:S(2)}, u32[]{:S(2)}) collective-permute-start(bf16[1,176,128]{2,1,0:T(8,128)(2,1)S(1)} %get-tuple-element.29), channel_id=1, source_target_pairs={{0,1},{1,0},{2,3},{3,2},{4,5},{5,4},{6,7},{7,6},{8,9},{9,8},{10,11... | collective-permute-start | bytes 135176 | tf_op jit(solution)/shard_map/ppermute | solution.py:27
  26.1 5.8 %collective-permute-start.12 = (bf16[1,176,128]{2,1,0:T(8,128)(2,1)S(1)}, bf16[1,176,128]{2,1,0:T(8,128)(2,1)S(1)}, u32[]{:S(2)}, u32[]{:S(2)}) collective-permute-start(bf16[1,176,128]{2,1,0:T(8,128)(2,1)S(1)} %get-tuple-element.32), channel_id=1, source_target_pairs={{0,8},{1,9},{2,10},{3,11},{4,12},{5,13},{6,14},{7,15},{8,0},{9,1},... | collective-permute-start | bytes 135176 | tf_op jit(solution)/shard_map/ppermute | solution.py:27
  28.6 3.2 %collective-permute-start.11 = (bf16[176,128]{1,0:T(8,128)(2,1)S(1)}, bf16[176,128]{1,0:T(8,128)(2,1)S(1)}, u32[]{:S(2)}, u32[]{:S(2)}) collective-permute-start(bf16[176,128]{1,0:T(8,128)(2,1)S(1)} %pick.5), channel_id=1, source_target_pairs={{0,1},{1,0},{2,3},{3,2},{4,5},{5,4},{6,7},{7,6},{8,9},{9,8},{10,11... | collective-permute-start | bytes 135176 | tf_op jit(solution)/shard_map/ppermute | solution.py:27
  28.7 3.2 %collective-permute-start.14 = (bf16[176,128]{1,0:T(8,128)(2,1)S(1)}, bf16[176,128]{1,0:T(8,128)(2,1)S(1)}, u32[]{:S(2)}, u32[]{:S(2)}) collective-permute-start(bf16[176,128]{1,0:T(8,128)(2,1)S(1)} %pick.4.refs_0_), channel_id=1, source_target_pairs={{0,1},{1,0},{2,3},{3,2},{4,5},{5,4},{6,7},{7,6},{8,9},{9,8},{10,11... | collective-permute-start | bytes 135176 | tf_op jit(solution)/shard_map/ppermute | solution.py:27

commit v8 on v7

--- a/solution.py
+++ b/solution.py
@@ -223,23 +223,31 @@
     lane = lax.broadcasted_iota(jnp.int32, (GROUP * rows, head), 1)
     stats = jnp.zeros((GROUP * rows, head), jnp.float32)
     contract = (((1,), (1,)), ((), ()))
+    def stacked(near, far, h):
+        lanes = slice(h * head, (h + 1) * head)
+        return jnp.concatenate([near[:, lanes], far[:, lanes]], axis=0)
+
+    scores = []
     for h in range(heads):
-        lanes = slice(h * head, (h + 1) * head)
-        query = query_ref[:, lanes]
-        keys = jnp.concatenate([near_keys[:, lanes], far_keys[:, lanes]], axis=0)
-        values = jnp.concatenate([near_values[:, lanes], far_values[:, lanes]], axis=0)
-        score = lax.dot_general(query, keys, contract, preferred_element_type=jnp.float32)
-        peak = jnp.max(score, axis=1, keepdims=True)
-        level = (peak * scale).astype(jnp.bfloat16).astype(jnp.float32)
-        probs = jnp.exp2(score * scale - level).astype(jnp.bfloat16)
+        query = query_ref[:, h * head : (h + 1) * head]
+        keys = stacked(near_keys, far_keys, h)
+        scores.append(lax.dot_general(query, keys, contract, preferred_element_type=jnp.float32))
+    peaks = [jnp.max(score, axis=1, keepdims=True) for score in scores]
+    levels = [(peak * scale).astype(jnp.bfloat16).astype(jnp.float32) for peak in peaks]
+    probs = [jnp.exp2(score * scale - level).astype(jnp.bfloat16) for score, level in zip(scores, levels)]
+    totals = []
+    for h in range(heads):
+        values = stacked(near_values, far_values, h)
         joined = jnp.concatenate([values, jnp.ones_like(values)], axis=1)
-        total = jnp.dot(probs, joined, preferred_element_type=jnp.float32)
-        weighted = total[:, :head].astype(jnp.bfloat16)
-        weight = total[:, head:]
+        totals.append(jnp.dot(probs[h], joined, preferred_element_type=jnp.float32))
+    for h in range(heads):
+        weight = totals[h][:, head:]
         high = weight.astype(jnp.bfloat16).astype(jnp.float32)
-        stats = jnp.where(lane == h, level, stats)
+        stats = jnp.where(lane == h, levels[h], stats)
         stats = jnp.where(lane == heads + h, high, stats)
         stats = jnp.where(lane == 2 * heads + h, weight - high, stats)
+    for h in range(heads):
+        weighted = totals[h][:, :head].astype(jnp.bfloat16)
         for k, out in sorted(outs.items()):
             out[h * rows : (h + 1) * rows, :] = weighted[k * rows : (k + 1) * rows]
     half = rows // 2
@@ -279,6 +287,7 @@
         weight = pltpu.roll(stats, head - heads, 1) + pltpu.roll(stats, head - 2 * heads, 1)
         return stats, weight
 
+    mixtures = []
     for k, (near, far) in enumerate(((n0, f0), (n1, f1), (n2, f2), (n3, f3))):
         near_level, near_weight = unpack(near)
         far_level, far_weight = unpack(far)
@@ -292,8 +301,10 @@
             place = slice(h * rows, (h + 1) * rows)
             mixed = near[0, place, :].astype(jnp.float32) * near_scale[:, h : h + 1]
             mixed = mixed + far[0, place, :].astype(jnp.float32) * far_scale[:, h : h + 1]
-            start = pl.multiple_of((member ^ k) * width + h * head, head)
-            out[:, pl.ds(start, head)] = mixed.astype(out.dtype)
+            mixtures.append((k, h, mixed.astype(out.dtype)))
+    for k, h, mixed in mixtures:
+        start = pl.multiple_of((member ^ k) * width + h * head, head)
+        out[:, pl.ds(start, head)] = mixed
 
 
 def merge(heads, near, far, rows):

time: 33.3 us -> 33.3 us (level)
  transfers between devices with their start and end apart: 15 -> 15, of which waited for: 6 -> 6; matrix products, arithmetic and copies ran while one was open for 0% -> 0% of each run, Pallas kernels for 8% -> 7%
where the time goes in v8:
time: 33.3 us; the launch traced here: 33 us
  starting transfers between devices  18.1 us (54%)
  waiting for transfers between devices  9.41 us (28%)
  Pallas kernels  5.4 us (16%)
    ppermute x15, starting transfers between devices, swapped(): return lax.ppermute(array, 'patch', [(i, i ^ mask) for i in range(size)])  18.1 us
    ppermute x15, waiting for transfers between devices, swapped(): return lax.ppermute(array, 'patch', [(i, i ^ mask) for i in range(size)])  9.41 us
    pallas_call x1, Pallas kernels, fetch(): pl.pallas_call(functools.partial(fetch_kernel, heads, count), out_shape=[...  1.29 us
    pallas_call x1, Pallas kernels, merge(): pl.pallas_call(functools.partial(merge_kernel, heads), out_shape=jax.Shap...  1.22 us
    pallas_call x2, Pallas kernels, attend(): pl.pallas_call(functools.partial(attend_kernel, heads, parts), out_shape=...  1.15 us
    pallas_call x1, Pallas kernels, cut(): pl.pallas_call(functools.partial(cut_kernel, len(slabs)), out_shape=[shap...  1.11 us
  transfers between devices with their start and end apart: 15, of which 6 were waited for; matrix products, arithmetic and copies ran while one was open for 0% of the time, Pallas kernels for 7%

profile of v8, /device:TPU:0, one launch (start us, length us, event | category | flops | bytes accessed | tf_op | source)
XLA Modules:
  0.0 33.0 jit_solution(17635409543722110211)
XLA Ops:
  0.0 1.1 %cut.1 = (bf16[3,2,32,640]{3,2,1,0:T(8,128)(2,1)S(1)}, bf16[3,2,32,640]{3,2,1,0:T(8,128)(2,1)S(1)}) custom-call(bf16[32,2560]{1,0:T(8,128)(2,1)} %refs_0_.1, bf16[32,2560]{1,0:T(8,128)(2,1)} %refs_1_.1, bf16[32,2560]{1,0:T(8,128)(2,1)} %refs_2_.1), custom_call_target="tpu_custom_call" | custom-call | bytes 1000 | tf_op jit(solution)/shard_map/cut/pallas_call | solution.py:62
  1.1 0.5 %collective-permute-start = (bf16[3,2,32,640]{3,2,1,0:T(8,128)(2,1)S(1)}, bf16[3,2,32,640]{3,2,1,0:T(8,128)(2,1)S(1)}, u32[]{:S(2)}, u32[]{:S(2)}) collective-permute-start(bf16[3,2,32,640]{3,2,1,0:T(8,128)(2,1)S(1)} %get-tuple-element.20), channel_id=1, source_target_pairs={{0,1},{1,0},{2,3},{3,2},{4,5},{5,4},{6,7},{7,6},{8,9},{9,8},{10,11... | collective-permute-start | bytes 737288 | tf_op jit(solution)/shard_map/ppermute | solution.py:27
  1.6 1.1 %collective-permute-done.arrived.beside = bf16[3,2,32,640]{3,2,1,0:T(8,128)(2,1)S(1)} collective-permute-done((bf16[3,2,32,640]{3,2,1,0:T(8,128)(2,1)S(1)}, bf16[3,2,32,640]{3,2,1,0:T(8,128)(2,1)S(1)}, u32[]{:S(2)}, u32[]{:S(2)}) %collective-permute-start) | collective-permute-done | bytes 245792 | tf_op jit(solution)/shard_map/ppermute | solution.py:27
  2.8 2.9 %collective-permute-start.1 = (bf16[64,640]{1,0:T(8,128)(2,1)S(1)}, bf16[64,640]{1,0:T(8,128)(2,1)S(1)}, u32[]{:S(2)}, u32[]{:S(2)}) collective-permute-start(bf16[64,640]{1,0:T(8,128)(2,1)S(1)} %get-tuple-element.21), channel_id=1, source_target_pairs={{0,2},{1,3},{2,0},{3,1},{4,6},{5,7},{6,4},{7,5},{8,10},{9,11},{10,... | collective-permute-start | bytes 245768 | tf_op jit(solution)/shard_map/ppermute | solution.py:27
  5.7 1.6 %collective-permute-start.5 = (bf16[2,64,640]{2,1,0:T(8,128)(2,1)S(1)}, bf16[2,64,640]{2,1,0:T(8,128)(2,1)S(1)}, u32[]{:S(2)}, u32[]{:S(2)}) collective-permute-start(bf16[2,64,640]{2,1,0:T(8,128)(2,1)S(1)} %get-tuple-element.25.this), channel_id=1, source_target_pairs={{0,4},{1,5},{2,6},{3,7},{4,0},{5,1},{6,2},{7,3},{8,12},{9,13},{10,... | collective-permute-start | bytes 491528 | tf_op jit(solution)/shard_map/ppermute | solution.py:27
  7.3 0.5 %collective-permute-start.2 = (bf16[64,640]{1,0:T(8,128)(2,1)S(1)}, bf16[64,640]{1,0:T(8,128)(2,1)S(1)}, u32[]{:S(2)}, u32[]{:S(2)}) collective-permute-start(bf16[64,640]{1,0:T(8,128)(2,1)S(1)} %get-tuple-element.22), channel_id=1, source_target_pairs={{0,2},{1,3},{2,0},{3,1},{4,6},{5,7},{6,4},{7,5},{8,10},{9,11},{10,... | collective-permute-start | bytes 245768 | tf_op jit(solution)/shard_map/ppermute | solution.py:27
  7.9 1.3 %fetch.1 = (bf16[3,128,640]{2,1,0:T(8,128)(2,1)S(1)}, f32[3,128,128]{2,1,0:T(8,128)S(1)}) custom-call(bf16[1,512,640]{2,1,0:T(8,128)(2,1)} %keys_copy.1, bf16[1,512,640]{2,1,0:T(8,128)(2,1)} %values_copy.1, f32[20,512]{1,0:T(8,128)S(1)} %bitcast.4, f32[20,512]{1,0:T(8,128)S(1)} %bitcast.5), custom_call_target="tpu_custom_call" | custom-call | bytes 1000 | tf_op jit(solution)/shard_map/fetch/pallas_call | solution.py:155
  9.2 2.7 %collective-permute-start.7 = (bf16[128,640]{1,0:T(8,128)(2,1)S(1)}, bf16[128,640]{1,0:T(8,128)(2,1)S(1)}, u32[]{:S(2)}, u32[]{:S(2)}) collective-permute-start(bf16[128,640]{1,0:T(8,128)(2,1)S(1)} %assemble.1._.refs_0_.query_ref), channel_id=1, source_target_pairs={{0,8},{1,9},{2,10},{3,11},{4,12},{5,13},{6,14},{7,15},{8,0},{9,1},... | collective-permute-start | bytes 491528 | tf_op jit(solution)/shard_map/ppermute | solution.py:27
  12.0 1.6 %collective-permute-start.4 = (bf16[128,640]{1,0:T(8,128)(2,1)S(1)}, bf16[128,640]{1,0:T(8,128)(2,1)S(1)}, u32[]{:S(2)}, u32[]{:S(2)}) collective-permute-start(bf16[128,640]{1,0:T(8,128)(2,1)S(1)} %rebuild.3.refs_0_.near_keys), channel_id=1, source_target_pairs={{0,4},{1,5},{2,6},{3,7},{4,0},{5,1},{6,2},{7,3},{8,12},{9,13},{10,... | collective-permute-start | bytes 491528 | tf_op jit(solution)/shard_map/ppermute | solution.py:27
  13.7 1.9 %collective-permute-start.3 = (bf16[64,640]{1,0:T(8,128)(2,1)S(1)}, bf16[64,640]{1,0:T(8,128)(2,1)S(1)}, u32[]{:S(2)}, u32[]{:S(2)}) collective-permute-start(bf16[64,640]{1,0:T(8,128)(2,1)S(1)} %get-tuple-element.26), channel_id=1, source_target_pairs={{0,2},{1,3},{2,0},{3,1},{4,6},{5,7},{6,4},{7,5},{8,10},{9,11},{10,... | collective-permute-start | bytes 245768 | tf_op jit(solution)/shard_map/ppermute | solution.py:27
  15.6 0.2 collective-permute-start.6
  15.8 2.3 %collective-permute-done.3.opposite = bf16[64,640]{1,0:T(8,128)(2,1)S(1)} collective-permute-done((bf16[64,640]{1,0:T(8,128)(2,1)S(1)}, bf16[64,640]{1,0:T(8,128)(2,1)S(1)}, u32[]{:S(2)}, u32[]{:S(2)}) %collective-permute-start.3) | collective-permute-done | bytes 81952 | tf_op jit(solution)/shard_map/ppermute | solution.py:27
  18.3 1.7 %collective-permute-done.6.opposite = bf16[64,640]{1,0:T(8,128)(2,1)S(1)} collective-permute-done((bf16[64,640]{1,0:T(8,128)(2,1)S(1)}, bf16[64,640]{1,0:T(8,128)(2,1)S(1)}, u32[]{:S(2)}, u32[]{:S(2)}) %collective-permute-start.6) | collective-permute-done | bytes 81952 | tf_op jit(solution)/shard_map/ppermute | solution.py:27
  20.3 0.6 %attend.2 = (bf16[2,176,128]{2,1,0:T(8,128)(2,1)S(1)}, bf16[1,176,128]{2,1,0:T(8,128)(2,1)S(1)}, bf16[1,176,128]{2,1,0:T(8,128)(2,1)S(1)}) custom-call(bf16[128,640]{1,0:T(8,128)(2,1)S(1)} %collective-permute-done.7.refs_0_.query_ref, bf16[128,640]{1,0:T(8,128)(2,1)S(1)} %rebuild.3.refs_0_.near_keys, bf16[128,640]{1,0:T(8,128)(2,1)S(1)} %rebuild.4.near_values, ...), custom_call_target="tpu_custom_call" | custom-call | bytes 1000 | tf_op jit(solution)/shard_map/attend/pallas_call | solution.py:267
  20.8 1.7 %collective-permute-start.10 = (bf16[2,176,128]{2,1,0:T(8,128)(2,1)S(1)}, bf16[2,176,128]{2,1,0:T(8,128)(2,1)S(1)}, u32[]{:S(2)}, u32[]{:S(2)}) collective-permute-start(bf16[2,176,128]{2,1,0:T(8,128)(2,1)S(1)} %get-tuple-element.31), channel_id=1, source_target_pairs={{0,10},{1,11},{2,8},{3,9},{4,14},{5,15},{6,12},{7,13},{8,2},{9,3},... | collective-permute-start | bytes 270344 | tf_op jit(solution)/shard_map/ppermute | solution.py:27
  22.5 0.6 %attend.3 = (bf16[1,176,128]{2,1,0:T(8,128)(2,1)S(1)}, bf16[1,176,128]{2,1,0:T(8,128)(2,1)S(1)}, bf16[2,176,128]{2,1,0:T(8,128)(2,1)S(1)}) custom-call(bf16[128,640]{1,0:T(8,128)(2,1)S(1)} %assemble.1._.refs_0_.query_ref, bf16[128,640]{1,0:T(8,128)(2,1)S(1)} %rebuild.3.refs_0_.near_keys, bf16[128,640]{1,0:T(8,128)(2,1)S(1)} %rebuild.4.near_values, ...), custom_call_target="tpu_custom_call" | custom-call | bytes 1000 | tf_op jit(solution)/shard_map/attend/pallas_call | solution.py:267
  23.1 0.9 %collective-permute-start.9 = (bf16[2,176,128]{2,1,0:T(8,128)(2,1)S(1)}, bf16[2,176,128]{2,1,0:T(8,128)(2,1)S(1)}, u32[]{:S(2)}, u32[]{:S(2)}) collective-permute-start(bf16[2,176,128]{2,1,0:T(8,128)(2,1)S(1)} %get-tuple-element.30), channel_id=1, source_target_pairs={{0,2},{1,3},{2,0},{3,1},{4,6},{5,7},{6,4},{7,5},{8,10},{9,11},{10,... | collective-permute-start | bytes 270344 | tf_op jit(solution)/shard_map/ppermute | solution.py:27
  24.0 2.0 %collective-permute-start.8 = (bf16[1,176,128]{2,1,0:T(8,128)(2,1)S(1)}, bf16[1,176,128]{2,1,0:T(8,128)(2,1)S(1)}, u32[]{:S(2)}, u32[]{:S(2)}) collective-permute-start(bf16[1,176,128]{2,1,0:T(8,128)(2,1)S(1)} %get-tuple-element.29), channel_id=1, source_target_pairs={{0,1},{1,0},{2,3},{3,2},{4,5},{5,4},{6,7},{7,6},{8,9},{9,8},{10,11... | collective-permute-start | bytes 135176 | tf_op jit(solution)/shard_map/ppermute | solution.py:27
  26.0 1.1 %collective-permute-start.12 = (bf16[1,176,128]{2,1,0:T(8,128)(2,1)S(1)}, bf16[1,176,128]{2,1,0:T(8,128)(2,1)S(1)}, u32[]{:S(2)}, u32[]{:S(2)}) collective-permute-start(bf16[1,176,128]{2,1,0:T(8,128)(2,1)S(1)} %get-tuple-element.32), channel_id=1, source_target_pairs={{0,8},{1,9},{2,10},{3,11},{4,12},{5,13},{6,14},{7,15},{8,0},{9,1},... | collective-permute-start | bytes 135176 | tf_op jit(solution)/shard_map/ppermute | solution.py:27
  27.1 1.2 %collective-permute-done.10.both.f2 = bf16[2,176,128]{2,1,0:T(8,128)(2,1)S(1)} collective-permute-done((bf16[2,176,128]{2,1,0:T(8,128)(2,1)S(1)}, bf16[2,176,128]{2,1,0:T(8,128)(2,1)S(1)}, u32[]{:S(2)}, u32[]{:S(2)}) %collective-permute-start.10) | collective-permute-done | bytes 90144 | tf_op jit(solution)/shard_map/ppermute | solution.py:27
  28.2 0.3 %collective-permute-done.9.both.n2 = bf16[2,176,128]{2,1,0:T(8,128)(2,1)S(1)} collective-permute-done((bf16[2,176,128]{2,1,0:T(8,128)(2,1)S(1)}, bf16[2,176,128]{2,1,0:T(8,128)(2,1)S(1)}, u32[]{:S(2)}, u32[]{:S(2)}) %collective-permute-start.9) | collective-permute-done | bytes 90144 | tf_op jit(solution)/shard_map/ppermute | solution.py:27
  28.6 0.5 %collective-permute-start.14 = (bf16[176,128]{1,0:T(8,128)(2,1)S(1)}, bf16[176,128]{1,0:T(8,128)(2,1)S(1)}, u32[]{:S(2)}, u32[]{:S(2)}) collective-permute-start(bf16[176,128]{1,0:T(8,128)(2,1)S(1)} %pick.4.refs_0_), channel_id=1, source_target_pairs={{0,1},{1,0},{2,3},{3,2},{4,5},{5,4},{6,7},{7,6},{8,9},{9,8},{10,11... | collective-permute-start | bytes 135176 | tf_op jit(solution)/shard_map/ppermute | solution.py:27
  29.1 2.7 %collective-permute-done.12.f0 = bf16[1,176,128]{2,1,0:T(8,128)(2,1)S(1)} collective-permute-done((bf16[1,176,128]{2,1,0:T(8,128)(2,1)S(1)}, bf16[1,176,128]{2,1,0:T(8,128)(2,1)S(1)}, u32[]{:S(2)}, u32[]{:S(2)}) %collective-permute-start.12) | collective-permute-done | bytes 45088 | tf_op jit(solution)/shard_map/ppermute | solution.py:27
  31.8 1.2 %merge.1 = bf16[32,2560]{1,0:T(8,128)(2,1)} custom-call(bf16[1,176,128]{2,1,0:T(8,128)(2,1)S(1)} %get-tuple-element.28.n0, bf16[1,176,128]{2,1,0:T(8,128)(2,1)S(1)} %collective-permute-done.8.n1, bf16[2,176,128]{2,1,0:T(8,128)(2,1)S(1)} %collective-permute-done.9.both.n2, bf16[1,176,128]{2,1,0:T(8,128)(2,1)S(1)} %bitcast.6, ...), custom_call_target="tpu_custom_call" | custom-call | bytes 1000 | tf_op jit(solution)/shard_map/merge/pallas_call | solution.py:312
  (23 shorter events, 0.7 us)
Async XLA Ops:
  1.1 1.7 %collective-permute-start = (bf16[3,2,32,640]{3,2,1,0:T(8,128)(2,1)S(1)}, bf16[3,2,32,640]{3,2,1,0:T(8,128)(2,1)S(1)}, u32[]{:S(2)}, u32[]{:S(2)}) collective-permute-start(bf16[3,2,32,640]{3,2,1,0:T(8,128)(2,1)S(1)} %get-tuple-element.20), channel_id=1, source_target_pairs={{0,1},{1,0},{2,3},{3,2},{4,5},{5,4},{6,7},{7,6},{8,9},{9,8},{10,11... | collective-permute-start | bytes 737288 | tf_op jit(solution)/shard_map/ppermute | solution.py:27
  2.8 5.1 %copy-start = (f32[512,20]{0,1:T(8,128)S(1)}, f32[512,20]{0,1:T(8,128)}, u32[]{:S(2)}) copy-start(f32[512,20]{0,1:T(8,128)} %param.12) | copy-start | bytes 122884
  2.8 5.1 %copy-start.1 = (f32[512,20]{0,1:T(8,128)S(1)}, f32[512,20]{0,1:T(8,128)}, u32[]{:S(2)}) copy-start(f32[512,20]{0,1:T(8,128)} %param.13) | copy-start | bytes 122884
  2.8 6.3 %collective-permute-start.1 = (bf16[64,640]{1,0:T(8,128)(2,1)S(1)}, bf16[64,640]{1,0:T(8,128)(2,1)S(1)}, u32[]{:S(2)}, u32[]{:S(2)}) collective-permute-start(bf16[64,640]{1,0:T(8,128)(2,1)S(1)} %get-tuple-element.21), channel_id=1, source_target_pairs={{0,2},{1,3},{2,0},{3,1},{4,6},{5,7},{6,4},{7,5},{8,10},{9,11},{10,... | collective-permute-start | bytes 245768 | tf_op jit(solution)/shard_map/ppermute | solution.py:27
  5.7 9.8 %collective-permute-start.5 = (bf16[2,64,640]{2,1,0:T(8,128)(2,1)S(1)}, bf16[2,64,640]{2,1,0:T(8,128)(2,1)S(1)}, u32[]{:S(2)}, u32[]{:S(2)}) collective-permute-start(bf16[2,64,640]{2,1,0:T(8,128)(2,1)S(1)} %get-tuple-element.25.this), channel_id=1, source_target_pairs={{0,4},{1,5},{2,6},{3,7},{4,0},{5,1},{6,2},{7,3},{8,12},{9,13},{10,... | collective-permute-start | bytes 491528 | tf_op jit(solution)/shard_map/ppermute | solution.py:27
  7.3 4.5 %collective-permute-start.2 = (bf16[64,640]{1,0:T(8,128)(2,1)S(1)}, bf16[64,640]{1,0:T(8,128)(2,1)S(1)}, u32[]{:S(2)}, u32[]{:S(2)}) collective-permute-start(bf16[64,640]{1,0:T(8,128)(2,1)S(1)} %get-tuple-element.22), channel_id=1, source_target_pairs={{0,2},{1,3},{2,0},{3,1},{4,6},{5,7},{6,4},{7,5},{8,10},{9,11},{10,... | collective-permute-start | bytes 245768 | tf_op jit(solution)/shard_map/ppermute | solution.py:27
  9.2 10.9 %collective-permute-start.7 = (bf16[128,640]{1,0:T(8,128)(2,1)S(1)}, bf16[128,640]{1,0:T(8,128)(2,1)S(1)}, u32[]{:S(2)}, u32[]{:S(2)}) collective-permute-start(bf16[128,640]{1,0:T(8,128)(2,1)S(1)} %assemble.1._.refs_0_.query_ref), channel_id=1, source_target_pairs={{0,8},{1,9},{2,10},{3,11},{4,12},{5,13},{6,14},{7,15},{8,0},{9,1},... | collective-permute-start | bytes 491528 | tf_op jit(solution)/shard_map/ppermute | solution.py:27
  12.0 8.2 %collective-permute-start.4 = (bf16[128,640]{1,0:T(8,128)(2,1)S(1)}, bf16[128,640]{1,0:T(8,128)(2,1)S(1)}, u32[]{:S(2)}, u32[]{:S(2)}) collective-permute-start(bf16[128,640]{1,0:T(8,128)(2,1)S(1)} %rebuild.3.refs_0_.near_keys), channel_id=1, source_target_pairs={{0,4},{1,5},{2,6},{3,7},{4,0},{5,1},{6,2},{7,3},{8,12},{9,13},{10,... | collective-permute-start | bytes 491528 | tf_op jit(solution)/shard_map/ppermute | solution.py:27
  13.7 4.4 %collective-permute-start.3 = (bf16[64,640]{1,0:T(8,128)(2,1)S(1)}, bf16[64,640]{1,0:T(8,128)(2,1)S(1)}, u32[]{:S(2)}, u32[]{:S(2)}) collective-permute-start(bf16[64,640]{1,0:T(8,128)(2,1)S(1)} %get-tuple-element.26), channel_id=1, source_target_pairs={{0,2},{1,3},{2,0},{3,1},{4,6},{5,7},{6,4},{7,5},{8,10},{9,11},{10,... | collective-permute-start | bytes 245768 | tf_op jit(solution)/shard_map/ppermute | solution.py:27
  15.6 4.5 %collective-permute-start.6 = (bf16[64,640]{1,0:T(8,128)(2,1)S(1)}, bf16[64,640]{1,0:T(8,128)(2,1)S(1)}, u32[]{:S(2)}, u32[]{:S(2)}) collective-permute-start(bf16[64,640]{1,0:T(8,128)(2,1)S(1)} %pick.3), channel_id=1, source_target_pairs={{0,2},{1,3},{2,0},{3,1},{4,6},{5,7},{6,4},{7,5},{8,10},{9,11},{10,... | collective-permute-start | bytes 245768 | tf_op jit(solution)/shard_map/ppermute | solution.py:27
  20.8 7.4 %collective-permute-start.10 = (bf16[2,176,128]{2,1,0:T(8,128)(2,1)S(1)}, bf16[2,176,128]{2,1,0:T(8,128)(2,1)S(1)}, u32[]{:S(2)}, u32[]{:S(2)}) collective-permute-start(bf16[2,176,128]{2,1,0:T(8,128)(2,1)S(1)} %get-tuple-element.31), channel_id=1, source_target_pairs={{0,10},{1,11},{2,8},{3,9},{4,14},{5,15},{6,12},{7,13},{8,2},{9,3},... | collective-permute-start | bytes 270344 | tf_op jit(solution)/shard_map/ppermute | solution.py:27
  23.1 5.5 %collective-permute-start.9 = (bf16[2,176,128]{2,1,0:T(8,128)(2,1)S(1)}, bf16[2,176,128]{2,1,0:T(8,128)(2,1)S(1)}, u32[]{:S(2)}, u32[]{:S(2)}) collective-permute-start(bf16[2,176,128]{2,1,0:T(8,128)(2,1)S(1)} %get-tuple-element.30), channel_id=1, source_target_pairs={{0,2},{1,3},{2,0},{3,1},{4,6},{5,7},{6,4},{7,5},{8,10},{9,11},{10,... | collective-permute-start | bytes 270344 | tf_op jit(solution)/shard_map/ppermute | solution.py:27
  24.0 7.7 %collective-permute-start.13 = (bf16[1,176,128]{2,1,0:T(8,128)(2,1)S(1)}, bf16[1,176,128]{2,1,0:T(8,128)(2,1)S(1)}, u32[]{:S(2)}, u32[]{:S(2)}) collective-permute-start(bf16[1,176,128]{2,1,0:T(8,128)(2,1)S(1)} %get-tuple-element.27.refs_0_), channel_id=1, source_target_pairs={{0,9},{1,8},{2,11},{3,10},{4,13},{5,12},{6,15},{7,14},{8,1},{9,0},... | collective-permute-start | bytes 135176 | tf_op jit(solution)/shard_map/ppermute | solution.py:27
  24.0 5.1 %collective-permute-start.8 = (bf16[1,176,128]{2,1,0:T(8,128)(2,1)S(1)}, bf16[1,176,128]{2,1,0:T(8,128)(2,1)S(1)}, u32[]{:S(2)}, u32[]{:S(2)}) collective-permute-start(bf16[1,176,128]{2,1,0:T(8,128)(2,1)S(1)} %get-tuple-element.29), channel_id=1, source_target_pairs={{0,1},{1,0},{2,3},{3,2},{4,5},{5,4},{6,7},{7,6},{8,9},{9,8},{10,11... | collective-permute-start | bytes 135176 | tf_op jit(solution)/shard_map/ppermute | solution.py:27
  26.0 5.8 %collective-permute-start.12 = (bf16[1,176,128]{2,1,0:T(8,128)(2,1)S(1)}, bf16[1,176,128]{2,1,0:T(8,128)(2,1)S(1)}, u32[]{:S(2)}, u32[]{:S(2)}) collective-permute-start(bf16[1,176,128]{2,1,0:T(8,128)(2,1)S(1)} %get-tuple-element.32), channel_id=1, source_target_pairs={{0,8},{1,9},{2,10},{3,11},{4,12},{5,13},{6,14},{7,15},{8,0},{9,1},... | collective-permute-start | bytes 135176 | tf_op jit(solution)/shard_map/ppermute | solution.py:27
  28.6 3.2 %collective-permute-start.11 = (bf16[176,128]{1,0:T(8,128)(2,1)S(1)}, bf16[176,128]{1,0:T(8,128)(2,1)S(1)}, u32[]{:S(2)}, u32[]{:S(2)}) collective-permute-start(bf16[176,128]{1,0:T(8,128)(2,1)S(1)} %pick.5), channel_id=1, source_target_pairs={{0,1},{1,0},{2,3},{3,2},{4,5},{5,4},{6,7},{7,6},{8,9},{9,8},{10,11... | collective-permute-start | bytes 135176 | tf_op jit(solution)/shard_map/ppermute | solution.py:27
  28.6 3.2 %collective-permute-start.14 = (bf16[176,128]{1,0:T(8,128)(2,1)S(1)}, bf16[176,128]{1,0:T(8,128)(2,1)S(1)}, u32[]{:S(2)}, u32[]{:S(2)}) collective-permute-start(bf16[176,128]{1,0:T(8,128)(2,1)S(1)} %pick.4.refs_0_), channel_id=1, source_target_pairs={{0,1},{1,0},{2,3},{3,2},{4,5},{5,4},{6,7},{7,6},{8,9},{9,8},{10,11... | collective-permute-start | bytes 135176 | tf_op jit(solution)/shard_map/ppermute | solution.py:27

commit v9 on v8

--- a/solution.py
+++ b/solution.py
@@ -44,31 +44,30 @@
         copy.wait()
 
 
-def cut_kernel(count, *refs):
-    slabs, sent, kept, sems = refs[:count], refs[-3], refs[-2], refs[-1]
+def cut_kernel(count, first, *refs):
+    slabs, out, sems = refs[:count], refs[-2], refs[-1]
     width = slabs[0].shape[1] // GROUP
     _, member = position()
     pairs = []
     for i, slab in enumerate(slabs):
         for k in range(2):
-            pairs.append((slab.at[:, part(member ^ (1 + 2 * k), width)], sent.at[i, k]))
-            pairs.append((slab.at[:, part(member ^ (2 * k), width)], kept.at[i, k]))
+            pairs.append((slab.at[:, part(member ^ (first + 2 * k), width)], out.at[i, k]))
     run_copies(pairs, sems)
 
 
-def cut(*slabs):
+def cut(first, slabs, *earlier):
     rows, features = slabs[0].shape
     shape = jax.ShapeDtypeStruct((len(slabs), 2, rows, features // GROUP), slabs[0].dtype)
     return pl.pallas_call(
-        functools.partial(cut_kernel, len(slabs)),
-        out_shape=[shape] * 2,
-        in_specs=[HBM] * len(slabs),
-        out_specs=[VMEM] * 2,
-        scratch_shapes=[pltpu.SemaphoreType.DMA((4 * len(slabs),))],
+        functools.partial(cut_kernel, len(slabs), first),
+        out_shape=shape,
+        in_specs=[HBM] * (len(slabs) + len(earlier)),
+        out_specs=VMEM,
+        scratch_shapes=[pltpu.SemaphoreType.DMA((2 * len(slabs),))],
         compiler_params=limit(4 * MB),
         cost_estimate=cost(1000),
         name="cut",
-    )(*slabs)
+    )(*slabs, *earlier)
 
 
 def join_kernel(kept, arrived, x_query, x_keys, x_values, z_values):
@@ -328,8 +327,9 @@
 
     pinned = [pltpu.with_memory_space_constraint(a, pltpu.HBM) for a in (keys_new, values_new, queries)]
     copies = [pltpu.with_memory_space_constraint(a, pltpu.HBM) for a in (keys_copy, values_copy)]
-    sent, kept = cut(*pinned)
+    sent = cut(1, pinned)
     beside = swapped(sent, 1)
+    kept = cut(0, pinned, sent)
     x_query, x_keys, x_own, near_raw = join(kept, beside)
     own_query = assemble(kept, beside, swapped(x_query, 2))
     far_query = swapped(own_query, across)
@@ -355,11 +355,11 @@
         kernel = functools.partial(rebuild_values_kernel, heads, first)
         halves.append(rebuild(kernel, block * count // 2, old, this, opposite, old, limits, earlier))
     near, far = (near_keys, halves[0]), (far_keys, halves[1])
+    parts = ((0,), (1,), (2, 3))
+    n0, n1, n23 = attend(heads, parts, own_query, near, far)
     parts = ((2, 3), (0,), (1,))
-    far_out = attend(heads, parts, far_query, near, far)
+    far_out = attend(heads, parts, far_query, near, far, n23)
     f23, f0, f1 = [swapped(a, across + group[0]) for a, group in zip(far_out, parts)]
-    parts = ((0,), (1,), (2, 3))
-    n0, n1, n23 = attend(heads, parts, own_query, near, far, far_out[2])
     n1, n23 = swapped(n1, 1), swapped(n23, 2)
     f3 = pick(f23)
     n3 = pick(n23, f3)

time: 33.3 us -> 33.2 us (level)
  waiting for transfers between devices: 9.41 us -> 8.46 us
  Pallas kernels: 5.4 us -> 6.15 us
    ppermute x15, waiting for transfers between devices: 9.41 us -> 8.46 us  [swapped(): return lax.ppermute(array, 'patch', [(i, i ^ mask) for i in range(size)])]
    pallas_call x1 -> x2, Pallas kernels: 1.11 us -> 1.86 us  [cut(): pl.pallas_call(functools.partial(cut_kernel, len(slabs), first), out_shap...]
  transfers between devices with their start and end apart: 15 -> 15, of which waited for: 6 -> 5; matrix products, arithmetic and copies ran while one was open for 0% -> 0% of each run, Pallas kernels for 7% -> 9%
where the time goes in v9:
time: 33.2 us; the launch traced here: 32.9 us
  starting transfers between devices  18.1 us (55%)
  waiting for transfers between devices  8.46 us (25%)
  Pallas kernels  6.15 us (19%)
    ppermute x15, starting transfers between devices, swapped(): return lax.ppermute(array, 'patch', [(i, i ^ mask) for i in range(size)])  18.1 us
    ppermute x15, waiting for transfers between devices, swapped(): return lax.ppermute(array, 'patch', [(i, i ^ mask) for i in range(size)])  8.46 us
    pallas_call x2, Pallas kernels, cut(): pl.pallas_call(functools.partial(cut_kernel, len(slabs), first), out_shap...  1.86 us
    pallas_call x1, Pallas kernels, fetch(): pl.pallas_call(functools.partial(fetch_kernel, heads, count), out_shape=[...  1.29 us
    pallas_call x1, Pallas kernels, merge(): pl.pallas_call(functools.partial(merge_kernel, heads), out_shape=jax.Shap...  1.22 us
    pallas_call x2, Pallas kernels, attend(): pl.pallas_call(functools.partial(attend_kernel, heads, parts), out_shape=...  1.14 us
  transfers between devices with their start and end apart: 15, of which 5 were waited for; matrix products, arithmetic and copies ran while one was open for 0% of the time, Pallas kernels for 9%

profile of v9, /device:TPU:0, one launch (start us, length us, event | category | flops | bytes accessed | tf_op | source)
XLA Modules:
  0.0 32.9 jit_solution(16790851268207051140)
XLA Ops:
  0.0 0.9 %cut.2.refs_3_ = bf16[3,2,32,640]{3,2,1,0:T(8,128)(2,1)S(1)} custom-call(bf16[32,2560]{1,0:T(8,128)(2,1)} %refs_0_.3, bf16[32,2560]{1,0:T(8,128)(2,1)} %refs_1_.3, bf16[32,2560]{1,0:T(8,128)(2,1)} %refs_2_.3), custom_call_target="tpu_custom_call" | custom-call | bytes 1000 | tf_op jit(solution)/shard_map/cut/pallas_call | solution.py:61
  0.9 0.5 %collective-permute-start = (bf16[3,2,32,640]{3,2,1,0:T(8,128)(2,1)S(1)}, bf16[3,2,32,640]{3,2,1,0:T(8,128)(2,1)S(1)}, u32[]{:S(2)}, u32[]{:S(2)}) collective-permute-start(bf16[3,2,32,640]{3,2,1,0:T(8,128)(2,1)S(1)} %cut.2.refs_3_), channel_id=1, source_target_pairs={{0,1},{1,0},{2,3},{3,2},{4,5},{5,4},{6,7},{7,6},{8,9},{9,8},{10,11... | collective-permute-start | bytes 737288 | tf_op jit(solution)/shard_map/ppermute | solution.py:27
  1.5 0.9 %cut.3.kept = bf16[3,2,32,640]{3,2,1,0:T(8,128)(2,1)S(1)} custom-call(bf16[32,2560]{1,0:T(8,128)(2,1)} %refs_0_.3, bf16[32,2560]{1,0:T(8,128)(2,1)} %refs_1_.3, bf16[32,2560]{1,0:T(8,128)(2,1)} %refs_2_.3, bf16[3,2,32,640]{3,2,1,0:T(8,128)(2,1)S(1)} %cut.2.refs_3_), custom_call_target="tpu_custom_call" | custom-call | bytes 1000 | tf_op jit(solution)/shard_map/cut/pallas_call | solution.py:61
  2.6 2.9 %collective-permute-start.1 = (bf16[64,640]{1,0:T(8,128)(2,1)S(1)}, bf16[64,640]{1,0:T(8,128)(2,1)S(1)}, u32[]{:S(2)}, u32[]{:S(2)}) collective-permute-start(bf16[64,640]{1,0:T(8,128)(2,1)S(1)} %get-tuple-element.17), channel_id=1, source_target_pairs={{0,2},{1,3},{2,0},{3,1},{4,6},{5,7},{6,4},{7,5},{8,10},{9,11},{10,... | collective-permute-start | bytes 245768 | tf_op jit(solution)/shard_map/ppermute | solution.py:27
  5.6 1.6 %collective-permute-start.5 = (bf16[2,64,640]{2,1,0:T(8,128)(2,1)S(1)}, bf16[2,64,640]{2,1,0:T(8,128)(2,1)S(1)}, u32[]{:S(2)}, u32[]{:S(2)}) collective-permute-start(bf16[2,64,640]{2,1,0:T(8,128)(2,1)S(1)} %get-tuple-element.21.this), channel_id=1, source_target_pairs={{0,4},{1,5},{2,6},{3,7},{4,0},{5,1},{6,2},{7,3},{8,12},{9,13},{10,... | collective-permute-start | bytes 491528 | tf_op jit(solution)/shard_map/ppermute | solution.py:27
  7.2 0.5 %collective-permute-start.2 = (bf16[64,640]{1,0:T(8,128)(2,1)S(1)}, bf16[64,640]{1,0:T(8,128)(2,1)S(1)}, u32[]{:S(2)}, u32[]{:S(2)}) collective-permute-start(bf16[64,640]{1,0:T(8,128)(2,1)S(1)} %get-tuple-element.18), channel_id=1, source_target_pairs={{0,2},{1,3},{2,0},{3,1},{4,6},{5,7},{6,4},{7,5},{8,10},{9,11},{10,... | collective-permute-start | bytes 245768 | tf_op jit(solution)/shard_map/ppermute | solution.py:27
  7.7 1.3 %fetch.1 = (bf16[3,128,640]{2,1,0:T(8,128)(2,1)S(1)}, f32[3,128,128]{2,1,0:T(8,128)S(1)}) custom-call(bf16[1,512,640]{2,1,0:T(8,128)(2,1)} %keys_copy.1, bf16[1,512,640]{2,1,0:T(8,128)(2,1)} %values_copy.1, f32[20,512]{1,0:T(8,128)S(1)} %bitcast.4, f32[20,512]{1,0:T(8,128)S(1)} %bitcast.5), custom_call_target="tpu_custom_call" | custom-call | bytes 1000 | tf_op jit(solution)/shard_map/fetch/pallas_call | solution.py:154
  9.0 2.7 %collective-permute-start.7 = (bf16[128,640]{1,0:T(8,128)(2,1)S(1)}, bf16[128,640]{1,0:T(8,128)(2,1)S(1)}, u32[]{:S(2)}, u32[]{:S(2)}) collective-permute-start(bf16[128,640]{1,0:T(8,128)(2,1)S(1)} %assemble.1._.refs_0_.query_ref), channel_id=1, source_target_pairs={{0,8},{1,9},{2,10},{3,11},{4,12},{5,13},{6,14},{7,15},{8,0},{9,1},... | collective-permute-start | bytes 491528 | tf_op jit(solution)/shard_map/ppermute | solution.py:27
  11.9 1.6 %collective-permute-start.4 = (bf16[128,640]{1,0:T(8,128)(2,1)S(1)}, bf16[128,640]{1,0:T(8,128)(2,1)S(1)}, u32[]{:S(2)}, u32[]{:S(2)}) collective-permute-start(bf16[128,640]{1,0:T(8,128)(2,1)S(1)} %rebuild.3.refs_0_.near_keys), channel_id=1, source_target_pairs={{0,4},{1,5},{2,6},{3,7},{4,0},{5,1},{6,2},{7,3},{8,12},{9,13},{10,... | collective-permute-start | bytes 491528 | tf_op jit(solution)/shard_map/ppermute | solution.py:27
  13.5 1.9 %collective-permute-start.3 = (bf16[64,640]{1,0:T(8,128)(2,1)S(1)}, bf16[64,640]{1,0:T(8,128)(2,1)S(1)}, u32[]{:S(2)}, u32[]{:S(2)}) collective-permute-start(bf16[64,640]{1,0:T(8,128)(2,1)S(1)} %get-tuple-element.22), channel_id=1, source_target_pairs={{0,2},{1,3},{2,0},{3,1},{4,6},{5,7},{6,4},{7,5},{8,10},{9,11},{10,... | collective-permute-start | bytes 245768 | tf_op jit(solution)/shard_map/ppermute | solution.py:27
  15.4 0.2 collective-permute-start.6
  15.6 2.3 %collective-permute-done.3.opposite = bf16[64,640]{1,0:T(8,128)(2,1)S(1)} collective-permute-done((bf16[64,640]{1,0:T(8,128)(2,1)S(1)}, bf16[64,640]{1,0:T(8,128)(2,1)S(1)}, u32[]{:S(2)}, u32[]{:S(2)}) %collective-permute-start.3) | collective-permute-done | bytes 81952 | tf_op jit(solution)/shard_map/ppermute | solution.py:27
  18.1 1.7 %collective-permute-done.6.opposite = bf16[64,640]{1,0:T(8,128)(2,1)S(1)} collective-permute-done((bf16[64,640]{1,0:T(8,128)(2,1)S(1)}, bf16[64,640]{1,0:T(8,128)(2,1)S(1)}, u32[]{:S(2)}, u32[]{:S(2)}) %collective-permute-start.6) | collective-permute-done | bytes 81952 | tf_op jit(solution)/shard_map/ppermute | solution.py:27
  19.9 0.2 rebuild.5.far_values
  20.1 0.6 %attend.2 = (bf16[1,176,128]{2,1,0:T(8,128)(2,1)S(1)}, bf16[1,176,128]{2,1,0:T(8,128)(2,1)S(1)}, bf16[2,176,128]{2,1,0:T(8,128)(2,1)S(1)}) custom-call(bf16[128,640]{1,0:T(8,128)(2,1)S(1)} %assemble.1._.refs_0_.query_ref, bf16[128,640]{1,0:T(8,128)(2,1)S(1)} %rebuild.3.refs_0_.near_keys, bf16[128,640]{1,0:T(8,128)(2,1)S(1)} %rebuild.4.near_values, ...), custom_call_target="tpu_custom_call" | custom-call | bytes 1000 | tf_op jit(solution)/shard_map/attend/pallas_call | solution.py:266
  20.7 0.6 %attend.3 = (bf16[2,176,128]{2,1,0:T(8,128)(2,1)S(1)}, bf16[1,176,128]{2,1,0:T(8,128)(2,1)S(1)}, bf16[1,176,128]{2,1,0:T(8,128)(2,1)S(1)}) custom-call(bf16[128,640]{1,0:T(8,128)(2,1)S(1)} %collective-permute-done.7.refs_0_.query_ref, bf16[128,640]{1,0:T(8,128)(2,1)S(1)} %rebuild.3.refs_0_.near_keys, bf16[128,640]{1,0:T(8,128)(2,1)S(1)} %rebuild.4.near_values, ...), custom_call_target="tpu_custom_call" | custom-call | bytes 1000 | tf_op jit(solution)/shard_map/attend/pallas_call | solution.py:266
  21.2 1.7 %collective-permute-start.10 = (bf16[2,176,128]{2,1,0:T(8,128)(2,1)S(1)}, bf16[2,176,128]{2,1,0:T(8,128)(2,1)S(1)}, u32[]{:S(2)}, u32[]{:S(2)}) collective-permute-start(bf16[2,176,128]{2,1,0:T(8,128)(2,1)S(1)} %get-tuple-element.26), channel_id=1, source_target_pairs={{0,10},{1,11},{2,8},{3,9},{4,14},{5,15},{6,12},{7,13},{8,2},{9,3},... | collective-permute-start | bytes 270344 | tf_op jit(solution)/shard_map/ppermute | solution.py:27
  22.9 0.9 %collective-permute-start.9 = (bf16[2,176,128]{2,1,0:T(8,128)(2,1)S(1)}, bf16[2,176,128]{2,1,0:T(8,128)(2,1)S(1)}, u32[]{:S(2)}, u32[]{:S(2)}) collective-permute-start(bf16[2,176,128]{2,1,0:T(8,128)(2,1)S(1)} %get-tuple-element.25.refs_0_), channel_id=1, source_target_pairs={{0,2},{1,3},{2,0},{3,1},{4,6},{5,7},{6,4},{7,5},{8,10},{9,11},{10,... | collective-permute-start | bytes 270344 | tf_op jit(solution)/shard_map/ppermute | solution.py:27
  23.8 1.8 %collective-permute-start.12 = (bf16[1,176,128]{2,1,0:T(8,128)(2,1)S(1)}, bf16[1,176,128]{2,1,0:T(8,128)(2,1)S(1)}, u32[]{:S(2)}, u32[]{:S(2)}) collective-permute-start(bf16[1,176,128]{2,1,0:T(8,128)(2,1)S(1)} %get-tuple-element.27), channel_id=1, source_target_pairs={{0,8},{1,9},{2,10},{3,11},{4,12},{5,13},{6,14},{7,15},{8,0},{9,1},... | collective-permute-start | bytes 135176 | tf_op jit(solution)/shard_map/ppermute | solution.py:27
  25.7 1.2 %collective-permute-start.8 = (bf16[1,176,128]{2,1,0:T(8,128)(2,1)S(1)}, bf16[1,176,128]{2,1,0:T(8,128)(2,1)S(1)}, u32[]{:S(2)}, u32[]{:S(2)}) collective-permute-start(bf16[1,176,128]{2,1,0:T(8,128)(2,1)S(1)} %get-tuple-element.24), channel_id=1, source_target_pairs={{0,1},{1,0},{2,3},{3,2},{4,5},{5,4},{6,7},{7,6},{8,9},{9,8},{10,11... | collective-permute-start | bytes 135176 | tf_op jit(solution)/shard_map/ppermute | solution.py:27
  26.9 2.2 %collective-permute-done.10.both.f2 = bf16[2,176,128]{2,1,0:T(8,128)(2,1)S(1)} collective-permute-done((bf16[2,176,128]{2,1,0:T(8,128)(2,1)S(1)}, bf16[2,176,128]{2,1,0:T(8,128)(2,1)S(1)}, u32[]{:S(2)}, u32[]{:S(2)}) %collective-permute-start.10) | collective-permute-done | bytes 90144 | tf_op jit(solution)/shard_map/ppermute | solution.py:27
  29.1 0.5 %collective-permute-start.14 = (bf16[176,128]{1,0:T(8,128)(2,1)S(1)}, bf16[176,128]{1,0:T(8,128)(2,1)S(1)}, u32[]{:S(2)}, u32[]{:S(2)}) collective-permute-start(bf16[176,128]{1,0:T(8,128)(2,1)S(1)} %pick.4.refs_0_), channel_id=1, source_target_pairs={{0,1},{1,0},{2,3},{3,2},{4,5},{5,4},{6,7},{7,6},{8,9},{9,8},{10,11... | collective-permute-start | bytes 135176 | tf_op jit(solution)/shard_map/ppermute | solution.py:27
  29.6 2.0 %collective-permute-done.13.f1 = bf16[1,176,128]{2,1,0:T(8,128)(2,1)S(1)} collective-permute-done((bf16[1,176,128]{2,1,0:T(8,128)(2,1)S(1)}, bf16[1,176,128]{2,1,0:T(8,128)(2,1)S(1)}, u32[]{:S(2)}, u32[]{:S(2)}) %collective-permute-start.13) | collective-permute-done | bytes 45088 | tf_op jit(solution)/shard_map/ppermute | solution.py:27
  31.7 1.2 %merge.1 = bf16[32,2560]{1,0:T(8,128)(2,1)} custom-call(bf16[1,176,128]{2,1,0:T(8,128)(2,1)S(1)} %get-tuple-element.23.n0, bf16[1,176,128]{2,1,0:T(8,128)(2,1)S(1)} %collective-permute-done.8.n1, bf16[2,176,128]{2,1,0:T(8,128)(2,1)S(1)} %collective-permute-done.9.both.n2, bf16[1,176,128]{2,1,0:T(8,128)(2,1)S(1)} %bitcast.6, ...), custom_call_target="tpu_custom_call" | custom-call | bytes 1000 | tf_op jit(solution)/shard_map/merge/pallas_call | solution.py:311
  (24 shorter events, 0.7 us)
Async XLA Ops:
  0.9 1.7 %collective-permute-start = (bf16[3,2,32,640]{3,2,1,0:T(8,128)(2,1)S(1)}, bf16[3,2,32,640]{3,2,1,0:T(8,128)(2,1)S(1)}, u32[]{:S(2)}, u32[]{:S(2)}) collective-permute-start(bf16[3,2,32,640]{3,2,1,0:T(8,128)(2,1)S(1)} %cut.2.refs_3_), channel_id=1, source_target_pairs={{0,1},{1,0},{2,3},{3,2},{4,5},{5,4},{6,7},{7,6},{8,9},{9,8},{10,11... | collective-permute-start | bytes 737288 | tf_op jit(solution)/shard_map/ppermute | solution.py:27
  2.4 5.3 %copy-start = (f32[512,20]{0,1:T(8,128)S(1)}, f32[512,20]{0,1:T(8,128)}, u32[]{:S(2)}) copy-start(f32[512,20]{0,1:T(8,128)} %param.12) | copy-start | bytes 122884
  2.4 5.3 %copy-start.1 = (f32[512,20]{0,1:T(8,128)S(1)}, f32[512,20]{0,1:T(8,128)}, u32[]{:S(2)}) copy-start(f32[512,20]{0,1:T(8,128)} %param.13) | copy-start | bytes 122884
  2.6 6.3 %collective-permute-start.1 = (bf16[64,640]{1,0:T(8,128)(2,1)S(1)}, bf16[64,640]{1,0:T(8,128)(2,1)S(1)}, u32[]{:S(2)}, u32[]{:S(2)}) collective-permute-start(bf16[64,640]{1,0:T(8,128)(2,1)S(1)} %get-tuple-element.17), channel_id=1, source_target_pairs={{0,2},{1,3},{2,0},{3,1},{4,6},{5,7},{6,4},{7,5},{8,10},{9,11},{10,... | collective-permute-start | bytes 245768 | tf_op jit(solution)/shard_map/ppermute | solution.py:27
  5.6 9.8 %collective-permute-start.5 = (bf16[2,64,640]{2,1,0:T(8,128)(2,1)S(1)}, bf16[2,64,640]{2,1,0:T(8,128)(2,1)S(1)}, u32[]{:S(2)}, u32[]{:S(2)}) collective-permute-start(bf16[2,64,640]{2,1,0:T(8,128)(2,1)S(1)} %get-tuple-element.21.this), channel_id=1, source_target_pairs={{0,4},{1,5},{2,6},{3,7},{4,0},{5,1},{6,2},{7,3},{8,12},{9,13},{10,... | collective-permute-start | bytes 491528 | tf_op jit(solution)/shard_map/ppermute | solution.py:27
  7.2 4.5 %collective-permute-start.2 = (bf16[64,640]{1,0:T(8,128)(2,1)S(1)}, bf16[64,640]{1,0:T(8,128)(2,1)S(1)}, u32[]{:S(2)}, u32[]{:S(2)}) collective-permute-start(bf16[64,640]{1,0:T(8,128)(2,1)S(1)} %get-tuple-element.18), channel_id=1, source_target_pairs={{0,2},{1,3},{2,0},{3,1},{4,6},{5,7},{6,4},{7,5},{8,10},{9,11},{10,... | collective-permute-start | bytes 245768 | tf_op jit(solution)/shard_map/ppermute | solution.py:27
  9.0 10.9 %collective-permute-start.7 = (bf16[128,640]{1,0:T(8,128)(2,1)S(1)}, bf16[128,640]{1,0:T(8,128)(2,1)S(1)}, u32[]{:S(2)}, u32[]{:S(2)}) collective-permute-start(bf16[128,640]{1,0:T(8,128)(2,1)S(1)} %assemble.1._.refs_0_.query_ref), channel_id=1, source_target_pairs={{0,8},{1,9},{2,10},{3,11},{4,12},{5,13},{6,14},{7,15},{8,0},{9,1},... | collective-permute-start | bytes 491528 | tf_op jit(solution)/shard_map/ppermute | solution.py:27
  11.9 8.2 %collective-permute-start.4 = (bf16[128,640]{1,0:T(8,128)(2,1)S(1)}, bf16[128,640]{1,0:T(8,128)(2,1)S(1)}, u32[]{:S(2)}, u32[]{:S(2)}) collective-permute-start(bf16[128,640]{1,0:T(8,128)(2,1)S(1)} %rebuild.3.refs_0_.near_keys), channel_id=1, source_target_pairs={{0,4},{1,5},{2,6},{3,7},{4,0},{5,1},{6,2},{7,3},{8,12},{9,13},{10,... | collective-permute-start | bytes 491528 | tf_op jit(solution)/shard_map/ppermute | solution.py:27
  13.5 4.4 %collective-permute-start.3 = (bf16[64,640]{1,0:T(8,128)(2,1)S(1)}, bf16[64,640]{1,0:T(8,128)(2,1)S(1)}, u32[]{:S(2)}, u32[]{:S(2)}) collective-permute-start(bf16[64,640]{1,0:T(8,128)(2,1)S(1)} %get-tuple-element.22), channel_id=1, source_target_pairs={{0,2},{1,3},{2,0},{3,1},{4,6},{5,7},{6,4},{7,5},{8,10},{9,11},{10,... | collective-permute-start | bytes 245768 | tf_op jit(solution)/shard_map/ppermute | solution.py:27
  15.4 4.5 %collective-permute-start.6 = (bf16[64,640]{1,0:T(8,128)(2,1)S(1)}, bf16[64,640]{1,0:T(8,128)(2,1)S(1)}, u32[]{:S(2)}, u32[]{:S(2)}) collective-permute-start(bf16[64,640]{1,0:T(8,128)(2,1)S(1)} %pick.3), channel_id=1, source_target_pairs={{0,2},{1,3},{2,0},{3,1},{4,6},{5,7},{6,4},{7,5},{8,10},{9,11},{10,... | collective-permute-start | bytes 245768 | tf_op jit(solution)/shard_map/ppermute | solution.py:27
  21.2 7.8 %collective-permute-start.10 = (bf16[2,176,128]{2,1,0:T(8,128)(2,1)S(1)}, bf16[2,176,128]{2,1,0:T(8,128)(2,1)S(1)}, u32[]{:S(2)}, u32[]{:S(2)}) collective-permute-start(bf16[2,176,128]{2,1,0:T(8,128)(2,1)S(1)} %get-tuple-element.26), channel_id=1, source_target_pairs={{0,10},{1,11},{2,8},{3,9},{4,14},{5,15},{6,12},{7,13},{8,2},{9,3},... | collective-permute-start | bytes 270344 | tf_op jit(solution)/shard_map/ppermute | solution.py:27
  22.9 6.1 %collective-permute-start.9 = (bf16[2,176,128]{2,1,0:T(8,128)(2,1)S(1)}, bf16[2,176,128]{2,1,0:T(8,128)(2,1)S(1)}, u32[]{:S(2)}, u32[]{:S(2)}) collective-permute-start(bf16[2,176,128]{2,1,0:T(8,128)(2,1)S(1)} %get-tuple-element.25.refs_0_), channel_id=1, source_target_pairs={{0,2},{1,3},{2,0},{3,1},{4,6},{5,7},{6,4},{7,5},{8,10},{9,11},{10,... | collective-permute-start | bytes 270344 | tf_op jit(solution)/shard_map/ppermute | solution.py:27
  23.8 5.8 %collective-permute-start.12 = (bf16[1,176,128]{2,1,0:T(8,128)(2,1)S(1)}, bf16[1,176,128]{2,1,0:T(8,128)(2,1)S(1)}, u32[]{:S(2)}, u32[]{:S(2)}) collective-permute-start(bf16[1,176,128]{2,1,0:T(8,128)(2,1)S(1)} %get-tuple-element.27), channel_id=1, source_target_pairs={{0,8},{1,9},{2,10},{3,11},{4,12},{5,13},{6,14},{7,15},{8,0},{9,1},... | collective-permute-start | bytes 135176 | tf_op jit(solution)/shard_map/ppermute | solution.py:27
  25.7 6.0 %collective-permute-start.13 = (bf16[1,176,128]{2,1,0:T(8,128)(2,1)S(1)}, bf16[1,176,128]{2,1,0:T(8,128)(2,1)S(1)}, u32[]{:S(2)}, u32[]{:S(2)}) collective-permute-start(bf16[1,176,128]{2,1,0:T(8,128)(2,1)S(1)} %get-tuple-element.28), channel_id=1, source_target_pairs={{0,9},{1,8},{2,11},{3,10},{4,13},{5,12},{6,15},{7,14},{8,1},{9,0},... | collective-permute-start | bytes 135176 | tf_op jit(solution)/shard_map/ppermute | solution.py:27
  25.7 6.0 %collective-permute-start.8 = (bf16[1,176,128]{2,1,0:T(8,128)(2,1)S(1)}, bf16[1,176,128]{2,1,0:T(8,128)(2,1)S(1)}, u32[]{:S(2)}, u32[]{:S(2)}) collective-permute-start(bf16[1,176,128]{2,1,0:T(8,128)(2,1)S(1)} %get-tuple-element.24), channel_id=1, source_target_pairs={{0,1},{1,0},{2,3},{3,2},{4,5},{5,4},{6,7},{7,6},{8,9},{9,8},{10,11... | collective-permute-start | bytes 135176 | tf_op jit(solution)/shard_map/ppermute | solution.py:27
  29.0 2.6 %collective-permute-start.11 = (bf16[176,128]{1,0:T(8,128)(2,1)S(1)}, bf16[176,128]{1,0:T(8,128)(2,1)S(1)}, u32[]{:S(2)}, u32[]{:S(2)}) collective-permute-start(bf16[176,128]{1,0:T(8,128)(2,1)S(1)} %pick.5), channel_id=1, source_target_pairs={{0,1},{1,0},{2,3},{3,2},{4,5},{5,4},{6,7},{7,6},{8,9},{9,8},{10,11... | collective-permute-start | bytes 135176 | tf_op jit(solution)/shard_map/ppermute | solution.py:27
  29.1 2.5 %collective-permute-start.14 = (bf16[176,128]{1,0:T(8,128)(2,1)S(1)}, bf16[176,128]{1,0:T(8,128)(2,1)S(1)}, u32[]{:S(2)}, u32[]{:S(2)}) collective-permute-start(bf16[176,128]{1,0:T(8,128)(2,1)S(1)} %pick.4.refs_0_), channel_id=1, source_target_pairs={{0,1},{1,0},{2,3},{3,2},{4,5},{5,4},{6,7},{7,6},{8,9},{9,8},{10,11... | collective-permute-start | bytes 135176 | tf_op jit(solution)/shard_map/ppermute | solution.py:27

commit v10 on v9

--- a/solution.py
+++ b/solution.py
@@ -355,11 +355,11 @@
         kernel = functools.partial(rebuild_values_kernel, heads, first)
         halves.append(rebuild(kernel, block * count // 2, old, this, opposite, old, limits, earlier))
     near, far = (near_keys, halves[0]), (far_keys, halves[1])
+    parts = ((2, 3), (0,), (1,))
+    far_out = attend(heads, parts, far_query, near, far)
+    f23, f0, f1 = [swapped(a, across + group[0]) for a, group in zip(far_out, parts)]
     parts = ((0,), (1,), (2, 3))
-    n0, n1, n23 = attend(heads, parts, own_query, near, far)
-    parts = ((2, 3), (0,), (1,))
-    far_out = attend(heads, parts, far_query, near, far, n23)
-    f23, f0, f1 = [swapped(a, across + group[0]) for a, group in zip(far_out, parts)]
+    n0, n1, n23 = attend(heads, parts, own_query, near, far, far_out[2])
     n1, n23 = swapped(n1, 1), swapped(n23, 2)
     f3 = pick(f23)
     n3 = pick(n23, f3)

time: 33.2 us -> 33.2 us (level)
  transfers between devices with their start and end apart: 15 -> 15, of which waited for: 5 -> 6; matrix products, arithmetic and copies ran while one was open for 0% -> 0% of each run, Pallas kernels for 9% -> 10%
where the time goes in v10:
time: 33.2 us; the launch traced here: 32.8 us
  starting transfers between devices  18.1 us (55%)
  waiting for transfers between devices  8.46 us (25%)
  Pallas kernels  6.15 us (19%)
    ppermute x15, starting transfers between devices, swapped(): return lax.ppermute(array, 'patch', [(i, i ^ mask) for i in range(size)])  18.1 us
    ppermute x15, waiting for transfers between devices, swapped(): return lax.ppermute(array, 'patch', [(i, i ^ mask) for i in range(size)])  8.46 us
    pallas_call x2, Pallas kernels, cut(): pl.pallas_call(functools.partial(cut_kernel, len(slabs), first), out_shap...  1.86 us
    pallas_call x1, Pallas kernels, fetch(): pl.pallas_call(functools.partial(fetch_kernel, heads, count), out_shape=[...  1.29 us
    pallas_call x1, Pallas kernels, merge(): pl.pallas_call(functools.partial(merge_kernel, heads), out_shape=jax.Shap...  1.22 us
    pallas_call x2, Pallas kernels, attend(): pl.pallas_call(functools.partial(attend_kernel, heads, parts), out_shape=...  1.14 us
  transfers between devices with their start and end apart: 15, of which 6 were waited for; matrix products, arithmetic and copies ran while one was open for 0% of the time, Pallas kernels for 10%

profile of v10, /device:TPU:0, one launch (start us, length us, event | category | flops | bytes accessed | tf_op | source)
XLA Modules:
  0.0 32.8 jit_solution(3695670110180678424)
XLA Ops:
  0.0 0.9 %cut.2.refs_3_ = bf16[3,2,32,640]{3,2,1,0:T(8,128)(2,1)S(1)} custom-call(bf16[32,2560]{1,0:T(8,128)(2,1)} %refs_0_.3, bf16[32,2560]{1,0:T(8,128)(2,1)} %refs_1_.3, bf16[32,2560]{1,0:T(8,128)(2,1)} %refs_2_.3), custom_call_target="tpu_custom_call" | custom-call | bytes 1000 | tf_op jit(solution)/shard_map/cut/pallas_call | solution.py:61
  0.9 0.5 %collective-permute-start = (bf16[3,2,32,640]{3,2,1,0:T(8,128)(2,1)S(1)}, bf16[3,2,32,640]{3,2,1,0:T(8,128)(2,1)S(1)}, u32[]{:S(2)}, u32[]{:S(2)}) collective-permute-start(bf16[3,2,32,640]{3,2,1,0:T(8,128)(2,1)S(1)} %cut.2.refs_3_), channel_id=1, source_target_pairs={{0,1},{1,0},{2,3},{3,2},{4,5},{5,4},{6,7},{7,6},{8,9},{9,8},{10,11... | collective-permute-start | bytes 737288 | tf_op jit(solution)/shard_map/ppermute | solution.py:27
  1.5 0.9 %cut.3.kept = bf16[3,2,32,640]{3,2,1,0:T(8,128)(2,1)S(1)} custom-call(bf16[32,2560]{1,0:T(8,128)(2,1)} %refs_0_.3, bf16[32,2560]{1,0:T(8,128)(2,1)} %refs_1_.3, bf16[32,2560]{1,0:T(8,128)(2,1)} %refs_2_.3, bf16[3,2,32,640]{3,2,1,0:T(8,128)(2,1)S(1)} %cut.2.refs_3_), custom_call_target="tpu_custom_call" | custom-call | bytes 1000 | tf_op jit(solution)/shard_map/cut/pallas_call | solution.py:61
  2.6 2.9 %collective-permute-start.1 = (bf16[64,640]{1,0:T(8,128)(2,1)S(1)}, bf16[64,640]{1,0:T(8,128)(2,1)S(1)}, u32[]{:S(2)}, u32[]{:S(2)}) collective-permute-start(bf16[64,640]{1,0:T(8,128)(2,1)S(1)} %get-tuple-element.17), channel_id=1, source_target_pairs={{0,2},{1,3},{2,0},{3,1},{4,6},{5,7},{6,4},{7,5},{8,10},{9,11},{10,... | collective-permute-start | bytes 245768 | tf_op jit(solution)/shard_map/ppermute | solution.py:27
  5.6 1.6 %collective-permute-start.5 = (bf16[2,64,640]{2,1,0:T(8,128)(2,1)S(1)}, bf16[2,64,640]{2,1,0:T(8,128)(2,1)S(1)}, u32[]{:S(2)}, u32[]{:S(2)}) collective-permute-start(bf16[2,64,640]{2,1,0:T(8,128)(2,1)S(1)} %get-tuple-element.21.this), channel_id=1, source_target_pairs={{0,4},{1,5},{2,6},{3,7},{4,0},{5,1},{6,2},{7,3},{8,12},{9,13},{10,... | collective-permute-start | bytes 491528 | tf_op jit(solution)/shard_map/ppermute | solution.py:27
  7.2 0.5 %collective-permute-start.2 = (bf16[64,640]{1,0:T(8,128)(2,1)S(1)}, bf16[64,640]{1,0:T(8,128)(2,1)S(1)}, u32[]{:S(2)}, u32[]{:S(2)}) collective-permute-start(bf16[64,640]{1,0:T(8,128)(2,1)S(1)} %get-tuple-element.18), channel_id=1, source_target_pairs={{0,2},{1,3},{2,0},{3,1},{4,6},{5,7},{6,4},{7,5},{8,10},{9,11},{10,... | collective-permute-start | bytes 245768 | tf_op jit(solution)/shard_map/ppermute | solution.py:27
  7.7 1.3 %fetch.1 = (bf16[3,128,640]{2,1,0:T(8,128)(2,1)S(1)}, f32[3,128,128]{2,1,0:T(8,128)S(1)}) custom-call(bf16[1,512,640]{2,1,0:T(8,128)(2,1)} %keys_copy.1, bf16[1,512,640]{2,1,0:T(8,128)(2,1)} %values_copy.1, f32[20,512]{1,0:T(8,128)S(1)} %bitcast.4, f32[20,512]{1,0:T(8,128)S(1)} %bitcast.5), custom_call_target="tpu_custom_call" | custom-call | bytes 1000 | tf_op jit(solution)/shard_map/fetch/pallas_call | solution.py:154
  9.0 2.7 %collective-permute-start.7 = (bf16[128,640]{1,0:T(8,128)(2,1)S(1)}, bf16[128,640]{1,0:T(8,128)(2,1)S(1)}, u32[]{:S(2)}, u32[]{:S(2)}) collective-permute-start(bf16[128,640]{1,0:T(8,128)(2,1)S(1)} %assemble.1._.refs_0_.query_ref), channel_id=1, source_target_pairs={{0,8},{1,9},{2,10},{3,11},{4,12},{5,13},{6,14},{7,15},{8,0},{9,1},... | collective-permute-start | bytes 491528 | tf_op jit(solution)/shard_map/ppermute | solution.py:27
  11.9 1.6 %collective-permute-start.4 = (bf16[128,640]{1,0:T(8,128)(2,1)S(1)}, bf16[128,640]{1,0:T(8,128)(2,1)S(1)}, u32[]{:S(2)}, u32[]{:S(2)}) collective-permute-start(bf16[128,640]{1,0:T(8,128)(2,1)S(1)} %rebuild.3.refs_0_.near_keys), channel_id=1, source_target_pairs={{0,4},{1,5},{2,6},{3,7},{4,0},{5,1},{6,2},{7,3},{8,12},{9,13},{10,... | collective-permute-start | bytes 491528 | tf_op jit(solution)/shard_map/ppermute | solution.py:27
  13.5 1.9 %collective-permute-start.3 = (bf16[64,640]{1,0:T(8,128)(2,1)S(1)}, bf16[64,640]{1,0:T(8,128)(2,1)S(1)}, u32[]{:S(2)}, u32[]{:S(2)}) collective-permute-start(bf16[64,640]{1,0:T(8,128)(2,1)S(1)} %get-tuple-element.22), channel_id=1, source_target_pairs={{0,2},{1,3},{2,0},{3,1},{4,6},{5,7},{6,4},{7,5},{8,10},{9,11},{10,... | collective-permute-start | bytes 245768 | tf_op jit(solution)/shard_map/ppermute | solution.py:27
  15.4 0.2 collective-permute-start.6
  15.6 2.3 %collective-permute-done.3.opposite = bf16[64,640]{1,0:T(8,128)(2,1)S(1)} collective-permute-done((bf16[64,640]{1,0:T(8,128)(2,1)S(1)}, bf16[64,640]{1,0:T(8,128)(2,1)S(1)}, u32[]{:S(2)}, u32[]{:S(2)}) %collective-permute-start.3) | collective-permute-done | bytes 81952 | tf_op jit(solution)/shard_map/ppermute | solution.py:27
  18.1 1.7 %collective-permute-done.6.opposite = bf16[64,640]{1,0:T(8,128)(2,1)S(1)} collective-permute-done((bf16[64,640]{1,0:T(8,128)(2,1)S(1)}, bf16[64,640]{1,0:T(8,128)(2,1)S(1)}, u32[]{:S(2)}, u32[]{:S(2)}) %collective-permute-start.6) | collective-permute-done | bytes 81952 | tf_op jit(solution)/shard_map/ppermute | solution.py:27
  20.1 0.6 %attend.2 = (bf16[2,176,128]{2,1,0:T(8,128)(2,1)S(1)}, bf16[1,176,128]{2,1,0:T(8,128)(2,1)S(1)}, bf16[1,176,128]{2,1,0:T(8,128)(2,1)S(1)}) custom-call(bf16[128,640]{1,0:T(8,128)(2,1)S(1)} %collective-permute-done.7.refs_0_.query_ref, bf16[128,640]{1,0:T(8,128)(2,1)S(1)} %rebuild.3.refs_0_.near_keys, bf16[128,640]{1,0:T(8,128)(2,1)S(1)} %rebuild.4.near_values, ...), custom_call_target="tpu_custom_call" | custom-call | bytes 1000 | tf_op jit(solution)/shard_map/attend/pallas_call | solution.py:266
  20.7 1.7 %collective-permute-start.10 = (bf16[2,176,128]{2,1,0:T(8,128)(2,1)S(1)}, bf16[2,176,128]{2,1,0:T(8,128)(2,1)S(1)}, u32[]{:S(2)}, u32[]{:S(2)}) collective-permute-start(bf16[2,176,128]{2,1,0:T(8,128)(2,1)S(1)} %get-tuple-element.27), channel_id=1, source_target_pairs={{0,10},{1,11},{2,8},{3,9},{4,14},{5,15},{6,12},{7,13},{8,2},{9,3},... | collective-permute-start | bytes 270344 | tf_op jit(solution)/shard_map/ppermute | solution.py:27
  22.3 0.6 %attend.3 = (bf16[1,176,128]{2,1,0:T(8,128)(2,1)S(1)}, bf16[1,176,128]{2,1,0:T(8,128)(2,1)S(1)}, bf16[2,176,128]{2,1,0:T(8,128)(2,1)S(1)}) custom-call(bf16[128,640]{1,0:T(8,128)(2,1)S(1)} %assemble.1._.refs_0_.query_ref, bf16[128,640]{1,0:T(8,128)(2,1)S(1)} %rebuild.3.refs_0_.near_keys, bf16[128,640]{1,0:T(8,128)(2,1)S(1)} %rebuild.4.near_values, ...), custom_call_target="tpu_custom_call" | custom-call | bytes 1000 | tf_op jit(solution)/shard_map/attend/pallas_call | solution.py:266
  22.9 1.0 %collective-permute-start.9 = (bf16[2,176,128]{2,1,0:T(8,128)(2,1)S(1)}, bf16[2,176,128]{2,1,0:T(8,128)(2,1)S(1)}, u32[]{:S(2)}, u32[]{:S(2)}) collective-permute-start(bf16[2,176,128]{2,1,0:T(8,128)(2,1)S(1)} %get-tuple-element.26), channel_id=1, source_target_pairs={{0,2},{1,3},{2,0},{3,1},{4,6},{5,7},{6,4},{7,5},{8,10},{9,11},{10,... | collective-permute-start | bytes 270344 | tf_op jit(solution)/shard_map/ppermute | solution.py:27
  23.9 2.0 %collective-permute-start.8 = (bf16[1,176,128]{2,1,0:T(8,128)(2,1)S(1)}, bf16[1,176,128]{2,1,0:T(8,128)(2,1)S(1)}, u32[]{:S(2)}, u32[]{:S(2)}) collective-permute-start(bf16[1,176,128]{2,1,0:T(8,128)(2,1)S(1)} %get-tuple-element.25), channel_id=1, source_target_pairs={{0,1},{1,0},{2,3},{3,2},{4,5},{5,4},{6,7},{7,6},{8,9},{9,8},{10,11... | collective-permute-start | bytes 135176 | tf_op jit(solution)/shard_map/ppermute | solution.py:27
  25.8 1.1 %collective-permute-start.12 = (bf16[1,176,128]{2,1,0:T(8,128)(2,1)S(1)}, bf16[1,176,128]{2,1,0:T(8,128)(2,1)S(1)}, u32[]{:S(2)}, u32[]{:S(2)}) collective-permute-start(bf16[1,176,128]{2,1,0:T(8,128)(2,1)S(1)} %get-tuple-element.28), channel_id=1, source_target_pairs={{0,8},{1,9},{2,10},{3,11},{4,12},{5,13},{6,14},{7,15},{8,0},{9,1},... | collective-permute-start | bytes 135176 | tf_op jit(solution)/shard_map/ppermute | solution.py:27
  26.9 1.2 %collective-permute-done.10.both.f2 = bf16[2,176,128]{2,1,0:T(8,128)(2,1)S(1)} collective-permute-done((bf16[2,176,128]{2,1,0:T(8,128)(2,1)S(1)}, bf16[2,176,128]{2,1,0:T(8,128)(2,1)S(1)}, u32[]{:S(2)}, u32[]{:S(2)}) %collective-permute-start.10) | collective-permute-done | bytes 90144 | tf_op jit(solution)/shard_map/ppermute | solution.py:27
  28.1 0.3 collective-permute-done.9.both.n2
  28.4 0.5 %collective-permute-start.14 = (bf16[176,128]{1,0:T(8,128)(2,1)S(1)}, bf16[176,128]{1,0:T(8,128)(2,1)S(1)}, u32[]{:S(2)}, u32[]{:S(2)}) collective-permute-start(bf16[176,128]{1,0:T(8,128)(2,1)S(1)} %pick.4.refs_0_), channel_id=1, source_target_pairs={{0,1},{1,0},{2,3},{3,2},{4,5},{5,4},{6,7},{7,6},{8,9},{9,8},{10,11... | collective-permute-start | bytes 135176 | tf_op jit(solution)/shard_map/ppermute | solution.py:27
  28.9 2.7 %collective-permute-done.12.f0 = bf16[1,176,128]{2,1,0:T(8,128)(2,1)S(1)} collective-permute-done((bf16[1,176,128]{2,1,0:T(8,128)(2,1)S(1)}, bf16[1,176,128]{2,1,0:T(8,128)(2,1)S(1)}, u32[]{:S(2)}, u32[]{:S(2)}) %collective-permute-start.12) | collective-permute-done | bytes 45088 | tf_op jit(solution)/shard_map/ppermute | solution.py:27
  31.6 1.2 %merge.1 = bf16[32,2560]{1,0:T(8,128)(2,1)} custom-call(bf16[1,176,128]{2,1,0:T(8,128)(2,1)S(1)} %get-tuple-element.24.n0, bf16[1,176,128]{2,1,0:T(8,128)(2,1)S(1)} %collective-permute-done.8.n1, bf16[2,176,128]{2,1,0:T(8,128)(2,1)S(1)} %collective-permute-done.9.both.n2, bf16[1,176,128]{2,1,0:T(8,128)(2,1)S(1)} %bitcast.6, ...), custom_call_target="tpu_custom_call" | custom-call | bytes 1000 | tf_op jit(solution)/shard_map/merge/pallas_call | solution.py:311
  (24 shorter events, 0.9 us)
Async XLA Ops:
  0.9 1.7 %collective-permute-start = (bf16[3,2,32,640]{3,2,1,0:T(8,128)(2,1)S(1)}, bf16[3,2,32,640]{3,2,1,0:T(8,128)(2,1)S(1)}, u32[]{:S(2)}, u32[]{:S(2)}) collective-permute-start(bf16[3,2,32,640]{3,2,1,0:T(8,128)(2,1)S(1)} %cut.2.refs_3_), channel_id=1, source_target_pairs={{0,1},{1,0},{2,3},{3,2},{4,5},{5,4},{6,7},{7,6},{8,9},{9,8},{10,11... | collective-permute-start | bytes 737288 | tf_op jit(solution)/shard_map/ppermute | solution.py:27
  2.4 5.3 %copy-start = (f32[512,20]{0,1:T(8,128)S(1)}, f32[512,20]{0,1:T(8,128)}, u32[]{:S(2)}) copy-start(f32[512,20]{0,1:T(8,128)} %param.12) | copy-start | bytes 122884
  2.4 5.3 %copy-start.1 = (f32[512,20]{0,1:T(8,128)S(1)}, f32[512,20]{0,1:T(8,128)}, u32[]{:S(2)}) copy-start(f32[512,20]{0,1:T(8,128)} %param.13) | copy-start | bytes 122884
  2.6 6.3 %collective-permute-start.1 = (bf16[64,640]{1,0:T(8,128)(2,1)S(1)}, bf16[64,640]{1,0:T(8,128)(2,1)S(1)}, u32[]{:S(2)}, u32[]{:S(2)}) collective-permute-start(bf16[64,640]{1,0:T(8,128)(2,1)S(1)} %get-tuple-element.17), channel_id=1, source_target_pairs={{0,2},{1,3},{2,0},{3,1},{4,6},{5,7},{6,4},{7,5},{8,10},{9,11},{10,... | collective-permute-start | bytes 245768 | tf_op jit(solution)/shard_map/ppermute | solution.py:27
  5.6 9.8 %collective-permute-start.5 = (bf16[2,64,640]{2,1,0:T(8,128)(2,1)S(1)}, bf16[2,64,640]{2,1,0:T(8,128)(2,1)S(1)}, u32[]{:S(2)}, u32[]{:S(2)}) collective-permute-start(bf16[2,64,640]{2,1,0:T(8,128)(2,1)S(1)} %get-tuple-element.21.this), channel_id=1, source_target_pairs={{0,4},{1,5},{2,6},{3,7},{4,0},{5,1},{6,2},{7,3},{8,12},{9,13},{10,... | collective-permute-start | bytes 491528 | tf_op jit(solution)/shard_map/ppermute | solution.py:27
  7.2 4.5 %collective-permute-start.2 = (bf16[64,640]{1,0:T(8,128)(2,1)S(1)}, bf16[64,640]{1,0:T(8,128)(2,1)S(1)}, u32[]{:S(2)}, u32[]{:S(2)}) collective-permute-start(bf16[64,640]{1,0:T(8,128)(2,1)S(1)} %get-tuple-element.18), channel_id=1, source_target_pairs={{0,2},{1,3},{2,0},{3,1},{4,6},{5,7},{6,4},{7,5},{8,10},{9,11},{10,... | collective-permute-start | bytes 245768 | tf_op jit(solution)/shard_map/ppermute | solution.py:27
  9.0 10.9 %collective-permute-start.7 = (bf16[128,640]{1,0:T(8,128)(2,1)S(1)}, bf16[128,640]{1,0:T(8,128)(2,1)S(1)}, u32[]{:S(2)}, u32[]{:S(2)}) collective-permute-start(bf16[128,640]{1,0:T(8,128)(2,1)S(1)} %assemble.1._.refs_0_.query_ref), channel_id=1, source_target_pairs={{0,8},{1,9},{2,10},{3,11},{4,12},{5,13},{6,14},{7,15},{8,0},{9,1},... | collective-permute-start | bytes 491528 | tf_op jit(solution)/shard_map/ppermute | solution.py:27
  11.9 8.2 %collective-permute-start.4 = (bf16[128,640]{1,0:T(8,128)(2,1)S(1)}, bf16[128,640]{1,0:T(8,128)(2,1)S(1)}, u32[]{:S(2)}, u32[]{:S(2)}) collective-permute-start(bf16[128,640]{1,0:T(8,128)(2,1)S(1)} %rebuild.3.refs_0_.near_keys), channel_id=1, source_target_pairs={{0,4},{1,5},{2,6},{3,7},{4,0},{5,1},{6,2},{7,3},{8,12},{9,13},{10,... | collective-permute-start | bytes 491528 | tf_op jit(solution)/shard_map/ppermute | solution.py:27
  13.5 4.4 %collective-permute-start.3 = (bf16[64,640]{1,0:T(8,128)(2,1)S(1)}, bf16[64,640]{1,0:T(8,128)(2,1)S(1)}, u32[]{:S(2)}, u32[]{:S(2)}) collective-permute-start(bf16[64,640]{1,0:T(8,128)(2,1)S(1)} %get-tuple-element.22), channel_id=1, source_target_pairs={{0,2},{1,3},{2,0},{3,1},{4,6},{5,7},{6,4},{7,5},{8,10},{9,11},{10,... | collective-permute-start | bytes 245768 | tf_op jit(solution)/shard_map/ppermute | solution.py:27
  15.4 4.5 %collective-permute-start.6 = (bf16[64,640]{1,0:T(8,128)(2,1)S(1)}, bf16[64,640]{1,0:T(8,128)(2,1)S(1)}, u32[]{:S(2)}, u32[]{:S(2)}) collective-permute-start(bf16[64,640]{1,0:T(8,128)(2,1)S(1)} %pick.3), channel_id=1, source_target_pairs={{0,2},{1,3},{2,0},{3,1},{4,6},{5,7},{6,4},{7,5},{8,10},{9,11},{10,... | collective-permute-start | bytes 245768 | tf_op jit(solution)/shard_map/ppermute | solution.py:27
  20.7 7.4 %collective-permute-start.10 = (bf16[2,176,128]{2,1,0:T(8,128)(2,1)S(1)}, bf16[2,176,128]{2,1,0:T(8,128)(2,1)S(1)}, u32[]{:S(2)}, u32[]{:S(2)}) collective-permute-start(bf16[2,176,128]{2,1,0:T(8,128)(2,1)S(1)} %get-tuple-element.27), channel_id=1, source_target_pairs={{0,10},{1,11},{2,8},{3,9},{4,14},{5,15},{6,12},{7,13},{8,2},{9,3},... | collective-permute-start | bytes 270344 | tf_op jit(solution)/shard_map/ppermute | solution.py:27
  22.9 5.5 %collective-permute-start.9 = (bf16[2,176,128]{2,1,0:T(8,128)(2,1)S(1)}, bf16[2,176,128]{2,1,0:T(8,128)(2,1)S(1)}, u32[]{:S(2)}, u32[]{:S(2)}) collective-permute-start(bf16[2,176,128]{2,1,0:T(8,128)(2,1)S(1)} %get-tuple-element.26), channel_id=1, source_target_pairs={{0,2},{1,3},{2,0},{3,1},{4,6},{5,7},{6,4},{7,5},{8,10},{9,11},{10,... | collective-permute-start | bytes 270344 | tf_op jit(solution)/shard_map/ppermute | solution.py:27
  23.9 7.8 %collective-permute-start.13 = (bf16[1,176,128]{2,1,0:T(8,128)(2,1)S(1)}, bf16[1,176,128]{2,1,0:T(8,128)(2,1)S(1)}, u32[]{:S(2)}, u32[]{:S(2)}) collective-permute-start(bf16[1,176,128]{2,1,0:T(8,128)(2,1)S(1)} %get-tuple-element.23.refs_0_), channel_id=1, source_target_pairs={{0,9},{1,8},{2,11},{3,10},{4,13},{5,12},{6,15},{7,14},{8,1},{9,0},... | collective-permute-start | bytes 135176 | tf_op jit(solution)/shard_map/ppermute | solution.py:27
  23.9 5.1 %collective-permute-start.8 = (bf16[1,176,128]{2,1,0:T(8,128)(2,1)S(1)}, bf16[1,176,128]{2,1,0:T(8,128)(2,1)S(1)}, u32[]{:S(2)}, u32[]{:S(2)}) collective-permute-start(bf16[1,176,128]{2,1,0:T(8,128)(2,1)S(1)} %get-tuple-element.25), channel_id=1, source_target_pairs={{0,1},{1,0},{2,3},{3,2},{4,5},{5,4},{6,7},{7,6},{8,9},{9,8},{10,11... | collective-permute-start | bytes 135176 | tf_op jit(solution)/shard_map/ppermute | solution.py:27
  25.8 5.8 %collective-permute-start.12 = (bf16[1,176,128]{2,1,0:T(8,128)(2,1)S(1)}, bf16[1,176,128]{2,1,0:T(8,128)(2,1)S(1)}, u32[]{:S(2)}, u32[]{:S(2)}) collective-permute-start(bf16[1,176,128]{2,1,0:T(8,128)(2,1)S(1)} %get-tuple-element.28), channel_id=1, source_target_pairs={{0,8},{1,9},{2,10},{3,11},{4,12},{5,13},{6,14},{7,15},{8,0},{9,1},... | collective-permute-start | bytes 135176 | tf_op jit(solution)/shard_map/ppermute | solution.py:27
  28.4 3.2 %collective-permute-start.11 = (bf16[176,128]{1,0:T(8,128)(2,1)S(1)}, bf16[176,128]{1,0:T(8,128)(2,1)S(1)}, u32[]{:S(2)}, u32[]{:S(2)}) collective-permute-start(bf16[176,128]{1,0:T(8,128)(2,1)S(1)} %pick.5), channel_id=1, source_target_pairs={{0,1},{1,0},{2,3},{3,2},{4,5},{5,4},{6,7},{7,6},{8,9},{9,8},{10,11... | collective-permute-start | bytes 135176 | tf_op jit(solution)/shard_map/ppermute | solution.py:27
  28.4 3.2 %collective-permute-start.14 = (bf16[176,128]{1,0:T(8,128)(2,1)S(1)}, bf16[176,128]{1,0:T(8,128)(2,1)S(1)}, u32[]{:S(2)}, u32[]{:S(2)}) collective-permute-start(bf16[176,128]{1,0:T(8,128)(2,1)S(1)} %pick.4.refs_0_), channel_id=1, source_target_pairs={{0,1},{1,0},{2,3},{3,2},{4,5},{5,4},{6,7},{7,6},{8,9},{9,8},{10,11... | collective-permute-start | bytes 135176 | tf_op jit(solution)/shard_map/ppermute | solution.py:27

commit v11 on v10

--- a/solution.py
+++ b/solution.py
@@ -112,6 +112,22 @@
         cost_estimate=cost(1000),
         name="assemble",
     )(kept, beside, opposite)
+
+
+def gate_kernel(array, _, out):
+    out[...] = array[...]
+
+
+def gate(array, earlier, size):
+    return pl.pallas_call(
+        gate_kernel,
+        out_shape=jax.ShapeDtypeStruct(array.shape, array.dtype),
+        in_specs=[VMEM, HBM],
+        out_specs=VMEM,
+        compiler_params=limit(4 * MB),
+        cost_estimate=cost(size),
+        name="gate",
+    )(array, earlier)
 
 
 def pick_kernel(both, *refs):
@@ -350,10 +366,11 @@
         near_keys = jnp.concatenate([near_keys, swapped(near_keys, bit)], axis=0)
     far_keys = swapped(near_keys, bits[-1])
     halves = []
-    sides = ((0, near_raw, x_own, own_query), (count // 2, far_raw, swapped(picked, 2), far_query))
+    sides = ((0, near_raw, x_own, own_query), (count // 2, far_raw, swapped(picked, 2), own_query))
     for first, this, opposite, earlier in sides:
         kernel = functools.partial(rebuild_values_kernel, heads, first)
         halves.append(rebuild(kernel, block * count // 2, old, this, opposite, old, limits, earlier))
+    far_query = gate(far_query, halves[1], 1000)
     near, far = (near_keys, halves[0]), (far_keys, halves[1])
     parts = ((2, 3), (0,), (1,))
     far_out = attend(heads, parts, far_query, near, far)

time: 33.2 us -> 33.1 us (level)
  no operation moved by 1% of the time
where the time goes in v11:
time: 33.1 us; the launch traced here: 32.8 us
  starting transfers between devices  18.1 us (55%)
  waiting for transfers between devices  8.44 us (25%)
  Pallas kernels  6.15 us (19%)
    ppermute x15, starting transfers between devices, swapped(): return lax.ppermute(array, 'patch', [(i, i ^ mask) for i in range(size)])  18.1 us
    ppermute x15, waiting for transfers between devices, swapped(): return lax.ppermute(array, 'patch', [(i, i ^ mask) for i in range(size)])  8.44 us
    pallas_call x2, Pallas kernels, cut(): pl.pallas_call(functools.partial(cut_kernel, len(slabs), first), out_shap...  1.86 us
    pallas_call x1, Pallas kernels, fetch(): pl.pallas_call(functools.partial(fetch_kernel, heads, count), out_shape=[...  1.29 us
    pallas_call x1, Pallas kernels, merge(): pl.pallas_call(functools.partial(merge_kernel, heads), out_shape=jax.Shap...  1.22 us
    pallas_call x2, Pallas kernels, attend(): pl.pallas_call(functools.partial(attend_kernel, heads, parts), out_shape=...  1.12 us
  transfers between devices with their start and end apart: 15, of which 6 were waited for; matrix products, arithmetic and copies ran while one was open for 0% of the time, Pallas kernels for 10%

profile of v11, /device:TPU:0, one launch (start us, length us, event | category | flops | bytes accessed | tf_op | source)
XLA Modules:
  0.0 32.8 jit_solution(6363223978626415129)
XLA Ops:
  0.0 0.9 %cut.2.refs_3_ = bf16[3,2,32,640]{3,2,1,0:T(8,128)(2,1)S(1)} custom-call(bf16[32,2560]{1,0:T(8,128)(2,1)} %refs_0_.3, bf16[32,2560]{1,0:T(8,128)(2,1)} %refs_1_.3, bf16[32,2560]{1,0:T(8,128)(2,1)} %refs_2_.3), custom_call_target="tpu_custom_call" | custom-call | bytes 1000 | tf_op jit(solution)/shard_map/cut/pallas_call | solution.py:61
  0.9 0.5 %collective-permute-start = (bf16[3,2,32,640]{3,2,1,0:T(8,128)(2,1)S(1)}, bf16[3,2,32,640]{3,2,1,0:T(8,128)(2,1)S(1)}, u32[]{:S(2)}, u32[]{:S(2)}) collective-permute-start(bf16[3,2,32,640]{3,2,1,0:T(8,128)(2,1)S(1)} %cut.2.refs_3_), channel_id=1, source_target_pairs={{0,1},{1,0},{2,3},{3,2},{4,5},{5,4},{6,7},{7,6},{8,9},{9,8},{10,11... | collective-permute-start | bytes 737288 | tf_op jit(solution)/shard_map/ppermute | solution.py:27
  1.5 0.9 %cut.3.kept = bf16[3,2,32,640]{3,2,1,0:T(8,128)(2,1)S(1)} custom-call(bf16[32,2560]{1,0:T(8,128)(2,1)} %refs_0_.3, bf16[32,2560]{1,0:T(8,128)(2,1)} %refs_1_.3, bf16[32,2560]{1,0:T(8,128)(2,1)} %refs_2_.3, bf16[3,2,32,640]{3,2,1,0:T(8,128)(2,1)S(1)} %cut.2.refs_3_), custom_call_target="tpu_custom_call" | custom-call | bytes 1000 | tf_op jit(solution)/shard_map/cut/pallas_call | solution.py:61
  2.6 2.9 %collective-permute-start.1 = (bf16[64,640]{1,0:T(8,128)(2,1)S(1)}, bf16[64,640]{1,0:T(8,128)(2,1)S(1)}, u32[]{:S(2)}, u32[]{:S(2)}) collective-permute-start(bf16[64,640]{1,0:T(8,128)(2,1)S(1)} %get-tuple-element.17), channel_id=1, source_target_pairs={{0,2},{1,3},{2,0},{3,1},{4,6},{5,7},{6,4},{7,5},{8,10},{9,11},{10,... | collective-permute-start | bytes 245768 | tf_op jit(solution)/shard_map/ppermute | solution.py:27
  5.6 1.6 %collective-permute-start.5 = (bf16[2,64,640]{2,1,0:T(8,128)(2,1)S(1)}, bf16[2,64,640]{2,1,0:T(8,128)(2,1)S(1)}, u32[]{:S(2)}, u32[]{:S(2)}) collective-permute-start(bf16[2,64,640]{2,1,0:T(8,128)(2,1)S(1)} %get-tuple-element.21.this), channel_id=1, source_target_pairs={{0,4},{1,5},{2,6},{3,7},{4,0},{5,1},{6,2},{7,3},{8,12},{9,13},{10,... | collective-permute-start | bytes 491528 | tf_op jit(solution)/shard_map/ppermute | solution.py:27
  7.2 0.5 %collective-permute-start.2 = (bf16[64,640]{1,0:T(8,128)(2,1)S(1)}, bf16[64,640]{1,0:T(8,128)(2,1)S(1)}, u32[]{:S(2)}, u32[]{:S(2)}) collective-permute-start(bf16[64,640]{1,0:T(8,128)(2,1)S(1)} %get-tuple-element.18), channel_id=1, source_target_pairs={{0,2},{1,3},{2,0},{3,1},{4,6},{5,7},{6,4},{7,5},{8,10},{9,11},{10,... | collective-permute-start | bytes 245768 | tf_op jit(solution)/shard_map/ppermute | solution.py:27
  7.7 1.3 %fetch.1 = (bf16[3,128,640]{2,1,0:T(8,128)(2,1)S(1)}, f32[3,128,128]{2,1,0:T(8,128)S(1)}) custom-call(bf16[1,512,640]{2,1,0:T(8,128)(2,1)} %keys_copy.1, bf16[1,512,640]{2,1,0:T(8,128)(2,1)} %values_copy.1, f32[20,512]{1,0:T(8,128)S(1)} %bitcast.4, f32[20,512]{1,0:T(8,128)S(1)} %bitcast.5), custom_call_target="tpu_custom_call" | custom-call | bytes 1000 | tf_op jit(solution)/shard_map/fetch/pallas_call | solution.py:170
  9.0 2.7 %collective-permute-start.7 = (bf16[128,640]{1,0:T(8,128)(2,1)S(1)}, bf16[128,640]{1,0:T(8,128)(2,1)S(1)}, u32[]{:S(2)}, u32[]{:S(2)}) collective-permute-start(bf16[128,640]{1,0:T(8,128)(2,1)S(1)} %assemble.1._.refs_0_.query_ref), channel_id=1, source_target_pairs={{0,8},{1,9},{2,10},{3,11},{4,12},{5,13},{6,14},{7,15},{8,0},{9,1},... | collective-permute-start | bytes 491528 | tf_op jit(solution)/shard_map/ppermute | solution.py:27
  11.9 1.6 %collective-permute-start.4 = (bf16[128,640]{1,0:T(8,128)(2,1)S(1)}, bf16[128,640]{1,0:T(8,128)(2,1)S(1)}, u32[]{:S(2)}, u32[]{:S(2)}) collective-permute-start(bf16[128,640]{1,0:T(8,128)(2,1)S(1)} %rebuild.3.refs_0_.near_keys), channel_id=1, source_target_pairs={{0,4},{1,5},{2,6},{3,7},{4,0},{5,1},{6,2},{7,3},{8,12},{9,13},{10,... | collective-permute-start | bytes 491528 | tf_op jit(solution)/shard_map/ppermute | solution.py:27
  13.5 1.9 %collective-permute-start.3 = (bf16[64,640]{1,0:T(8,128)(2,1)S(1)}, bf16[64,640]{1,0:T(8,128)(2,1)S(1)}, u32[]{:S(2)}, u32[]{:S(2)}) collective-permute-start(bf16[64,640]{1,0:T(8,128)(2,1)S(1)} %get-tuple-element.22), channel_id=1, source_target_pairs={{0,2},{1,3},{2,0},{3,1},{4,6},{5,7},{6,4},{7,5},{8,10},{9,11},{10,... | collective-permute-start | bytes 245768 | tf_op jit(solution)/shard_map/ppermute | solution.py:27
  15.4 0.2 collective-permute-start.6
  15.6 2.3 %collective-permute-done.3.opposite = bf16[64,640]{1,0:T(8,128)(2,1)S(1)} collective-permute-done((bf16[64,640]{1,0:T(8,128)(2,1)S(1)}, bf16[64,640]{1,0:T(8,128)(2,1)S(1)}, u32[]{:S(2)}, u32[]{:S(2)}) %collective-permute-start.3) | collective-permute-done | bytes 81952 | tf_op jit(solution)/shard_map/ppermute | solution.py:27
  18.1 1.7 %collective-permute-done.6.opposite = bf16[64,640]{1,0:T(8,128)(2,1)S(1)} collective-permute-done((bf16[64,640]{1,0:T(8,128)(2,1)S(1)}, bf16[64,640]{1,0:T(8,128)(2,1)S(1)}, u32[]{:S(2)}, u32[]{:S(2)}) %collective-permute-start.6) | collective-permute-done | bytes 81952 | tf_op jit(solution)/shard_map/ppermute | solution.py:27
  20.1 0.6 %attend.2 = (bf16[2,176,128]{2,1,0:T(8,128)(2,1)S(1)}, bf16[1,176,128]{2,1,0:T(8,128)(2,1)S(1)}, bf16[1,176,128]{2,1,0:T(8,128)(2,1)S(1)}) custom-call(bf16[128,640]{1,0:T(8,128)(2,1)S(1)} %gate.1.query_ref, bf16[128,640]{1,0:T(8,128)(2,1)S(1)} %rebuild.3.refs_0_.near_keys, bf16[128,640]{1,0:T(8,128)(2,1)S(1)} %rebuild.4.near_values, ...), custom_call_target="tpu_custom_call" | custom-call | bytes 1000 | tf_op jit(solution)/shard_map/attend/pallas_call | solution.py:282
  20.7 1.6 %collective-permute-start.10 = (bf16[2,176,128]{2,1,0:T(8,128)(2,1)S(1)}, bf16[2,176,128]{2,1,0:T(8,128)(2,1)S(1)}, u32[]{:S(2)}, u32[]{:S(2)}) collective-permute-start(bf16[2,176,128]{2,1,0:T(8,128)(2,1)S(1)} %get-tuple-element.27), channel_id=1, source_target_pairs={{0,10},{1,11},{2,8},{3,9},{4,14},{5,15},{6,12},{7,13},{8,2},{9,3},... | collective-permute-start | bytes 270344 | tf_op jit(solution)/shard_map/ppermute | solution.py:27
  22.3 0.6 %attend.3 = (bf16[1,176,128]{2,1,0:T(8,128)(2,1)S(1)}, bf16[1,176,128]{2,1,0:T(8,128)(2,1)S(1)}, bf16[2,176,128]{2,1,0:T(8,128)(2,1)S(1)}) custom-call(bf16[128,640]{1,0:T(8,128)(2,1)S(1)} %assemble.1._.refs_0_.query_ref, bf16[128,640]{1,0:T(8,128)(2,1)S(1)} %rebuild.3.refs_0_.near_keys, bf16[128,640]{1,0:T(8,128)(2,1)S(1)} %rebuild.4.near_values, ...), custom_call_target="tpu_custom_call" | custom-call | bytes 1000 | tf_op jit(solution)/shard_map/attend/pallas_call | solution.py:282
  22.9 1.0 %collective-permute-start.9 = (bf16[2,176,128]{2,1,0:T(8,128)(2,1)S(1)}, bf16[2,176,128]{2,1,0:T(8,128)(2,1)S(1)}, u32[]{:S(2)}, u32[]{:S(2)}) collective-permute-start(bf16[2,176,128]{2,1,0:T(8,128)(2,1)S(1)} %get-tuple-element.26), channel_id=1, source_target_pairs={{0,2},{1,3},{2,0},{3,1},{4,6},{5,7},{6,4},{7,5},{8,10},{9,11},{10,... | collective-permute-start | bytes 270344 | tf_op jit(solution)/shard_map/ppermute | solution.py:27
  23.9 2.0 %collective-permute-start.8 = (bf16[1,176,128]{2,1,0:T(8,128)(2,1)S(1)}, bf16[1,176,128]{2,1,0:T(8,128)(2,1)S(1)}, u32[]{:S(2)}, u32[]{:S(2)}) collective-permute-start(bf16[1,176,128]{2,1,0:T(8,128)(2,1)S(1)} %get-tuple-element.25), channel_id=1, source_target_pairs={{0,1},{1,0},{2,3},{3,2},{4,5},{5,4},{6,7},{7,6},{8,9},{9,8},{10,11... | collective-permute-start | bytes 135176 | tf_op jit(solution)/shard_map/ppermute | solution.py:27
  25.8 1.1 %collective-permute-start.12 = (bf16[1,176,128]{2,1,0:T(8,128)(2,1)S(1)}, bf16[1,176,128]{2,1,0:T(8,128)(2,1)S(1)}, u32[]{:S(2)}, u32[]{:S(2)}) collective-permute-start(bf16[1,176,128]{2,1,0:T(8,128)(2,1)S(1)} %get-tuple-element.28), channel_id=1, source_target_pairs={{0,8},{1,9},{2,10},{3,11},{4,12},{5,13},{6,14},{7,15},{8,0},{9,1},... | collective-permute-start | bytes 135176 | tf_op jit(solution)/shard_map/ppermute | solution.py:27
  26.9 1.2 %collective-permute-done.10.both.f2 = bf16[2,176,128]{2,1,0:T(8,128)(2,1)S(1)} collective-permute-done((bf16[2,176,128]{2,1,0:T(8,128)(2,1)S(1)}, bf16[2,176,128]{2,1,0:T(8,128)(2,1)S(1)}, u32[]{:S(2)}, u32[]{:S(2)}) %collective-permute-start.10) | collective-permute-done | bytes 90144 | tf_op jit(solution)/shard_map/ppermute | solution.py:27
  28.1 0.3 collective-permute-done.9.both.n2
  28.4 0.5 %collective-permute-start.14 = (bf16[176,128]{1,0:T(8,128)(2,1)S(1)}, bf16[176,128]{1,0:T(8,128)(2,1)S(1)}, u32[]{:S(2)}, u32[]{:S(2)}) collective-permute-start(bf16[176,128]{1,0:T(8,128)(2,1)S(1)} %pick.4.refs_0_), channel_id=1, source_target_pairs={{0,1},{1,0},{2,3},{3,2},{4,5},{5,4},{6,7},{7,6},{8,9},{9,8},{10,11... | collective-permute-start | bytes 135176 | tf_op jit(solution)/shard_map/ppermute | solution.py:27
  28.9 2.7 %collective-permute-done.12.f0 = bf16[1,176,128]{2,1,0:T(8,128)(2,1)S(1)} collective-permute-done((bf16[1,176,128]{2,1,0:T(8,128)(2,1)S(1)}, bf16[1,176,128]{2,1,0:T(8,128)(2,1)S(1)}, u32[]{:S(2)}, u32[]{:S(2)}) %collective-permute-start.12) | collective-permute-done | bytes 45088 | tf_op jit(solution)/shard_map/ppermute | solution.py:27
  31.6 1.2 %merge.1 = bf16[32,2560]{1,0:T(8,128)(2,1)} custom-call(bf16[1,176,128]{2,1,0:T(8,128)(2,1)S(1)} %get-tuple-element.24.n0, bf16[1,176,128]{2,1,0:T(8,128)(2,1)S(1)} %collective-permute-done.8.n1, bf16[2,176,128]{2,1,0:T(8,128)(2,1)S(1)} %collective-permute-done.9.both.n2, bf16[1,176,128]{2,1,0:T(8,128)(2,1)S(1)} %bitcast.6, ...), custom_call_target="tpu_custom_call" | custom-call | bytes 1000 | tf_op jit(solution)/shard_map/merge/pallas_call | solution.py:327
  (25 shorter events, 0.9 us)
Async XLA Ops:
  0.9 1.7 %collective-permute-start = (bf16[3,2,32,640]{3,2,1,0:T(8,128)(2,1)S(1)}, bf16[3,2,32,640]{3,2,1,0:T(8,128)(2,1)S(1)}, u32[]{:S(2)}, u32[]{:S(2)}) collective-permute-start(bf16[3,2,32,640]{3,2,1,0:T(8,128)(2,1)S(1)} %cut.2.refs_3_), channel_id=1, source_target_pairs={{0,1},{1,0},{2,3},{3,2},{4,5},{5,4},{6,7},{7,6},{8,9},{9,8},{10,11... | collective-permute-start | bytes 737288 | tf_op jit(solution)/shard_map/ppermute | solution.py:27
  2.4 5.3 %copy-start = (f32[512,20]{0,1:T(8,128)S(1)}, f32[512,20]{0,1:T(8,128)}, u32[]{:S(2)}) copy-start(f32[512,20]{0,1:T(8,128)} %param.12) | copy-start | bytes 122884
  2.4 5.3 %copy-start.1 = (f32[512,20]{0,1:T(8,128)S(1)}, f32[512,20]{0,1:T(8,128)}, u32[]{:S(2)}) copy-start(f32[512,20]{0,1:T(8,128)} %param.13) | copy-start | bytes 122884
  2.6 6.3 %collective-permute-start.1 = (bf16[64,640]{1,0:T(8,128)(2,1)S(1)}, bf16[64,640]{1,0:T(8,128)(2,1)S(1)}, u32[]{:S(2)}, u32[]{:S(2)}) collective-permute-start(bf16[64,640]{1,0:T(8,128)(2,1)S(1)} %get-tuple-element.17), channel_id=1, source_target_pairs={{0,2},{1,3},{2,0},{3,1},{4,6},{5,7},{6,4},{7,5},{8,10},{9,11},{10,... | collective-permute-start | bytes 245768 | tf_op jit(solution)/shard_map/ppermute | solution.py:27
  5.6 9.8 %collective-permute-start.5 = (bf16[2,64,640]{2,1,0:T(8,128)(2,1)S(1)}, bf16[2,64,640]{2,1,0:T(8,128)(2,1)S(1)}, u32[]{:S(2)}, u32[]{:S(2)}) collective-permute-start(bf16[2,64,640]{2,1,0:T(8,128)(2,1)S(1)} %get-tuple-element.21.this), channel_id=1, source_target_pairs={{0,4},{1,5},{2,6},{3,7},{4,0},{5,1},{6,2},{7,3},{8,12},{9,13},{10,... | collective-permute-start | bytes 491528 | tf_op jit(solution)/shard_map/ppermute | solution.py:27
  7.2 4.5 %collective-permute-start.2 = (bf16[64,640]{1,0:T(8,128)(2,1)S(1)}, bf16[64,640]{1,0:T(8,128)(2,1)S(1)}, u32[]{:S(2)}, u32[]{:S(2)}) collective-permute-start(bf16[64,640]{1,0:T(8,128)(2,1)S(1)} %get-tuple-element.18), channel_id=1, source_target_pairs={{0,2},{1,3},{2,0},{3,1},{4,6},{5,7},{6,4},{7,5},{8,10},{9,11},{10,... | collective-permute-start | bytes 245768 | tf_op jit(solution)/shard_map/ppermute | solution.py:27
  9.0 11.1 %collective-permute-start.7 = (bf16[128,640]{1,0:T(8,128)(2,1)S(1)}, bf16[128,640]{1,0:T(8,128)(2,1)S(1)}, u32[]{:S(2)}, u32[]{:S(2)}) collective-permute-start(bf16[128,640]{1,0:T(8,128)(2,1)S(1)} %assemble.1._.refs_0_.query_ref), channel_id=1, source_target_pairs={{0,8},{1,9},{2,10},{3,11},{4,12},{5,13},{6,14},{7,15},{8,0},{9,1},... | collective-permute-start | bytes 491528 | tf_op jit(solution)/shard_map/ppermute | solution.py:27
  11.9 8.3 %collective-permute-start.4 = (bf16[128,640]{1,0:T(8,128)(2,1)S(1)}, bf16[128,640]{1,0:T(8,128)(2,1)S(1)}, u32[]{:S(2)}, u32[]{:S(2)}) collective-permute-start(bf16[128,640]{1,0:T(8,128)(2,1)S(1)} %rebuild.3.refs_0_.near_keys), channel_id=1, source_target_pairs={{0,4},{1,5},{2,6},{3,7},{4,0},{5,1},{6,2},{7,3},{8,12},{9,13},{10,... | collective-permute-start | bytes 491528 | tf_op jit(solution)/shard_map/ppermute | solution.py:27
  13.5 4.4 %collective-permute-start.3 = (bf16[64,640]{1,0:T(8,128)(2,1)S(1)}, bf16[64,640]{1,0:T(8,128)(2,1)S(1)}, u32[]{:S(2)}, u32[]{:S(2)}) collective-permute-start(bf16[64,640]{1,0:T(8,128)(2,1)S(1)} %get-tuple-element.22), channel_id=1, source_target_pairs={{0,2},{1,3},{2,0},{3,1},{4,6},{5,7},{6,4},{7,5},{8,10},{9,11},{10,... | collective-permute-start | bytes 245768 | tf_op jit(solution)/shard_map/ppermute | solution.py:27
  15.4 4.5 %collective-permute-start.6 = (bf16[64,640]{1,0:T(8,128)(2,1)S(1)}, bf16[64,640]{1,0:T(8,128)(2,1)S(1)}, u32[]{:S(2)}, u32[]{:S(2)}) collective-permute-start(bf16[64,640]{1,0:T(8,128)(2,1)S(1)} %pick.3), channel_id=1, source_target_pairs={{0,2},{1,3},{2,0},{3,1},{4,6},{5,7},{6,4},{7,5},{8,10},{9,11},{10,... | collective-permute-start | bytes 245768 | tf_op jit(solution)/shard_map/ppermute | solution.py:27
  20.7 7.4 %collective-permute-start.10 = (bf16[2,176,128]{2,1,0:T(8,128)(2,1)S(1)}, bf16[2,176,128]{2,1,0:T(8,128)(2,1)S(1)}, u32[]{:S(2)}, u32[]{:S(2)}) collective-permute-start(bf16[2,176,128]{2,1,0:T(8,128)(2,1)S(1)} %get-tuple-element.27), channel_id=1, source_target_pairs={{0,10},{1,11},{2,8},{3,9},{4,14},{5,15},{6,12},{7,13},{8,2},{9,3},... | collective-permute-start | bytes 270344 | tf_op jit(solution)/shard_map/ppermute | solution.py:27
  22.9 5.5 %collective-permute-start.9 = (bf16[2,176,128]{2,1,0:T(8,128)(2,1)S(1)}, bf16[2,176,128]{2,1,0:T(8,128)(2,1)S(1)}, u32[]{:S(2)}, u32[]{:S(2)}) collective-permute-start(bf16[2,176,128]{2,1,0:T(8,128)(2,1)S(1)} %get-tuple-element.26), channel_id=1, source_target_pairs={{0,2},{1,3},{2,0},{3,1},{4,6},{5,7},{6,4},{7,5},{8,10},{9,11},{10,... | collective-permute-start | bytes 270344 | tf_op jit(solution)/shard_map/ppermute | solution.py:27
  23.8 7.7 %collective-permute-start.13 = (bf16[1,176,128]{2,1,0:T(8,128)(2,1)S(1)}, bf16[1,176,128]{2,1,0:T(8,128)(2,1)S(1)}, u32[]{:S(2)}, u32[]{:S(2)}) collective-permute-start(bf16[1,176,128]{2,1,0:T(8,128)(2,1)S(1)} %get-tuple-element.23.refs_0_), channel_id=1, source_target_pairs={{0,9},{1,8},{2,11},{3,10},{4,13},{5,12},{6,15},{7,14},{8,1},{9,0},... | collective-permute-start | bytes 135176 | tf_op jit(solution)/shard_map/ppermute | solution.py:27
  23.9 5.1 %collective-permute-start.8 = (bf16[1,176,128]{2,1,0:T(8,128)(2,1)S(1)}, bf16[1,176,128]{2,1,0:T(8,128)(2,1)S(1)}, u32[]{:S(2)}, u32[]{:S(2)}) collective-permute-start(bf16[1,176,128]{2,1,0:T(8,128)(2,1)S(1)} %get-tuple-element.25), channel_id=1, source_target_pairs={{0,1},{1,0},{2,3},{3,2},{4,5},{5,4},{6,7},{7,6},{8,9},{9,8},{10,11... | collective-permute-start | bytes 135176 | tf_op jit(solution)/shard_map/ppermute | solution.py:27
  25.8 5.8 %collective-permute-start.12 = (bf16[1,176,128]{2,1,0:T(8,128)(2,1)S(1)}, bf16[1,176,128]{2,1,0:T(8,128)(2,1)S(1)}, u32[]{:S(2)}, u32[]{:S(2)}) collective-permute-start(bf16[1,176,128]{2,1,0:T(8,128)(2,1)S(1)} %get-tuple-element.28), channel_id=1, source_target_pairs={{0,8},{1,9},{2,10},{3,11},{4,12},{5,13},{6,14},{7,15},{8,0},{9,1},... | collective-permute-start | bytes 135176 | tf_op jit(solution)/shard_map/ppermute | solution.py:27
  28.4 3.2 %collective-permute-start.11 = (bf16[176,128]{1,0:T(8,128)(2,1)S(1)}, bf16[176,128]{1,0:T(8,128)(2,1)S(1)}, u32[]{:S(2)}, u32[]{:S(2)}) collective-permute-start(bf16[176,128]{1,0:T(8,128)(2,1)S(1)} %pick.5), channel_id=1, source_target_pairs={{0,1},{1,0},{2,3},{3,2},{4,5},{5,4},{6,7},{7,6},{8,9},{9,8},{10,11... | collective-permute-start | bytes 135176 | tf_op jit(solution)/shard_map/ppermute | solution.py:27
  28.4 3.2 %collective-permute-start.14 = (bf16[176,128]{1,0:T(8,128)(2,1)S(1)}, bf16[176,128]{1,0:T(8,128)(2,1)S(1)}, u32[]{:S(2)}, u32[]{:S(2)}) collective-permute-start(bf16[176,128]{1,0:T(8,128)(2,1)S(1)} %pick.4.refs_0_), channel_id=1, source_target_pairs={{0,1},{1,0},{2,3},{3,2},{4,5},{5,4},{6,7},{7,6},{8,9},{9,8},{10,11... | collective-permute-start | bytes 135176 | tf_op jit(solution)/shard_map/ppermute | solution.py:27

commit v12 on v8

--- a/solution.py
+++ b/solution.py
@@ -113,6 +113,22 @@
         cost_estimate=cost(1000),
         name="assemble",
     )(kept, beside, opposite)
+
+
+def gate_kernel(array, out):
+    out[...] = array[...]
+
+
+def gate(array):
+    return pl.pallas_call(
+        gate_kernel,
+        out_shape=jax.ShapeDtypeStruct(array.shape, array.dtype),
+        in_specs=[VMEM],
+        out_specs=VMEM,
+        compiler_params=limit(4 * MB),
+        cost_estimate=cost(20_000_000),
+        name="gate",
+    )(array)
 
 
 def pick_kernel(both, *refs):
@@ -275,49 +291,74 @@
     )(query, *near, *far, *earlier)
 
 
-def merge_kernel(heads, n0, n1, n2, n3, f0, f1, f2, f3, out):
-    rows = out.shape[0]
-    head = n0.shape[2]
-    width = heads * head
+def unpack(ref, heads, rows):
+    head = ref.shape[2]
+    packed = ref[0, heads * rows :, :].astype(jnp.float32)
+    stats = jnp.concatenate([packed, pltpu.roll(packed, head - 16, 1)], axis=0)
+    weight = pltpu.roll(stats, head - heads, 1) + pltpu.roll(stats, head - 2 * heads, 1)
+    return stats, weight
+
+
+def mix(heads, near, far, out):
+    rows, width = out.shape
+    head = width // heads
+    near_level, near_weight = unpack(near, heads, rows)
+    far_level, far_weight = unpack(far, heads, rows)
+    top = jnp.maximum(near_level, far_level)
+    near_scale = jnp.exp2(near_level - top)
+    far_scale = jnp.exp2(far_level - top)
+    total = near_scale * near_weight + far_scale * far_weight
+    near_scale = near_scale / total
+    far_scale = far_scale / total
+    for h in range(heads):
+        place = slice(h * rows, (h + 1) * rows)
+        mixed = near[0, place, :].astype(jnp.float32) * near_scale[:, h : h + 1]
+        mixed = mixed + far[0, place, :].astype(jnp.float32) * far_scale[:, h : h + 1]
+        out[:, h * head : (h + 1) * head] = mixed.astype(out.dtype)
+
+
+def mix_kernel(heads, n2, f2, n3, f3, out):
+    mix(heads, n2, f2, out.at[0])
+    mix(heads, n3, f3, out.at[1])
+
+
+def merge_kernel(heads, n0, f0, n1, f1, done, out, mixture, sems):
     _, member = position()
-
-    def unpack(ref):
-        packed = ref[0, heads * rows :, :].astype(jnp.float32)
-        stats = jnp.concatenate([packed, pltpu.roll(packed, head - 16, 1)], axis=0)
-        weight = pltpu.roll(stats, head - heads, 1) + pltpu.roll(stats, head - 2 * heads, 1)
-        return stats, weight
-
-    mixtures = []
-    for k, (near, far) in enumerate(((n0, f0), (n1, f1), (n2, f2), (n3, f3))):
-        near_level, near_weight = unpack(near)
-        far_level, far_weight = unpack(far)
-        top = jnp.maximum(near_level, far_level)
-        near_scale = jnp.exp2(near_level - top)
-        far_scale = jnp.exp2(far_level - top)
-        total = near_scale * near_weight + far_scale * far_weight
-        near_scale = near_scale / total
-        far_scale = far_scale / total
-        for h in range(heads):
-            place = slice(h * rows, (h + 1) * rows)
-            mixed = near[0, place, :].astype(jnp.float32) * near_scale[:, h : h + 1]
-            mixed = mixed + far[0, place, :].astype(jnp.float32) * far_scale[:, h : h + 1]
-            mixtures.append((k, h, mixed.astype(out.dtype)))
-    for k, h, mixed in mixtures:
-        start = pl.multiple_of((member ^ k) * width + h * head, head)
-        out[:, pl.ds(start, head)] = mixed
+    width = mixture.shape[2]
+    copies = []
+    for k in (2, 3, 0, 1):
+        if k < 2:
+            mix(heads, (n0, n1)[k], (f0, f1)[k], mixture.at[k])
+        source = mixture.at[k] if k < 2 else done.at[k - 2]
+        copies.append(pltpu.make_async_copy(source, out.at[:, part(member ^ k, width)], sems.at[k]))
+        copies[-1].start()
+    for copy in copies:
+        copy.wait()
 
 
 def merge(heads, near, far, rows):
     head = near[0].shape[2]
+    kind = near[0].dtype
+    half = (2, rows, heads * head)
+    done = pl.pallas_call(
+        functools.partial(mix_kernel, heads),
+        out_shape=jax.ShapeDtypeStruct(half, kind),
+        in_specs=[VMEM] * 4,
+        out_specs=VMEM,
+        compiler_params=limit(4 * MB),
+        cost_estimate=cost(1000),
+        name="mix",
+    )(near[2], far[2], near[3], far[3])
     return pl.pallas_call(
         functools.partial(merge_kernel, heads),
-        out_shape=jax.ShapeDtypeStruct((rows, GROUP * heads * head), near[0].dtype),
-        in_specs=[VMEM] * 8,
-        out_specs=VMEM,
+        out_shape=jax.ShapeDtypeStruct((rows, GROUP * heads * head), kind),
+        in_specs=[VMEM] * 5,
+        out_specs=HBM,
+        scratch_shapes=[pltpu.VMEM(half, kind), pltpu.SemaphoreType.DMA((GROUP,))],
         compiler_params=limit(4 * MB),
         cost_estimate=cost(1000),
         name="merge",
-    )(*near, *far)
+    )(near[0], far[0], near[1], far[1], done)
 
 
 def shards(queries, keys_new, values_new, keys_copy, values_copy, key_bounds, value_bounds):
@@ -363,8 +404,8 @@
     n1, n23 = swapped(n1, 1), swapped(n23, 2)
     f3 = pick(f23)
     n3 = pick(n23, f3)
-    near_parts = (n0, n1, n23, swapped(n3, 1)[None])
-    far_parts = (f0, f1, f23, swapped(f3, 1)[None])
+    near_parts = (n0, gate(n1), n23, swapped(n3, 1)[None])
+    far_parts = (gate(f0), gate(f1), f23, swapped(f3, 1)[None])
     return merge(heads, near_parts, far_parts, rows)
 
 

time: 33.3 us -> 33.3 us (level)
  transfers between devices with their start and end apart: 15 -> 15, of which waited for: 6 -> 6; matrix products, arithmetic and copies ran while one was open for 0% -> 0% of each run, Pallas kernels for 7% -> 8%
where the time goes in v12:
time: 33.3 us; the launch traced here: 33 us
  starting transfers between devices  18.1 us (54%)
  waiting for transfers between devices  9.41 us (28%)
  Pallas kernels  5.4 us (16%)
    ppermute x15, starting transfers between devices, swapped(): return lax.ppermute(array, 'patch', [(i, i ^ mask) for i in range(size)])  18.1 us
    ppermute x15, waiting for transfers between devices, swapped(): return lax.ppermute(array, 'patch', [(i, i ^ mask) for i in range(size)])  9.41 us
    pallas_call x1, Pallas kernels, fetch(): pl.pallas_call(functools.partial(fetch_kernel, heads, count), out_shape=[...  1.29 us
    pallas_call x2, Pallas kernels, attend(): pl.pallas_call(functools.partial(attend_kernel, heads, parts), out_shape=...  1.15 us
    pallas_call x1, Pallas kernels, cut(): pl.pallas_call(functools.partial(cut_kernel, len(slabs)), out_shape=[shap...  1.11 us
    pallas_call x1, Pallas kernels, merge(): pl.pallas_call(functools.partial(merge_kernel, heads), out_shape=jax.Shap...  0.93 us
  transfers between devices with their start and end apart: 15, of which 6 were waited for; matrix products, arithmetic and copies ran while one was open for 0% of the time, Pallas kernels for 8%

profile of v12, /device:TPU:0, one launch (start us, length us, event | category | flops | bytes accessed | tf_op | source)
XLA Modules:
  0.0 33.0 jit_solution(8856241040921210125)
XLA Ops:
  0.0 1.1 %cut.1 = (bf16[3,2,32,640]{3,2,1,0:T(8,128)(2,1)S(1)}, bf16[3,2,32,640]{3,2,1,0:T(8,128)(2,1)S(1)}) custom-call(bf16[32,2560]{1,0:T(8,128)(2,1)} %refs_0_.1, bf16[32,2560]{1,0:T(8,128)(2,1)} %refs_1_.1, bf16[32,2560]{1,0:T(8,128)(2,1)} %refs_2_.1), custom_call_target="tpu_custom_call" | custom-call | bytes 1000 | tf_op jit(solution)/shard_map/cut/pallas_call | solution.py:62
  1.1 0.5 %collective-permute-start = (bf16[3,2,32,640]{3,2,1,0:T(8,128)(2,1)S(1)}, bf16[3,2,32,640]{3,2,1,0:T(8,128)(2,1)S(1)}, u32[]{:S(2)}, u32[]{:S(2)}) collective-permute-start(bf16[3,2,32,640]{3,2,1,0:T(8,128)(2,1)S(1)} %get-tuple-element.20), channel_id=1, source_target_pairs={{0,1},{1,0},{2,3},{3,2},{4,5},{5,4},{6,7},{7,6},{8,9},{9,8},{10,11... | collective-permute-start | bytes 737288 | tf_op jit(solution)/shard_map/ppermute | solution.py:27
  1.6 1.1 %collective-permute-done.arrived.beside = bf16[3,2,32,640]{3,2,1,0:T(8,128)(2,1)S(1)} collective-permute-done((bf16[3,2,32,640]{3,2,1,0:T(8,128)(2,1)S(1)}, bf16[3,2,32,640]{3,2,1,0:T(8,128)(2,1)S(1)}, u32[]{:S(2)}, u32[]{:S(2)}) %collective-permute-start) | collective-permute-done | bytes 245792 | tf_op jit(solution)/shard_map/ppermute | solution.py:27
  2.8 2.9 %collective-permute-start.1 = (bf16[64,640]{1,0:T(8,128)(2,1)S(1)}, bf16[64,640]{1,0:T(8,128)(2,1)S(1)}, u32[]{:S(2)}, u32[]{:S(2)}) collective-permute-start(bf16[64,640]{1,0:T(8,128)(2,1)S(1)} %get-tuple-element.21), channel_id=1, source_target_pairs={{0,2},{1,3},{2,0},{3,1},{4,6},{5,7},{6,4},{7,5},{8,10},{9,11},{10,... | collective-permute-start | bytes 245768 | tf_op jit(solution)/shard_map/ppermute | solution.py:27
  5.7 1.6 %collective-permute-start.5 = (bf16[2,64,640]{2,1,0:T(8,128)(2,1)S(1)}, bf16[2,64,640]{2,1,0:T(8,128)(2,1)S(1)}, u32[]{:S(2)}, u32[]{:S(2)}) collective-permute-start(bf16[2,64,640]{2,1,0:T(8,128)(2,1)S(1)} %get-tuple-element.25.this), channel_id=1, source_target_pairs={{0,4},{1,5},{2,6},{3,7},{4,0},{5,1},{6,2},{7,3},{8,12},{9,13},{10,... | collective-permute-start | bytes 491528 | tf_op jit(solution)/shard_map/ppermute | solution.py:27
  7.3 0.5 %collective-permute-start.2 = (bf16[64,640]{1,0:T(8,128)(2,1)S(1)}, bf16[64,640]{1,0:T(8,128)(2,1)S(1)}, u32[]{:S(2)}, u32[]{:S(2)}) collective-permute-start(bf16[64,640]{1,0:T(8,128)(2,1)S(1)} %get-tuple-element.22), channel_id=1, source_target_pairs={{0,2},{1,3},{2,0},{3,1},{4,6},{5,7},{6,4},{7,5},{8,10},{9,11},{10,... | collective-permute-start | bytes 245768 | tf_op jit(solution)/shard_map/ppermute | solution.py:27
  7.9 1.3 %fetch.1 = (bf16[3,128,640]{2,1,0:T(8,128)(2,1)S(1)}, f32[3,128,128]{2,1,0:T(8,128)S(1)}) custom-call(bf16[1,512,640]{2,1,0:T(8,128)(2,1)} %keys_copy.1, bf16[1,512,640]{2,1,0:T(8,128)(2,1)} %values_copy.1, f32[20,512]{1,0:T(8,128)S(1)} %bitcast.4, f32[20,512]{1,0:T(8,128)S(1)} %bitcast.5), custom_call_target="tpu_custom_call" | custom-call | bytes 1000 | tf_op jit(solution)/shard_map/fetch/pallas_call | solution.py:171
  9.2 2.7 %collective-permute-start.7 = (bf16[128,640]{1,0:T(8,128)(2,1)S(1)}, bf16[128,640]{1,0:T(8,128)(2,1)S(1)}, u32[]{:S(2)}, u32[]{:S(2)}) collective-permute-start(bf16[128,640]{1,0:T(8,128)(2,1)S(1)} %assemble.1._.refs_0_.query_ref), channel_id=1, source_target_pairs={{0,8},{1,9},{2,10},{3,11},{4,12},{5,13},{6,14},{7,15},{8,0},{9,1},... | collective-permute-start | bytes 491528 | tf_op jit(solution)/shard_map/ppermute | solution.py:27
  12.0 1.6 %collective-permute-start.4 = (bf16[128,640]{1,0:T(8,128)(2,1)S(1)}, bf16[128,640]{1,0:T(8,128)(2,1)S(1)}, u32[]{:S(2)}, u32[]{:S(2)}) collective-permute-start(bf16[128,640]{1,0:T(8,128)(2,1)S(1)} %rebuild.3.refs_0_.near_keys), channel_id=1, source_target_pairs={{0,4},{1,5},{2,6},{3,7},{4,0},{5,1},{6,2},{7,3},{8,12},{9,13},{10,... | collective-permute-start | bytes 491528 | tf_op jit(solution)/shard_map/ppermute | solution.py:27
  13.7 1.9 %collective-permute-start.3 = (bf16[64,640]{1,0:T(8,128)(2,1)S(1)}, bf16[64,640]{1,0:T(8,128)(2,1)S(1)}, u32[]{:S(2)}, u32[]{:S(2)}) collective-permute-start(bf16[64,640]{1,0:T(8,128)(2,1)S(1)} %get-tuple-element.26), channel_id=1, source_target_pairs={{0,2},{1,3},{2,0},{3,1},{4,6},{5,7},{6,4},{7,5},{8,10},{9,11},{10,... | collective-permute-start | bytes 245768 | tf_op jit(solution)/shard_map/ppermute | solution.py:27
  15.8 2.3 %collective-permute-done.3.opposite = bf16[64,640]{1,0:T(8,128)(2,1)S(1)} collective-permute-done((bf16[64,640]{1,0:T(8,128)(2,1)S(1)}, bf16[64,640]{1,0:T(8,128)(2,1)S(1)}, u32[]{:S(2)}, u32[]{:S(2)}) %collective-permute-start.3) | collective-permute-done | bytes 81952 | tf_op jit(solution)/shard_map/ppermute | solution.py:27
  18.3 1.7 %collective-permute-done.6.opposite = bf16[64,640]{1,0:T(8,128)(2,1)S(1)} collective-permute-done((bf16[64,640]{1,0:T(8,128)(2,1)S(1)}, bf16[64,640]{1,0:T(8,128)(2,1)S(1)}, u32[]{:S(2)}, u32[]{:S(2)}) %collective-permute-start.6) | collective-permute-done | bytes 81952 | tf_op jit(solution)/shard_map/ppermute | solution.py:27
  20.3 0.6 %attend.2 = (bf16[2,176,128]{2,1,0:T(8,128)(2,1)S(1)}, bf16[1,176,128]{2,1,0:T(8,128)(2,1)S(1)}, bf16[1,176,128]{2,1,0:T(8,128)(2,1)S(1)}) custom-call(bf16[128,640]{1,0:T(8,128)(2,1)S(1)} %collective-permute-done.7.refs_0_.query_ref, bf16[128,640]{1,0:T(8,128)(2,1)S(1)} %rebuild.3.refs_0_.near_keys, bf16[128,640]{1,0:T(8,128)(2,1)S(1)} %rebuild.4.near_values, ...), custom_call_target="tpu_custom_call" | custom-call | bytes 1000 | tf_op jit(solution)/shard_map/attend/pallas_call | solution.py:283
  20.8 1.7 %collective-permute-start.12 = (bf16[2,176,128]{2,1,0:T(8,128)(2,1)S(1)}, bf16[2,176,128]{2,1,0:T(8,128)(2,1)S(1)}, u32[]{:S(2)}, u32[]{:S(2)}) collective-permute-start(bf16[2,176,128]{2,1,0:T(8,128)(2,1)S(1)} %get-tuple-element.32), channel_id=1, source_target_pairs={{0,10},{1,11},{2,8},{3,9},{4,14},{5,15},{6,12},{7,13},{8,2},{9,3},... | collective-permute-start | bytes 270344 | tf_op jit(solution)/shard_map/ppermute | solution.py:27
  22.5 0.6 %attend.3 = (bf16[1,176,128]{2,1,0:T(8,128)(2,1)S(1)}, bf16[1,176,128]{2,1,0:T(8,128)(2,1)S(1)}, bf16[2,176,128]{2,1,0:T(8,128)(2,1)S(1)}) custom-call(bf16[128,640]{1,0:T(8,128)(2,1)S(1)} %assemble.1._.refs_0_.query_ref, bf16[128,640]{1,0:T(8,128)(2,1)S(1)} %rebuild.3.refs_0_.near_keys, bf16[128,640]{1,0:T(8,128)(2,1)S(1)} %rebuild.4.near_values, ...), custom_call_target="tpu_custom_call" | custom-call | bytes 1000 | tf_op jit(solution)/shard_map/attend/pallas_call | solution.py:283
  23.1 0.9 %collective-permute-start.11 = (bf16[2,176,128]{2,1,0:T(8,128)(2,1)S(1)}, bf16[2,176,128]{2,1,0:T(8,128)(2,1)S(1)}, u32[]{:S(2)}, u32[]{:S(2)}) collective-permute-start(bf16[2,176,128]{2,1,0:T(8,128)(2,1)S(1)} %get-tuple-element.31), channel_id=1, source_target_pairs={{0,2},{1,3},{2,0},{3,1},{4,6},{5,7},{6,4},{7,5},{8,10},{9,11},{10,... | collective-permute-start | bytes 270344 | tf_op jit(solution)/shard_map/ppermute | solution.py:27
  24.0 2.0 %collective-permute-start.9 = (bf16[1,176,128]{2,1,0:T(8,128)(2,1)S(1)}, bf16[1,176,128]{2,1,0:T(8,128)(2,1)S(1)}, u32[]{:S(2)}, u32[]{:S(2)}) collective-permute-start(bf16[1,176,128]{2,1,0:T(8,128)(2,1)S(1)} %get-tuple-element.30), channel_id=1, source_target_pairs={{0,1},{1,0},{2,3},{3,2},{4,5},{5,4},{6,7},{7,6},{8,9},{9,8},{10,11... | collective-permute-start | bytes 135176 | tf_op jit(solution)/shard_map/ppermute | solution.py:27
  26.0 1.1 %collective-permute-start.8 = (bf16[1,176,128]{2,1,0:T(8,128)(2,1)S(1)}, bf16[1,176,128]{2,1,0:T(8,128)(2,1)S(1)}, u32[]{:S(2)}, u32[]{:S(2)}) collective-permute-start(bf16[1,176,128]{2,1,0:T(8,128)(2,1)S(1)} %get-tuple-element.29), channel_id=1, source_target_pairs={{0,8},{1,9},{2,10},{3,11},{4,12},{5,13},{6,14},{7,15},{8,0},{9,1},... | collective-permute-start | bytes 135176 | tf_op jit(solution)/shard_map/ppermute | solution.py:27
  27.1 1.2 %collective-permute-done.12.both.f2 = bf16[2,176,128]{2,1,0:T(8,128)(2,1)S(1)} collective-permute-done((bf16[2,176,128]{2,1,0:T(8,128)(2,1)S(1)}, bf16[2,176,128]{2,1,0:T(8,128)(2,1)S(1)}, u32[]{:S(2)}, u32[]{:S(2)}) %collective-permute-start.12) | collective-permute-done | bytes 90144 | tf_op jit(solution)/shard_map/ppermute | solution.py:27
  28.2 0.3 %collective-permute-done.11.both.n2 = bf16[2,176,128]{2,1,0:T(8,128)(2,1)S(1)} collective-permute-done((bf16[2,176,128]{2,1,0:T(8,128)(2,1)S(1)}, bf16[2,176,128]{2,1,0:T(8,128)(2,1)S(1)}, u32[]{:S(2)}, u32[]{:S(2)}) %collective-permute-start.11) | collective-permute-done | bytes 90144 | tf_op jit(solution)/shard_map/ppermute | solution.py:27
  28.6 0.5 %collective-permute-start.14 = (bf16[176,128]{1,0:T(8,128)(2,1)S(1)}, bf16[176,128]{1,0:T(8,128)(2,1)S(1)}, u32[]{:S(2)}, u32[]{:S(2)}) collective-permute-start(bf16[176,128]{1,0:T(8,128)(2,1)S(1)} %pick.4.refs_0_), channel_id=1, source_target_pairs={{0,1},{1,0},{2,3},{3,2},{4,5},{5,4},{6,7},{7,6},{8,9},{9,8},{10,11... | collective-permute-start | bytes 135176 | tf_op jit(solution)/shard_map/ppermute | solution.py:27
  29.1 2.7 %collective-permute-done.8.array = bf16[1,176,128]{2,1,0:T(8,128)(2,1)S(1)} collective-permute-done((bf16[1,176,128]{2,1,0:T(8,128)(2,1)S(1)}, bf16[1,176,128]{2,1,0:T(8,128)(2,1)S(1)}, u32[]{:S(2)}, u32[]{:S(2)}) %collective-permute-start.8) | collective-permute-done | bytes 45088 | tf_op jit(solution)/shard_map/ppermute | solution.py:27
  31.8 0.3 mix.1.done
  32.1 0.9 %merge.1 = bf16[32,2560]{1,0:T(8,128)(2,1)} custom-call(bf16[1,176,128]{2,1,0:T(8,128)(2,1)S(1)} %get-tuple-element.28.n0, bf16[1,176,128]{2,1,0:T(8,128)(2,1)S(1)} %gate.3.f0, bf16[1,176,128]{2,1,0:T(8,128)(2,1)S(1)} %gate.4.n1, bf16[1,176,128]{2,1,0:T(8,128)(2,1)S(1)} %gate.5.f1, bf16[2,32,640]{2,1,0:T(8,128)(2,1)S(1)} %mix.1.done), custom_call_target="tpu_custom_call" | custom-call | bytes 1000 | tf_op jit(solution)/shard_map/merge/pallas_call | solution.py:352
  (27 shorter events, 0.9 us)
Async XLA Ops:
  1.1 1.7 %collective-permute-start = (bf16[3,2,32,640]{3,2,1,0:T(8,128)(2,1)S(1)}, bf16[3,2,32,640]{3,2,1,0:T(8,128)(2,1)S(1)}, u32[]{:S(2)}, u32[]{:S(2)}) collective-permute-start(bf16[3,2,32,640]{3,2,1,0:T(8,128)(2,1)S(1)} %get-tuple-element.20), channel_id=1, source_target_pairs={{0,1},{1,0},{2,3},{3,2},{4,5},{5,4},{6,7},{7,6},{8,9},{9,8},{10,11... | collective-permute-start | bytes 737288 | tf_op jit(solution)/shard_map/ppermute | solution.py:27
  2.8 5.1 %copy-start = (f32[512,20]{0,1:T(8,128)S(1)}, f32[512,20]{0,1:T(8,128)}, u32[]{:S(2)}) copy-start(f32[512,20]{0,1:T(8,128)} %param.12) | copy-start | bytes 122884
  2.8 5.1 %copy-start.1 = (f32[512,20]{0,1:T(8,128)S(1)}, f32[512,20]{0,1:T(8,128)}, u32[]{:S(2)}) copy-start(f32[512,20]{0,1:T(8,128)} %param.13) | copy-start | bytes 122884
  2.8 6.3 %collective-permute-start.1 = (bf16[64,640]{1,0:T(8,128)(2,1)S(1)}, bf16[64,640]{1,0:T(8,128)(2,1)S(1)}, u32[]{:S(2)}, u32[]{:S(2)}) collective-permute-start(bf16[64,640]{1,0:T(8,128)(2,1)S(1)} %get-tuple-element.21), channel_id=1, source_target_pairs={{0,2},{1,3},{2,0},{3,1},{4,6},{5,7},{6,4},{7,5},{8,10},{9,11},{10,... | collective-permute-start | bytes 245768 | tf_op jit(solution)/shard_map/ppermute | solution.py:27
  5.7 9.8 %collective-permute-start.5 = (bf16[2,64,640]{2,1,0:T(8,128)(2,1)S(1)}, bf16[2,64,640]{2,1,0:T(8,128)(2,1)S(1)}, u32[]{:S(2)}, u32[]{:S(2)}) collective-permute-start(bf16[2,64,640]{2,1,0:T(8,128)(2,1)S(1)} %get-tuple-element.25.this), channel_id=1, source_target_pairs={{0,4},{1,5},{2,6},{3,7},{4,0},{5,1},{6,2},{7,3},{8,12},{9,13},{10,... | collective-permute-start | bytes 491528 | tf_op jit(solution)/shard_map/ppermute | solution.py:27
  7.3 4.5 %collective-permute-start.2 = (bf16[64,640]{1,0:T(8,128)(2,1)S(1)}, bf16[64,640]{1,0:T(8,128)(2,1)S(1)}, u32[]{:S(2)}, u32[]{:S(2)}) collective-permute-start(bf16[64,640]{1,0:T(8,128)(2,1)S(1)} %get-tuple-element.22), channel_id=1, source_target_pairs={{0,2},{1,3},{2,0},{3,1},{4,6},{5,7},{6,4},{7,5},{8,10},{9,11},{10,... | collective-permute-start | bytes 245768 | tf_op jit(solution)/shard_map/ppermute | solution.py:27
  9.2 10.9 %collective-permute-start.7 = (bf16[128,640]{1,0:T(8,128)(2,1)S(1)}, bf16[128,640]{1,0:T(8,128)(2,1)S(1)}, u32[]{:S(2)}, u32[]{:S(2)}) collective-permute-start(bf16[128,640]{1,0:T(8,128)(2,1)S(1)} %assemble.1._.refs_0_.query_ref), channel_id=1, source_target_pairs={{0,8},{1,9},{2,10},{3,11},{4,12},{5,13},{6,14},{7,15},{8,0},{9,1},... | collective-permute-start | bytes 491528 | tf_op jit(solution)/shard_map/ppermute | solution.py:27
  12.0 8.2 %collective-permute-start.4 = (bf16[128,640]{1,0:T(8,128)(2,1)S(1)}, bf16[128,640]{1,0:T(8,128)(2,1)S(1)}, u32[]{:S(2)}, u32[]{:S(2)}) collective-permute-start(bf16[128,640]{1,0:T(8,128)(2,1)S(1)} %rebuild.3.refs_0_.near_keys), channel_id=1, source_target_pairs={{0,4},{1,5},{2,6},{3,7},{4,0},{5,1},{6,2},{7,3},{8,12},{9,13},{10,... | collective-permute-start | bytes 491528 | tf_op jit(solution)/shard_map/ppermute | solution.py:27
  13.7 4.4 %collective-permute-start.3 = (bf16[64,640]{1,0:T(8,128)(2,1)S(1)}, bf16[64,640]{1,0:T(8,128)(2,1)S(1)}, u32[]{:S(2)}, u32[]{:S(2)}) collective-permute-start(bf16[64,640]{1,0:T(8,128)(2,1)S(1)} %get-tuple-element.26), channel_id=1, source_target_pairs={{0,2},{1,3},{2,0},{3,1},{4,6},{5,7},{6,4},{7,5},{8,10},{9,11},{10,... | collective-permute-start | bytes 245768 | tf_op jit(solution)/shard_map/ppermute | solution.py:27
  15.6 4.5 %collective-permute-start.6 = (bf16[64,640]{1,0:T(8,128)(2,1)S(1)}, bf16[64,640]{1,0:T(8,128)(2,1)S(1)}, u32[]{:S(2)}, u32[]{:S(2)}) collective-permute-start(bf16[64,640]{1,0:T(8,128)(2,1)S(1)} %pick.3), channel_id=1, source_target_pairs={{0,2},{1,3},{2,0},{3,1},{4,6},{5,7},{6,4},{7,5},{8,10},{9,11},{10,... | collective-permute-start | bytes 245768 | tf_op jit(solution)/shard_map/ppermute | solution.py:27
  20.8 7.4 %collective-permute-start.12 = (bf16[2,176,128]{2,1,0:T(8,128)(2,1)S(1)}, bf16[2,176,128]{2,1,0:T(8,128)(2,1)S(1)}, u32[]{:S(2)}, u32[]{:S(2)}) collective-permute-start(bf16[2,176,128]{2,1,0:T(8,128)(2,1)S(1)} %get-tuple-element.32), channel_id=1, source_target_pairs={{0,10},{1,11},{2,8},{3,9},{4,14},{5,15},{6,12},{7,13},{8,2},{9,3},... | collective-permute-start | bytes 270344 | tf_op jit(solution)/shard_map/ppermute | solution.py:27
  23.1 5.5 %collective-permute-start.11 = (bf16[2,176,128]{2,1,0:T(8,128)(2,1)S(1)}, bf16[2,176,128]{2,1,0:T(8,128)(2,1)S(1)}, u32[]{:S(2)}, u32[]{:S(2)}) collective-permute-start(bf16[2,176,128]{2,1,0:T(8,128)(2,1)S(1)} %get-tuple-element.31), channel_id=1, source_target_pairs={{0,2},{1,3},{2,0},{3,1},{4,6},{5,7},{6,4},{7,5},{8,10},{9,11},{10,... | collective-permute-start | bytes 270344 | tf_op jit(solution)/shard_map/ppermute | solution.py:27
  24.0 7.8 %collective-permute-start.10 = (bf16[1,176,128]{2,1,0:T(8,128)(2,1)S(1)}, bf16[1,176,128]{2,1,0:T(8,128)(2,1)S(1)}, u32[]{:S(2)}, u32[]{:S(2)}) collective-permute-start(bf16[1,176,128]{2,1,0:T(8,128)(2,1)S(1)} %get-tuple-element.27.refs_0_), channel_id=1, source_target_pairs={{0,9},{1,8},{2,11},{3,10},{4,13},{5,12},{6,15},{7,14},{8,1},{9,0},... | collective-permute-start | bytes 135176 | tf_op jit(solution)/shard_map/ppermute | solution.py:27
  24.0 5.1 %collective-permute-start.9 = (bf16[1,176,128]{2,1,0:T(8,128)(2,1)S(1)}, bf16[1,176,128]{2,1,0:T(8,128)(2,1)S(1)}, u32[]{:S(2)}, u32[]{:S(2)}) collective-permute-start(bf16[1,176,128]{2,1,0:T(8,128)(2,1)S(1)} %get-tuple-element.30), channel_id=1, source_target_pairs={{0,1},{1,0},{2,3},{3,2},{4,5},{5,4},{6,7},{7,6},{8,9},{9,8},{10,11... | collective-permute-start | bytes 135176 | tf_op jit(solution)/shard_map/ppermute | solution.py:27
  26.0 5.8 %collective-permute-start.8 = (bf16[1,176,128]{2,1,0:T(8,128)(2,1)S(1)}, bf16[1,176,128]{2,1,0:T(8,128)(2,1)S(1)}, u32[]{:S(2)}, u32[]{:S(2)}) collective-permute-start(bf16[1,176,128]{2,1,0:T(8,128)(2,1)S(1)} %get-tuple-element.29), channel_id=1, source_target_pairs={{0,8},{1,9},{2,10},{3,11},{4,12},{5,13},{6,14},{7,15},{8,0},{9,1},... | collective-permute-start | bytes 135176 | tf_op jit(solution)/shard_map/ppermute | solution.py:27
  28.6 3.2 %collective-permute-start.13 = (bf16[176,128]{1,0:T(8,128)(2,1)S(1)}, bf16[176,128]{1,0:T(8,128)(2,1)S(1)}, u32[]{:S(2)}, u32[]{:S(2)}) collective-permute-start(bf16[176,128]{1,0:T(8,128)(2,1)S(1)} %pick.5), channel_id=1, source_target_pairs={{0,1},{1,0},{2,3},{3,2},{4,5},{5,4},{6,7},{7,6},{8,9},{9,8},{10,11... | collective-permute-start | bytes 135176 | tf_op jit(solution)/shard_map/ppermute | solution.py:27
  28.6 3.2 %collective-permute-start.14 = (bf16[176,128]{1,0:T(8,128)(2,1)S(1)}, bf16[176,128]{1,0:T(8,128)(2,1)S(1)}, u32[]{:S(2)}, u32[]{:S(2)}) collective-permute-start(bf16[176,128]{1,0:T(8,128)(2,1)S(1)} %pick.4.refs_0_), channel_id=1, source_target_pairs={{0,1},{1,0},{2,3},{3,2},{4,5},{5,4},{6,7},{7,6},{8,9},{9,8},{10,11... | collective-permute-start | bytes 135176 | tf_op jit(solution)/shard_map/ppermute | solution.py:27
